TPU v7x, 32 devices: a whole 2x2x4 slice. The times are simulated.
32 devices in a mesh: ctx: 16 (over z, y, core), head: 2 (over x).
Axes of the slice: x: 2, y: 2, z: 4, core: 2. Of those that a mesh axis runs over, the one named last changes fastest.
Arguments:
- query_raw: bfloat16 [2048, 4096], P('ctx', 'head'), may hold values from -6 to 6
- key_raw: bfloat16 [2048, 512], P('ctx', 'head'), may hold values from -6 to 6
- value_in: bfloat16 [2048, 512], P('ctx', 'head'), may hold values from -6 to 6
- grad_out: bfloat16 [2048, 4096], P('ctx', 'head'), may hold values from -16 to 16
- query_gain: float32 [128], replicated, may hold values from 0.25 to 1.75
- key_gain: float32 [128], replicated, may hold values from 0.25 to 1.75
- loss_table: float32 [16], replicated, may hold values from 0.5 to 8
- loss_bucket: int32 [2048], P('ctx'), may hold values from 0 to 15
- block_docs: int32 [16], P('ctx'), may hold values from 0 to 3, never falling along the last dimension, each value on 1 to 11 neighbouring positions
- query_weight: bfloat16 [4096, 4096], P(None, 'head'), may hold values from -0.09375 to 0.09375
Outputs:
- grad_input: bfloat16 [2048, 4096], P('ctx', 'head')
- grad_key: bfloat16 [2048, 512], P('ctx', 'head')
- grad_value: bfloat16 [2048, 512], P('ctx', 'head')
Inputs may be any that keep to these rules, and one draw needn't show every extreme that they name: `block_docs`: document ids never decrease along the sequence; every document covers 1 to 11 consecutive blocks, and some document covers exactly 11.
All inputs are finite; a program needn't handle non-finite values.
Results may differ from a plain program's by a relative error of at most 0.012.
Values may be sent and summed in bfloat16 or wider, within the bound.
No kernel may reach another device: no remote copies, remote signals or barrier semaphores. Data moves between devices by JAX's collectives and lax.ppermute only.
A program may use at most 64 MiB of HBM per device.

v0:
```python
import jax
import jax.numpy as jnp
from jax import lax
from jax.sharding import PartitionSpec as P

QH = 32
KVH = 4
HD = 128
BLOCK = 128
HOPS = 10
NBUCKET = 16


norm_eps = 1e-06


def passed_along(array, axis, by):
    size = lax.axis_size(axis)
    pairs = [(i, i + by) for i in range(size) if 0 <= i + by < size]
    return lax.ppermute(array, axis, pairs)


def rms_apply(values, gain):
    mean_square = jnp.mean(values * values, axis=-1, keepdims=True)
    return values * lax.rsqrt(mean_square + norm_eps) * gain


def rms_back(values, gain, cotangent):
    result, pullback = jax.vjp(lambda inner: rms_apply(inner, gain), values)
    return pullback(cotangent)[0]


def spread_docs(docs):
    return jnp.broadcast_to(docs[:, None], (docs.shape[0], BLOCK)).reshape(-1)


def local(
    query_raw,
    key_raw,
    value_in,
    grad_out,
    query_gain,
    key_gain,
    loss_table,
    loss_bucket,
    block_docs,
    query_weight,
):
    tokens = query_raw.shape[0]
    kv_local = key_raw.shape[1] // HD
    group = QH // KVH
    scale = HD ** (-0.5)
    rank = lax.axis_index("ctx")
    q_float = query_raw.astype(jnp.float32).reshape(tokens, kv_local, group, HD)
    q_hat = rms_apply(q_float, query_gain).astype(jnp.bfloat16)
    k_float = key_raw.astype(jnp.float32).reshape(tokens, kv_local, HD)
    k_hat = rms_apply(k_float, key_gain).astype(jnp.bfloat16)
    values = value_in.reshape(tokens, kv_local, HD)
    grad_rows = grad_out.reshape(tokens, kv_local, group, HD)
    picks = loss_bucket[:, None] == jnp.arange(NBUCKET, dtype=jnp.int32)[None, :]
    tok_weight = jnp.sum(jnp.where(picks, loss_table[None, :], 0.0), axis=1)
    offsets = jnp.arange(tokens, dtype=jnp.int32)
    q_pos = rank * tokens + offsets
    q_docs = spread_docs(block_docs)

    def block_scores(block, step):
        keys, block_values, docs = block
        source = rank - step
        k_pos = source * tokens + offsets
        allowed = (
            (q_docs[:, None] == spread_docs(docs)[None, :])
            & (k_pos[None, :] <= q_pos[:, None])
            & (source >= 0)
        )
        scores = (
            jnp.einsum("tkgd,skd->kgts", q_hat, keys, preferred_element_type=jnp.float32) * scale
        )
        return jnp.where(allowed[None, None], jnp.exp(scores), 0.0)

    def add_stats(block, step, total, weighted):
        exponent = block_scores(block, step)
        total = total + jnp.sum(exponent, axis=-1)
        weighted = weighted + jnp.einsum(
            "kgts,skd->tkgd",
            exponent.astype(jnp.bfloat16),
            block[1],
            preferred_element_type=jnp.float32,
        )
        return (total, weighted)

    def forward_step(carry, step):
        block, total, weighted = carry
        total, weighted = add_stats(block, step, total, weighted)
        moved = passed_along((block[0], block[1], block[2]), "ctx", 1)
        return ((moved, total, weighted), block)

    start_block = (k_hat, values, block_docs)
    zero_total = jnp.zeros((kv_local, group, tokens), jnp.float32)
    zero_weighted = jnp.zeros((tokens, kv_local, group, HD), jnp.float32)
    (last_block, total, weighted), stash = lax.scan(
        forward_step, (start_block, zero_total, zero_weighted), jnp.arange(HOPS, dtype=jnp.int32)
    )
    total, weighted = add_stats(last_block, HOPS, total, weighted)
    stash = tuple(
        (
            jnp.concatenate([earlier, final[None]], axis=0)
            for earlier, final in zip(stash, last_block)
        )
    )
    attn_out = weighted / jnp.transpose(total, (2, 0, 1))[..., None]
    delta = tok_weight[:, None, None] * jnp.sum(grad_rows.astype(jnp.float32) * attn_out, axis=-1)
    delta_kgt = jnp.transpose(delta, (1, 2, 0))
    weight_row = tok_weight[None, None, :, None]

    def block_grads(block, step):
        keys, block_values, docs = block
        exponent = block_scores(block, step)
        attention = exponent / total[..., None]
        value_dots = jnp.einsum(
            "tkgd,skd->kgts", grad_rows, block_values, preferred_element_type=jnp.float32
        )
        score_grad = attention * (weight_row * value_dots - delta_kgt[..., None])
        ds_half = score_grad.astype(jnp.bfloat16)
        pw_half = (attention * weight_row).astype(jnp.bfloat16)
        dv_part = jnp.einsum(
            "kgts,tkgd->skd", pw_half, grad_rows, preferred_element_type=jnp.float32
        )
        dk_part = (
            jnp.einsum("kgts,tkgd->skd", ds_half, q_hat, preferred_element_type=jnp.float32) * scale
        )
        dq_part = (
            jnp.einsum("kgts,skd->tkgd", ds_half, keys, preferred_element_type=jnp.float32) * scale
        )
        return ((dk_part, dv_part), dq_part)

    zero_kv = jnp.zeros((tokens, kv_local, HD), jnp.float32)
    dq_sum = zero_weighted
    dk_hat = zero_kv
    dv_sum = zero_kv
    for step in range(HOPS + 1):
        pieces, dq_part = block_grads(tuple((member[step] for member in stash)), step)
        dq_sum = dq_sum + dq_part
        if step > 0:
            pieces = (
                passed_along(pieces[0].astype(jnp.bfloat16), "ctx", -step).astype(jnp.float32),
                passed_along(pieces[1].astype(jnp.bfloat16), "ctx", -step).astype(jnp.float32),
            )
        dk_hat = dk_hat + pieces[0]
        dv_sum = dv_sum + pieces[1]
    dq_raw = (
        rms_back(q_float, query_gain, dq_sum)
        .astype(jnp.bfloat16)
        .reshape(tokens, kv_local * group * HD)
    )
    term = lax.dot_general(
        dq_raw, query_weight, (((1,), (1,)), ((), ())), preferred_element_type=jnp.float32
    )
    grad_input = lax.psum_scatter(
        term.astype(jnp.bfloat16), "head", scatter_dimension=1, tiled=True
    )
    grad_key = (
        rms_back(k_float, key_gain, dk_hat).astype(jnp.bfloat16).reshape(tokens, kv_local * HD)
    )
    grad_value = dv_sum.astype(jnp.bfloat16).reshape(tokens, kv_local * HD)
    return (grad_input, grad_key, grad_value)


def solution(mesh):
    placed = (
        P("ctx", "head"),
        P("ctx", "head"),
        P("ctx", "head"),
        P("ctx", "head"),
        P(),
        P(),
        P(),
        P("ctx"),
        P("ctx"),
        P(None, "head"),
    )
    return jax.shard_map(
        local,
        mesh=mesh,
        in_specs=placed,
        out_specs=(P("ctx", "head"), P("ctx", "head"), P("ctx", "head")),
        check_vma=False,
    )
```

profile of v0, /device:TPU:0, one launch (start us, length us, event | category | flops | bytes accessed | tf_op | source)
XLA Modules:
  0.0 321.5 jit_solution(9857710044519543708)
XLA Ops:
  16.6 168.3 %while.25 = (s32[]{:T(128)}, bf16[128,2,128]{2,0,1:T(8,128)(2,1)S(1)}, bf16[128,2,128]{2,0,1:T(8,128)(2,1)S(1)}, s32[1]{0:T(128)}, f32[2,8,128]{2,1,0:T(8,128)S(...) while((s32[]{:T(128)}, ...), condition=%wide.region_4.5_spmd.clone, body=%wide.region_2.0_spmd.clone.sunk | while | flops 135842048 | bytes 4917648 | solution.py:100
  16.6 3.3 %collective-permute-start.2 = (s32[1]{0:T(128)}, s32[1]{0:T(128)}, u32[]{:S(2)}, u32[]{:S(2)}) collective-permute-start(s32[1]{0:T(128)} %copy.442), channel_id=1, source_target_pairs={{0,2},{2,4},{4,6},{6,8},{8,10},{10,12},{12,14},{14,16},{16,18},{18... | collective-permute-start | bytes 20 | tf_op jit(solution)/shard_map/while/body/eval_jaxpr/ppermute | solution.py:20
  19.9 4.3 %collective-permute-start = (bf16[128,2,128]{2,0,1:T(8,128)(2,1)S(1)}, bf16[128,2,128]{2,0,1:T(8,128)(2,1)S(1)}, u32[]{:S(2)}, u32[]{:S(2)}) collective-permute-start(bf16[128,2,128]{2,0,1:T(8,128)(2,1)S(1)} %copy.440), channel_id=1, source_target_pairs={{0,2},{2,4},{4,6},{6,8},{8,10},{10,12},{12,14},{14,16},{16,18},{18... | collective-permute-start | bytes 196616 | tf_op jit(solution)/shard_map/while/body/eval_jaxpr/ppermute | solution.py:20
  24.3 2.1 collective-permute-start.1
  35.2 4.2 %collective-permute-start.2 = (s32[1]{0:T(128)}, s32[1]{0:T(128)}, u32[]{:S(2)}, u32[]{:S(2)}) collective-permute-start(s32[1]{0:T(128)} %copy.442), channel_id=1, source_target_pairs={{0,2},{2,4},{4,6},{6,8},{8,10},{10,12},{12,14},{14,16},{16,18},{18... | collective-permute-start | bytes 20 | tf_op jit(solution)/shard_map/while/body/eval_jaxpr/ppermute | solution.py:20
  39.4 1.9 collective-permute-start
  41.4 3.5 %collective-permute-start.1 = (bf16[128,2,128]{2,0,1:T(8,128)(2,1)S(1)}, bf16[128,2,128]{2,0,1:T(8,128)(2,1)S(1)}, u32[]{:S(2)}, u32[]{:S(2)}) collective-permute-start(bf16[128,2,128]{2,0,1:T(8,128)(2,1)S(1)} %copy.441), channel_id=1, source_target_pairs={{0,2},{2,4},{4,6},{6,8},{8,10},{10,12},{12,14},{14,16},{16,18},{18... | collective-permute-start | bytes 196616 | tf_op jit(solution)/shard_map/while/body/eval_jaxpr/ppermute | solution.py:20
  53.7 2.9 collective-permute-start.2
  56.6 3.3 %collective-permute-start = (bf16[128,2,128]{2,0,1:T(8,128)(2,1)S(1)}, bf16[128,2,128]{2,0,1:T(8,128)(2,1)S(1)}, u32[]{:S(2)}, u32[]{:S(2)}) collective-permute-start(bf16[128,2,128]{2,0,1:T(8,128)(2,1)S(1)} %copy.440), channel_id=1, source_target_pairs={{0,2},{2,4},{4,6},{6,8},{8,10},{10,12},{12,14},{14,16},{16,18},{18... | collective-permute-start | bytes 196616 | tf_op jit(solution)/shard_map/while/body/eval_jaxpr/ppermute | solution.py:20
  59.9 2.1 collective-permute-start.1
  70.9 4.2 %collective-permute-start.2 = (s32[1]{0:T(128)}, s32[1]{0:T(128)}, u32[]{:S(2)}, u32[]{:S(2)}) collective-permute-start(s32[1]{0:T(128)} %copy.442), channel_id=1, source_target_pairs={{0,2},{2,4},{4,6},{6,8},{8,10},{10,12},{12,14},{14,16},{16,18},{18... | collective-permute-start | bytes 20 | tf_op jit(solution)/shard_map/while/body/eval_jaxpr/ppermute | solution.py:20
  75.2 1.9 collective-permute-start
  77.1 3.5 %collective-permute-start.1 = (bf16[128,2,128]{2,0,1:T(8,128)(2,1)S(1)}, bf16[128,2,128]{2,0,1:T(8,128)(2,1)S(1)}, u32[]{:S(2)}, u32[]{:S(2)}) collective-permute-start(bf16[128,2,128]{2,0,1:T(8,128)(2,1)S(1)} %copy.441), channel_id=1, source_target_pairs={{0,2},{2,4},{4,6},{6,8},{8,10},{10,12},{12,14},{14,16},{16,18},{18... | collective-permute-start | bytes 196616 | tf_op jit(solution)/shard_map/while/body/eval_jaxpr/ppermute | solution.py:20
  89.5 2.9 collective-permute-start.2
  92.3 3.3 %collective-permute-start = (bf16[128,2,128]{2,0,1:T(8,128)(2,1)S(1)}, bf16[128,2,128]{2,0,1:T(8,128)(2,1)S(1)}, u32[]{:S(2)}, u32[]{:S(2)}) collective-permute-start(bf16[128,2,128]{2,0,1:T(8,128)(2,1)S(1)} %copy.440), channel_id=1, source_target_pairs={{0,2},{2,4},{4,6},{6,8},{8,10},{10,12},{12,14},{14,16},{16,18},{18... | collective-permute-start | bytes 196616 | tf_op jit(solution)/shard_map/while/body/eval_jaxpr/ppermute | solution.py:20
  95.7 2.2 collective-permute-start.1
  106.6 2.9 collective-permute-start.2
  109.5 1.9 collective-permute-start
  111.4 2.2 collective-permute-start.1
  122.4 2.9 collective-permute-start.2
  125.3 1.9 collective-permute-start
  127.2 2.2 collective-permute-start.1
  138.2 2.9 collective-permute-start.2
  141.1 1.7 collective-permute-start
  142.8 2.1 collective-permute-start.1
  153.8 2.9 collective-permute-start.2
  156.6 1.7 collective-permute-start
  158.3 2.1 collective-permute-start.1
  169.3 2.9 collective-permute-start.2
  172.2 1.7 collective-permute-start
  173.9 2.1 collective-permute-start.1
  184.9 1.7 fusion.240
  192.5 2.0 fusion.105
  230.5 12.7 %convolution_convert_fusion = bf16[128,4096]{1,0:T(8,128)(2,1)} fusion(bf16[128,2048]{0,1:T(8,128)(2,1)} %bitcast.755, bf16[4096,2048]{1,0:T(8,128)(2,1)} %param.21), kind=kOutput, calls=%fused_computation.18 | convolution fusion | flops 2148007936 | bytes 18350080 | tf_op jit(solution)/shard_map/dot_general | solution.py:155
  243.3 1.7 fusion.147
  248.0 1.5 fusion.144
  252.4 2.2 fusion.142
  254.6 1.6 fusion.153
  256.2 2.2 fusion.141
  259.0 1.5 fusion.140
  268.0 2.3 collective-permute-done.7
  271.6 1.7 collective-permute-done.8
  274.7 1.8 collective-permute-done.9
  277.7 7.7 %collective-permute-done.10 = bf16[128,2,128]{0,2,1:T(8,128)(2,1)S(1)} collective-permute-done((bf16[128,2,128]{0,2,1:T(8,128)(2,1)S(1)}, bf16[128,2,128]{0,2,1:T(8,128)(2,1)S(1)}, u32[]{:S(2)}, u32[]{:S(2)}) %collective-permute-start.10) | collective-permute-done | bytes 65568 | tf_op jit(solution)/shard_map/ppermute | solution.py:20
  298.3 2.7 collective-permute-done.18
  301.0 3.1 collective-permute-done.19
  304.1 8.0 %collective-permute-done.20 = bf16[128,2,128]{0,2,1:T(8,128)(2,1)S(1)} collective-permute-done((bf16[128,2,128]{0,2,1:T(8,128)(2,1)S(1)}, bf16[128,2,128]{0,2,1:T(8,128)(2,1)S(1)}, u32[]{:S(2)}, u32[]{:S(2)}) %collective-permute-start.20) | collective-permute-done | bytes 65568 | tf_op jit(solution)/shard_map/ppermute | solution.py:20
  312.3 1.5 add_convert_fusion
  (328 shorter events, 144.4 us)
Async XLA Ops:
  7.2 307.4 %reduce-scatter.2.cloned.1.call-start = ((), (), s32[]{:S(2)}) async-start(), calls=%async_computation.1 | async-start | bytes 1572864 | tf_op jit(solution)/shard_map/reduce_scatter | solution.py:158
  16.6 18.0 %collective-permute-start.2 = (s32[1]{0:T(128)}, s32[1]{0:T(128)}, u32[]{:S(2)}, u32[]{:S(2)}) collective-permute-start(s32[1]{0:T(128)} %copy.442), channel_id=1, source_target_pairs={{0,2},{2,4},{4,6},{6,8},{8,10},{10,12},{12,14},{14,16},{16,18},{18... | collective-permute-start | bytes 20 | tf_op jit(solution)/shard_map/while/body/eval_jaxpr/ppermute | solution.py:20
  19.9 14.7 %collective-permute-start = (bf16[128,2,128]{2,0,1:T(8,128)(2,1)S(1)}, bf16[128,2,128]{2,0,1:T(8,128)(2,1)S(1)}, u32[]{:S(2)}, u32[]{:S(2)}) collective-permute-start(bf16[128,2,128]{2,0,1:T(8,128)(2,1)S(1)} %copy.440), channel_id=1, source_target_pairs={{0,2},{2,4},{4,6},{6,8},{8,10},{10,12},{12,14},{14,16},{16,18},{18... | collective-permute-start | bytes 196616 | tf_op jit(solution)/shard_map/while/body/eval_jaxpr/ppermute | solution.py:20
  24.3 10.4 %collective-permute-start.1 = (bf16[128,2,128]{2,0,1:T(8,128)(2,1)S(1)}, bf16[128,2,128]{2,0,1:T(8,128)(2,1)S(1)}, u32[]{:S(2)}, u32[]{:S(2)}) collective-permute-start(bf16[128,2,128]{2,0,1:T(8,128)(2,1)S(1)} %copy.441), channel_id=1, source_target_pairs={{0,2},{2,4},{4,6},{6,8},{8,10},{10,12},{12,14},{14,16},{16,18},{18... | collective-permute-start | bytes 196616 | tf_op jit(solution)/shard_map/while/body/eval_jaxpr/ppermute | solution.py:20
  35.2 18.0 %collective-permute-start.2 = (s32[1]{0:T(128)}, s32[1]{0:T(128)}, u32[]{:S(2)}, u32[]{:S(2)}) collective-permute-start(s32[1]{0:T(128)} %copy.442), channel_id=1, source_target_pairs={{0,2},{2,4},{4,6},{6,8},{8,10},{10,12},{12,14},{14,16},{16,18},{18... | collective-permute-start | bytes 20 | tf_op jit(solution)/shard_map/while/body/eval_jaxpr/ppermute | solution.py:20
  39.4 13.7 %collective-permute-start = (bf16[128,2,128]{2,0,1:T(8,128)(2,1)S(1)}, bf16[128,2,128]{2,0,1:T(8,128)(2,1)S(1)}, u32[]{:S(2)}, u32[]{:S(2)}) collective-permute-start(bf16[128,2,128]{2,0,1:T(8,128)(2,1)S(1)} %copy.440), channel_id=1, source_target_pairs={{0,2},{2,4},{4,6},{6,8},{8,10},{10,12},{12,14},{14,16},{16,18},{18... | collective-permute-start | bytes 196616 | tf_op jit(solution)/shard_map/while/body/eval_jaxpr/ppermute | solution.py:20
  41.4 11.8 %collective-permute-start.1 = (bf16[128,2,128]{2,0,1:T(8,128)(2,1)S(1)}, bf16[128,2,128]{2,0,1:T(8,128)(2,1)S(1)}, u32[]{:S(2)}, u32[]{:S(2)}) collective-permute-start(bf16[128,2,128]{2,0,1:T(8,128)(2,1)S(1)} %copy.441), channel_id=1, source_target_pairs={{0,2},{2,4},{4,6},{6,8},{8,10},{10,12},{12,14},{14,16},{16,18},{18... | collective-permute-start | bytes 196616 | tf_op jit(solution)/shard_map/while/body/eval_jaxpr/ppermute | solution.py:20
  53.7 16.6 %collective-permute-start.2 = (s32[1]{0:T(128)}, s32[1]{0:T(128)}, u32[]{:S(2)}, u32[]{:S(2)}) collective-permute-start(s32[1]{0:T(128)} %copy.442), channel_id=1, source_target_pairs={{0,2},{2,4},{4,6},{6,8},{8,10},{10,12},{12,14},{14,16},{16,18},{18... | collective-permute-start | bytes 20 | tf_op jit(solution)/shard_map/while/body/eval_jaxpr/ppermute | solution.py:20
  56.6 13.7 %collective-permute-start = (bf16[128,2,128]{2,0,1:T(8,128)(2,1)S(1)}, bf16[128,2,128]{2,0,1:T(8,128)(2,1)S(1)}, u32[]{:S(2)}, u32[]{:S(2)}) collective-permute-start(bf16[128,2,128]{2,0,1:T(8,128)(2,1)S(1)} %copy.440), channel_id=1, source_target_pairs={{0,2},{2,4},{4,6},{6,8},{8,10},{10,12},{12,14},{14,16},{16,18},{18... | collective-permute-start | bytes 196616 | tf_op jit(solution)/shard_map/while/body/eval_jaxpr/ppermute | solution.py:20
  59.9 10.4 %collective-permute-start.1 = (bf16[128,2,128]{2,0,1:T(8,128)(2,1)S(1)}, bf16[128,2,128]{2,0,1:T(8,128)(2,1)S(1)}, u32[]{:S(2)}, u32[]{:S(2)}) collective-permute-start(bf16[128,2,128]{2,0,1:T(8,128)(2,1)S(1)} %copy.441), channel_id=1, source_target_pairs={{0,2},{2,4},{4,6},{6,8},{8,10},{10,12},{12,14},{14,16},{16,18},{18... | collective-permute-start | bytes 196616 | tf_op jit(solution)/shard_map/while/body/eval_jaxpr/ppermute | solution.py:20
  70.9 18.0 %collective-permute-start.2 = (s32[1]{0:T(128)}, s32[1]{0:T(128)}, u32[]{:S(2)}, u32[]{:S(2)}) collective-permute-start(s32[1]{0:T(128)} %copy.442), channel_id=1, source_target_pairs={{0,2},{2,4},{4,6},{6,8},{8,10},{10,12},{12,14},{14,16},{16,18},{18... | collective-permute-start | bytes 20 | tf_op jit(solution)/shard_map/while/body/eval_jaxpr/ppermute | solution.py:20
  75.2 13.8 %collective-permute-start = (bf16[128,2,128]{2,0,1:T(8,128)(2,1)S(1)}, bf16[128,2,128]{2,0,1:T(8,128)(2,1)S(1)}, u32[]{:S(2)}, u32[]{:S(2)}) collective-permute-start(bf16[128,2,128]{2,0,1:T(8,128)(2,1)S(1)} %copy.440), channel_id=1, source_target_pairs={{0,2},{2,4},{4,6},{6,8},{8,10},{10,12},{12,14},{14,16},{16,18},{18... | collective-permute-start | bytes 196616 | tf_op jit(solution)/shard_map/while/body/eval_jaxpr/ppermute | solution.py:20
  77.1 11.8 %collective-permute-start.1 = (bf16[128,2,128]{2,0,1:T(8,128)(2,1)S(1)}, bf16[128,2,128]{2,0,1:T(8,128)(2,1)S(1)}, u32[]{:S(2)}, u32[]{:S(2)}) collective-permute-start(bf16[128,2,128]{2,0,1:T(8,128)(2,1)S(1)} %copy.441), channel_id=1, source_target_pairs={{0,2},{2,4},{4,6},{6,8},{8,10},{10,12},{12,14},{14,16},{16,18},{18... | collective-permute-start | bytes 196616 | tf_op jit(solution)/shard_map/while/body/eval_jaxpr/ppermute | solution.py:20
  89.5 16.6 %collective-permute-start.2 = (s32[1]{0:T(128)}, s32[1]{0:T(128)}, u32[]{:S(2)}, u32[]{:S(2)}) collective-permute-start(s32[1]{0:T(128)} %copy.442), channel_id=1, source_target_pairs={{0,2},{2,4},{4,6},{6,8},{8,10},{10,12},{12,14},{14,16},{16,18},{18... | collective-permute-start | bytes 20 | tf_op jit(solution)/shard_map/while/body/eval_jaxpr/ppermute | solution.py:20
  92.3 13.7 %collective-permute-start = (bf16[128,2,128]{2,0,1:T(8,128)(2,1)S(1)}, bf16[128,2,128]{2,0,1:T(8,128)(2,1)S(1)}, u32[]{:S(2)}, u32[]{:S(2)}) collective-permute-start(bf16[128,2,128]{2,0,1:T(8,128)(2,1)S(1)} %copy.440), channel_id=1, source_target_pairs={{0,2},{2,4},{4,6},{6,8},{8,10},{10,12},{12,14},{14,16},{16,18},{18... | collective-permute-start | bytes 196616 | tf_op jit(solution)/shard_map/while/body/eval_jaxpr/ppermute | solution.py:20
  95.7 10.4 %collective-permute-start.1 = (bf16[128,2,128]{2,0,1:T(8,128)(2,1)S(1)}, bf16[128,2,128]{2,0,1:T(8,128)(2,1)S(1)}, u32[]{:S(2)}, u32[]{:S(2)}) collective-permute-start(bf16[128,2,128]{2,0,1:T(8,128)(2,1)S(1)} %copy.441), channel_id=1, source_target_pairs={{0,2},{2,4},{4,6},{6,8},{8,10},{10,12},{12,14},{14,16},{16,18},{18... | collective-permute-start | bytes 196616 | tf_op jit(solution)/shard_map/while/body/eval_jaxpr/ppermute | solution.py:20
  106.6 15.2 %collective-permute-start.2 = (s32[1]{0:T(128)}, s32[1]{0:T(128)}, u32[]{:S(2)}, u32[]{:S(2)}) collective-permute-start(s32[1]{0:T(128)} %copy.442), channel_id=1, source_target_pairs={{0,2},{2,4},{4,6},{6,8},{8,10},{10,12},{12,14},{14,16},{16,18},{18... | collective-permute-start | bytes 20 | tf_op jit(solution)/shard_map/while/body/eval_jaxpr/ppermute | solution.py:20
  109.5 12.3 %collective-permute-start = (bf16[128,2,128]{2,0,1:T(8,128)(2,1)S(1)}, bf16[128,2,128]{2,0,1:T(8,128)(2,1)S(1)}, u32[]{:S(2)}, u32[]{:S(2)}) collective-permute-start(bf16[128,2,128]{2,0,1:T(8,128)(2,1)S(1)} %copy.440), channel_id=1, source_target_pairs={{0,2},{2,4},{4,6},{6,8},{8,10},{10,12},{12,14},{14,16},{16,18},{18... | collective-permute-start | bytes 196616 | tf_op jit(solution)/shard_map/while/body/eval_jaxpr/ppermute | solution.py:20
  111.4 10.4 %collective-permute-start.1 = (bf16[128,2,128]{2,0,1:T(8,128)(2,1)S(1)}, bf16[128,2,128]{2,0,1:T(8,128)(2,1)S(1)}, u32[]{:S(2)}, u32[]{:S(2)}) collective-permute-start(bf16[128,2,128]{2,0,1:T(8,128)(2,1)S(1)} %copy.441), channel_id=1, source_target_pairs={{0,2},{2,4},{4,6},{6,8},{8,10},{10,12},{12,14},{14,16},{16,18},{18... | collective-permute-start | bytes 196616 | tf_op jit(solution)/shard_map/while/body/eval_jaxpr/ppermute | solution.py:20
  122.4 15.2 %collective-permute-start.2 = (s32[1]{0:T(128)}, s32[1]{0:T(128)}, u32[]{:S(2)}, u32[]{:S(2)}) collective-permute-start(s32[1]{0:T(128)} %copy.442), channel_id=1, source_target_pairs={{0,2},{2,4},{4,6},{6,8},{8,10},{10,12},{12,14},{14,16},{16,18},{18... | collective-permute-start | bytes 20 | tf_op jit(solution)/shard_map/while/body/eval_jaxpr/ppermute | solution.py:20
  125.3 12.3 %collective-permute-start = (bf16[128,2,128]{2,0,1:T(8,128)(2,1)S(1)}, bf16[128,2,128]{2,0,1:T(8,128)(2,1)S(1)}, u32[]{:S(2)}, u32[]{:S(2)}) collective-permute-start(bf16[128,2,128]{2,0,1:T(8,128)(2,1)S(1)} %copy.440), channel_id=1, source_target_pairs={{0,2},{2,4},{4,6},{6,8},{8,10},{10,12},{12,14},{14,16},{16,18},{18... | collective-permute-start | bytes 196616 | tf_op jit(solution)/shard_map/while/body/eval_jaxpr/ppermute | solution.py:20
  127.2 10.4 %collective-permute-start.1 = (bf16[128,2,128]{2,0,1:T(8,128)(2,1)S(1)}, bf16[128,2,128]{2,0,1:T(8,128)(2,1)S(1)}, u32[]{:S(2)}, u32[]{:S(2)}) collective-permute-start(bf16[128,2,128]{2,0,1:T(8,128)(2,1)S(1)} %copy.441), channel_id=1, source_target_pairs={{0,2},{2,4},{4,6},{6,8},{8,10},{10,12},{12,14},{14,16},{16,18},{18... | collective-permute-start | bytes 196616 | tf_op jit(solution)/shard_map/while/body/eval_jaxpr/ppermute | solution.py:20
  138.2 15.0 %collective-permute-start.2 = (s32[1]{0:T(128)}, s32[1]{0:T(128)}, u32[]{:S(2)}, u32[]{:S(2)}) collective-permute-start(s32[1]{0:T(128)} %copy.442), channel_id=1, source_target_pairs={{0,2},{2,4},{4,6},{6,8},{8,10},{10,12},{12,14},{14,16},{16,18},{18... | collective-permute-start | bytes 20 | tf_op jit(solution)/shard_map/while/body/eval_jaxpr/ppermute | solution.py:20
  141.1 12.1 %collective-permute-start = (bf16[128,2,128]{2,0,1:T(8,128)(2,1)S(1)}, bf16[128,2,128]{2,0,1:T(8,128)(2,1)S(1)}, u32[]{:S(2)}, u32[]{:S(2)}) collective-permute-start(bf16[128,2,128]{2,0,1:T(8,128)(2,1)S(1)} %copy.440), channel_id=1, source_target_pairs={{0,2},{2,4},{4,6},{6,8},{8,10},{10,12},{12,14},{14,16},{16,18},{18... | collective-permute-start | bytes 196616 | tf_op jit(solution)/shard_map/while/body/eval_jaxpr/ppermute | solution.py:20
  142.8 10.4 %collective-permute-start.1 = (bf16[128,2,128]{2,0,1:T(8,128)(2,1)S(1)}, bf16[128,2,128]{2,0,1:T(8,128)(2,1)S(1)}, u32[]{:S(2)}, u32[]{:S(2)}) collective-permute-start(bf16[128,2,128]{2,0,1:T(8,128)(2,1)S(1)} %copy.441), channel_id=1, source_target_pairs={{0,2},{2,4},{4,6},{6,8},{8,10},{10,12},{12,14},{14,16},{16,18},{18... | collective-permute-start | bytes 196616 | tf_op jit(solution)/shard_map/while/body/eval_jaxpr/ppermute | solution.py:20
  153.8 15.0 %collective-permute-start.2 = (s32[1]{0:T(128)}, s32[1]{0:T(128)}, u32[]{:S(2)}, u32[]{:S(2)}) collective-permute-start(s32[1]{0:T(128)} %copy.442), channel_id=1, source_target_pairs={{0,2},{2,4},{4,6},{6,8},{8,10},{10,12},{12,14},{14,16},{16,18},{18... | collective-permute-start | bytes 20 | tf_op jit(solution)/shard_map/while/body/eval_jaxpr/ppermute | solution.py:20
  156.6 12.1 %collective-permute-start = (bf16[128,2,128]{2,0,1:T(8,128)(2,1)S(1)}, bf16[128,2,128]{2,0,1:T(8,128)(2,1)S(1)}, u32[]{:S(2)}, u32[]{:S(2)}) collective-permute-start(bf16[128,2,128]{2,0,1:T(8,128)(2,1)S(1)} %copy.440), channel_id=1, source_target_pairs={{0,2},{2,4},{4,6},{6,8},{8,10},{10,12},{12,14},{14,16},{16,18},{18... | collective-permute-start | bytes 196616 | tf_op jit(solution)/shard_map/while/body/eval_jaxpr/ppermute | solution.py:20
  158.3 10.4 %collective-permute-start.1 = (bf16[128,2,128]{2,0,1:T(8,128)(2,1)S(1)}, bf16[128,2,128]{2,0,1:T(8,128)(2,1)S(1)}, u32[]{:S(2)}, u32[]{:S(2)}) collective-permute-start(bf16[128,2,128]{2,0,1:T(8,128)(2,1)S(1)} %copy.441), channel_id=1, source_target_pairs={{0,2},{2,4},{4,6},{6,8},{8,10},{10,12},{12,14},{14,16},{16,18},{18... | collective-permute-start | bytes 196616 | tf_op jit(solution)/shard_map/while/body/eval_jaxpr/ppermute | solution.py:20
  169.3 15.0 %collective-permute-start.2 = (s32[1]{0:T(128)}, s32[1]{0:T(128)}, u32[]{:S(2)}, u32[]{:S(2)}) collective-permute-start(s32[1]{0:T(128)} %copy.442), channel_id=1, source_target_pairs={{0,2},{2,4},{4,6},{6,8},{8,10},{10,12},{12,14},{14,16},{16,18},{18... | collective-permute-start | bytes 20 | tf_op jit(solution)/shard_map/while/body/eval_jaxpr/ppermute | solution.py:20
  172.2 12.1 %collective-permute-start = (bf16[128,2,128]{2,0,1:T(8,128)(2,1)S(1)}, bf16[128,2,128]{2,0,1:T(8,128)(2,1)S(1)}, u32[]{:S(2)}, u32[]{:S(2)}) collective-permute-start(bf16[128,2,128]{2,0,1:T(8,128)(2,1)S(1)} %copy.440), channel_id=1, source_target_pairs={{0,2},{2,4},{4,6},{6,8},{8,10},{10,12},{12,14},{14,16},{16,18},{18... | collective-permute-start | bytes 196616 | tf_op jit(solution)/shard_map/while/body/eval_jaxpr/ppermute | solution.py:20
  173.9 10.4 %collective-permute-start.1 = (bf16[128,2,128]{2,0,1:T(8,128)(2,1)S(1)}, bf16[128,2,128]{2,0,1:T(8,128)(2,1)S(1)}, u32[]{:S(2)}, u32[]{:S(2)}) collective-permute-start(bf16[128,2,128]{2,0,1:T(8,128)(2,1)S(1)} %copy.441), channel_id=1, source_target_pairs={{0,2},{2,4},{4,6},{6,8},{8,10},{10,12},{12,14},{14,16},{16,18},{18... | collective-permute-start | bytes 196616 | tf_op jit(solution)/shard_map/while/body/eval_jaxpr/ppermute | solution.py:20
  195.9 65.2 %collective-permute-start.12 = (bf16[128,2,128]{0,2,1:T(8,128)(2,1)S(1)}, bf16[128,2,128]{0,2,1:T(8,128)(2,1)S(1)}, u32[]{:S(2)}, u32[]{:S(2)}) collective-permute-start(bf16[128,2,128]{0,2,1:T(8,128)(2,1)S(1)} %fusion.157), channel_id=1, source_target_pairs={{20,0},{22,2},{24,4},{26,6},{28,8},{30,10},{21,1},{23,3},{25,5},{2... | collective-permute-start | bytes 196616 | tf_op jit(solution)/shard_map/ppermute | solution.py:20
  204.4 58.0 %collective-permute-start.3 = (bf16[128,2,128]{0,2,1:T(8,128)(2,1)}, bf16[128,2,128]{0,2,1:T(8,128)(2,1)}, u32[]{:S(2)}, u32[]{:S(2)}) collective-permute-start(bf16[128,2,128]{0,2,1:T(8,128)(2,1)} %fusion.148), channel_id=1, source_target_pairs={{2,0},{4,2},{6,4},{8,6},{10,8},{12,10},{14,12},{16,14},{18,16},{20... | collective-permute-start | bytes 196616 | tf_op jit(solution)/shard_map/ppermute | solution.py:20
  208.2 55.6 %collective-permute-start.4 = (bf16[128,2,128]{0,2,1:T(8,128)(2,1)}, bf16[128,2,128]{0,2,1:T(8,128)(2,1)}, u32[]{:S(2)}, u32[]{:S(2)}) collective-permute-start(bf16[128,2,128]{0,2,1:T(8,128)(2,1)} %fusion.149), channel_id=1, source_target_pairs={{4,0},{6,2},{8,4},{10,6},{12,8},{14,10},{16,12},{18,14},{20,16},{2... | collective-permute-start | bytes 196616 | tf_op jit(solution)/shard_map/ppermute | solution.py:20
  211.9 53.2 %collective-permute-start.5 = (bf16[128,2,128]{0,2,1:T(8,128)(2,1)}, bf16[128,2,128]{0,2,1:T(8,128)(2,1)}, u32[]{:S(2)}, u32[]{:S(2)}) collective-permute-start(bf16[128,2,128]{0,2,1:T(8,128)(2,1)} %fusion.150), channel_id=1, source_target_pairs={{6,0},{8,2},{10,4},{12,6},{14,8},{16,10},{18,12},{20,14},{22,16},{... | collective-permute-start | bytes 196616 | tf_op jit(solution)/shard_map/ppermute | solution.py:20
  214.8 51.6 %collective-permute-start.6 = (bf16[128,2,128]{0,2,1:T(8,128)(2,1)}, bf16[128,2,128]{0,2,1:T(8,128)(2,1)}, u32[]{:S(2)}, u32[]{:S(2)}) collective-permute-start(bf16[128,2,128]{0,2,1:T(8,128)(2,1)} %fusion.151), channel_id=1, source_target_pairs={{8,0},{10,2},{12,4},{14,6},{16,8},{18,10},{20,12},{22,14},{24,16},... | collective-permute-start | bytes 196616 | tf_op jit(solution)/shard_map/ppermute | solution.py:20
  261.2 9.2 %collective-permute-start.7 = (bf16[128,2,128]{0,2,1:T(8,128)(2,1)S(1)}, bf16[128,2,128]{0,2,1:T(8,128)(2,1)S(1)}, u32[]{:S(2)}, u32[]{:S(2)}) collective-permute-start(bf16[128,2,128]{0,2,1:T(8,128)(2,1)S(1)} %fusion.152), channel_id=1, source_target_pairs={{10,0},{12,2},{14,4},{16,6},{18,8},{20,10},{22,12},{24,14},{26,16}... | collective-permute-start | bytes 196616 | tf_op jit(solution)/shard_map/ppermute | solution.py:20
  262.5 10.9 %collective-permute-start.8 = (bf16[128,2,128]{0,2,1:T(8,128)(2,1)S(1)}, bf16[128,2,128]{0,2,1:T(8,128)(2,1)S(1)}, u32[]{:S(2)}, u32[]{:S(2)}) collective-permute-start(bf16[128,2,128]{0,2,1:T(8,128)(2,1)S(1)} %fusion.153), channel_id=1, source_target_pairs={{12,0},{14,2},{16,4},{18,6},{20,8},{22,10},{24,12},{26,14},{28,16}... | collective-permute-start | bytes 196616 | tf_op jit(solution)/shard_map/ppermute | solution.py:20
  263.8 12.6 %collective-permute-start.9 = (bf16[128,2,128]{0,2,1:T(8,128)(2,1)S(1)}, bf16[128,2,128]{0,2,1:T(8,128)(2,1)S(1)}, u32[]{:S(2)}, u32[]{:S(2)}) collective-permute-start(bf16[128,2,128]{0,2,1:T(8,128)(2,1)S(1)} %fusion.154), channel_id=1, source_target_pairs={{14,0},{16,2},{18,4},{20,6},{22,8},{24,10},{26,12},{28,14},{30,16}... | collective-permute-start | bytes 196616 | tf_op jit(solution)/shard_map/ppermute | solution.py:20
  265.1 20.3 %collective-permute-start.10 = (bf16[128,2,128]{0,2,1:T(8,128)(2,1)S(1)}, bf16[128,2,128]{0,2,1:T(8,128)(2,1)S(1)}, u32[]{:S(2)}, u32[]{:S(2)}) collective-permute-start(bf16[128,2,128]{0,2,1:T(8,128)(2,1)S(1)} %fusion.155), channel_id=1, source_target_pairs={{16,0},{18,2},{20,4},{22,6},{24,8},{26,10},{28,12},{30,14},{17,1},... | collective-permute-start | bytes 196616 | tf_op jit(solution)/shard_map/ppermute | solution.py:20
  266.4 20.3 %collective-permute-start.11 = (bf16[128,2,128]{0,2,1:T(8,128)(2,1)S(1)}, bf16[128,2,128]{0,2,1:T(8,128)(2,1)S(1)}, u32[]{:S(2)}, u32[]{:S(2)}) collective-permute-start(bf16[128,2,128]{0,2,1:T(8,128)(2,1)S(1)} %fusion.156), channel_id=1, source_target_pairs={{18,0},{20,2},{22,4},{24,6},{26,8},{28,10},{30,12},{19,1},{21,3},{... | collective-permute-start | bytes 196616 | tf_op jit(solution)/shard_map/ppermute | solution.py:20
  270.4 19.0 %collective-permute-start.22 = (bf16[128,2,128]{0,2,1:T(8,128)(2,1)S(1)}, bf16[128,2,128]{0,2,1:T(8,128)(2,1)S(1)}, u32[]{:S(2)}, u32[]{:S(2)}) collective-permute-start(bf16[128,2,128]{0,2,1:T(8,128)(2,1)S(1)} %fusion.138), channel_id=1, source_target_pairs={{20,0},{22,2},{24,4},{26,6},{28,8},{30,10},{21,1},{23,3},{25,5},{2... | collective-permute-start | bytes 196616 | tf_op jit(solution)/shard_map/ppermute | solution.py:20
  273.4 17.3 %collective-permute-start.13 = (bf16[128,2,128]{0,2,1:T(8,128)(2,1)S(1)}, bf16[128,2,128]{0,2,1:T(8,128)(2,1)S(1)}, u32[]{:S(2)}, u32[]{:S(2)}) collective-permute-start(bf16[128,2,128]{0,2,1:T(8,128)(2,1)S(1)} %fusion.147), channel_id=1, source_target_pairs={{2,0},{4,2},{6,4},{8,6},{10,8},{12,10},{14,12},{16,14},{18,16},{20... | collective-permute-start | bytes 196616 | tf_op jit(solution)/shard_map/ppermute | solution.py:20
  276.4 15.6 %collective-permute-start.14 = (bf16[128,2,128]{0,2,1:T(8,128)(2,1)S(1)}, bf16[128,2,128]{0,2,1:T(8,128)(2,1)S(1)}, u32[]{:S(2)}, u32[]{:S(2)}) collective-permute-start(bf16[128,2,128]{0,2,1:T(8,128)(2,1)S(1)} %fusion.146), channel_id=1, source_target_pairs={{4,0},{6,2},{8,4},{10,6},{12,8},{14,10},{16,12},{18,14},{20,16},{2... | collective-permute-start | bytes 196616 | tf_op jit(solution)/shard_map/ppermute | solution.py:20
  290.7 10.3 %collective-permute-start.18 = (bf16[128,2,128]{0,2,1:T(8,128)(2,1)}, bf16[128,2,128]{0,2,1:T(8,128)(2,1)S(1)}, u32[]{:S(2)}, u32[]{:S(2)}) collective-permute-start(bf16[128,2,128]{0,2,1:T(8,128)(2,1)} %fusion.142), channel_id=1, source_target_pairs={{12,0},{14,2},{16,4},{18,6},{20,8},{22,10},{24,12},{26,14},{28,16}... | collective-permute-start | bytes 196616 | tf_op jit(solution)/shard_map/ppermute | solution.py:20
  292.0 12.2 %collective-permute-start.19 = (bf16[128,2,128]{0,2,1:T(8,128)(2,1)}, bf16[128,2,128]{0,2,1:T(8,128)(2,1)S(1)}, u32[]{:S(2)}, u32[]{:S(2)}) collective-permute-start(bf16[128,2,128]{0,2,1:T(8,128)(2,1)} %fusion.141), channel_id=1, source_target_pairs={{14,0},{16,2},{18,4},{20,6},{22,8},{24,10},{26,12},{28,14},{30,16}... | collective-permute-start | bytes 196616 | tf_op jit(solution)/shard_map/ppermute | solution.py:20
  293.3 18.8 %collective-permute-start.20 = (bf16[128,2,128]{0,2,1:T(8,128)(2,1)S(1)}, bf16[128,2,128]{0,2,1:T(8,128)(2,1)S(1)}, u32[]{:S(2)}, u32[]{:S(2)}) collective-permute-start(bf16[128,2,128]{0,2,1:T(8,128)(2,1)S(1)} %fusion.140), channel_id=1, source_target_pairs={{16,0},{18,2},{20,4},{22,6},{24,8},{26,10},{28,12},{30,14},{17,1},... | collective-permute-start | bytes 196616 | tf_op jit(solution)/shard_map/ppermute | solution.py:20
  295.7 16.6 %collective-permute-start.21 = (bf16[128,2,128]{0,2,1:T(8,128)(2,1)S(1)}, bf16[128,2,128]{0,2,1:T(8,128)(2,1)S(1)}, u32[]{:S(2)}, u32[]{:S(2)}) collective-permute-start(bf16[128,2,128]{0,2,1:T(8,128)(2,1)S(1)} %fusion.139), channel_id=1, source_target_pairs={{18,0},{20,2},{22,4},{24,6},{26,8},{28,10},{30,12},{19,1},{21,3},{... | collective-permute-start | bytes 196616 | tf_op jit(solution)/shard_map/ppermute | solution.py:20
  (36 other events, 471.8 us)
Sparse Core Ops, SparseCore 0:
  243.4 27.0 reduce-scatter.1
where the time goes:
time: 325 us; the launch traced here: 321 us
  starting transfers between devices  106 us (33%)
  matrix products  74.9 us (23%)
  local copies, waits for them, and re-layouts  46.1 us (14%)
  waiting for transfers between devices  29.2 us (9%)
  other arithmetic  24.1 us (7%)
  between operations  22.2 us (7%)
  loops' own time  19.4 us (6%)
    ppermute x50, starting transfers between devices, passed_along(): return lax.ppermute(array, axis, pairs)  106 us
    ppermute x50, waiting for transfers between devices, passed_along(): return lax.ppermute(array, axis, pairs)  29.2 us
    dot_general x21, matrix products, block_scores(): jnp.einsum('tkgd,skd->kgts', q_hat, keys, preferred_element_type=jnp.floa...  21.5 us
    another operation x1, loops' own time, local(): lax.scan(forward_step, (start_block, zero_total, zero_weighted), jnp.aran...  19.4 us
    dynamic_update_slice x20, local copies, waits for them, and re-layouts, local(): lax.scan(forward_step, (start_block, zero_total, zero_weighted), jnp.aran...  19.2 us
    dot_general x11, matrix products, block_grads(): jnp.einsum('kgts,tkgd->skd', pw_half, grad_rows, preferred_element_type=j...  15.8 us
    dot_general x1, matrix products, local(): lax.dot_general(dq_raw, query_weight, (((1,), (1,)), ((), ())), preferred...  12.7 us
    dynamic_slice x10, local copies, waits for them, and re-layouts, local(): lax.scan(forward_step, (start_block, zero_total, zero_weighted), jnp.aran...  12.5 us
  transfers between devices with their start and end apart: 51, of which 10 were waited for; matrix products, arithmetic and copies ran while one was open for 39% of the time, Pallas kernels for 0%

commit v1 on v0

v1 whole, which is shorter than its diff:
```python
import functools
import math

import jax
import jax.numpy as jnp
from jax import lax
from jax.experimental import pallas as pl
from jax.experimental.pallas import tpu as pltpu
from jax.sharding import PartitionSpec as P

HD = 128
BLOCK = 128
EXTRA = 16
norm_eps = 1e-06
SCALE = HD ** (-0.5)
NEG = -1e30
NT = (((1,), (1,)), ((), ()))
F32 = jnp.float32
BF16 = jnp.bfloat16


def moved(array, axis, target):
    size = lax.axis_size(axis)
    pairs = [(i, target(i)) for i in range(size)]
    return lax.ppermute(array, axis, [(i, t) for i, t in pairs if t is not None and 0 <= t < size])


def vmem(shape=None):
    return pl.BlockSpec(memory_space=pltpu.VMEM)


def smem():
    return pl.BlockSpec(memory_space=pltpu.SMEM)


def params(mib):
    return pltpu.CompilerParams(vmem_limit_bytes=mib << 20)


def keys_kernel(kv_local, pos, docs, key, value, gain, bucket, keep, send):
    core = pos[0]
    mine = core if kv_local > 1 else 0
    for out, head in ((keep, mine), (send, (1 - core) if kv_local > 1 else 0)):
        lanes = pl.ds(pl.multiple_of(head * HD, HD), HD)
        raw = key[:, lanes].astype(F32)
        mean_square = jnp.mean(raw * raw, axis=-1, keepdims=True)
        out[:BLOCK, :HD] = (raw * lax.rsqrt(mean_square + norm_eps) * gain[...]).astype(BF16)
        out[:BLOCK, HD:] = value[:, lanes]
        row = lax.broadcasted_iota(jnp.int32, (EXTRA, HD), 0)
        doc = jnp.full((EXTRA, HD), docs[0] + 1, jnp.int32).astype(F32)
        buckets = jnp.broadcast_to(bucket[...].astype(F32), (EXTRA, HD))
        extra = jnp.where(row == 0, doc, jnp.where(row == 1, buckets, 0.0)).astype(BF16)
        out[BLOCK:, :HD] = extra
        out[BLOCK:, HD:] = extra


def join_kernel(keep, recv, out):
    out[:BLOCK, :] = keep[:BLOCK, :]
    out[BLOCK : 2 * BLOCK, :] = recv[:BLOCK, :]
    first = keep[BLOCK:, :].astype(F32)
    second = recv[BLOCK:, :].astype(F32)
    row = lax.broadcasted_iota(jnp.int32, (EXTRA, 2 * HD), 0)
    top = jnp.broadcast_to(first[0:1], (EXTRA, 2 * HD))
    next_row = jnp.broadcast_to(second[0:1], (EXTRA, 2 * HD))
    extra = jnp.where(row == 0, top, jnp.where(row == 1, next_row, 0.0))
    out[2 * BLOCK :, :] = extra.astype(BF16)


def split_kernel(half, pos, query, grad, out):
    other = pl.ds(pl.multiple_of((1 - pos[0]) * half, HD), half)
    out[:, :half] = query[:, other]
    out[:, half:] = grad[:, other]


def queries_kernel(
    heads, pos, table, query, grad, other, gain, keep, recv, q_hat, rows, raw_t, inverse_t, weight
):
    half = heads * HD
    own = pl.ds(pl.multiple_of(pos[0] * half, HD), half)
    for side in range(2):
        if side == 0:
            raw_all, grad_all = query[:, own], grad[:, own]
        else:
            raw_all, grad_all = other[:, :half], other[:, half:]
        for head in range(heads):
            at = (side * heads + head) * BLOCK
            raw = raw_all[:, head * HD : (head + 1) * HD].astype(F32)
            mean_square = jnp.mean(raw * raw, axis=-1, keepdims=True)
            q_hat[at : at + BLOCK, :] = (
                raw * lax.rsqrt(mean_square + norm_eps) * gain[...]
            ).astype(BF16)
            rows[at : at + BLOCK, :] = grad_all[:, head * HD : (head + 1) * HD]
            turned = raw.T
            raw_t[:, at : at + BLOCK] = turned.astype(BF16)
            mean_t = jnp.mean(turned * turned, axis=0, keepdims=True)
            inverse_t[:, at : at + BLOCK] = jnp.broadcast_to(
                lax.rsqrt(mean_t + norm_eps), (8, BLOCK)
            )
    for side, source in enumerate((keep, recv)):
        picks = source[BLOCK:, :HD].astype(F32)[1:2]
        found = jnp.zeros((1, HD), F32)
        for b in range(table.shape[0]):
            found = found + jnp.where(picks == float(b), table[b], 0.0)
        weight[:, side * HD : (side + 1) * HD] = jnp.broadcast_to(found, (8, HD))


def attention_kernel(
    heads,
    pos,
    own,
    far_a,
    far_b,
    far_c,
    far_d,
    far_e,
    q_hat,
    rows,
    raw_t,
    inverse_t,
    weight,
    gain,
    dq_keep,
    dq_send,
    part_own,
    part_a,
    part_b,
    part_c,
    part_d,
    part_e,
    keys,
    values,
    keys_t,
    expo,
    dots,
    pw_half,
    ds_half,
    dk,
    dv,
):
    core = pos[0]
    sources = (own, far_a, far_b, far_c, far_d, far_e)
    outs = (part_own, part_a, part_b, part_c, part_d, part_e)
    span = 2 * BLOCK
    wide = 2 * BLOCK
    total_rows = len(sources) * span
    for index, source in enumerate(sources):
        at = index * span
        block = source[:span, :HD]
        keys[at : at + span, :] = block
        values[at : at + span, :] = source[:span, HD:]
        keys_t[:, at : at + span] = block.astype(F32).T.astype(BF16)
    dk[...] = jnp.zeros_like(dk)
    dv[...] = jnp.zeros_like(dv)
    docs = [source[span:, :].astype(F32) for source in sources]
    own_docs = docs[0]
    row = lax.broadcasted_iota(jnp.int32, (BLOCK, wide), 0)
    col = lax.rem(lax.broadcasted_iota(jnp.int32, (BLOCK, wide), 1), BLOCK)
    triangle = row <= col
    factor = SCALE * math.log2(math.e)
    gain_t = gain[...]
    pairs = heads // 2

    for side in range(2):
        q_doc = own_docs[side : side + 1]
        bias = []
        for index in range(len(sources)):
            for block in range(2):
                k_doc = docs[index][block : block + 1]
                same = (k_doc == q_doc) & (k_doc > 0.0)
                if index == 0 and block != side:
                    later = (core == 1) if side == 0 else (core == 0)
                    same = same & later
                bias.append(jnp.where(same, 0.0, NEG))
        w_row = jnp.concatenate([weight[0:1, side * HD : (side + 1) * HD]] * 2, axis=1)

        def one_pair(pair, _, side=side, bias=bias, w_row=w_row):
            at = pl.multiple_of(side * heads * BLOCK + pair * wide, wide)
            here = pl.ds(at, wide)
            q_two = q_hat[here, :]
            g_two = rows[here, :]
            expo[...] = lax.dot_general(keys[...], q_two, NT, preferred_element_type=F32)
            dots[...] = lax.dot_general(values[...], g_two, NT, preferred_element_type=F32)
            total = jnp.zeros((8, wide), F32)
            weighted = jnp.zeros((8, wide), F32)
            for block in range(len(bias)):
                r = slice(block * BLOCK, (block + 1) * BLOCK)
                value = jnp.exp2(expo[r, :] * factor + bias[block])
                if block == side:
                    value = jnp.where(triangle, value, 0.0)
                expo[r, :] = value
                total = total + jnp.sum(value.reshape(BLOCK // 8, 8, wide), axis=0)
                weighted = weighted + jnp.sum(
                    (value * dots[r, :]).reshape(BLOCK // 8, 8, wide), axis=0
                )
            inverse = 1.0 / jnp.sum(total, axis=0, keepdims=True)
            shift = jnp.sum(weighted, axis=0, keepdims=True) * inverse
            level = inverse * w_row
            for block in range(len(bias)):
                r = slice(block * BLOCK, (block + 1) * BLOCK)
                scaled = expo[r, :] * level
                pw_half[r, :] = scaled.astype(BF16)
                ds_half[r, :] = (scaled * (dots[r, :] - shift)).astype(BF16)
            dv[...] += jnp.dot(pw_half[...], g_two, preferred_element_type=F32)
            dk[...] += jnp.dot(ds_half[...], q_two, preferred_element_type=F32)
            dq_t = jnp.dot(keys_t[...], ds_half[...], preferred_element_type=F32)
            x = raw_t[:, here].astype(F32)
            r_row = inverse_t[0:1, here]
            dy = dq_t * (gain_t * SCALE)
            inner = jnp.mean(x * dy, axis=0, keepdims=True)
            dx = r_row * dy - x * (r_row * r_row * r_row * inner)
            out = dq_keep if side == 0 else dq_send
            for part in range(2):
                lanes = pl.ds(pl.multiple_of(pair * wide + part * HD, HD), HD)
                out[:, lanes] = dx[:, part * BLOCK : (part + 1) * BLOCK].T.astype(BF16)
            return 0

        lax.fori_loop(0, pairs, one_pair, 0)

    for index, out in enumerate(outs):
        r = slice(index * span, (index + 1) * span)
        out[:, :HD] = (dk[r, :] * SCALE).astype(out.dtype)
        out[:, HD:] = dv[r, :].astype(out.dtype)


def project_kernel(half, pos, keep, recv, weight, out, lhs):
    @pl.when(pl.program_id(0) == 0)
    def _():
        core = pos[0]
        lhs[:, pl.ds(pl.multiple_of(core * half, HD), half)] = keep[...]
        lhs[:, pl.ds(pl.multiple_of((1 - core) * half, HD), half)] = recv[...]

    out[...] = lax.dot_general(
        lhs[...], weight[...], NT, preferred_element_type=F32
    ).astype(out.dtype)


def project(pos, keep, recv, query_weight, slice_index, width, out_dtype):
    tokens, half = keep.shape
    features = query_weight.shape[1]
    tile = min(512, width)
    steps = width // tile
    where = jnp.stack([pos[0], slice_index]).astype(jnp.int32)
    return pl.pallas_call(
        functools.partial(project_kernel, half),
        grid_spec=pltpu.PrefetchScalarGridSpec(
            num_scalar_prefetch=1,
            grid=(steps,),
            in_specs=[
                pl.BlockSpec((tokens, half), lambda i, w: (0, 0)),
                pl.BlockSpec((tokens, half), lambda i, w: (0, 0)),
                pl.BlockSpec((tile, features), lambda i, w: (w[1] * steps + i, 0)),
            ],
            out_specs=pl.BlockSpec((tokens, tile), lambda i, w: (0, i)),
            scratch_shapes=[pltpu.VMEM((tokens, features), BF16)],
        ),
        out_shape=jax.ShapeDtypeStruct((tokens, width), out_dtype),
        compiler_params=params(24),
        cost_estimate=pl.CostEstimate(
            flops=2 * tokens * features * width,
            bytes_accessed=2 * features * width,
            transcendentals=0,
        ),
    )(where, keep, recv, query_weight)


def collect_kernel(part_own, a, b, c, d, e, keep, send):
    result = part_own[...]
    for back in (a, b, c, d, e):
        result = result + back[...].astype(F32)
    keep[...] = result[:BLOCK]
    send[...] = result[BLOCK:].astype(BF16)


def finish_kernel(kv_local, pos, keep, recv, key, gain, grad_key, grad_value):
    core = pos[0]
    parts = []
    if kv_local > 1:
        parts = [(core, keep[...]), (1 - core, recv[...].astype(F32))]
    else:
        parts = [(0, keep[...] + recv[...].astype(F32))]
    for head, part in parts:
        lanes = pl.ds(pl.multiple_of(head * HD, HD), HD)
        raw = key[:, lanes].astype(F32)
        inverse = lax.rsqrt(jnp.mean(raw * raw, axis=-1, keepdims=True) + norm_eps)
        dy = part[:, :HD] * gain[...]
        inner = jnp.mean(raw * dy, axis=-1, keepdims=True)
        dx = inverse * dy - raw * (inverse * inverse * inverse * inner)
        grad_key[:, lanes] = dx.astype(BF16)
        grad_value[:, lanes] = part[:, HD:].astype(BF16)


def local(
    query_raw,
    key_raw,
    value_in,
    grad_out,
    query_gain,
    key_gain,
    loss_table,
    loss_bucket,
    block_docs,
    query_weight,
):
    tokens = query_raw.shape[0]
    kv_local = key_raw.shape[1] // HD
    half = query_raw.shape[1] // 2
    heads = half // HD
    rank = lax.axis_index("ctx")
    pos = jnp.stack([rank % 2]).astype(jnp.int32)
    key_row = key_gain.reshape(1, HD)
    query_row = query_gain.reshape(1, HD)
    query_col = query_gain.reshape(HD, 1)
    shape = jax.ShapeDtypeStruct

    keep, send = pl.pallas_call(
        functools.partial(keys_kernel, kv_local),
        in_specs=[smem(), smem(), vmem(), vmem(), vmem(), vmem()],
        out_specs=[vmem(), vmem()],
        out_shape=[shape((BLOCK + EXTRA, 2 * HD), BF16)] * 2,
    )(pos, block_docs, key_raw, value_in, key_row, loss_bucket.reshape(1, tokens))
    partner = lambda i: i ^ 1
    recv = moved(send, "ctx", partner)
    message = pl.pallas_call(
        join_kernel,
        in_specs=[vmem(), vmem()],
        out_specs=vmem(),
        out_shape=shape((2 * BLOCK + EXTRA, 2 * HD), BF16),
    )(keep, recv)

    far_d = moved(message, "ctx", lambda i: i + 8)
    far_b = moved(message, "ctx", lambda i: i + 4)
    far_a = moved(message, "ctx", lambda i: i + 2 if (i // 2) % 2 == 0 else i + 10)
    far_c = moved(far_b, "ctx", lambda i: i ^ 2)
    far_e = moved(far_d, "ctx", lambda i: i ^ 2)

    halves = pl.pallas_call(
        functools.partial(split_kernel, half),
        in_specs=[smem(), vmem(), vmem()],
        out_specs=vmem(),
        out_shape=shape((tokens, 2 * half), BF16),
    )(pos, query_raw, grad_out)
    other = moved(halves, "ctx", partner)
    total = 2 * heads * BLOCK
    q_hat, rows, raw_t, inverse_t, weight = pl.pallas_call(
        functools.partial(queries_kernel, heads),
        in_specs=[smem(), smem()] + [vmem()] * 6,
        out_specs=[vmem()] * 5,
        out_shape=[
            shape((total, HD), BF16),
            shape((total, HD), BF16),
            shape((HD, total), BF16),
            shape((8, total), F32),
            shape((8, 2 * HD), F32),
        ],
        compiler_params=params(24),
        cost_estimate=pl.CostEstimate(
            flops=20 * total * HD, bytes_accessed=12 * total * HD, transcendentals=0
        ),
    )(pos, loss_table, query_raw, grad_out, other, query_row, keep, recv)

    span = 2 * BLOCK
    n_rows = 6 * span
    far_shape = shape((span, 2 * HD), BF16)
    outs = pl.pallas_call(
        functools.partial(attention_kernel, heads),
        in_specs=[smem()] + [vmem()] * 12,
        out_specs=[vmem()] * 8,
        out_shape=[
            shape((tokens, half), BF16),
            shape((tokens, half), BF16),
            shape((span, 2 * HD), F32),
        ]
        + [far_shape] * 5,
        scratch_shapes=[
            pltpu.VMEM((n_rows, HD), BF16),
            pltpu.VMEM((n_rows, HD), BF16),
            pltpu.VMEM((HD, n_rows), BF16),
            pltpu.VMEM((n_rows, span), F32),
            pltpu.VMEM((n_rows, span), F32),
            pltpu.VMEM((n_rows, span), BF16),
            pltpu.VMEM((n_rows, span), BF16),
            pltpu.VMEM((n_rows, HD), F32),
            pltpu.VMEM((n_rows, HD), F32),
        ],
        compiler_params=params(32),
        cost_estimate=pl.CostEstimate(
            flops=10 * n_rows * total * HD,
            bytes_accessed=12 * total * HD,
            transcendentals=n_rows * total,
        ),
    )(
        pos,
        message,
        far_a,
        far_b,
        far_c,
        far_d,
        far_e,
        q_hat,
        rows,
        raw_t,
        inverse_t,
        weight,
        query_col,
    )
    dq_keep, dq_send, part_own, part_a, part_b, part_c, part_d, part_e = outs

    dq_recv = moved(dq_send, "ctx", partner)
    n_head = lax.axis_size("head")
    head = lax.axis_index("head")
    width = query_weight.shape[0] // n_head
    arrived = []
    for shift in range(1, n_head):
        term = project(
            pos, dq_keep, dq_recv, query_weight, (head + shift) % n_head, width, BF16
        )
        arrived.append(moved(term, "head", lambda i, s=shift: (i + s) % n_head))
    mine = project(pos, dq_keep, dq_recv, query_weight, head, width, F32)

    back_d = moved(part_d, "ctx", lambda i: i - 8)
    back_e = moved(part_e, "ctx", lambda i: (i ^ 2) - 8)
    back_c = moved(part_c, "ctx", lambda i: (i ^ 2) - 4)
    back_b = moved(part_b, "ctx", lambda i: i - 4)
    back_a = moved(part_a, "ctx", lambda i: i - 2 if (i // 2) % 2 == 1 else i - 10)
    sum_keep, sum_send = pl.pallas_call(
        collect_kernel,
        in_specs=[vmem()] * 6,
        out_specs=[vmem()] * 2,
        out_shape=[shape((BLOCK, 2 * HD), F32), shape((BLOCK, 2 * HD), BF16)],
    )(part_own, back_a, back_b, back_c, back_d, back_e)
    sum_recv = moved(sum_send, "ctx", partner)
    grad_key, grad_value = pl.pallas_call(
        functools.partial(finish_kernel, kv_local),
        in_specs=[smem()] + [vmem()] * 4,
        out_specs=[vmem()] * 2,
        out_shape=[shape(key_raw.shape, BF16), shape(value_in.shape, BF16)],
    )(pos, sum_keep, sum_recv, key_raw, key_row)

    grad_input = mine
    for piece in arrived:
        grad_input = grad_input + piece.astype(F32)
    return (grad_input.astype(BF16), grad_key, grad_value)


def solution(mesh):
    placed = (
        P("ctx", "head"),
        P("ctx", "head"),
        P("ctx", "head"),
        P("ctx", "head"),
        P(),
        P(),
        P(),
        P("ctx"),
        P("ctx"),
        P(None, "head"),
    )
    return jax.shard_map(
        local,
        mesh=mesh,
        in_specs=placed,
        out_specs=(P("ctx", "head"), P("ctx", "head"), P("ctx", "head")),
        check_vma=False,
    )
```

time: 325 us -> 105 us (0.32)
  starting transfers between devices: 106 us -> 23.5 us
  matrix products: 74.9 us -> 0 us
  Pallas kernels: 0 us -> 32 us
  local copies, waits for them, and re-layouts: 46.1 us -> 21 us
  other arithmetic: 24.1 us -> 1.05 us
  between operations: 22.2 us -> 1.51 us
  loops' own time: 19.4 us -> 0 us
  waiting for transfers between devices: 29.2 us -> 24.7 us
    ppermute x50 -> x15, starting transfers between devices: 106 us -> 23.5 us  [moved(): lax.ppermute(array, axis, [(i, t) for i, t in pairs if t is not None and...]
    dot_general x77 -> x0, matrix products: 74.9 us -> none  [the longest x21 21.5 us: block_scores(): jnp.einsum('tkgd,skd->kgts', q_hat, keys, preferred_element_type=jnp.floa...]
    pallas_call x0 -> x9, Pallas kernels: none -> 32 us  [the longest x1 14 us: local(): pl.pallas_call(functools.partial(attention_kernel, heads), in_specs=[smem...]
    another operation x1 -> x0, loops' own time: 19.4 us -> none  [local(): lax.scan(forward_step, (start_block, zero_total, zero_weighted), jnp.aran...]
    dynamic_update_slice x20 -> x0, local copies, waits for them, and re-layouts: 19.2 us -> none  [local(): lax.scan(forward_step, (start_block, zero_total, zero_weighted), jnp.aran...]
    dynamic_slice x10 -> x0, local copies, waits for them, and re-layouts: 12.5 us -> none  [local(): lax.scan(forward_step, (start_block, zero_total, zero_weighted), jnp.aran...]
    unnamed x73 -> x34, local copies, waits for them, and re-layouts: 8.6 us -> 20.3 us
    add x37 -> x0, other arithmetic: 11.2 us -> none  [the longest x11 5.71 us: local(): q_pos = rank * tokens + offsets]
  transfers between devices with their start and end apart: 51 -> 15, of which waited for: 10 -> 6; matrix products, arithmetic and copies ran while one was open for 39% -> 1% of each run, Pallas kernels for 0% -> 12%
where the time goes in v1:
time: 105 us; the launch traced here: 104 us
  Pallas kernels  32 us (30%)
  waiting for transfers between devices  24.7 us (24%)
  starting transfers between devices  23.5 us (22%)
  local copies, waits for them, and re-layouts  21 us (20%)
  between operations  1.51 us (1%)
  other arithmetic  1.05 us (1%)
    ppermute x15, waiting for transfers between devices, moved(): lax.ppermute(array, axis, [(i, t) for i, t in pairs if t is not None and...  24.7 us
    ppermute x15, starting transfers between devices, moved(): lax.ppermute(array, axis, [(i, t) for i, t in pairs if t is not None and...  23.5 us
    unnamed x34, local copies, waits for them, and re-layouts  20.3 us
    pallas_call x1, Pallas kernels, local(): pl.pallas_call(functools.partial(attention_kernel, heads), in_specs=[smem...  14 us
    pallas_call x2, Pallas kernels, project(): pl.pallas_call(functools.partial(project_kernel, half), grid_spec=pltpu.P...  8.02 us
  transfers between devices with their start and end apart: 15, of which 6 were waited for; matrix products, arithmetic and copies ran while one was open for 1% of the time, Pallas kernels for 12%

profile of v1, /device:TPU:0, one launch (start us, length us, event | category | flops | bytes accessed | tf_op | source)
XLA Modules:
  0.0 103.8 jit_solution(10166576146360817905)
XLA Ops:
  0.6 2.0 %shard_map.123 = bf16[128,2048]{1,0:T(8,128)(2,1)} custom-call(s32[1]{0:T(128)} %bitcast.pos, bf16[128,2048]{1,0:T(8,128)(2,1)} %query.3, bf16[128,2048]{1,0:T(8,128)(2,1)} %grad.3), custom_call_target="tpu_custom_call" | custom-call | tf_op jit(solution)/shard_map/pallas_call | solution.py:336
  2.7 0.5 collective-permute-start.6
  3.8 1.7 %shard_map.121 = (bf16[144,256]{1,0:T(8,128)(2,1)}, bf16[144,256]{1,0:T(8,128)(2,1)}) custom-call(s32[1]{0:T(128)} %bitcast.pos, s32[1]{0:T(128)S(6)} %copy.14.docs, bf16[128,256]{1,0:T(8,128)(2,1)} %key.3, bf16[128,256]{1,0:T(8,128)(2,1)} %value.1, f32[1,128]{1,0:T(1,128)} %bitcast.9, s32[1,128]{1,0:T(1,128)} %bitcast.11), custom_call_target="tpu_custom_call" | custom-call | tf_op jit(solution)/shard_map/pallas_call | solution.py:315
  5.4 0.1 collective-permute-start
  5.5 1.4 %collective-permute-done.recv = bf16[144,256]{1,0:T(8,128)(2,1)S(1)} collective-permute-done((bf16[144,256]{1,0:T(8,128)(2,1)}, bf16[144,256]{1,0:T(8,128)(2,1)S(1)}, u32[]{:S(2)}, u32[]{:S(2)}) %collective-permute-start) | collective-permute-done | bytes 73760 | tf_op jit(solution)/shard_map/ppermute | solution.py:25
  6.9 0.6 copy-done.5
  7.5 1.6 %shard_map.122.own = bf16[272,256]{1,0:T(8,128)(2,1)} custom-call(bf16[144,256]{1,0:T(8,128)(2,1)} %get-tuple-element.22.keep, bf16[144,256]{1,0:T(8,128)(2,1)} %copy-done.5), custom_call_target="tpu_custom_call" | custom-call | tf_op jit(solution)/shard_map/pallas_call | solution.py:323
  9.1 4.6 %collective-permute-start.2 = (bf16[272,256]{1,0:T(8,128)(2,1)}, bf16[272,256]{1,0:T(8,128)(2,1)S(1)}, u32[]{:S(2)}, u32[]{:S(2)}) collective-permute-start(bf16[272,256]{1,0:T(8,128)(2,1)} %shard_map.122.own), channel_id=1, source_target_pairs={{0,8},{2,10},{4,12},{6,14},{8,16},{10,18},{12,20},{14,22},{16,24},... | collective-permute-start | bytes 417800 | tf_op jit(solution)/shard_map/ppermute | solution.py:25
  13.8 4.5 %collective-permute-start.4 = (bf16[272,256]{1,0:T(8,128)(2,1)}, bf16[272,256]{1,0:T(8,128)(2,1)S(1)}, u32[]{:S(2)}, u32[]{:S(2)}) collective-permute-start(bf16[272,256]{1,0:T(8,128)(2,1)} %shard_map.122.own), channel_id=1, source_target_pairs={{0,16},{2,18},{4,20},{6,22},{8,24},{10,26},{12,28},{14,30},{1,17},... | collective-permute-start | bytes 417800 | tf_op jit(solution)/shard_map/ppermute | solution.py:25
  18.3 3.4 %collective-permute-start.1 = (bf16[272,256]{1,0:T(8,128)(2,1)}, bf16[272,256]{1,0:T(8,128)(2,1)S(1)}, u32[]{:S(2)}, u32[]{:S(2)}) collective-permute-start(bf16[272,256]{1,0:T(8,128)(2,1)} %shard_map.122.own), channel_id=1, source_target_pairs={{0,4},{2,6},{4,24},{6,26},{8,12},{10,14},{16,20},{18,22},{24,28},{... | collective-permute-start | bytes 417800 | tf_op jit(solution)/shard_map/ppermute | solution.py:25
  21.7 0.1 collective-permute-start.3
  21.8 2.4 %collective-permute-start.5 = (bf16[272,256]{1,0:T(8,128)(2,1)S(1)}, bf16[272,256]{1,0:T(8,128)(2,1)S(1)}, u32[]{:S(2)}, u32[]{:S(2)}) collective-permute-start(bf16[272,256]{1,0:T(8,128)(2,1)S(1)} %collective-permute-done.4.far_d), channel_id=1, source_target_pairs={{0,4},{2,6},{4,0},{6,2},{8,12},{10,14},{12,8},{14,10},{16,20},{18,... | collective-permute-start | bytes 417800 | tf_op jit(solution)/shard_map/ppermute | solution.py:25
  24.2 0.8 copy.13.gain
  25.0 1.0 copy-done.2
  26.0 1.0 %copy-done.3 = bf16[128,2048]{1,0:T(8,128)(2,1)S(1)} copy-done((bf16[128,2048]{1,0:T(8,128)(2,1)S(1)}, bf16[128,2048]{1,0:T(8,128)(2,1)}, u32[]{:S(2)}) %copy-start.3) | copy-done | bytes 524312
  27.0 0.9 copy-done.4
  27.9 0.9 copy-done.6
  28.8 0.7 copy-done.9
  29.5 0.7 copy-done.10
  30.1 1.1 %shard_map.124 = (bf16[2048,128]{1,0:T(8,128)(2,1)S(1)}, bf16[2048,128]{1,0:T(8,128)(2,1)S(1)}, bf16[128,2048]{1,0:T(8,128)(2,1)S(1)}, f32[8,2048]{1,0:T(8,128)S(1)}, f32[8,256]{1,0:T(8,128)S(1)}) custom-call(s32[1]{0:T(128)} %bitcast.pos, f32[16]{0:T(128)S(1)} %copy-done.10, bf16[128,2048]{1,0:T(8,128)(2,1)S(1)} %copy-done.2, ...), custom_call_target="tpu_custom_call" | custom-call | flops 5242880 | bytes 3145728 | tf_op jit(solution)/shard_map/pallas_call | solution.py:344
  31.3 0.9 copy-done.8
  32.2 14.0 %shard_map.125 = (bf16[128,1024]{1,0:T(8,128)(2,1)S(1)}, bf16[128,1024]{1,0:T(8,128)(2,1)S(1)}, f32[256,256]{1,0:T(8,128)S(1)}, bf16[256,256]{1,0:T(8,128)(2,1)S...) custom-call(s32[1]{0:T(128)} %bitcast.pos, ...), custom_call_target="tpu_custom_call" | custom-call | flops 4026531840 | bytes 3145728 | tf_op jit(solution)/shard_map/pallas_call | solution.py:364
  46.2 0.0 copy-start.7
  46.2 0.7 copy-done.7
  46.9 0.1 pad_add_fusion.1.pos
  46.9 1.5 %collective-permute-done.7.recv = bf16[128,1024]{1,0:T(8,128)(2,1)S(1)} collective-permute-done((bf16[128,1024]{1,0:T(8,128)(2,1)S(1)}, bf16[128,1024]{1,0:T(8,128)(2,1)S(1)}, u32[]{:S(2)}, u32[]{:S(2)}) %collective-permute-start.7) | collective-permute-done | bytes 262176 | tf_op jit(solution)/shard_map/ppermute | solution.py:25
  48.4 5.8 %copy-done = bf16[4096,2048]{1,0:T(8,128)(2,1)S(1)} copy-done((bf16[4096,2048]{1,0:T(8,128)(2,1)S(1)}, bf16[4096,2048]{1,0:T(8,128)(2,1)}, u32[]{:S(2)}) %copy-start) | copy-done | bytes 16777240
  54.2 4.0 %shard_map.127 = bf16[128,2048]{1,0:T(8,128)(2,1)S(1)} custom-call(s32[2]{0:T(128)S(1)} %pad_add_fusion.1.pos, bf16[128,1024]{1,0:T(8,128)(2,1)S(1)} %get-tuple-element.29.keep, bf16[128,1024]{1,0:T(8,128)(2,1)S(1)} %collective-permute-done.7.recv, bf16[4096,2048]{1,0:T(8,128)(2,1)S(1)} %copy-done), custom_call_target="tpu_custom_call" | custom-call | flops 1073741824 | bytes 8388608 | tf_op jit(solution)/shard_map/pallas_call | solution.py:243
  58.2 1.6 %collective-permute-start.8 = (bf16[128,2048]{1,0:T(8,128)(2,1)S(1)}, bf16[128,2048]{1,0:T(8,128)(2,1)S(1)}, u32[]{:S(2)}, u32[]{:S(2)}) collective-permute-start(bf16[128,2048]{1,0:T(8,128)(2,1)S(1)} %shard_map.127), channel_id=1, source_target_pairs={{0,1},{1,0},{2,3},{3,2},{4,5},{5,4},{6,7},{7,6},{8,9},{9,8},{10,11... | collective-permute-start | bytes 1572872 | tf_op jit(solution)/shard_map/ppermute | solution.py:25
  59.7 1.3 %collective-permute-start.10 = (bf16[256,256]{1,0:T(8,128)(2,1)S(1)}, bf16[256,256]{1,0:T(8,128)(2,1)S(1)}, u32[]{:S(2)}, u32[]{:S(2)}) collective-permute-start(bf16[256,256]{1,0:T(8,128)(2,1)S(1)} %get-tuple-element.33), channel_id=1, source_target_pairs={{8,0},{10,2},{12,4},{14,6},{16,8},{18,10},{20,12},{22,14},{24,16},... | collective-permute-start | bytes 393224 | tf_op jit(solution)/shard_map/ppermute | solution.py:25
  61.0 1.3 %collective-permute-start.11 = (bf16[256,256]{1,0:T(8,128)(2,1)S(1)}, bf16[256,256]{1,0:T(8,128)(2,1)S(1)}, u32[]{:S(2)}, u32[]{:S(2)}) collective-permute-start(bf16[256,256]{1,0:T(8,128)(2,1)S(1)} %get-tuple-element.34), channel_id=1, source_target_pairs={{8,4},{10,6},{12,0},{14,2},{16,12},{18,14},{20,8},{22,10},{24,20},... | collective-permute-start | bytes 393224 | tf_op jit(solution)/shard_map/ppermute | solution.py:25
  62.3 1.3 %collective-permute-start.12 = (bf16[256,256]{1,0:T(8,128)(2,1)S(1)}, bf16[256,256]{1,0:T(8,128)(2,1)S(1)}, u32[]{:S(2)}, u32[]{:S(2)}) collective-permute-start(bf16[256,256]{1,0:T(8,128)(2,1)S(1)} %get-tuple-element.35), channel_id=1, source_target_pairs={{16,0},{18,2},{20,4},{22,6},{24,8},{26,10},{28,12},{30,14},{17,1},... | collective-permute-start | bytes 393224 | tf_op jit(solution)/shard_map/ppermute | solution.py:25
  63.6 1.3 %collective-permute-start.13 = (bf16[256,256]{1,0:T(8,128)(2,1)S(1)}, bf16[256,256]{1,0:T(8,128)(2,1)S(1)}, u32[]{:S(2)}, u32[]{:S(2)}) collective-permute-start(bf16[256,256]{1,0:T(8,128)(2,1)S(1)} %get-tuple-element.36), channel_id=1, source_target_pairs={{16,4},{18,6},{20,0},{22,2},{24,12},{26,14},{28,8},{30,10},{17,5},... | collective-permute-start | bytes 393224 | tf_op jit(solution)/shard_map/ppermute | solution.py:25
  64.9 6.4 %collective-permute-done.10.b = bf16[256,256]{1,0:T(8,128)(2,1)S(1)} collective-permute-done((bf16[256,256]{1,0:T(8,128)(2,1)S(1)}, bf16[256,256]{1,0:T(8,128)(2,1)S(1)}, u32[]{:S(2)}, u32[]{:S(2)}) %collective-permute-start.10) | collective-permute-done | bytes 131104 | tf_op jit(solution)/shard_map/ppermute | solution.py:25
  71.3 1.3 %collective-permute-start.9 = (bf16[256,256]{1,0:T(8,128)(2,1)S(1)}, bf16[256,256]{1,0:T(8,128)(2,1)S(1)}, u32[]{:S(2)}, u32[]{:S(2)}) collective-permute-start(bf16[256,256]{1,0:T(8,128)(2,1)S(1)} %get-tuple-element.32), channel_id=1, source_target_pairs={{4,0},{6,2},{12,8},{14,10},{20,16},{22,18},{24,4},{26,6},{28,24},{... | collective-permute-start | bytes 393224 | tf_op jit(solution)/shard_map/ppermute | solution.py:25
  72.6 0.1 collective-permute-done.11.c
  72.8 13.9 %collective-permute-done.12.d = bf16[256,256]{1,0:T(8,128)(2,1)S(1)} collective-permute-done((bf16[256,256]{1,0:T(8,128)(2,1)S(1)}, bf16[256,256]{1,0:T(8,128)(2,1)S(1)}, u32[]{:S(2)}, u32[]{:S(2)}) %collective-permute-start.12) | collective-permute-done | bytes 131104 | tf_op jit(solution)/shard_map/ppermute | solution.py:25
  86.7 0.6 copy-done.13
  87.3 0.0 copy-done.14
  87.3 0.0 copy-done.15
  87.4 1.9 %shard_map.128 = (f32[128,256]{1,0:T(8,128)}, bf16[128,256]{1,0:T(8,128)(2,1)}) custom-call(f32[256,256]{1,0:T(8,128)} %copy-done.7, bf16[256,256]{1,0:T(8,128)(2,1)} %copy-done.15, bf16[256,256]{1,0:T(8,128)(2,1)} %copy-done.11, bf16[256,256]{1,0:T(8,128)(2,1)} %copy-done.12, bf16[256,256]{1,0:T(8,128)(2,1)} %copy-done.13, bf16[256,256]{1,0:T(8,128)(2,1)} %copy-done.14), custom_call_target="tpu_custom_call" | custom-call | tf_op jit(solution)/shard_map/pallas_call | solution.py:425
  89.3 0.1 pad_add_fusion.pos
  89.4 1.4 %collective-permute-done.14.recv = bf16[128,256]{1,0:T(8,128)(2,1)S(1)} collective-permute-done((bf16[128,256]{1,0:T(8,128)(2,1)}, bf16[128,256]{1,0:T(8,128)(2,1)S(1)}, u32[]{:S(2)}, u32[]{:S(2)}) %collective-permute-start.14) | collective-permute-done | bytes 65568 | tf_op jit(solution)/shard_map/ppermute | solution.py:25
  90.8 0.6 copy-done.16
  91.4 1.7 %shard_map.129 = (bf16[128,256]{1,0:T(8,128)(2,1)}, bf16[128,256]{1,0:T(8,128)(2,1)}) custom-call(s32[1]{0:T(128)} %bitcast.pos, f32[128,256]{1,0:T(8,128)} %get-tuple-element.37.keep, bf16[128,256]{1,0:T(8,128)(2,1)} %copy-done.16, bf16[128,256]{1,0:T(8,128)(2,1)} %key.3, f32[1,128]{1,0:T(1,128)} %bitcast.10), custom_call_target="tpu_custom_call" | custom-call | tf_op jit(solution)/shard_map/pallas_call | solution.py:432
  93.1 5.8 %copy-done.1 = bf16[4096,2048]{1,0:T(8,128)(2,1)S(1)} copy-done((bf16[4096,2048]{1,0:T(8,128)(2,1)S(1)}, bf16[4096,2048]{1,0:T(8,128)(2,1)}, u32[]{:S(2)}) %copy-start.1) | copy-done | bytes 16777240
  98.9 4.0 %shard_map.126 = f32[128,2048]{1,0:T(8,128)S(1)} custom-call(s32[2]{0:T(128)S(1)} %pad_add_fusion.pos, bf16[128,1024]{1,0:T(8,128)(2,1)S(1)} %get-tuple-element.29.keep, bf16[128,1024]{1,0:T(8,128)(2,1)S(1)} %collective-permute-done.7.recv, bf16[4096,2048]{1,0:T(8,128)(2,1)S(1)} %copy-done.1), custom_call_target="tpu_custom_call" | custom-call | flops 1073741824 | bytes 8388608 | tf_op jit(solution)/shard_map/pallas_call | solution.py:243
  102.9 0.9 add_convert_fusion
  (29 shorter events, 0.1 us)
Async XLA Ops:
  2.7 22.3 %collective-permute-start.6 = (bf16[128,2048]{1,0:T(8,128)(2,1)}, bf16[128,2048]{1,0:T(8,128)(2,1)S(1)}, u32[]{:S(2)}, u32[]{:S(2)}) collective-permute-start(bf16[128,2048]{1,0:T(8,128)(2,1)} %shard_map.123), channel_id=1, source_target_pairs={{0,2},{2,0},{4,6},{6,4},{8,10},{10,8},{12,14},{14,12},{16,18},{18,... | collective-permute-start | bytes 1572872 | tf_op jit(solution)/shard_map/ppermute | solution.py:25
  5.4 1.5 %collective-permute-start = (bf16[144,256]{1,0:T(8,128)(2,1)}, bf16[144,256]{1,0:T(8,128)(2,1)S(1)}, u32[]{:S(2)}, u32[]{:S(2)}) collective-permute-start(bf16[144,256]{1,0:T(8,128)(2,1)} %get-tuple-element.23), channel_id=1, source_target_pairs={{0,2},{2,0},{4,6},{6,4},{8,10},{10,8},{12,14},{14,12},{16,18},{18,... | collective-permute-start | bytes 221192 | tf_op jit(solution)/shard_map/ppermute | solution.py:25
  6.9 0.6 copy-start.5
  9.1 12.6 %collective-permute-start.2 = (bf16[272,256]{1,0:T(8,128)(2,1)}, bf16[272,256]{1,0:T(8,128)(2,1)S(1)}, u32[]{:S(2)}, u32[]{:S(2)}) collective-permute-start(bf16[272,256]{1,0:T(8,128)(2,1)} %shard_map.122.own), channel_id=1, source_target_pairs={{0,8},{2,10},{4,12},{6,14},{8,16},{10,18},{12,20},{14,22},{16,24},... | collective-permute-start | bytes 417800 | tf_op jit(solution)/shard_map/ppermute | solution.py:25
  13.8 8.0 %collective-permute-start.4 = (bf16[272,256]{1,0:T(8,128)(2,1)}, bf16[272,256]{1,0:T(8,128)(2,1)S(1)}, u32[]{:S(2)}, u32[]{:S(2)}) collective-permute-start(bf16[272,256]{1,0:T(8,128)(2,1)} %shard_map.122.own), channel_id=1, source_target_pairs={{0,16},{2,18},{4,20},{6,22},{8,24},{10,26},{12,28},{14,30},{1,17},... | collective-permute-start | bytes 417800 | tf_op jit(solution)/shard_map/ppermute | solution.py:25
  18.3 13.0 %collective-permute-start.1 = (bf16[272,256]{1,0:T(8,128)(2,1)}, bf16[272,256]{1,0:T(8,128)(2,1)S(1)}, u32[]{:S(2)}, u32[]{:S(2)}) collective-permute-start(bf16[272,256]{1,0:T(8,128)(2,1)} %shard_map.122.own), channel_id=1, source_target_pairs={{0,4},{2,6},{4,24},{6,26},{8,12},{10,14},{16,20},{18,22},{24,28},{... | collective-permute-start | bytes 417800 | tf_op jit(solution)/shard_map/ppermute | solution.py:25
  21.7 9.5 %collective-permute-start.3 = (bf16[272,256]{1,0:T(8,128)(2,1)S(1)}, bf16[272,256]{1,0:T(8,128)(2,1)S(1)}, u32[]{:S(2)}, u32[]{:S(2)}) collective-permute-start(bf16[272,256]{1,0:T(8,128)(2,1)S(1)} %collective-permute-done.2.far_b), channel_id=1, source_target_pairs={{0,4},{2,6},{4,0},{6,2},{8,12},{10,14},{12,8},{14,10},{16,20},{18,... | collective-permute-start | bytes 417800 | tf_op jit(solution)/shard_map/ppermute | solution.py:25
  21.8 9.5 %collective-permute-start.5 = (bf16[272,256]{1,0:T(8,128)(2,1)S(1)}, bf16[272,256]{1,0:T(8,128)(2,1)S(1)}, u32[]{:S(2)}, u32[]{:S(2)}) collective-permute-start(bf16[272,256]{1,0:T(8,128)(2,1)S(1)} %collective-permute-done.4.far_d), channel_id=1, source_target_pairs={{0,4},{2,6},{4,0},{6,2},{8,12},{10,14},{12,8},{14,10},{16,20},{18,... | collective-permute-start | bytes 417800 | tf_op jit(solution)/shard_map/ppermute | solution.py:25
  24.9 1.0 %copy-start.2 = (bf16[128,2048]{1,0:T(8,128)(2,1)S(1)}, bf16[128,2048]{1,0:T(8,128)(2,1)}, u32[]{:S(2)}) copy-start(bf16[128,2048]{1,0:T(8,128)(2,1)} %query.3) | copy-start | bytes 1572868
  26.0 1.0 %copy-start.3 = (bf16[128,2048]{1,0:T(8,128)(2,1)S(1)}, bf16[128,2048]{1,0:T(8,128)(2,1)}, u32[]{:S(2)}) copy-start(bf16[128,2048]{1,0:T(8,128)(2,1)} %grad.3) | copy-start | bytes 1572868
  27.0 0.9 copy-start.4
  27.9 0.9 copy-start.6
  28.8 0.7 copy-start.9
  29.5 0.7 copy-start.10
  31.3 0.9 copy-start.8
  46.2 0.7 copy-start.7
  46.9 1.5 %collective-permute-start.7 = (bf16[128,1024]{1,0:T(8,128)(2,1)S(1)}, bf16[128,1024]{1,0:T(8,128)(2,1)S(1)}, u32[]{:S(2)}, u32[]{:S(2)}) collective-permute-start(bf16[128,1024]{1,0:T(8,128)(2,1)S(1)} %get-tuple-element.30), channel_id=1, source_target_pairs={{0,2},{2,0},{4,6},{6,4},{8,10},{10,8},{12,14},{14,12},{16,18},{18,... | collective-permute-start | bytes 786440 | tf_op jit(solution)/shard_map/ppermute | solution.py:25
  48.4 5.8 %copy-start = (bf16[4096,2048]{1,0:T(8,128)(2,1)S(1)}, bf16[4096,2048]{1,0:T(8,128)(2,1)}, u32[]{:S(2)}) copy-start(bf16[4096,2048]{1,0:T(8,128)(2,1)} %weight.3) | copy-start | bytes 50331652
  58.2 44.7 %collective-permute-start.8 = (bf16[128,2048]{1,0:T(8,128)(2,1)S(1)}, bf16[128,2048]{1,0:T(8,128)(2,1)S(1)}, u32[]{:S(2)}, u32[]{:S(2)}) collective-permute-start(bf16[128,2048]{1,0:T(8,128)(2,1)S(1)} %shard_map.127), channel_id=1, source_target_pairs={{0,1},{1,0},{2,3},{3,2},{4,5},{5,4},{6,7},{7,6},{8,9},{9,8},{10,11... | collective-permute-start | bytes 1572872 | tf_op jit(solution)/shard_map/ppermute | solution.py:25
  59.7 11.6 %collective-permute-start.10 = (bf16[256,256]{1,0:T(8,128)(2,1)S(1)}, bf16[256,256]{1,0:T(8,128)(2,1)S(1)}, u32[]{:S(2)}, u32[]{:S(2)}) collective-permute-start(bf16[256,256]{1,0:T(8,128)(2,1)S(1)} %get-tuple-element.33), channel_id=1, source_target_pairs={{8,0},{10,2},{12,4},{14,6},{16,8},{18,10},{20,12},{22,14},{24,16},... | collective-permute-start | bytes 393224 | tf_op jit(solution)/shard_map/ppermute | solution.py:25
  61.0 11.7 %collective-permute-start.11 = (bf16[256,256]{1,0:T(8,128)(2,1)S(1)}, bf16[256,256]{1,0:T(8,128)(2,1)S(1)}, u32[]{:S(2)}, u32[]{:S(2)}) collective-permute-start(bf16[256,256]{1,0:T(8,128)(2,1)S(1)} %get-tuple-element.34), channel_id=1, source_target_pairs={{8,4},{10,6},{12,0},{14,2},{16,12},{18,14},{20,8},{22,10},{24,20},... | collective-permute-start | bytes 393224 | tf_op jit(solution)/shard_map/ppermute | solution.py:25
  62.3 24.3 %collective-permute-start.12 = (bf16[256,256]{1,0:T(8,128)(2,1)S(1)}, bf16[256,256]{1,0:T(8,128)(2,1)S(1)}, u32[]{:S(2)}, u32[]{:S(2)}) collective-permute-start(bf16[256,256]{1,0:T(8,128)(2,1)S(1)} %get-tuple-element.35), channel_id=1, source_target_pairs={{16,0},{18,2},{20,4},{22,6},{24,8},{26,10},{28,12},{30,14},{17,1},... | collective-permute-start | bytes 393224 | tf_op jit(solution)/shard_map/ppermute | solution.py:25
  63.6 23.0 %collective-permute-start.13 = (bf16[256,256]{1,0:T(8,128)(2,1)S(1)}, bf16[256,256]{1,0:T(8,128)(2,1)S(1)}, u32[]{:S(2)}, u32[]{:S(2)}) collective-permute-start(bf16[256,256]{1,0:T(8,128)(2,1)S(1)} %get-tuple-element.36), channel_id=1, source_target_pairs={{16,4},{18,6},{20,0},{22,2},{24,12},{26,14},{28,8},{30,10},{17,5},... | collective-permute-start | bytes 393224 | tf_op jit(solution)/shard_map/ppermute | solution.py:25
  71.3 15.3 %copy-start.11 = (bf16[256,256]{1,0:T(8,128)(2,1)}, bf16[256,256]{1,0:T(8,128)(2,1)S(1)}, u32[]{:S(2)}) copy-start(bf16[256,256]{1,0:T(8,128)(2,1)S(1)} %collective-permute-done.10.b) | copy-start | bytes 393220
  71.3 15.3 %collective-permute-start.9 = (bf16[256,256]{1,0:T(8,128)(2,1)S(1)}, bf16[256,256]{1,0:T(8,128)(2,1)S(1)}, u32[]{:S(2)}, u32[]{:S(2)}) collective-permute-start(bf16[256,256]{1,0:T(8,128)(2,1)S(1)} %get-tuple-element.32), channel_id=1, source_target_pairs={{4,0},{6,2},{12,8},{14,10},{20,16},{22,18},{24,4},{26,6},{28,24},{... | collective-permute-start | bytes 393224 | tf_op jit(solution)/shard_map/ppermute | solution.py:25
  72.8 13.9 %copy-start.12 = (bf16[256,256]{1,0:T(8,128)(2,1)}, bf16[256,256]{1,0:T(8,128)(2,1)S(1)}, u32[]{:S(2)}) copy-start(bf16[256,256]{1,0:T(8,128)(2,1)S(1)} %collective-permute-done.11.c) | copy-start | bytes 393220
  86.6 0.6 copy-start.13
  86.6 0.7 copy-start.14
  86.7 0.7 copy-start.15
  89.3 1.5 %collective-permute-start.14 = (bf16[128,256]{1,0:T(8,128)(2,1)}, bf16[128,256]{1,0:T(8,128)(2,1)S(1)}, u32[]{:S(2)}, u32[]{:S(2)}) collective-permute-start(bf16[128,256]{1,0:T(8,128)(2,1)} %get-tuple-element.38), channel_id=1, source_target_pairs={{0,2},{2,0},{4,6},{6,4},{8,10},{10,8},{12,14},{14,12},{16,18},{18,... | collective-permute-start | bytes 196616 | tf_op jit(solution)/shard_map/ppermute | solution.py:25
  90.8 0.6 copy-start.16
  93.1 5.8 %copy-start.1 = (bf16[4096,2048]{1,0:T(8,128)(2,1)S(1)}, bf16[4096,2048]{1,0:T(8,128)(2,1)}, u32[]{:S(2)}) copy-start(bf16[4096,2048]{1,0:T(8,128)(2,1)} %weight.3) | copy-start | bytes 50331652

commit v2 on v1

--- a/solution.py
+++ b/solution.py
@@ -25,8 +25,12 @@
     return lax.ppermute(array, axis, [(i, t) for i, t in pairs if t is not None and 0 <= t < size])
 
 
-def vmem(shape=None):
+def vmem():
     return pl.BlockSpec(memory_space=pltpu.VMEM)
+
+
+def hbm():
+    return pl.BlockSpec(memory_space=pltpu.HBM)
 
 
 def smem():
@@ -37,57 +41,78 @@
     return pltpu.CompilerParams(vmem_limit_bytes=mib << 20)
 
 
-def keys_kernel(kv_local, pos, docs, key, value, gain, bucket, keep, send):
-    core = pos[0]
-    mine = core if kv_local > 1 else 0
-    for out, head in ((keep, mine), (send, (1 - core) if kv_local > 1 else 0)):
-        lanes = pl.ds(pl.multiple_of(head * HD, HD), HD)
-        raw = key[:, lanes].astype(F32)
+def message_kernel(
+    kv_local, docs, docs_p, key, value, gain, key_p, value_p, out, key_v, value_v, gain_v, sems
+):
+    core = lax.rem(lax.axis_index("ctx"), 2)
+    lanes = pl.ds(pl.multiple_of((core if kv_local > 1 else 0) * HD, HD), HD)
+    copies = [
+        pltpu.make_async_copy(source, target, sems.at[i])
+        for i, (source, target) in enumerate(
+            ((key.at[:, lanes], key_v), (value.at[:, lanes], value_v), (gain, gain_v))
+        )
+    ]
+    for copy in copies:
+        copy.start()
+    for copy in copies:
+        copy.wait()
+    for side in range(2):
+        at = side * BLOCK
+        raw = (key_v[...] if side == 0 else key_p[:, lanes]).astype(F32)
         mean_square = jnp.mean(raw * raw, axis=-1, keepdims=True)
-        out[:BLOCK, :HD] = (raw * lax.rsqrt(mean_square + norm_eps) * gain[...]).astype(BF16)
-        out[:BLOCK, HD:] = value[:, lanes]
-        row = lax.broadcasted_iota(jnp.int32, (EXTRA, HD), 0)
-        doc = jnp.full((EXTRA, HD), docs[0] + 1, jnp.int32).astype(F32)
-        buckets = jnp.broadcast_to(bucket[...].astype(F32), (EXTRA, HD))
-        extra = jnp.where(row == 0, doc, jnp.where(row == 1, buckets, 0.0)).astype(BF16)
-        out[BLOCK:, :HD] = extra
-        out[BLOCK:, HD:] = extra
-
-
-def join_kernel(keep, recv, out):
-    out[:BLOCK, :] = keep[:BLOCK, :]
-    out[BLOCK : 2 * BLOCK, :] = recv[:BLOCK, :]
-    first = keep[BLOCK:, :].astype(F32)
-    second = recv[BLOCK:, :].astype(F32)
+        out[at : at + BLOCK, :HD] = (
+            raw * lax.rsqrt(mean_square + norm_eps) * gain_v[...]
+        ).astype(BF16)
+        out[at : at + BLOCK, HD:] = value_v[...] if side == 0 else value_p[:, lanes]
     row = lax.broadcasted_iota(jnp.int32, (EXTRA, 2 * HD), 0)
-    top = jnp.broadcast_to(first[0:1], (EXTRA, 2 * HD))
-    next_row = jnp.broadcast_to(second[0:1], (EXTRA, 2 * HD))
-    extra = jnp.where(row == 0, top, jnp.where(row == 1, next_row, 0.0))
-    out[2 * BLOCK :, :] = extra.astype(BF16)
-
-
-def split_kernel(half, pos, query, grad, out):
-    other = pl.ds(pl.multiple_of((1 - pos[0]) * half, HD), half)
-    out[:, :half] = query[:, other]
-    out[:, half:] = grad[:, other]
+    extra = jnp.where(row == 0, docs[0] + 1, jnp.where(row == 1, docs_p[0] + 1, 0))
+    out[2 * BLOCK :, :] = extra.astype(F32).astype(BF16)
 
 
 def queries_kernel(
-    heads, pos, table, query, grad, other, gain, keep, recv, q_hat, rows, raw_t, inverse_t, weight
+    heads,
+    table,
+    bucket,
+    bucket_p,
+    query,
+    grad,
+    gain,
+    query_p,
+    grad_p,
+    q_hat,
+    rows,
+    raw_t,
+    inverse_t,
+    weight,
+    query_v,
+    grad_v,
+    gain_v,
+    sems,
 ):
     half = heads * HD
-    own = pl.ds(pl.multiple_of(pos[0] * half, HD), half)
+    core = lax.rem(lax.axis_index("ctx"), 2)
+    own = pl.ds(pl.multiple_of(core * half, HD), half)
+    copies = [
+        pltpu.make_async_copy(source, target, sems.at[i])
+        for i, (source, target) in enumerate(
+            ((query.at[:, own], query_v), (grad.at[:, own], grad_v), (gain, gain_v))
+        )
+    ]
+    for copy in copies:
+        copy.start()
+    for copy in copies:
+        copy.wait()
     for side in range(2):
         if side == 0:
-            raw_all, grad_all = query[:, own], grad[:, own]
+            raw_all, grad_all = query_v[...], grad_v[...]
         else:
-            raw_all, grad_all = other[:, :half], other[:, half:]
+            raw_all, grad_all = query_p[:, own], grad_p[:, own]
         for head in range(heads):
             at = (side * heads + head) * BLOCK
             raw = raw_all[:, head * HD : (head + 1) * HD].astype(F32)
             mean_square = jnp.mean(raw * raw, axis=-1, keepdims=True)
             q_hat[at : at + BLOCK, :] = (
-                raw * lax.rsqrt(mean_square + norm_eps) * gain[...]
+                raw * lax.rsqrt(mean_square + norm_eps) * gain_v[...]
             ).astype(BF16)
             rows[at : at + BLOCK, :] = grad_all[:, head * HD : (head + 1) * HD]
             turned = raw.T
@@ -96,17 +121,16 @@
             inverse_t[:, at : at + BLOCK] = jnp.broadcast_to(
                 lax.rsqrt(mean_t + norm_eps), (8, BLOCK)
             )
-    for side, source in enumerate((keep, recv)):
-        picks = source[BLOCK:, :HD].astype(F32)[1:2]
+    for side, source in enumerate((bucket, bucket_p)):
+        picks = source[...]
         found = jnp.zeros((1, HD), F32)
         for b in range(table.shape[0]):
-            found = found + jnp.where(picks == float(b), table[b], 0.0)
+            found = found + jnp.where(picks == b, table[b], 0.0)
         weight[:, side * HD : (side + 1) * HD] = jnp.broadcast_to(found, (8, HD))
 
 
 def attention_kernel(
     heads,
-    pos,
     own,
     far_a,
     far_b,
@@ -137,7 +161,7 @@
     dk,
     dv,
 ):
-    core = pos[0]
+    core = lax.rem(lax.axis_index("ctx"), 2)
     sources = (own, far_a, far_b, far_c, far_d, far_e)
     outs = (part_own, part_a, part_b, part_c, part_d, part_e)
     span = 2 * BLOCK
@@ -210,8 +234,8 @@
             dx = r_row * dy - x * (r_row * r_row * r_row * inner)
             out = dq_keep if side == 0 else dq_send
             for part in range(2):
-                lanes = pl.ds(pl.multiple_of(pair * wide + part * HD, HD), HD)
-                out[:, lanes] = dx[:, part * BLOCK : (part + 1) * BLOCK].T.astype(BF16)
+                features = pl.ds(pl.multiple_of(pair * wide + part * HD, HD), HD)
+                out[features, :] = dx[:, part * BLOCK : (part + 1) * BLOCK].astype(BF16)
             return 0
 
         lax.fori_loop(0, pairs, one_pair, 0)
@@ -222,37 +246,40 @@
         out[:, HD:] = dv[r, :].astype(out.dtype)
 
 
-def project_kernel(half, pos, keep, recv, weight, out, lhs):
-    @pl.when(pl.program_id(0) == 0)
-    def _():
-        core = pos[0]
-        lhs[:, pl.ds(pl.multiple_of(core * half, HD), half)] = keep[...]
-        lhs[:, pl.ds(pl.multiple_of((1 - core) * half, HD), half)] = recv[...]
-
-    out[...] = lax.dot_general(
-        lhs[...], weight[...], NT, preferred_element_type=F32
-    ).astype(out.dtype)
-
-
-def project(pos, keep, recv, query_weight, slice_index, width, out_dtype):
-    tokens, half = keep.shape
+def project_kernel(half, chunks, width, where, keep, recv, weight, out, lhs, held, sems):
+    rows = width // chunks
+    copies = [
+        pltpu.make_async_copy(
+            weight.at[pl.ds(pl.multiple_of(where[0] * width + i * rows, rows), rows), :],
+            held.at[pl.ds(i * rows, rows), :],
+            sems.at[i],
+        )
+        for i in range(chunks)
+    ]
+    for copy in copies:
+        copy.start()
+    core = lax.rem(lax.axis_index("ctx"), 2)
+    lhs[pl.ds(pl.multiple_of(core * half, HD), half), :] = keep[...]
+    lhs[pl.ds(pl.multiple_of((1 - core) * half, HD), half), :] = recv[...]
+    for i, copy in enumerate(copies):
+        copy.wait()
+        term = jnp.dot(held[i * rows : (i + 1) * rows, :], lhs[...], preferred_element_type=F32)
+        out[:, i * rows : (i + 1) * rows] = term.T.astype(out.dtype)
+
+
+def project(keep, recv, query_weight, slice_index, width, out_dtype):
+    half, tokens = keep.shape
     features = query_weight.shape[1]
-    tile = min(512, width)
-    steps = width // tile
-    where = jnp.stack([pos[0], slice_index]).astype(jnp.int32)
+    chunks = max(1, width // 512)
     return pl.pallas_call(
-        functools.partial(project_kernel, half),
-        grid_spec=pltpu.PrefetchScalarGridSpec(
-            num_scalar_prefetch=1,
-            grid=(steps,),
-            in_specs=[
-                pl.BlockSpec((tokens, half), lambda i, w: (0, 0)),
-                pl.BlockSpec((tokens, half), lambda i, w: (0, 0)),
-                pl.BlockSpec((tile, features), lambda i, w: (w[1] * steps + i, 0)),
-            ],
-            out_specs=pl.BlockSpec((tokens, tile), lambda i, w: (0, i)),
-            scratch_shapes=[pltpu.VMEM((tokens, features), BF16)],
-        ),
+        functools.partial(project_kernel, half, chunks, width),
+        in_specs=[smem(), vmem(), vmem(), hbm()],
+        out_specs=vmem(),
+        scratch_shapes=[
+            pltpu.VMEM((features, tokens), BF16),
+            pltpu.VMEM((width, features), BF16),
+            pltpu.SemaphoreType.DMA((chunks,)),
+        ],
         out_shape=jax.ShapeDtypeStruct((tokens, width), out_dtype),
         compiler_params=params(24),
         cost_estimate=pl.CostEstimate(
@@ -260,7 +287,7 @@
             bytes_accessed=2 * features * width,
             transcendentals=0,
         ),
-    )(where, keep, recv, query_weight)
+    )(slice_index.reshape(1).astype(jnp.int32), keep, recv, query_weight)
 
 
 def collect_kernel(part_own, a, b, c, d, e, keep, send):
@@ -271,18 +298,27 @@
     send[...] = result[BLOCK:].astype(BF16)
 
 
-def finish_kernel(kv_local, pos, keep, recv, key, gain, grad_key, grad_value):
-    core = pos[0]
-    parts = []
+def finish_kernel(
+    kv_local, keep, recv, key, gain, grad_key, grad_value, key_v, gain_v, sems
+):
+    copies = [
+        pltpu.make_async_copy(key, key_v, sems.at[0]),
+        pltpu.make_async_copy(gain, gain_v, sems.at[1]),
+    ]
+    for copy in copies:
+        copy.start()
+    for copy in copies:
+        copy.wait()
+    core = lax.rem(lax.axis_index("ctx"), 2)
     if kv_local > 1:
         parts = [(core, keep[...]), (1 - core, recv[...].astype(F32))]
     else:
         parts = [(0, keep[...] + recv[...].astype(F32))]
     for head, part in parts:
         lanes = pl.ds(pl.multiple_of(head * HD, HD), HD)
-        raw = key[:, lanes].astype(F32)
+        raw = key_v[:, lanes].astype(F32)
         inverse = lax.rsqrt(jnp.mean(raw * raw, axis=-1, keepdims=True) + norm_eps)
-        dy = part[:, :HD] * gain[...]
+        dy = part[:, :HD] * gain_v[...]
         inner = jnp.mean(raw * dy, axis=-1, keepdims=True)
         dx = inverse * dy - raw * (inverse * inverse * inverse * inner)
         grad_key[:, lanes] = dx.astype(BF16)
@@ -305,45 +341,40 @@
     kv_local = key_raw.shape[1] // HD
     half = query_raw.shape[1] // 2
     heads = half // HD
-    rank = lax.axis_index("ctx")
-    pos = jnp.stack([rank % 2]).astype(jnp.int32)
     key_row = key_gain.reshape(1, HD)
     query_row = query_gain.reshape(1, HD)
     query_col = query_gain.reshape(HD, 1)
     shape = jax.ShapeDtypeStruct
 
-    keep, send = pl.pallas_call(
-        functools.partial(keys_kernel, kv_local),
-        in_specs=[smem(), smem(), vmem(), vmem(), vmem(), vmem()],
-        out_specs=[vmem(), vmem()],
-        out_shape=[shape((BLOCK + EXTRA, 2 * HD), BF16)] * 2,
-    )(pos, block_docs, key_raw, value_in, key_row, loss_bucket.reshape(1, tokens))
     partner = lambda i: i ^ 1
-    recv = moved(send, "ctx", partner)
+    key_p = moved(key_raw, "ctx", partner)
+    value_p = moved(value_in, "ctx", partner)
+    docs_p = moved(block_docs, "ctx", partner)
+    bucket_p = moved(loss_bucket, "ctx", partner)
     message = pl.pallas_call(
-        join_kernel,
-        in_specs=[vmem(), vmem()],
+        functools.partial(message_kernel, kv_local),
+        in_specs=[smem(), smem(), hbm(), hbm(), hbm(), vmem(), vmem()],
         out_specs=vmem(),
         out_shape=shape((2 * BLOCK + EXTRA, 2 * HD), BF16),
-    )(keep, recv)
+        scratch_shapes=[
+            pltpu.VMEM((BLOCK, HD), BF16),
+            pltpu.VMEM((BLOCK, HD), BF16),
+            pltpu.VMEM((1, HD), F32),
+            pltpu.SemaphoreType.DMA((3,)),
+        ],
+        compiler_params=params(16),
+    )(block_docs, docs_p, key_raw, value_in, key_row, key_p, value_p)
 
     far_d = moved(message, "ctx", lambda i: i + 8)
     far_b = moved(message, "ctx", lambda i: i + 4)
     far_a = moved(message, "ctx", lambda i: i + 2 if (i // 2) % 2 == 0 else i + 10)
-    far_c = moved(far_b, "ctx", lambda i: i ^ 2)
-    far_e = moved(far_d, "ctx", lambda i: i ^ 2)
-
-    halves = pl.pallas_call(
-        functools.partial(split_kernel, half),
-        in_specs=[smem(), vmem(), vmem()],
-        out_specs=vmem(),
-        out_shape=shape((tokens, 2 * half), BF16),
-    )(pos, query_raw, grad_out)
-    other = moved(halves, "ctx", partner)
+    query_in, grad_in, _ = lax.optimization_barrier((query_raw, grad_out, message))
+    query_p = moved(query_in, "ctx", partner)
+    grad_p = moved(grad_in, "ctx", partner)
     total = 2 * heads * BLOCK
     q_hat, rows, raw_t, inverse_t, weight = pl.pallas_call(
         functools.partial(queries_kernel, heads),
-        in_specs=[smem(), smem()] + [vmem()] * 6,
+        in_specs=[smem(), vmem(), vmem(), hbm(), hbm(), hbm(), vmem(), vmem()],
         out_specs=[vmem()] * 5,
         out_shape=[
             shape((total, HD), BF16),
@@ -352,22 +383,37 @@
             shape((8, total), F32),
             shape((8, 2 * HD), F32),
         ],
-        compiler_params=params(24),
-        cost_estimate=pl.CostEstimate(
-            flops=20 * total * HD, bytes_accessed=12 * total * HD, transcendentals=0
-        ),
-    )(pos, loss_table, query_raw, grad_out, other, query_row, keep, recv)
+        scratch_shapes=[
+            pltpu.VMEM((BLOCK, half), BF16),
+            pltpu.VMEM((BLOCK, half), BF16),
+            pltpu.VMEM((1, HD), F32),
+            pltpu.SemaphoreType.DMA((3,)),
+        ],
+        compiler_params=params(16),
+    )(
+        loss_table,
+        loss_bucket.reshape(1, tokens),
+        bucket_p.reshape(1, tokens),
+        query_raw,
+        grad_out,
+        query_row,
+        query_p,
+        grad_p,
+    )
+    far_c = moved(far_b, "ctx", lambda i: i ^ 2)
+    far_d, q_hat = lax.optimization_barrier((far_d, q_hat))
+    far_e = moved(far_d, "ctx", lambda i: i ^ 2)
 
     span = 2 * BLOCK
     n_rows = 6 * span
     far_shape = shape((span, 2 * HD), BF16)
     outs = pl.pallas_call(
         functools.partial(attention_kernel, heads),
-        in_specs=[smem()] + [vmem()] * 12,
+        in_specs=[vmem()] * 12,
         out_specs=[vmem()] * 8,
         out_shape=[
-            shape((tokens, half), BF16),
-            shape((tokens, half), BF16),
+            shape((half, tokens), BF16),
+            shape((half, tokens), BF16),
             shape((span, 2 * HD), F32),
         ]
         + [far_shape] * 5,
@@ -389,7 +435,6 @@
             transcendentals=n_rows * total,
         ),
     )(
-        pos,
         message,
         far_a,
         far_b,
@@ -411,11 +456,9 @@
     width = query_weight.shape[0] // n_head
     arrived = []
     for shift in range(1, n_head):
-        term = project(
-            pos, dq_keep, dq_recv, query_weight, (head + shift) % n_head, width, BF16
-        )
+        term = project(dq_keep, dq_recv, query_weight, (head + shift) % n_head, width, BF16)
         arrived.append(moved(term, "head", lambda i, s=shift: (i + s) % n_head))
-    mine = project(pos, dq_keep, dq_recv, query_weight, head, width, F32)
+    mine = project(dq_keep, dq_recv, query_weight, head, width, F32)
 
     back_d = moved(part_d, "ctx", lambda i: i - 8)
     back_e = moved(part_e, "ctx", lambda i: (i ^ 2) - 8)
@@ -427,14 +470,21 @@
         in_specs=[vmem()] * 6,
         out_specs=[vmem()] * 2,
         out_shape=[shape((BLOCK, 2 * HD), F32), shape((BLOCK, 2 * HD), BF16)],
+        compiler_params=params(16),
     )(part_own, back_a, back_b, back_c, back_d, back_e)
     sum_recv = moved(sum_send, "ctx", partner)
     grad_key, grad_value = pl.pallas_call(
         functools.partial(finish_kernel, kv_local),
-        in_specs=[smem()] + [vmem()] * 4,
+        in_specs=[vmem(), vmem(), hbm(), hbm()],
         out_specs=[vmem()] * 2,
         out_shape=[shape(key_raw.shape, BF16), shape(value_in.shape, BF16)],
-    )(pos, sum_keep, sum_recv, key_raw, key_row)
+        scratch_shapes=[
+            pltpu.VMEM(key_raw.shape, BF16),
+            pltpu.VMEM((1, HD), F32),
+            pltpu.SemaphoreType.DMA((2,)),
+        ],
+        compiler_params=params(16),
+    )(sum_keep, sum_recv, key_raw, key_row)
 
     grad_input = mine
     for piece in arrived:

time: 105 us -> 103 us (0.981)
  Pallas kernels: 32 us -> 28 us
  local copies, waits for them, and re-layouts: 21 us -> 22.8 us
    pallas_call x7 -> x5, Pallas kernels: 29 us -> 26.7 us  [the longest x1 13.3 us: local(): pl.pallas_call(functools.partial(attention_kernel, heads), in_specs=[vmem...]
    pallas_call x1, Pallas kernels: 1.92 us -> 0.09 us  [local(): pl.pallas_call(collect_kernel, in_specs=[vmem()] * 6, out_specs=[vmem()]...]
    unnamed x34 -> x44, local copies, waits for them, and re-layouts: 20.3 us -> 22 us
    ppermute x15 -> x19, starting transfers between devices: 23.5 us -> 24.5 us  [moved(): lax.ppermute(array, axis, [(i, t) for i, t in pairs if t is not None and...]
    ppermute x15 -> x19, waiting for transfers between devices: 24.7 us -> 24.4 us  [moved(): lax.ppermute(array, axis, [(i, t) for i, t in pairs if t is not None and...]
  transfers between devices with their start and end apart: 15 -> 19, of which waited for: 6 -> 10; matrix products, arithmetic and copies ran while one was open for 1% -> 1% of each run, Pallas kernels for 12% -> 8%
where the time goes in v2:
time: 103 us; the launch traced here: 102 us
  Pallas kernels  28 us (27%)
  starting transfers between devices  24.5 us (24%)
  waiting for transfers between devices  24.4 us (24%)
  local copies, waits for them, and re-layouts  22.8 us (22%)
  between operations  1.55 us (2%)
    ppermute x19, starting transfers between devices, moved(): lax.ppermute(array, axis, [(i, t) for i, t in pairs if t is not None and...  24.5 us
    ppermute x19, waiting for transfers between devices, moved(): lax.ppermute(array, axis, [(i, t) for i, t in pairs if t is not None and...  24.4 us
    unnamed x44, local copies, waits for them, and re-layouts  22 us
    pallas_call x1, Pallas kernels, local(): pl.pallas_call(functools.partial(attention_kernel, heads), in_specs=[vmem...  13.3 us
    pallas_call x2, Pallas kernels, project(): pl.pallas_call(functools.partial(project_kernel, half, chunks, width), in...  11.7 us
  transfers between devices with their start and end apart: 19, of which 10 were waited for; matrix products, arithmetic and copies ran while one was open for 1% of the time, Pallas kernels for 8%

profile of v2, /device:TPU:0, one launch (start us, length us, event | category | flops | bytes accessed | tf_op | source)
XLA Modules:
  0.0 102.1 jit_solution(15918334105813042904)
XLA Ops:
  0.6 0.5 collective-permute-start.1
  1.2 0.4 collective-permute-start
  2.3 0.4 collective-permute-done.docs_p
  2.8 0.8 copy-done.4
  3.6 0.8 copy-done.6
  4.4 0.7 copy-done.8
  5.1 0.8 shard_map.121.own
  5.9 0.4 collective-permute-start.8
  6.3 0.2 collective-permute-start.9
  6.5 4.8 %collective-permute-start.4 = (bf16[272,256]{1,0:T(8,128)(2,1)S(1)}, bf16[272,256]{1,0:T(8,128)(2,1)S(1)}, u32[]{:S(2)}, u32[]{:S(2)}) collective-permute-start(bf16[272,256]{1,0:T(8,128)(2,1)S(1)} %shard_map.121.own), channel_id=1, source_target_pairs={{0,8},{2,10},{4,12},{6,14},{8,16},{10,18},{12,20},{14,22},{16,24},... | collective-permute-start | bytes 417800 | tf_op jit(solution)/shard_map/ppermute | solution.py:25
  11.3 4.5 %collective-permute-start.6 = (bf16[272,256]{1,0:T(8,128)(2,1)S(1)}, bf16[272,256]{1,0:T(8,128)(2,1)S(1)}, u32[]{:S(2)}, u32[]{:S(2)}) collective-permute-start(bf16[272,256]{1,0:T(8,128)(2,1)S(1)} %shard_map.121.own), channel_id=1, source_target_pairs={{0,16},{2,18},{4,20},{6,22},{8,24},{10,26},{12,28},{14,30},{1,17},... | collective-permute-start | bytes 417800 | tf_op jit(solution)/shard_map/ppermute | solution.py:25
  15.8 1.2 %collective-permute-done.7 = s32[128]{0:T(128)S(1)} collective-permute-done((s32[128]{0:T(128)}, s32[128]{0:T(128)S(1)}, u32[]{:S(2)}, u32[]{:S(2)}) %collective-permute-start.7) | collective-permute-done | bytes 544 | tf_op jit(solution)/shard_map/ppermute | solution.py:25
  17.1 3.4 %collective-permute-start.3 = (bf16[272,256]{1,0:T(8,128)(2,1)S(1)}, bf16[272,256]{1,0:T(8,128)(2,1)S(1)}, u32[]{:S(2)}, u32[]{:S(2)}) collective-permute-start(bf16[272,256]{1,0:T(8,128)(2,1)S(1)} %shard_map.121.own), channel_id=1, source_target_pairs={{0,4},{2,6},{4,24},{6,26},{8,12},{10,14},{16,20},{18,22},{24,28},{... | collective-permute-start | bytes 417800 | tf_op jit(solution)/shard_map/ppermute | solution.py:25
  20.6 1.0 %copy-done.2 = bf16[128,2048]{1,0:T(8,128)(2,1)S(1)} copy-done((bf16[128,2048]{1,0:T(8,128)(2,1)S(1)}, bf16[128,2048]{1,0:T(8,128)(2,1)}, u32[]{:S(2)}) %copy-start.2) | copy-done | bytes 524312
  21.7 1.0 %copy-done.3 = bf16[128,2048]{1,0:T(8,128)(2,1)S(1)} copy-done((bf16[128,2048]{1,0:T(8,128)(2,1)S(1)}, bf16[128,2048]{1,0:T(8,128)(2,1)}, u32[]{:S(2)}) %copy-start.3) | copy-done | bytes 524312
  22.7 0.7 copy-done.7
  23.4 0.7 copy-done.10
  24.0 0.7 copy-done.11
  24.7 1.2 %shard_map.122 = (bf16[2048,128]{1,0:T(8,128)(2,1)S(1)}, bf16[2048,128]{1,0:T(8,128)(2,1)S(1)}, bf16[128,2048]{1,0:T(8,128)(2,1)S(1)}, f32[8,2048]{1,0:T(8,128)S(1)}, f32[8,256]{1,0:T(8,128)S(1)}) custom-call(f32[16]{0:T(128)S(1)} %copy-done.10, s32[1,128]{1,0:T(1,128)S(1)} %bitcast.11, s32[1,128]{1,0:T(1,128)S(1)} %bitcast.12, ...), custom_call_target="tpu_custom_call" | custom-call | tf_op jit(solution)/shard_map/pallas_call | solution.py:375
  25.9 0.6 copy-done.20
  26.6 2.0 %collective-permute-start.10 = (bf16[272,256]{1,0:T(8,128)(2,1)S(1)}, bf16[272,256]{1,0:T(8,128)(2,1)S(1)}, u32[]{:S(2)}, u32[]{:S(2)}) collective-permute-start(bf16[272,256]{1,0:T(8,128)(2,1)S(1)} %collective-permute-done.6.far_d), channel_id=1, source_target_pairs={{0,4},{2,6},{4,0},{6,2},{8,12},{10,14},{12,8},{14,10},{16,20},{18,... | collective-permute-start | bytes 417800 | tf_op jit(solution)/shard_map/ppermute | solution.py:25
  28.5 0.8 copy.13.gain
  29.3 2.7 %collective-permute-done.10.far_e = bf16[272,256]{1,0:T(8,128)(2,1)S(1)} collective-permute-done((bf16[272,256]{1,0:T(8,128)(2,1)S(1)}, bf16[272,256]{1,0:T(8,128)(2,1)S(1)}, u32[]{:S(2)}, u32[]{:S(2)}) %collective-permute-start.10) | collective-permute-done | bytes 139296 | tf_op jit(solution)/shard_map/ppermute | solution.py:25
  32.1 0.8 copy-done.21
  32.9 13.3 %shard_map.123 = (bf16[1024,128]{1,0:T(8,128)(2,1)S(1)}, bf16[1024,128]{1,0:T(8,128)(2,1)S(1)}, f32[256,256]{1,0:T(8,128)S(1)}, bf16[256,256]{1,0:T(8,128)(2,1)S...) custom-call(bf16[272,256]{1,0:T(8,128)(2,1)S(1)} %shard_map.121.own,, ...), custom_call_target="tpu_custom_call" | custom-call | flops 4026531840 | bytes 3145728 | tf_op jit(solution)/shard_map/pallas_call | solution.py:410
  46.2 0.6 copy-done.12
  46.9 0.6 copy-done.14
  47.5 0.7 copy-done.16
  48.2 0.7 copy-done.18
  48.8 1.5 %collective-permute-done.11.recv = bf16[1024,128]{1,0:T(8,128)(2,1)S(1)} collective-permute-done((bf16[1024,128]{1,0:T(8,128)(2,1)S(1)}, bf16[1024,128]{1,0:T(8,128)(2,1)S(1)}, u32[]{:S(2)}, u32[]{:S(2)}) %collective-permute-start.11) | collective-permute-done | bytes 262176 | tf_op jit(solution)/shard_map/ppermute | solution.py:25
  50.4 5.8 %copy-done = bf16[4096,2048]{1,0:T(8,128)(2,1)S(1)} copy-done((bf16[4096,2048]{1,0:T(8,128)(2,1)S(1)}, bf16[4096,2048]{1,0:T(8,128)(2,1)}, u32[]{:S(2)}) %copy-start) | copy-done | bytes 16777240
  56.1 5.9 %shard_map.125 = bf16[128,2048]{1,0:T(8,128)(2,1)S(1)} custom-call(s32[1]{0:T(128)} %bitcast.6.where, bf16[1024,128]{1,0:T(8,128)(2,1)S(1)} %get-tuple-element.33.keep, bf16[1024,128]{1,0:T(8,128)(2,1)S(1)} %collective-permute-done.11.recv, bf16[4096,2048]{1,0:T(8,128)(2,1)S(1)} %copy-done), custom_call_target="tpu_custom_call" | custom-call | flops 1073741824 | bytes 8388608 | tf_op jit(solution)/shard_map/pallas_call | solution.py:274
  62.0 1.6 %collective-permute-start.12 = (bf16[128,2048]{1,0:T(8,128)(2,1)S(1)}, bf16[128,2048]{1,0:T(8,128)(2,1)S(1)}, u32[]{:S(2)}, u32[]{:S(2)}) collective-permute-start(bf16[128,2048]{1,0:T(8,128)(2,1)S(1)} %shard_map.125), channel_id=1, source_target_pairs={{0,1},{1,0},{2,3},{3,2},{4,5},{5,4},{6,7},{7,6},{8,9},{9,8},{10,11... | collective-permute-start | bytes 1572872 | tf_op jit(solution)/shard_map/ppermute | solution.py:25
  63.6 1.3 %collective-permute-start.13 = (bf16[256,256]{1,0:T(8,128)(2,1)S(1)}, bf16[256,256]{1,0:T(8,128)(2,1)S(1)}, u32[]{:S(2)}, u32[]{:S(2)}) collective-permute-start(bf16[256,256]{1,0:T(8,128)(2,1)S(1)} %copy-done.19), channel_id=1, source_target_pairs={{4,0},{6,2},{12,8},{14,10},{20,16},{22,18},{24,4},{26,6},{28,24},{... | collective-permute-start | bytes 393224 | tf_op jit(solution)/shard_map/ppermute | solution.py:25
  64.9 1.3 %collective-permute-start.14 = (bf16[256,256]{1,0:T(8,128)(2,1)S(1)}, bf16[256,256]{1,0:T(8,128)(2,1)S(1)}, u32[]{:S(2)}, u32[]{:S(2)}) collective-permute-start(bf16[256,256]{1,0:T(8,128)(2,1)S(1)} %copy-done.17), channel_id=1, source_target_pairs={{8,0},{10,2},{12,4},{14,6},{16,8},{18,10},{20,12},{22,14},{24,16},... | collective-permute-start | bytes 393224 | tf_op jit(solution)/shard_map/ppermute | solution.py:25
  66.2 1.3 %collective-permute-start.15 = (bf16[256,256]{1,0:T(8,128)(2,1)S(1)}, bf16[256,256]{1,0:T(8,128)(2,1)S(1)}, u32[]{:S(2)}, u32[]{:S(2)}) collective-permute-start(bf16[256,256]{1,0:T(8,128)(2,1)S(1)} %copy-done.15), channel_id=1, source_target_pairs={{8,4},{10,6},{12,0},{14,2},{16,12},{18,14},{20,8},{22,10},{24,20},... | collective-permute-start | bytes 393224 | tf_op jit(solution)/shard_map/ppermute | solution.py:25
  67.5 1.3 %collective-permute-start.16 = (bf16[256,256]{1,0:T(8,128)(2,1)S(1)}, bf16[256,256]{1,0:T(8,128)(2,1)S(1)}, u32[]{:S(2)}, u32[]{:S(2)}) collective-permute-start(bf16[256,256]{1,0:T(8,128)(2,1)S(1)} %copy-done.13), channel_id=1, source_target_pairs={{16,0},{18,2},{20,4},{22,6},{24,8},{26,10},{28,12},{30,14},{17,1},... | collective-permute-start | bytes 393224 | tf_op jit(solution)/shard_map/ppermute | solution.py:25
  68.8 1.9 %collective-permute-done.13.a = bf16[256,256]{1,0:T(8,128)(2,1)S(1)} collective-permute-done((bf16[256,256]{1,0:T(8,128)(2,1)S(1)}, bf16[256,256]{1,0:T(8,128)(2,1)S(1)}, u32[]{:S(2)}, u32[]{:S(2)}) %collective-permute-start.13) | collective-permute-done | bytes 131104 | tf_op jit(solution)/shard_map/ppermute | solution.py:25
  70.7 1.3 %collective-permute-start.17 = (bf16[256,256]{1,0:T(8,128)(2,1)S(1)}, bf16[256,256]{1,0:T(8,128)(2,1)S(1)}, u32[]{:S(2)}, u32[]{:S(2)}) collective-permute-start(bf16[256,256]{1,0:T(8,128)(2,1)S(1)} %get-tuple-element.40), channel_id=1, source_target_pairs={{16,4},{18,6},{20,0},{22,2},{24,12},{26,14},{28,8},{30,10},{17,5},... | collective-permute-start | bytes 393224 | tf_op jit(solution)/shard_map/ppermute | solution.py:25
  72.0 3.9 %collective-permute-done.14.b = bf16[256,256]{1,0:T(8,128)(2,1)S(1)} collective-permute-done((bf16[256,256]{1,0:T(8,128)(2,1)S(1)}, bf16[256,256]{1,0:T(8,128)(2,1)S(1)}, u32[]{:S(2)}, u32[]{:S(2)}) %collective-permute-start.14) | collective-permute-done | bytes 131104 | tf_op jit(solution)/shard_map/ppermute | solution.py:25
  75.9 1.9 %collective-permute-done.15.c = bf16[256,256]{1,0:T(8,128)(2,1)S(1)} collective-permute-done((bf16[256,256]{1,0:T(8,128)(2,1)S(1)}, bf16[256,256]{1,0:T(8,128)(2,1)S(1)}, u32[]{:S(2)}, u32[]{:S(2)}) %collective-permute-start.15) | collective-permute-done | bytes 131104 | tf_op jit(solution)/shard_map/ppermute | solution.py:25
  77.9 9.2 %collective-permute-done.16.d = bf16[256,256]{1,0:T(8,128)(2,1)S(1)} collective-permute-done((bf16[256,256]{1,0:T(8,128)(2,1)S(1)}, bf16[256,256]{1,0:T(8,128)(2,1)S(1)}, u32[]{:S(2)}, u32[]{:S(2)}) %collective-permute-start.16) | collective-permute-done | bytes 131104 | tf_op jit(solution)/shard_map/ppermute | solution.py:25
  87.1 0.2 collective-permute-done.17.e
  87.4 1.2 %collective-permute-done.18.recv = bf16[128,256]{1,0:T(8,128)(2,1)S(1)} collective-permute-done((bf16[128,256]{1,0:T(8,128)(2,1)S(1)}, bf16[128,256]{1,0:T(8,128)(2,1)S(1)}, u32[]{:S(2)}, u32[]{:S(2)}) %collective-permute-start.18) | collective-permute-done | bytes 65568 | tf_op jit(solution)/shard_map/ppermute | solution.py:25
  88.7 0.9 shard_map.127
  89.6 5.8 %copy-done.1 = bf16[4096,2048]{1,0:T(8,128)(2,1)S(1)} copy-done((bf16[4096,2048]{1,0:T(8,128)(2,1)S(1)}, bf16[4096,2048]{1,0:T(8,128)(2,1)}, u32[]{:S(2)}) %copy-start.1) | copy-done | bytes 16777240
  95.4 5.8 %shard_map.124 = f32[128,2048]{1,0:T(8,128)S(1)} custom-call(s32[1]{0:T(128)} %bitcast.where, bf16[1024,128]{1,0:T(8,128)(2,1)S(1)} %get-tuple-element.33.keep, bf16[1024,128]{1,0:T(8,128)(2,1)S(1)} %collective-permute-done.11.recv, bf16[4096,2048]{1,0:T(8,128)(2,1)S(1)} %copy-done.1), custom_call_target="tpu_custom_call" | custom-call | flops 1073741824 | bytes 8388608 | tf_op jit(solution)/shard_map/pallas_call | solution.py:274
  101.2 0.9 add_convert_fusion
  (43 shorter events, 0.5 us)
Async XLA Ops:
  0.6 2.1 %collective-permute-start.1 = (bf16[128,256]{1,0:T(8,128)(2,1)}, bf16[128,256]{1,0:T(8,128)(2,1)S(1)}, u32[]{:S(2)}, u32[]{:S(2)}) collective-permute-start(bf16[128,256]{1,0:T(8,128)(2,1)} %key.3), channel_id=1, source_target_pairs={{0,2},{2,0},{4,6},{6,4},{8,10},{10,8},{12,14},{14,12},{16,18},{18,... | collective-permute-start | bytes 196616 | tf_op jit(solution)/shard_map/ppermute | solution.py:25
  1.1 1.6 %collective-permute-start.2 = (bf16[128,256]{1,0:T(8,128)(2,1)}, bf16[128,256]{1,0:T(8,128)(2,1)S(1)}, u32[]{:S(2)}, u32[]{:S(2)}) collective-permute-start(bf16[128,256]{1,0:T(8,128)(2,1)} %value.1), channel_id=1, source_target_pairs={{0,2},{2,0},{4,6},{6,4},{8,10},{10,8},{12,14},{14,12},{16,18},{18,... | collective-permute-start | bytes 196616 | tf_op jit(solution)/shard_map/ppermute | solution.py:25
  1.2 1.5 %collective-permute-start = (s32[1]{0:T(128)}, s32[1]{0:T(128)}, u32[]{:S(2)}, u32[]{:S(2)}) collective-permute-start(s32[1]{0:T(128)} %param.18), channel_id=1, source_target_pairs={{0,2},{2,0},{4,6},{6,4},{8,10},{10,8},{12,14},{14,12},{16,18},{18,... | collective-permute-start | bytes 20 | tf_op jit(solution)/shard_map/ppermute | solution.py:25
  2.8 0.8 copy-start.4
  3.6 0.8 copy-start.6
  4.4 0.7 copy-start.8
  5.9 14.7 %collective-permute-start.8 = (bf16[128,2048]{1,0:T(8,128)(2,1)}, bf16[128,2048]{1,0:T(8,128)(2,1)S(1)}, u32[]{:S(2)}, u32[]{:S(2)}) collective-permute-start(bf16[128,2048]{1,0:T(8,128)(2,1)} %query.1), channel_id=1, source_target_pairs={{0,2},{2,0},{4,6},{6,4},{8,10},{10,8},{12,14},{14,12},{16,18},{18,... | collective-permute-start | bytes 1572872 | tf_op jit(solution)/shard_map/ppermute | solution.py:25
  6.3 14.3 %collective-permute-start.9 = (bf16[128,2048]{1,0:T(8,128)(2,1)}, bf16[128,2048]{1,0:T(8,128)(2,1)S(1)}, u32[]{:S(2)}, u32[]{:S(2)}) collective-permute-start(bf16[128,2048]{1,0:T(8,128)(2,1)} %grad.1), channel_id=1, source_target_pairs={{0,2},{2,0},{4,6},{6,4},{8,10},{10,8},{12,14},{14,12},{16,18},{18,... | collective-permute-start | bytes 1572872 | tf_op jit(solution)/shard_map/ppermute | solution.py:25
  6.5 14.0 %collective-permute-start.4 = (bf16[272,256]{1,0:T(8,128)(2,1)S(1)}, bf16[272,256]{1,0:T(8,128)(2,1)S(1)}, u32[]{:S(2)}, u32[]{:S(2)}) collective-permute-start(bf16[272,256]{1,0:T(8,128)(2,1)S(1)} %shard_map.121.own), channel_id=1, source_target_pairs={{0,8},{2,10},{4,12},{6,14},{8,16},{10,18},{12,20},{14,22},{16,24},... | collective-permute-start | bytes 417800 | tf_op jit(solution)/shard_map/ppermute | solution.py:25
  11.3 15.3 %collective-permute-start.6 = (bf16[272,256]{1,0:T(8,128)(2,1)S(1)}, bf16[272,256]{1,0:T(8,128)(2,1)S(1)}, u32[]{:S(2)}, u32[]{:S(2)}) collective-permute-start(bf16[272,256]{1,0:T(8,128)(2,1)S(1)} %shard_map.121.own), channel_id=1, source_target_pairs={{0,16},{2,18},{4,20},{6,22},{8,24},{10,26},{12,28},{14,30},{1,17},... | collective-permute-start | bytes 417800 | tf_op jit(solution)/shard_map/ppermute | solution.py:25
  15.8 1.3 %collective-permute-start.7 = (s32[128]{0:T(128)}, s32[128]{0:T(128)S(1)}, u32[]{:S(2)}, u32[]{:S(2)}) collective-permute-start(s32[128]{0:T(128)} %param.17), channel_id=1, source_target_pairs={{0,2},{2,0},{4,6},{6,4},{8,10},{10,8},{12,14},{14,12},{16,18},{18,... | collective-permute-start | bytes 1544 | tf_op jit(solution)/shard_map/ppermute | solution.py:25
  17.1 12.2 %collective-permute-start.3 = (bf16[272,256]{1,0:T(8,128)(2,1)S(1)}, bf16[272,256]{1,0:T(8,128)(2,1)S(1)}, u32[]{:S(2)}, u32[]{:S(2)}) collective-permute-start(bf16[272,256]{1,0:T(8,128)(2,1)S(1)} %shard_map.121.own), channel_id=1, source_target_pairs={{0,4},{2,6},{4,24},{6,26},{8,12},{10,14},{16,20},{18,22},{24,28},{... | collective-permute-start | bytes 417800 | tf_op jit(solution)/shard_map/ppermute | solution.py:25
  20.5 8.8 %collective-permute-start.5 = (bf16[272,256]{1,0:T(8,128)(2,1)S(1)}, bf16[272,256]{1,0:T(8,128)(2,1)S(1)}, u32[]{:S(2)}, u32[]{:S(2)}) collective-permute-start(bf16[272,256]{1,0:T(8,128)(2,1)S(1)} %collective-permute-done.4.far_b), channel_id=1, source_target_pairs={{0,4},{2,6},{4,0},{6,2},{8,12},{10,14},{12,8},{14,10},{16,20},{18,... | collective-permute-start | bytes 417800 | tf_op jit(solution)/shard_map/ppermute | solution.py:25
  20.6 1.0 %copy-start.2 = (bf16[128,2048]{1,0:T(8,128)(2,1)S(1)}, bf16[128,2048]{1,0:T(8,128)(2,1)}, u32[]{:S(2)}) copy-start(bf16[128,2048]{1,0:T(8,128)(2,1)} %query.1) | copy-start | bytes 1572868
  21.7 1.0 %copy-start.3 = (bf16[128,2048]{1,0:T(8,128)(2,1)S(1)}, bf16[128,2048]{1,0:T(8,128)(2,1)}, u32[]{:S(2)}) copy-start(bf16[128,2048]{1,0:T(8,128)(2,1)} %grad.1) | copy-start | bytes 1572868
  22.7 0.7 copy-start.7
  23.4 0.7 copy-start.10
  24.0 0.7 copy-start.11
  25.9 0.6 copy-start.20
  26.6 5.5 %collective-permute-start.10 = (bf16[272,256]{1,0:T(8,128)(2,1)S(1)}, bf16[272,256]{1,0:T(8,128)(2,1)S(1)}, u32[]{:S(2)}, u32[]{:S(2)}) collective-permute-start(bf16[272,256]{1,0:T(8,128)(2,1)S(1)} %collective-permute-done.6.far_d), channel_id=1, source_target_pairs={{0,4},{2,6},{4,0},{6,2},{8,12},{10,14},{12,8},{14,10},{16,20},{18,... | collective-permute-start | bytes 417800 | tf_op jit(solution)/shard_map/ppermute | solution.py:25
  32.1 0.8 copy-start.21
  32.9 55.8 %copy-start.5 = (bf16[128,256]{1,0:T(8,128)(2,1)S(1)}, bf16[128,256]{1,0:T(8,128)(2,1)}, u32[]{:S(2)}) copy-start(bf16[128,256]{1,0:T(8,128)(2,1)} %key.3) | copy-start | bytes 196612
  32.9 55.8 %copy-start.9 = (f32[128]{0:T(128)S(1)}, f32[128]{0:T(128)}, u32[]{:S(2)}) copy-start(f32[128]{0:T(128)} %param.15) | copy-start | bytes 1540
  46.2 0.7 copy-start.12
  46.9 0.6 copy-start.14
  47.5 0.7 copy-start.16
  48.2 0.7 copy-start.18
  48.8 1.5 %collective-permute-start.11 = (bf16[1024,128]{1,0:T(8,128)(2,1)S(1)}, bf16[1024,128]{1,0:T(8,128)(2,1)S(1)}, u32[]{:S(2)}, u32[]{:S(2)}) collective-permute-start(bf16[1024,128]{1,0:T(8,128)(2,1)S(1)} %get-tuple-element.34), channel_id=1, source_target_pairs={{0,2},{2,0},{4,6},{6,4},{8,10},{10,8},{12,14},{14,12},{16,18},{18,... | collective-permute-start | bytes 786440 | tf_op jit(solution)/shard_map/ppermute | solution.py:25
  50.4 5.8 %copy-start = (bf16[4096,2048]{1,0:T(8,128)(2,1)S(1)}, bf16[4096,2048]{1,0:T(8,128)(2,1)}, u32[]{:S(2)}) copy-start(bf16[4096,2048]{1,0:T(8,128)(2,1)} %weight.3) | copy-start | bytes 50331652
  56.1 7.4 %copy-start.19 = (bf16[256,256]{1,0:T(8,128)(2,1)S(1)}, bf16[256,256]{1,0:T(8,128)(2,1)}, u32[]{:S(2)}) copy-start(bf16[256,256]{1,0:T(8,128)(2,1)} %copy-done.18) | copy-start | bytes 393220
  56.1 8.7 %copy-start.17 = (bf16[256,256]{1,0:T(8,128)(2,1)S(1)}, bf16[256,256]{1,0:T(8,128)(2,1)}, u32[]{:S(2)}) copy-start(bf16[256,256]{1,0:T(8,128)(2,1)} %copy-done.16) | copy-start | bytes 393220
  56.1 10.0 %copy-start.15 = (bf16[256,256]{1,0:T(8,128)(2,1)S(1)}, bf16[256,256]{1,0:T(8,128)(2,1)}, u32[]{:S(2)}) copy-start(bf16[256,256]{1,0:T(8,128)(2,1)} %copy-done.14) | copy-start | bytes 393220
  56.1 11.3 %copy-start.13 = (bf16[256,256]{1,0:T(8,128)(2,1)S(1)}, bf16[256,256]{1,0:T(8,128)(2,1)}, u32[]{:S(2)}) copy-start(bf16[256,256]{1,0:T(8,128)(2,1)} %copy-done.12) | copy-start | bytes 393220
  62.0 39.2 %collective-permute-start.12 = (bf16[128,2048]{1,0:T(8,128)(2,1)S(1)}, bf16[128,2048]{1,0:T(8,128)(2,1)S(1)}, u32[]{:S(2)}, u32[]{:S(2)}) collective-permute-start(bf16[128,2048]{1,0:T(8,128)(2,1)S(1)} %shard_map.125), channel_id=1, source_target_pairs={{0,1},{1,0},{2,3},{3,2},{4,5},{5,4},{6,7},{7,6},{8,9},{9,8},{10,11... | collective-permute-start | bytes 1572872 | tf_op jit(solution)/shard_map/ppermute | solution.py:25
  63.6 7.1 %collective-permute-start.13 = (bf16[256,256]{1,0:T(8,128)(2,1)S(1)}, bf16[256,256]{1,0:T(8,128)(2,1)S(1)}, u32[]{:S(2)}, u32[]{:S(2)}) collective-permute-start(bf16[256,256]{1,0:T(8,128)(2,1)S(1)} %copy-done.19), channel_id=1, source_target_pairs={{4,0},{6,2},{12,8},{14,10},{20,16},{22,18},{24,4},{26,6},{28,24},{... | collective-permute-start | bytes 393224 | tf_op jit(solution)/shard_map/ppermute | solution.py:25
  64.9 11.1 %collective-permute-start.14 = (bf16[256,256]{1,0:T(8,128)(2,1)S(1)}, bf16[256,256]{1,0:T(8,128)(2,1)S(1)}, u32[]{:S(2)}, u32[]{:S(2)}) collective-permute-start(bf16[256,256]{1,0:T(8,128)(2,1)S(1)} %copy-done.17), channel_id=1, source_target_pairs={{8,0},{10,2},{12,4},{14,6},{16,8},{18,10},{20,12},{22,14},{24,16},... | collective-permute-start | bytes 393224 | tf_op jit(solution)/shard_map/ppermute | solution.py:25
  66.2 11.7 %collective-permute-start.15 = (bf16[256,256]{1,0:T(8,128)(2,1)S(1)}, bf16[256,256]{1,0:T(8,128)(2,1)S(1)}, u32[]{:S(2)}, u32[]{:S(2)}) collective-permute-start(bf16[256,256]{1,0:T(8,128)(2,1)S(1)} %copy-done.15), channel_id=1, source_target_pairs={{8,4},{10,6},{12,0},{14,2},{16,12},{18,14},{20,8},{22,10},{24,20},... | collective-permute-start | bytes 393224 | tf_op jit(solution)/shard_map/ppermute | solution.py:25
  67.5 19.6 %collective-permute-start.16 = (bf16[256,256]{1,0:T(8,128)(2,1)S(1)}, bf16[256,256]{1,0:T(8,128)(2,1)S(1)}, u32[]{:S(2)}, u32[]{:S(2)}) collective-permute-start(bf16[256,256]{1,0:T(8,128)(2,1)S(1)} %copy-done.13), channel_id=1, source_target_pairs={{16,0},{18,2},{20,4},{22,6},{24,8},{26,10},{28,12},{30,14},{17,1},... | collective-permute-start | bytes 393224 | tf_op jit(solution)/shard_map/ppermute | solution.py:25
  70.7 16.6 %collective-permute-start.17 = (bf16[256,256]{1,0:T(8,128)(2,1)S(1)}, bf16[256,256]{1,0:T(8,128)(2,1)S(1)}, u32[]{:S(2)}, u32[]{:S(2)}) collective-permute-start(bf16[256,256]{1,0:T(8,128)(2,1)S(1)} %get-tuple-element.40), channel_id=1, source_target_pairs={{16,4},{18,6},{20,0},{22,2},{24,12},{26,14},{28,8},{30,10},{17,5},... | collective-permute-start | bytes 393224 | tf_op jit(solution)/shard_map/ppermute | solution.py:25
  87.4 1.3 %collective-permute-start.18 = (bf16[128,256]{1,0:T(8,128)(2,1)S(1)}, bf16[128,256]{1,0:T(8,128)(2,1)S(1)}, u32[]{:S(2)}, u32[]{:S(2)}) collective-permute-start(bf16[128,256]{1,0:T(8,128)(2,1)S(1)} %get-tuple-element.42), channel_id=1, source_target_pairs={{0,2},{2,0},{4,6},{6,4},{8,10},{10,8},{12,14},{14,12},{16,18},{18,... | collective-permute-start | bytes 196616 | tf_op jit(solution)/shard_map/ppermute | solution.py:25
  89.6 5.8 %copy-start.1 = (bf16[4096,2048]{1,0:T(8,128)(2,1)S(1)}, bf16[4096,2048]{1,0:T(8,128)(2,1)}, u32[]{:S(2)}) copy-start(bf16[4096,2048]{1,0:T(8,128)(2,1)} %weight.3) | copy-start | bytes 50331652

commit v3 on v0

v3 whole, which is shorter than its diff:
```python
import functools
import math

import jax
import jax.numpy as jnp
from jax import lax
from jax.experimental import pallas as pl
from jax.experimental.pallas import tpu as pltpu
from jax.sharding import PartitionSpec as P

HD = 128
BLOCK = 128
EXTRA = 16
HOPS = 10
norm_eps = 1e-06
SCALE = HD ** (-0.5)
NEG = -1e30
NT = (((1,), (1,)), ((), ()))
F32 = jnp.float32
BF16 = jnp.bfloat16


def moved(array, axis, target):
    size = lax.axis_size(axis)
    pairs = [(i, target(i)) for i in range(size)]
    return lax.ppermute(array, axis, [(i, t) for i, t in pairs if t is not None and 0 <= t < size])


def vmem():
    return pl.BlockSpec(memory_space=pltpu.VMEM)


def hbm():
    return pl.BlockSpec(memory_space=pltpu.HBM)


def smem():
    return pl.BlockSpec(memory_space=pltpu.SMEM)


def params(mib):
    return pltpu.CompilerParams(vmem_limit_bytes=mib << 20)


def normed(raw, gain):
    mean_square = jnp.mean(raw * raw, axis=-1, keepdims=True)
    return raw * lax.rsqrt(mean_square + norm_eps) * gain


def message_kernel(
    kv_local, docs, table, key, value, key_gain, query_gain, bucket, out, facts
):
    core = lax.rem(lax.axis_index("ctx"), 2)
    for part in range(kv_local):
        head = part if kv_local == 1 else (core if part == 0 else 1 - core)
        lanes = pl.ds(pl.multiple_of(head * HD, HD), HD)
        rows = slice(part * BLOCK, (part + 1) * BLOCK)
        out[rows, :HD] = normed(key[:, lanes].astype(F32), key_gain[...]).astype(BF16)
        out[rows, HD:] = value[:, lanes]
    doc = jnp.full((EXTRA, 2 * HD), docs[0] + 1, jnp.int32).astype(F32)
    out[kv_local * BLOCK :, :] = doc.astype(BF16)
    facts[:8, :] = jnp.broadcast_to(query_gain[...], (8, HD))
    picks = bucket[...]
    found = jnp.zeros((1, HD), F32)
    for b in range(table.shape[0]):
        found = found + jnp.where(picks == b, table[b], 0.0)
    facts[8:, :] = jnp.broadcast_to(found, (8, HD))


def queries_kernel(
    heads,
    query,
    grad,
    facts,
    message,
    query_p,
    grad_p,
    facts_p,
    q_hat,
    rows,
    raw_t,
    both,
    kept,
):
    half = heads * HD
    core = lax.rem(lax.axis_index("ctx"), 2)
    own = pl.ds(pl.multiple_of(core * half, HD), half)
    gain = facts[0:1]
    for side in range(2):
        raw_all = query_p[:, own] if side else query[:, own]
        grad_all = grad_p[:, own] if side else grad[:, own]
        parity = 1 - core if side else core
        for head in range(heads):
            here = pl.ds(pl.multiple_of(parity * half + head * BLOCK, BLOCK), BLOCK)
            raw = raw_all[:, head * HD : (head + 1) * HD].astype(F32)
            q_hat[here, :] = normed(raw, gain).astype(BF16)
            rows[here, :] = grad_all[:, head * HD : (head + 1) * HD]
            raw_t[:, here] = raw.T.astype(BF16)
        weight = facts_p if side else facts
        both[pl.ds(pl.multiple_of(8 + 8 * parity, 8), 8), :] = weight[8:]
    both[:8, :] = facts[:8]
    kept[...] = message[...]


def attention_kernel(kv_local, heads, hops, *refs):
    n_src = hops // 2 + 1
    mine, others = refs[:n_src], refs[n_src : 2 * n_src]
    q_hat, rows, raw_t, facts, weight = refs[2 * n_src : 2 * n_src + 5]
    dq, held = refs[2 * n_src + 5 : 2 * n_src + 7]
    outs = refs[2 * n_src + 7 : 3 * n_src + 7]
    docs, keys, values, keys_t, expo, dots, pw_half, ds_half, dk, dv, sems = refs[3 * n_src + 7 :]
    half = heads * HD
    rank = lax.axis_index("ctx")
    core = lax.rem(rank, 2)
    odd_chip = lax.rem(lax.div(rank, 2), 2)

    features = pl.ds(pl.multiple_of(core * half, HD), half)
    pieces = sems.shape[0]
    part = held.shape[0] // pieces
    copies = [
        pltpu.make_async_copy(
            weight.at[pl.ds(i * part, part), features],
            held.at[pl.ds(i * part, part), :],
            sems.at[i],
        )
        for i in range(pieces)
    ]
    for copy in copies:
        copy.start()

    blocks = 2 * n_src
    chips_back = (
        0,
        jnp.where(odd_chip == 1, 1, 5),
        2,
        jnp.where(odd_chip == 1, 3, 1),
        4,
        jnp.where(odd_chip == 1, 5, 3),
    )
    after = (kv_local - 1) * BLOCK
    slots = []
    for index, back in enumerate(chips_back):
        for source, first, parity in (
            (mine[index], 0, core),
            (others[index], after, 1 - core),
        ):
            slot = 2 * (n_src - 1 - back) + parity
            at = pl.ds(pl.multiple_of(slot * BLOCK, BLOCK), BLOCK)
            key = source[first : first + BLOCK, :HD]
            keys[at, :] = key
            values[at, :] = source[first : first + BLOCK, HD:]
            keys_t[:, at] = key.astype(F32).T.astype(BF16)
            docs[slot] = source[kv_local * BLOCK :, :].astype(F32)[0:8]
            slots.append(at)

    wide = 2 * BLOCK
    reach = (blocks - 1) * BLOCK
    row = lax.broadcasted_iota(jnp.int32, (BLOCK, wide), 0)
    col = lax.rem(lax.broadcasted_iota(jnp.int32, (BLOCK, wide), 1), BLOCK)
    triangle = row <= col
    factor = SCALE * math.log2(math.e)
    gain_t = jnp.broadcast_to(facts[0:1] * SCALE, (HD, HD)).T
    gain_t = jnp.concatenate([gain_t] * 2, axis=1)
    pairs = heads // 2
    doc_rows = [docs[slot][0:1] for slot in range(blocks)]
    biases, weights = [], []
    for side in range(2):
        own_doc = doc_rows[blocks - 2 + side]
        biases.append(
            [
                jnp.where((doc == own_doc) & (doc > 0.0), 0.0, NEG)
                for doc in doc_rows[side : side + blocks - 1]
            ]
        )
        weights.append(jnp.concatenate([facts[8 * (side + 1) : 8 * (side + 1) + 1]] * 2, axis=1))

    def scores(step):
        side, here, buf = step // pairs, slice(step * wide, (step + 1) * wide), step % 2
        span = slice(side * BLOCK, side * BLOCK + reach)
        expo[buf] = lax.dot_general(
            keys[span, :], q_hat[here, :], NT, preferred_element_type=F32
        )
        dots[buf] = lax.dot_general(
            values[span, :], rows[here, :], NT, preferred_element_type=F32
        )

    def middle(step):
        side, buf = step // pairs, step % 2
        total = jnp.zeros((8, wide), F32)
        weighted = jnp.zeros((8, wide), F32)
        for block in range(blocks - 1):
            r = slice(block * BLOCK, (block + 1) * BLOCK)
            value = jnp.exp2(expo[buf, r, :] * factor + biases[side][block])
            if block == blocks - 2:
                value = jnp.where(triangle, value, 0.0)
            expo[buf, r, :] = value
            total = total + jnp.sum(value.reshape(BLOCK // 8, 8, wide), axis=0)
            weighted = weighted + jnp.sum(
                (value * dots[buf, r, :]).reshape(BLOCK // 8, 8, wide), axis=0
            )
        inverse = 1.0 / jnp.sum(total, axis=0, keepdims=True)
        shift = jnp.sum(weighted, axis=0, keepdims=True) * inverse
        level = inverse * weights[side]
        for block in range(blocks - 1):
            r = slice(block * BLOCK, (block + 1) * BLOCK)
            scaled = expo[buf, r, :] * level
            pw_half[buf, r, :] = scaled.astype(BF16)
            ds_half[buf, r, :] = (scaled * (dots[buf, r, :] - shift)).astype(BF16)

    def backward(step):
        side, here, buf = step // pairs, slice(step * wide, (step + 1) * wide), step % 2
        span = slice(side * BLOCK, side * BLOCK + reach)
        dv_part = jnp.dot(pw_half[buf], rows[here, :], preferred_element_type=F32)
        dk_part = jnp.dot(ds_half[buf], q_hat[here, :], preferred_element_type=F32)
        if step == 0:
            dv[span, :] = dv_part
            dk[span, :] = dk_part
            dv[reach:, :] = jnp.zeros((BLOCK, HD), F32)
            dk[reach:, :] = jnp.zeros((BLOCK, HD), F32)
        else:
            dv[span, :] += dv_part
            dk[span, :] += dk_part
        dq_t = jnp.dot(keys_t[:, span], ds_half[buf], preferred_element_type=F32)
        x = raw_t[:, here].astype(F32)
        inverse = lax.rsqrt(jnp.mean(x * x, axis=0, keepdims=True) + norm_eps)
        dy = dq_t * gain_t
        inner = jnp.mean(x * dy, axis=0, keepdims=True)
        dx = inverse * dy - x * (inverse * inverse * inverse * inner)
        for part in range(2):
            at = (step % pairs) * wide + part * HD
            dq[at : at + HD, side * BLOCK : (side + 1) * BLOCK] = dx[
                :, part * BLOCK : (part + 1) * BLOCK
            ].astype(BF16)

    steps = 2 * pairs
    scores(0)
    for step in range(steps):
        if step + 1 < steps:
            scores(step + 1)
        middle(step)
        backward(step)

    for index, out in enumerate(outs):
        for block in range(2):
            at = slots[2 * index + block]
            r = slice(block * BLOCK, (block + 1) * BLOCK)
            out[r, :HD] = (dk[at, :] * SCALE).astype(out.dtype)
            out[r, HD:] = dv[at, :].astype(out.dtype)
    for copy in copies:
        copy.wait()


def project_kernel(width, where, dq, weight, keep, send):
    core = lax.rem(lax.axis_index("ctx"), 2)
    rows = min(256, width)
    for i in range(width // rows):
        lanes = slice(i * rows, (i + 1) * rows)
        at = pl.ds(pl.multiple_of(where[0] * width + i * rows, rows), rows)
        term = jnp.dot(weight[at, :], dq[...], preferred_element_type=F32).T
        even, odd = term[:BLOCK], term[BLOCK:]
        keep[:, lanes] = jnp.where(core == 0, even, odd).astype(keep.dtype)
        send[:, lanes] = jnp.where(core == 0, odd, even).astype(send.dtype)


def project(dq, weight, slice_index, width):
    tokens = dq.shape[1]
    out = jax.ShapeDtypeStruct((tokens // 2, width), BF16)
    return pl.pallas_call(
        functools.partial(project_kernel, width),
        in_specs=[smem(), vmem(), vmem()],
        out_specs=[vmem()] * 2,
        out_shape=[out, out],
        compiler_params=params(16),
        cost_estimate=pl.CostEstimate(flops=1, bytes_accessed=1, transcendentals=0),
    )(slice_index.reshape(1).astype(jnp.int32), dq, weight)


def add_kernel(a, b, out):
    out[...] = (a[...].astype(F32) + b[...].astype(F32)).astype(out.dtype)


def add_three_kernel(a, b, c, out):
    out[...] = (a[...].astype(F32) + b[...].astype(F32) + c[...].astype(F32)).astype(out.dtype)


def collect_kernel(part_own, a, b, c, d, e, keep, send):
    result = part_own[...]
    for back in (a, b, c, d, e):
        result = result + back[...].astype(F32)
    keep[...] = result[:BLOCK]
    send[...] = result[BLOCK:].astype(BF16)


def finish_kernel(
    kv_local, keep, recv, key, gain, grad_key, grad_value, key_v, gain_v, sems
):
    copies = [
        pltpu.make_async_copy(key, key_v, sems.at[0]),
        pltpu.make_async_copy(gain, gain_v, sems.at[1]),
    ]
    for copy in copies:
        copy.start()
    for copy in copies:
        copy.wait()
    core = lax.rem(lax.axis_index("ctx"), 2)
    if kv_local > 1:
        parts = [(core, keep[...]), (1 - core, recv[...].astype(F32))]
    else:
        parts = [(0, keep[...] + recv[...].astype(F32))]
    for head, part in parts:
        lanes = pl.ds(pl.multiple_of(head * HD, HD), HD)
        raw = key_v[:, lanes].astype(F32)
        inverse = lax.rsqrt(jnp.mean(raw * raw, axis=-1, keepdims=True) + norm_eps)
        dy = part[:, :HD] * gain_v[...]
        inner = jnp.mean(raw * dy, axis=-1, keepdims=True)
        dx = inverse * dy - raw * (inverse * inverse * inverse * inner)
        grad_key[:, lanes] = dx.astype(BF16)
        grad_value[:, lanes] = part[:, HD:].astype(BF16)


def local(
    query_raw,
    key_raw,
    value_in,
    grad_out,
    query_gain,
    key_gain,
    loss_table,
    loss_bucket,
    block_docs,
    query_weight,
):
    tokens = query_raw.shape[0]
    kv_local = key_raw.shape[1] // HD
    half = query_raw.shape[1] // 2
    heads = half // HD
    key_row = key_gain.reshape(1, HD)
    query_row = query_gain.reshape(1, HD)
    shape = jax.ShapeDtypeStruct

    partner = lambda i: i ^ 1
    message, facts = pl.pallas_call(
        functools.partial(message_kernel, kv_local),
        in_specs=[smem(), smem()] + [vmem()] * 5,
        out_specs=[vmem()] * 2,
        out_shape=[
            shape((kv_local * BLOCK + EXTRA, 2 * HD), BF16),
            shape((16, HD), F32),
        ],
    )(
        block_docs,
        loss_table,
        key_raw,
        value_in,
        key_row,
        query_row,
        loss_bucket.reshape(1, tokens),
    )

    far_d = moved(message, "ctx", lambda i: i + 8)
    far_b = moved(message, "ctx", lambda i: i + 4)
    far_a = moved(message, "ctx", lambda i: i + 2 if (i // 2) % 2 == 0 else i + 10)
    query_in, grad_in, _ = lax.optimization_barrier((query_raw, grad_out, message))
    query_p = moved(query_in, "ctx", partner)
    grad_p = moved(grad_in, "ctx", partner)
    facts_p = moved(facts, "ctx", partner)
    total = 2 * heads * BLOCK
    queries = pl.pallas_call(
        functools.partial(queries_kernel, heads),
        in_specs=[vmem()] * 7,
        out_specs=[vmem()] * 5,
        out_shape=[
            shape((total, HD), BF16),
            shape((total, HD), BF16),
            shape((HD, total), BF16),
            shape((24, HD), F32),
            shape(message.shape, BF16),
        ],
        compiler_params=params(16),
    )(query_in, grad_in, facts, message, query_p, grad_p, facts_p)
    far_c = moved(far_b, "ctx", lambda i: i ^ 2)
    far_d, *queries = lax.optimization_barrier((far_d, *queries))
    far_e = moved(far_d, "ctx", lambda i: i ^ 2)
    *queries, kept = queries
    sources = (kept, far_a, far_b, far_c, far_d, far_e)
    shared = [moved(source, "ctx", partner) for source in (message, *sources[1:])]

    span = 2 * BLOCK
    n_rows = 6 * span
    far_shape = shape((span, 2 * HD), BF16)
    reach = n_rows - BLOCK
    dq, weight, part_own, part_a, part_b, part_c, part_d, part_e = pl.pallas_call(
        functools.partial(attention_kernel, kv_local, heads, HOPS),
        in_specs=[vmem()] * 16 + [hbm()],
        out_specs=[vmem()] * 8,
        out_shape=[
            shape((half, 2 * tokens), BF16),
            shape((query_weight.shape[0], half), BF16),
            shape((span, 2 * HD), F32),
        ]
        + [far_shape] * 5,
        scratch_shapes=[
            pltpu.VMEM((12, 8, 2 * HD), F32),
            pltpu.VMEM((n_rows, HD), BF16),
            pltpu.VMEM((n_rows, HD), BF16),
            pltpu.VMEM((HD, n_rows), BF16),
            pltpu.VMEM((2, reach, span), F32),
            pltpu.VMEM((2, reach, span), F32),
            pltpu.VMEM((2, reach, span), BF16),
            pltpu.VMEM((2, reach, span), BF16),
            pltpu.VMEM((n_rows, HD), F32),
            pltpu.VMEM((n_rows, HD), F32),
            pltpu.SemaphoreType.DMA((4,)),
        ],
        compiler_params=params(36),
    )(*sources, *shared, *queries, query_weight)

    n_head = lax.axis_size("head")
    head = lax.axis_index("head")
    width = query_weight.shape[0] // n_head
    term_shape = shape((tokens, width), BF16)
    arrived = []
    for shift in range(1, n_head):
        keep, send = project(dq, weight, (head + shift) % n_head, width)
        recv = moved(send, "ctx", partner)
        term = pl.pallas_call(
            add_kernel,
            in_specs=[vmem()] * 2,
            out_specs=vmem(),
            out_shape=term_shape,
            compiler_params=params(16),
        )(keep, recv)
        arrived.append(moved(term, "head", lambda i, s=shift: (i + s) % n_head))
    dq, weight, part_a, part_b, part_c, _ = lax.optimization_barrier(
        (dq, weight, part_a, part_b, part_c, term)
    )
    mine, mine_send = project(dq, weight, head, width)
    mine_recv = moved(mine_send, "ctx", partner)

    back_d = moved(part_d, "ctx", lambda i: i - 8)
    back_e = moved(part_e, "ctx", lambda i: (i ^ 2) - 8)
    back_c = moved(part_c, "ctx", lambda i: (i ^ 2) - 4)
    back_b = moved(part_b, "ctx", lambda i: i - 4)
    back_a = moved(part_a, "ctx", lambda i: i - 2 if (i // 2) % 2 == 1 else i - 10)
    grad_input = mine
    for index, piece in enumerate(arrived):
        last = index == len(arrived) - 1
        grad_input = pl.pallas_call(
            add_three_kernel if last else add_kernel,
            in_specs=[vmem()] * (3 if last else 2),
            out_specs=vmem(),
            out_shape=shape((tokens, width), BF16 if last else F32),
            compiler_params=params(16),
        )(grad_input, *([mine_recv] if last else []), piece)
    back_a, grad_input = lax.optimization_barrier((back_a, grad_input))
    sum_keep, sum_send = pl.pallas_call(
        collect_kernel,
        in_specs=[vmem()] * 6,
        out_specs=[vmem()] * 2,
        out_shape=[shape((BLOCK, 2 * HD), F32), shape((BLOCK, 2 * HD), BF16)],
        compiler_params=params(16),
    )(part_own, back_a, back_b, back_c, back_d, back_e)
    sum_recv = moved(sum_send, "ctx", partner)
    grad_key, grad_value = pl.pallas_call(
        functools.partial(finish_kernel, kv_local),
        in_specs=[vmem(), vmem(), hbm(), hbm()],
        out_specs=[vmem()] * 2,
        out_shape=[shape(key_raw.shape, BF16), shape(value_in.shape, BF16)],
        scratch_shapes=[
            pltpu.VMEM(key_raw.shape, BF16),
            pltpu.VMEM((1, HD), F32),
            pltpu.SemaphoreType.DMA((2,)),
        ],
        compiler_params=params(16),
    )(sum_keep, sum_recv, key_raw, key_row)

    return grad_input, grad_key, grad_value


def solution(mesh):
    placed = (
        P("ctx", "head"),
        P("ctx", "head"),
        P("ctx", "head"),
        P("ctx", "head"),
        P(),
        P(),
        P(),
        P("ctx"),
        P("ctx"),
        P(None, "head"),
    )
    return jax.shard_map(
        local,
        mesh=mesh,
        in_specs=placed,
        out_specs=(P("ctx", "head"), P("ctx", "head"), P("ctx", "head")),
        check_vma=False,
    )
```

time: 325 us -> 73.3 us (0.23)
  starting transfers between devices: 106 us -> 25.1 us
  matrix products: 74.9 us -> 0 us
  local copies, waits for them, and re-layouts: 46.1 us -> 3.69 us
  other arithmetic: 24.1 us -> 0 us
  between operations: 22.2 us -> 1.48 us
  Pallas kernels: 0 us -> 19.5 us
  loops' own time: 19.4 us -> 0 us
  waiting for transfers between devices: 29.2 us -> 22.6 us
    ppermute x50 -> x23, starting transfers between devices: 106 us -> 25.1 us  [moved(): lax.ppermute(array, axis, [(i, t) for i, t in pairs if t is not None and...]
    dot_general x77 -> x0, matrix products: 74.9 us -> none  [the longest x21 21.5 us: block_scores(): jnp.einsum('tkgd,skd->kgts', q_hat, keys, preferred_element_type=jnp.floa...]
    pallas_call x0 -> x9, Pallas kernels: none -> 19.5 us  [the longest x1 12.5 us: local(): pl.pallas_call(functools.partial(attention_kernel, kv_local, heads, HOPS)...]
    another operation x1 -> x0, loops' own time: 19.4 us -> none  [local(): lax.scan(forward_step, (start_block, zero_total, zero_weighted), jnp.aran...]
    dynamic_update_slice x20 -> x0, local copies, waits for them, and re-layouts: 19.2 us -> none  [local(): lax.scan(forward_step, (start_block, zero_total, zero_weighted), jnp.aran...]
    dynamic_slice x10 -> x0, local copies, waits for them, and re-layouts: 12.5 us -> none  [local(): lax.scan(forward_step, (start_block, zero_total, zero_weighted), jnp.aran...]
    add x37 -> x0, other arithmetic: 11.2 us -> none  [the longest x11 5.71 us: local(): q_pos = rank * tokens + offsets]
    and x12 -> x0, other arithmetic: 9.26 us -> none  [block_scores(): (q_docs[:, None] == spread_docs(docs)[None, :]) & (k_pos[None, :] <= q_po...]
  transfers between devices with their start and end apart: 51 -> 23, of which waited for: 10 -> 10; matrix products, arithmetic and copies ran while one was open for 39% -> 0% of each run, Pallas kernels for 0% -> 2%
where the time goes in v3:
time: 73.3 us; the launch traced here: 72.4 us
  starting transfers between devices  25.1 us (34%)
  waiting for transfers between devices  22.6 us (31%)
  Pallas kernels  19.5 us (27%)
  local copies, waits for them, and re-layouts  3.69 us (5%)
  between operations  1.48 us (2%)
    ppermute x23, starting transfers between devices, moved(): lax.ppermute(array, axis, [(i, t) for i, t in pairs if t is not None and...  25.1 us
    ppermute x23, waiting for transfers between devices, moved(): lax.ppermute(array, axis, [(i, t) for i, t in pairs if t is not None and...  22.6 us
    pallas_call x1, Pallas kernels, local(): pl.pallas_call(functools.partial(attention_kernel, kv_local, heads, HOPS)...  12.5 us
    unnamed x12, local copies, waits for them, and re-layouts  3.69 us
    pallas_call x2, Pallas kernels, project(): pl.pallas_call(functools.partial(project_kernel, width), in_specs=[smem()...  2.72 us
    pallas_call x1, Pallas kernels, local(): pl.pallas_call(functools.partial(message_kernel, kv_local), in_specs=[sme...  1.7 us
  transfers between devices with their start and end apart: 23, of which 10 were waited for; matrix products, arithmetic and copies ran while one was open for 0% of the time, Pallas kernels for 2%

profile of v3, /device:TPU:0, one launch (start us, length us, event | category | flops | bytes accessed | tf_op | source)
XLA Modules:
  0.0 72.4 jit_solution(15577108707723831345)
XLA Ops:
  1.3 1.7 %shard_map.121 = (bf16[272,256]{1,0:T(8,128)(2,1)}, f32[16,128]{1,0:T(8,128)}) custom-call(s32[1]{0:T(128)S(6)} %copy.13.docs, f32[16]{0:T(128)} %table.1, bf16[128,256]{1,0:T(8,128)(2,1)} %key.3, bf16[128,256]{1,0:T(8,128)(2,1)} %value.1, f32[1,128]{1,0:T(1,128)} %bitcast.5, f32[1,128]{1,0:T(1,128)} %bitcast.7, s32[1,128]{1,0:T(1,128)} %bitcast.8), custom_call_target="tpu_custom_call" | custom-call | tf_op jit(solution)/shard_map/pallas_call | solution.py:342
  3.0 0.5 collective-permute-start.1
  3.4 0.1 collective-permute-start.2
  3.5 4.9 %collective-permute-start.5 = (bf16[272,256]{1,0:T(8,128)(2,1)}, bf16[272,256]{1,0:T(8,128)(2,1)S(1)}, u32[]{:S(2)}, u32[]{:S(2)}) collective-permute-start(bf16[272,256]{1,0:T(8,128)(2,1)} %get-tuple-element.41.message), channel_id=1, source_target_pairs={{0,8},{2,10},{4,12},{6,14},{8,16},{10,18},{12,20},{14,22},{16,24},... | collective-permute-start | bytes 417800 | tf_op jit(solution)/shard_map/ppermute | solution.py:26
  8.4 4.5 %collective-permute-start = (bf16[272,256]{1,0:T(8,128)(2,1)}, bf16[272,256]{1,0:T(8,128)(2,1)S(1)}, u32[]{:S(2)}, u32[]{:S(2)}) collective-permute-start(bf16[272,256]{1,0:T(8,128)(2,1)} %get-tuple-element.41.message), channel_id=1, source_target_pairs={{0,16},{2,18},{4,20},{6,22},{8,24},{10,26},{12,28},{14,30},{1,17},... | collective-permute-start | bytes 417800 | tf_op jit(solution)/shard_map/ppermute | solution.py:26
  12.9 0.1 collective-permute-start.3
  13.0 1.4 %collective-permute-done.3.facts_p = f32[16,128]{1,0:T(8,128)S(1)} collective-permute-done((f32[16,128]{1,0:T(8,128)}, f32[16,128]{1,0:T(8,128)S(1)}, u32[]{:S(2)}, u32[]{:S(2)}) %collective-permute-start.3) | collective-permute-done | bytes 8224 | tf_op jit(solution)/shard_map/ppermute | solution.py:26
  14.4 3.4 %collective-permute-start.4 = (bf16[272,256]{1,0:T(8,128)(2,1)}, bf16[272,256]{1,0:T(8,128)(2,1)S(1)}, u32[]{:S(2)}, u32[]{:S(2)}) collective-permute-start(bf16[272,256]{1,0:T(8,128)(2,1)} %get-tuple-element.41.message), channel_id=1, source_target_pairs={{0,4},{2,6},{4,24},{6,26},{8,12},{10,14},{16,20},{18,22},{24,28},{... | collective-permute-start | bytes 417800 | tf_op jit(solution)/shard_map/ppermute | solution.py:26
  17.8 0.1 collective-permute-start.8
  17.9 0.0 collective-permute-done.1.query_p
  17.9 0.2 collective-permute-start.6
  18.1 1.0 %copy-done = bf16[128,2048]{1,0:T(8,128)(2,1)S(1)} copy-done((bf16[128,2048]{1,0:T(8,128)(2,1)S(1)}, bf16[128,2048]{1,0:T(8,128)(2,1)}, u32[]{:S(2)}) %copy-start) | copy-done | bytes 524312
  19.1 1.0 %copy-done.1 = bf16[128,2048]{1,0:T(8,128)(2,1)S(1)} copy-done((bf16[128,2048]{1,0:T(8,128)(2,1)S(1)}, bf16[128,2048]{1,0:T(8,128)(2,1)}, u32[]{:S(2)}) %copy-start.1) | copy-done | bytes 524312
  20.1 0.9 %copy-done.3 = bf16[272,256]{1,0:T(8,128)(2,1)S(1)} copy-done((bf16[272,256]{1,0:T(8,128)(2,1)S(1)}, bf16[272,256]{1,0:T(8,128)(2,1)}, u32[]{:S(2)}) %copy-start.3) | copy-done | bytes 139288
  21.1 0.7 copy-done.4
  21.8 0.5 shard_map.122
  22.3 2.0 %collective-permute-start.7 = (bf16[272,256]{1,0:T(8,128)(2,1)S(1)}, bf16[272,256]{1,0:T(8,128)(2,1)S(1)}, u32[]{:S(2)}, u32[]{:S(2)}) collective-permute-start(bf16[272,256]{1,0:T(8,128)(2,1)S(1)} %collective-permute-done.refs_4_), channel_id=1, source_target_pairs={{0,4},{2,6},{4,0},{6,2},{8,12},{10,14},{12,8},{14,10},{16,20},{18,... | collective-permute-start | bytes 417800 | tf_op jit(solution)/shard_map/ppermute | solution.py:26
  24.3 0.0 collective-permute-start.10
  24.3 0.0 collective-permute-done.4.refs_1_
  24.3 0.5 collective-permute-start.9
  24.8 0.0 collective-permute-done.6.refs_3_
  24.8 0.1 collective-permute-start.11
  24.9 0.4 collective-permute-start.12
  25.3 3.0 %collective-permute-done.7.refs_5_ = bf16[272,256]{1,0:T(8,128)(2,1)S(1)} collective-permute-done((bf16[272,256]{1,0:T(8,128)(2,1)S(1)}, bf16[272,256]{1,0:T(8,128)(2,1)S(1)}, u32[]{:S(2)}, u32[]{:S(2)}) %collective-permute-start.7) | collective-permute-done | bytes 139296 | tf_op jit(solution)/shard_map/ppermute | solution.py:26
  28.3 1.3 %collective-permute-done.13.refs_11_ = bf16[272,256]{1,0:T(8,128)(2,1)S(1)} collective-permute-done((bf16[272,256]{1,0:T(8,128)(2,1)S(1)}, bf16[272,256]{1,0:T(8,128)(2,1)S(1)}, u32[]{:S(2)}, u32[]{:S(2)}) %collective-permute-start.13) | collective-permute-done | bytes 139296 | tf_op jit(solution)/shard_map/ppermute | solution.py:26
  29.7 12.5 %shard_map.123 = (bf16[1024,256]{1,0:T(8,128)(2,1)S(1)}, bf16[4096,1024]{1,0:T(8,128)(2,1)S(1)}, f32[256,256]{1,0:T(8,128)S(1)}, bf16[256,256]{1,0:T(8,128)(2,1)...) custom-call(bf16[272,256]{1,0:T(8,128)(2,1)S(1)} %get-tuple-element., ...), custom_call_target="tpu_custom_call" | custom-call | tf_op jit(solution)/shard_map/pallas_call | solution.py:392
  42.1 1.4 %shard_map.124 = (bf16[128,2048]{1,0:T(8,128)(2,1)S(1)}, bf16[128,2048]{1,0:T(8,128)(2,1)S(1)}) custom-call(s32[1]{0:T(128)} %bitcast.3.where, bf16[1024,256]{1,0:T(8,128)(2,1)S(1)} %get-tuple-element.64.dq, bf16[4096,1024]{1,0:T(8,128)(2,1)S(1)} %get-tuple-element.65.weight), custom_call_target="tpu_custom_call" | custom-call | flops 1 | bytes 1 | tf_op jit(solution)/shard_map/pallas_call | solution.py:268
  43.5 0.2 collective-permute-start.14
  43.7 1.8 %collective-permute-done.14.b = bf16[128,2048]{1,0:T(8,128)(2,1)S(1)} collective-permute-done((bf16[128,2048]{1,0:T(8,128)(2,1)S(1)}, bf16[128,2048]{1,0:T(8,128)(2,1)S(1)}, u32[]{:S(2)}, u32[]{:S(2)}) %collective-permute-start.14) | collective-permute-done | bytes 524320 | tf_op jit(solution)/shard_map/ppermute | solution.py:26
  45.5 0.1 shard_map.125
  45.6 1.4 %shard_map.126 = (bf16[128,2048]{1,0:T(8,128)(2,1)S(1)}, bf16[128,2048]{1,0:T(8,128)(2,1)S(1)}) custom-call(s32[1]{0:T(128)} %bitcast.4.where, bf16[1024,256]{1,0:T(8,128)(2,1)S(1)} %get-tuple-element.64.dq, bf16[4096,1024]{1,0:T(8,128)(2,1)S(1)} %get-tuple-element.65.weight), custom_call_target="tpu_custom_call" | custom-call | flops 1 | bytes 1 | tf_op jit(solution)/shard_map/pallas_call | solution.py:268
  47.0 0.2 collective-permute-start.16
  47.2 1.5 %collective-permute-start.17 = (bf16[128,2048]{1,0:T(8,128)(2,1)S(1)}, bf16[128,2048]{1,0:T(8,128)(2,1)S(1)}, u32[]{:S(2)}, u32[]{:S(2)}) collective-permute-start(bf16[128,2048]{1,0:T(8,128)(2,1)S(1)} %shard_map.125), channel_id=1, source_target_pairs={{0,1},{1,0},{2,3},{3,2},{4,5},{5,4},{6,7},{7,6},{8,9},{9,8},{10,11... | collective-permute-start | bytes 1572872 | tf_op jit(solution)/shard_map/ppermute | solution.py:26
  48.7 1.3 %collective-permute-start.20 = (bf16[256,256]{1,0:T(8,128)(2,1)S(1)}, bf16[256,256]{1,0:T(8,128)(2,1)S(1)}, u32[]{:S(2)}, u32[]{:S(2)}) collective-permute-start(bf16[256,256]{1,0:T(8,128)(2,1)S(1)} %get-tuple-element.73), channel_id=1, source_target_pairs={{16,0},{18,2},{20,4},{22,6},{24,8},{26,10},{28,12},{30,14},{17,1},... | collective-permute-start | bytes 393224 | tf_op jit(solution)/shard_map/ppermute | solution.py:26
  50.0 1.3 %collective-permute-start.21 = (bf16[256,256]{1,0:T(8,128)(2,1)S(1)}, bf16[256,256]{1,0:T(8,128)(2,1)S(1)}, u32[]{:S(2)}, u32[]{:S(2)}) collective-permute-start(bf16[256,256]{1,0:T(8,128)(2,1)S(1)} %get-tuple-element.74), channel_id=1, source_target_pairs={{16,4},{18,6},{20,0},{22,2},{24,12},{26,14},{28,8},{30,10},{17,5},... | collective-permute-start | bytes 393224 | tf_op jit(solution)/shard_map/ppermute | solution.py:26
  51.3 1.3 %collective-permute-start.15 = (bf16[256,256]{1,0:T(8,128)(2,1)S(1)}, bf16[256,256]{1,0:T(8,128)(2,1)S(1)}, u32[]{:S(2)}, u32[]{:S(2)}) collective-permute-start(bf16[256,256]{1,0:T(8,128)(2,1)S(1)} %get-tuple-element.63), channel_id=1, source_target_pairs={{4,0},{6,2},{12,8},{14,10},{20,16},{22,18},{24,4},{26,6},{28,24},{... | collective-permute-start | bytes 393224 | tf_op jit(solution)/shard_map/ppermute | solution.py:26
  52.6 1.3 %collective-permute-start.18 = (bf16[256,256]{1,0:T(8,128)(2,1)S(1)}, bf16[256,256]{1,0:T(8,128)(2,1)S(1)}, u32[]{:S(2)}, u32[]{:S(2)}) collective-permute-start(bf16[256,256]{1,0:T(8,128)(2,1)S(1)} %get-tuple-element.71), channel_id=1, source_target_pairs={{8,0},{10,2},{12,4},{14,6},{16,8},{18,10},{20,12},{22,14},{24,16},... | collective-permute-start | bytes 393224 | tf_op jit(solution)/shard_map/ppermute | solution.py:26
  53.9 7.5 %collective-permute-done.17.c = bf16[128,2048]{1,0:T(8,128)(2,1)S(1)} collective-permute-done((bf16[128,2048]{1,0:T(8,128)(2,1)S(1)}, bf16[128,2048]{1,0:T(8,128)(2,1)S(1)}, u32[]{:S(2)}, u32[]{:S(2)}) %collective-permute-start.17) | collective-permute-done | bytes 524320 | tf_op jit(solution)/shard_map/ppermute | solution.py:26
  61.4 1.3 %collective-permute-start.19 = (bf16[256,256]{1,0:T(8,128)(2,1)S(1)}, bf16[256,256]{1,0:T(8,128)(2,1)S(1)}, u32[]{:S(2)}, u32[]{:S(2)}) collective-permute-start(bf16[256,256]{1,0:T(8,128)(2,1)S(1)} %get-tuple-element.72), channel_id=1, source_target_pairs={{8,4},{10,6},{12,0},{14,2},{16,12},{18,14},{20,8},{22,10},{24,20},... | collective-permute-start | bytes 393224 | tf_op jit(solution)/shard_map/ppermute | solution.py:26
  62.7 1.0 %shard_map.127 = bf16[128,2048]{1,0:T(8,128)(2,1)} custom-call(bf16[128,2048]{1,0:T(8,128)(2,1)S(1)} %get-tuple-element.66.a, bf16[128,2048]{1,0:T(8,128)(2,1)S(1)} %collective-permute-done.16.b, bf16[128,2048]{1,0:T(8,128)(2,1)S(1)} %collective-permute-done.17.c), custom_call_target="tpu_custom_call" | custom-call | tf_op jit(solution)/shard_map/pallas_call | solution.py:448
  63.6 0.7 %collective-permute-done.20.d = bf16[256,256]{1,0:T(8,128)(2,1)S(1)} collective-permute-done((bf16[256,256]{1,0:T(8,128)(2,1)S(1)}, bf16[256,256]{1,0:T(8,128)(2,1)S(1)}, u32[]{:S(2)}, u32[]{:S(2)}) %collective-permute-start.20) | collective-permute-done | bytes 131104 | tf_op jit(solution)/shard_map/ppermute | solution.py:26
  64.4 1.1 %collective-permute-done.21.e = bf16[256,256]{1,0:T(8,128)(2,1)S(1)} collective-permute-done((bf16[256,256]{1,0:T(8,128)(2,1)S(1)}, bf16[256,256]{1,0:T(8,128)(2,1)S(1)}, u32[]{:S(2)}, u32[]{:S(2)}) %collective-permute-start.21) | collective-permute-done | bytes 131104 | tf_op jit(solution)/shard_map/ppermute | solution.py:26
  65.5 3.6 %collective-permute-done.18.b = bf16[256,256]{1,0:T(8,128)(2,1)S(1)} collective-permute-done((bf16[256,256]{1,0:T(8,128)(2,1)S(1)}, bf16[256,256]{1,0:T(8,128)(2,1)S(1)}, u32[]{:S(2)}, u32[]{:S(2)}) %collective-permute-start.18) | collective-permute-done | bytes 131104 | tf_op jit(solution)/shard_map/ppermute | solution.py:26
  69.2 0.9 %collective-permute-done.19.c = bf16[256,256]{1,0:T(8,128)(2,1)S(1)} collective-permute-done((bf16[256,256]{1,0:T(8,128)(2,1)S(1)}, bf16[256,256]{1,0:T(8,128)(2,1)S(1)}, u32[]{:S(2)}, u32[]{:S(2)}) %collective-permute-start.19) | collective-permute-done | bytes 131104 | tf_op jit(solution)/shard_map/ppermute | solution.py:26
  70.0 0.1 shard_map.128
  70.1 0.1 collective-permute-start.22
  70.2 1.2 %collective-permute-done.22.recv = bf16[128,256]{1,0:T(8,128)(2,1)S(1)} collective-permute-done((bf16[128,256]{1,0:T(8,128)(2,1)S(1)}, bf16[128,256]{1,0:T(8,128)(2,1)S(1)}, u32[]{:S(2)}, u32[]{:S(2)}) %collective-permute-start.22) | collective-permute-done | bytes 65568 | tf_op jit(solution)/shard_map/ppermute | solution.py:26
  71.5 0.9 %shard_map.129 = (bf16[128,256]{1,0:T(8,128)(2,1)}, bf16[128,256]{1,0:T(8,128)(2,1)}) custom-call(f32[128,256]{1,0:T(8,128)S(1)} %get-tuple-element.75.keep, bf16[128,256]{1,0:T(8,128)(2,1)S(1)} %collective-permute-done.22.recv, bf16[128,256]{1,0:T(8,128)(2,1)S(1)} %copy-done.2, f32[1,128]{1,0:T(1,128)S(1)} %bitcast.6), custom_call_target="tpu_custom_call" | custom-call | tf_op jit(solution)/shard_map/pallas_call | solution.py:464
  (19 shorter events, 0.0 us)
Async XLA Ops:
  3.0 14.9 %collective-permute-start.1 = (bf16[128,2048]{1,0:T(8,128)(2,1)}, bf16[128,2048]{1,0:T(8,128)(2,1)S(1)}, u32[]{:S(2)}, u32[]{:S(2)}) collective-permute-start(bf16[128,2048]{1,0:T(8,128)(2,1)} %query), channel_id=1, source_target_pairs={{0,2},{2,0},{4,6},{6,4},{8,10},{10,8},{12,14},{14,12},{16,18},{18,... | collective-permute-start | bytes 1572872 | tf_op jit(solution)/shard_map/ppermute | solution.py:26
  3.4 14.6 %collective-permute-start.2 = (bf16[128,2048]{1,0:T(8,128)(2,1)}, bf16[128,2048]{1,0:T(8,128)(2,1)S(1)}, u32[]{:S(2)}, u32[]{:S(2)}) collective-permute-start(bf16[128,2048]{1,0:T(8,128)(2,1)} %grad), channel_id=1, source_target_pairs={{0,2},{2,0},{4,6},{6,4},{8,10},{10,8},{12,14},{14,12},{16,18},{18,... | collective-permute-start | bytes 1572872 | tf_op jit(solution)/shard_map/ppermute | solution.py:26
  3.5 14.3 %collective-permute-start.5 = (bf16[272,256]{1,0:T(8,128)(2,1)}, bf16[272,256]{1,0:T(8,128)(2,1)S(1)}, u32[]{:S(2)}, u32[]{:S(2)}) collective-permute-start(bf16[272,256]{1,0:T(8,128)(2,1)} %get-tuple-element.41.message), channel_id=1, source_target_pairs={{0,8},{2,10},{4,12},{6,14},{8,16},{10,18},{12,20},{14,22},{16,24},... | collective-permute-start | bytes 417800 | tf_op jit(solution)/shard_map/ppermute | solution.py:26
  8.4 13.9 %collective-permute-start = (bf16[272,256]{1,0:T(8,128)(2,1)}, bf16[272,256]{1,0:T(8,128)(2,1)S(1)}, u32[]{:S(2)}, u32[]{:S(2)}) collective-permute-start(bf16[272,256]{1,0:T(8,128)(2,1)} %get-tuple-element.41.message), channel_id=1, source_target_pairs={{0,16},{2,18},{4,20},{6,22},{8,24},{10,26},{12,28},{14,30},{1,17},... | collective-permute-start | bytes 417800 | tf_op jit(solution)/shard_map/ppermute | solution.py:26
  12.9 1.4 %collective-permute-start.3 = (f32[16,128]{1,0:T(8,128)}, f32[16,128]{1,0:T(8,128)S(1)}, u32[]{:S(2)}, u32[]{:S(2)}) collective-permute-start(f32[16,128]{1,0:T(8,128)} %get-tuple-element.44.facts), channel_id=1, source_target_pairs={{0,2},{2,0},{4,6},{6,4},{8,10},{10,8},{12,14},{14,12},{16,18},{18,... | collective-permute-start | bytes 24584 | tf_op jit(solution)/shard_map/ppermute | solution.py:26
  14.4 9.9 %collective-permute-start.4 = (bf16[272,256]{1,0:T(8,128)(2,1)}, bf16[272,256]{1,0:T(8,128)(2,1)S(1)}, u32[]{:S(2)}, u32[]{:S(2)}) collective-permute-start(bf16[272,256]{1,0:T(8,128)(2,1)} %get-tuple-element.41.message), channel_id=1, source_target_pairs={{0,4},{2,6},{4,24},{6,26},{8,12},{10,14},{16,20},{18,22},{24,28},{... | collective-permute-start | bytes 417800 | tf_op jit(solution)/shard_map/ppermute | solution.py:26
  17.8 7.1 %collective-permute-start.8 = (bf16[272,256]{1,0:T(8,128)(2,1)}, bf16[272,256]{1,0:T(8,128)(2,1)S(1)}, u32[]{:S(2)}, u32[]{:S(2)}) collective-permute-start(bf16[272,256]{1,0:T(8,128)(2,1)} %get-tuple-element.41.message), channel_id=1, source_target_pairs={{0,2},{2,0},{4,6},{6,4},{8,10},{10,8},{12,14},{14,12},{16,18},{18,... | collective-permute-start | bytes 417800 | tf_op jit(solution)/shard_map/ppermute | solution.py:26
  17.9 6.9 %collective-permute-start.6 = (bf16[272,256]{1,0:T(8,128)(2,1)S(1)}, bf16[272,256]{1,0:T(8,128)(2,1)S(1)}, u32[]{:S(2)}, u32[]{:S(2)}) collective-permute-start(bf16[272,256]{1,0:T(8,128)(2,1)S(1)} %collective-permute-done.5.refs_2_), channel_id=1, source_target_pairs={{0,4},{2,6},{4,0},{6,2},{8,12},{10,14},{12,8},{14,10},{16,20},{18,... | collective-permute-start | bytes 417800 | tf_op jit(solution)/shard_map/ppermute | solution.py:26
  18.1 1.0 %copy-start = (bf16[128,2048]{1,0:T(8,128)(2,1)S(1)}, bf16[128,2048]{1,0:T(8,128)(2,1)}, u32[]{:S(2)}) copy-start(bf16[128,2048]{1,0:T(8,128)(2,1)} %query) | copy-start | bytes 1572868
  19.1 1.0 %copy-start.1 = (bf16[128,2048]{1,0:T(8,128)(2,1)S(1)}, bf16[128,2048]{1,0:T(8,128)(2,1)}, u32[]{:S(2)}) copy-start(bf16[128,2048]{1,0:T(8,128)(2,1)} %grad) | copy-start | bytes 1572868
  20.1 0.9 %copy-start.3 = (bf16[272,256]{1,0:T(8,128)(2,1)S(1)}, bf16[272,256]{1,0:T(8,128)(2,1)}, u32[]{:S(2)}) copy-start(bf16[272,256]{1,0:T(8,128)(2,1)} %get-tuple-element.41.message) | copy-start | bytes 417796
  21.1 0.7 copy-start.4
  22.3 6.0 %collective-permute-start.7 = (bf16[272,256]{1,0:T(8,128)(2,1)S(1)}, bf16[272,256]{1,0:T(8,128)(2,1)S(1)}, u32[]{:S(2)}, u32[]{:S(2)}) collective-permute-start(bf16[272,256]{1,0:T(8,128)(2,1)S(1)} %collective-permute-done.refs_4_), channel_id=1, source_target_pairs={{0,4},{2,6},{4,0},{6,2},{8,12},{10,14},{12,8},{14,10},{16,20},{18,... | collective-permute-start | bytes 417800 | tf_op jit(solution)/shard_map/ppermute | solution.py:26
  24.3 4.0 %collective-permute-start.10 = (bf16[272,256]{1,0:T(8,128)(2,1)S(1)}, bf16[272,256]{1,0:T(8,128)(2,1)S(1)}, u32[]{:S(2)}, u32[]{:S(2)}) collective-permute-start(bf16[272,256]{1,0:T(8,128)(2,1)S(1)} %collective-permute-done.5.refs_2_), channel_id=1, source_target_pairs={{0,2},{2,0},{4,6},{6,4},{8,10},{10,8},{12,14},{14,12},{16,18},{18,... | collective-permute-start | bytes 417800 | tf_op jit(solution)/shard_map/ppermute | solution.py:26
  24.3 4.0 %collective-permute-start.9 = (bf16[272,256]{1,0:T(8,128)(2,1)S(1)}, bf16[272,256]{1,0:T(8,128)(2,1)S(1)}, u32[]{:S(2)}, u32[]{:S(2)}) collective-permute-start(bf16[272,256]{1,0:T(8,128)(2,1)S(1)} %collective-permute-done.4.refs_1_), channel_id=1, source_target_pairs={{0,2},{2,0},{4,6},{6,4},{8,10},{10,8},{12,14},{14,12},{16,18},{18,... | collective-permute-start | bytes 417800 | tf_op jit(solution)/shard_map/ppermute | solution.py:26
  24.8 3.5 %collective-permute-start.11 = (bf16[272,256]{1,0:T(8,128)(2,1)S(1)}, bf16[272,256]{1,0:T(8,128)(2,1)S(1)}, u32[]{:S(2)}, u32[]{:S(2)}) collective-permute-start(bf16[272,256]{1,0:T(8,128)(2,1)S(1)} %collective-permute-done.6.refs_3_), channel_id=1, source_target_pairs={{0,2},{2,0},{4,6},{6,4},{8,10},{10,8},{12,14},{14,12},{16,18},{18,... | collective-permute-start | bytes 417800 | tf_op jit(solution)/shard_map/ppermute | solution.py:26
  24.9 3.4 %collective-permute-start.12 = (bf16[272,256]{1,0:T(8,128)(2,1)S(1)}, bf16[272,256]{1,0:T(8,128)(2,1)S(1)}, u32[]{:S(2)}, u32[]{:S(2)}) collective-permute-start(bf16[272,256]{1,0:T(8,128)(2,1)S(1)} %collective-permute-done.refs_4_), channel_id=1, source_target_pairs={{0,2},{2,0},{4,6},{6,4},{8,10},{10,8},{12,14},{14,12},{16,18},{18,... | collective-permute-start | bytes 417800 | tf_op jit(solution)/shard_map/ppermute | solution.py:26
  28.3 1.4 %collective-permute-start.13 = (bf16[272,256]{1,0:T(8,128)(2,1)S(1)}, bf16[272,256]{1,0:T(8,128)(2,1)S(1)}, u32[]{:S(2)}, u32[]{:S(2)}) collective-permute-start(bf16[272,256]{1,0:T(8,128)(2,1)S(1)} %collective-permute-done.7.refs_5_), channel_id=1, source_target_pairs={{0,2},{2,0},{4,6},{6,4},{8,10},{10,8},{12,14},{14,12},{16,18},{18,... | collective-permute-start | bytes 417800 | tf_op jit(solution)/shard_map/ppermute | solution.py:26
  28.3 43.2 %copy-start.2 = (bf16[128,256]{1,0:T(8,128)(2,1)S(1)}, bf16[128,256]{1,0:T(8,128)(2,1)}, u32[]{:S(2)}) copy-start(bf16[128,256]{1,0:T(8,128)(2,1)} %key.3) | copy-start | bytes 196612
  28.3 43.2 %copy-start.5 = (f32[128]{0:T(128)S(1)}, f32[128]{0:T(128)}, u32[]{:S(2)}) copy-start(f32[128]{0:T(128)} %param.15) | copy-start | bytes 1540
  43.5 2.0 %collective-permute-start.14 = (bf16[128,2048]{1,0:T(8,128)(2,1)S(1)}, bf16[128,2048]{1,0:T(8,128)(2,1)S(1)}, u32[]{:S(2)}, u32[]{:S(2)}) collective-permute-start(bf16[128,2048]{1,0:T(8,128)(2,1)S(1)} %get-tuple-element.62), channel_id=1, source_target_pairs={{0,2},{2,0},{4,6},{6,4},{8,10},{10,8},{12,14},{14,12},{16,18},{18,... | collective-permute-start | bytes 1572872 | tf_op jit(solution)/shard_map/ppermute | solution.py:26
  47.0 5.6 %collective-permute-start.16 = (bf16[128,2048]{1,0:T(8,128)(2,1)S(1)}, bf16[128,2048]{1,0:T(8,128)(2,1)S(1)}, u32[]{:S(2)}, u32[]{:S(2)}) collective-permute-start(bf16[128,2048]{1,0:T(8,128)(2,1)S(1)} %get-tuple-element.67), channel_id=1, source_target_pairs={{0,2},{2,0},{4,6},{6,4},{8,10},{10,8},{12,14},{14,12},{16,18},{18,... | collective-permute-start | bytes 1572872 | tf_op jit(solution)/shard_map/ppermute | solution.py:26
  47.2 14.2 %collective-permute-start.17 = (bf16[128,2048]{1,0:T(8,128)(2,1)S(1)}, bf16[128,2048]{1,0:T(8,128)(2,1)S(1)}, u32[]{:S(2)}, u32[]{:S(2)}) collective-permute-start(bf16[128,2048]{1,0:T(8,128)(2,1)S(1)} %shard_map.125), channel_id=1, source_target_pairs={{0,1},{1,0},{2,3},{3,2},{4,5},{5,4},{6,7},{7,6},{8,9},{9,8},{10,11... | collective-permute-start | bytes 1572872 | tf_op jit(solution)/shard_map/ppermute | solution.py:26
  48.7 15.7 %collective-permute-start.20 = (bf16[256,256]{1,0:T(8,128)(2,1)S(1)}, bf16[256,256]{1,0:T(8,128)(2,1)S(1)}, u32[]{:S(2)}, u32[]{:S(2)}) collective-permute-start(bf16[256,256]{1,0:T(8,128)(2,1)S(1)} %get-tuple-element.73), channel_id=1, source_target_pairs={{16,0},{18,2},{20,4},{22,6},{24,8},{26,10},{28,12},{30,14},{17,1},... | collective-permute-start | bytes 393224 | tf_op jit(solution)/shard_map/ppermute | solution.py:26
  50.0 15.5 %collective-permute-start.21 = (bf16[256,256]{1,0:T(8,128)(2,1)S(1)}, bf16[256,256]{1,0:T(8,128)(2,1)S(1)}, u32[]{:S(2)}, u32[]{:S(2)}) collective-permute-start(bf16[256,256]{1,0:T(8,128)(2,1)S(1)} %get-tuple-element.74), channel_id=1, source_target_pairs={{16,4},{18,6},{20,0},{22,2},{24,12},{26,14},{28,8},{30,10},{17,5},... | collective-permute-start | bytes 393224 | tf_op jit(solution)/shard_map/ppermute | solution.py:26
  51.3 12.4 %collective-permute-start.15 = (bf16[256,256]{1,0:T(8,128)(2,1)S(1)}, bf16[256,256]{1,0:T(8,128)(2,1)S(1)}, u32[]{:S(2)}, u32[]{:S(2)}) collective-permute-start(bf16[256,256]{1,0:T(8,128)(2,1)S(1)} %get-tuple-element.63), channel_id=1, source_target_pairs={{4,0},{6,2},{12,8},{14,10},{20,16},{22,18},{24,4},{26,6},{28,24},{... | collective-permute-start | bytes 393224 | tf_op jit(solution)/shard_map/ppermute | solution.py:26
  52.6 16.6 %collective-permute-start.18 = (bf16[256,256]{1,0:T(8,128)(2,1)S(1)}, bf16[256,256]{1,0:T(8,128)(2,1)S(1)}, u32[]{:S(2)}, u32[]{:S(2)}) collective-permute-start(bf16[256,256]{1,0:T(8,128)(2,1)S(1)} %get-tuple-element.71), channel_id=1, source_target_pairs={{8,0},{10,2},{12,4},{14,6},{16,8},{18,10},{20,12},{22,14},{24,16},... | collective-permute-start | bytes 393224 | tf_op jit(solution)/shard_map/ppermute | solution.py:26
  61.4 8.7 %collective-permute-start.19 = (bf16[256,256]{1,0:T(8,128)(2,1)S(1)}, bf16[256,256]{1,0:T(8,128)(2,1)S(1)}, u32[]{:S(2)}, u32[]{:S(2)}) collective-permute-start(bf16[256,256]{1,0:T(8,128)(2,1)S(1)} %get-tuple-element.72), channel_id=1, source_target_pairs={{8,4},{10,6},{12,0},{14,2},{16,12},{18,14},{20,8},{22,10},{24,20},... | collective-permute-start | bytes 393224 | tf_op jit(solution)/shard_map/ppermute | solution.py:26
  70.1 1.3 %collective-permute-start.22 = (bf16[128,256]{1,0:T(8,128)(2,1)S(1)}, bf16[128,256]{1,0:T(8,128)(2,1)S(1)}, u32[]{:S(2)}, u32[]{:S(2)}) collective-permute-start(bf16[128,256]{1,0:T(8,128)(2,1)S(1)} %get-tuple-element.76), channel_id=1, source_target_pairs={{0,2},{2,0},{4,6},{6,4},{8,10},{10,8},{12,14},{14,12},{16,18},{18,... | collective-permute-start | bytes 196616 | tf_op jit(solution)/shard_map/ppermute | solution.py:26

commit v4 on v3

v4 whole, which is shorter than its diff:
```python
import functools
import math

import jax
import jax.numpy as jnp
from jax import lax
from jax.experimental import pallas as pl
from jax.experimental.pallas import tpu as pltpu
from jax.sharding import PartitionSpec as P

HD = 128
BLOCK = 128
EXTRA = 16
norm_eps = 1e-06
SCALE = HD ** (-0.5)
NEG = -1e30
NT = (((1,), (1,)), ((), ()))
F32 = jnp.float32
BF16 = jnp.bfloat16
SMALL = pl.CostEstimate(flops=1, bytes_accessed=1, transcendentals=0)


def moved(array, axis, target):
    size = lax.axis_size(axis)
    pairs = [(i, target(i)) for i in range(size)]
    return lax.ppermute(array, axis, [(i, t) for i, t in pairs if t is not None and 0 <= t < size])


def vmem():
    return pl.BlockSpec(memory_space=pltpu.VMEM)


def hbm():
    return pl.BlockSpec(memory_space=pltpu.HBM)


def smem():
    return pl.BlockSpec(memory_space=pltpu.SMEM)


def params(mib):
    return pltpu.CompilerParams(vmem_limit_bytes=mib << 20)


def normed(raw, gain):
    mean_square = jnp.mean(raw * raw, axis=-1, keepdims=True)
    return raw * lax.rsqrt(mean_square + norm_eps) * gain


def message_kernel(
    kv_local, docs, table, key, value, key_gain, query_gain, bucket, out, facts
):
    core = lax.rem(lax.axis_index("ctx"), 2)
    for part in range(kv_local):
        head = part if kv_local == 1 else (core if part == 0 else 1 - core)
        lanes = pl.ds(pl.multiple_of(head * HD, HD), HD)
        rows = slice(part * BLOCK, (part + 1) * BLOCK)
        out[rows, :HD] = normed(key[:, lanes].astype(F32), key_gain[...]).astype(BF16)
        out[rows, HD:] = value[:, lanes]
    doc = jnp.full((EXTRA, 2 * HD), docs[0] + 1, jnp.int32).astype(F32)
    out[kv_local * BLOCK :, :] = doc.astype(BF16)
    facts[:8, :] = jnp.broadcast_to(query_gain[...], (8, HD))
    picks = bucket[...]
    found = jnp.zeros((1, HD), F32)
    for b in range(table.shape[0]):
        found = found + jnp.where(picks == b, table[b], 0.0)
    facts[8:, :] = jnp.broadcast_to(found, (8, HD))


def fetch(weight, held, sems, heads):
    n_head = lax.axis_size("head")
    width = weight.shape[0] // n_head
    core = lax.rem(lax.axis_index("ctx"), 2)
    features = pl.ds(pl.multiple_of(core * heads * HD, HD), heads * HD)
    pieces = sems.shape[0] // n_head
    part = width // pieces
    copies = []
    for i in range(sems.shape[0]):
        owner = lax.rem(lax.axis_index("head") + i // pieces, n_head)
        at = pl.multiple_of(owner * width + (i % pieces) * part, part)
        copies.append(
            pltpu.make_async_copy(
                weight.at[pl.ds(at, part), features],
                held.at[pl.ds(i * part, part), :],
                sems.at[i],
            )
        )
        copies[-1].start()
    return copies


def queries_kernel(
    heads,
    query,
    grad,
    facts,
    message,
    query_p,
    grad_p,
    facts_p,
    q_hat,
    rows,
    raw_t,
    both,
    kept,
):
    half = heads * HD
    core = lax.rem(lax.axis_index("ctx"), 2)
    own = pl.ds(pl.multiple_of(core * half, HD), half)
    gain = facts[0:1]
    for side in range(2):
        raw_all = query_p[:, own] if side else query[:, own]
        grad_all = grad_p[:, own] if side else grad[:, own]
        parity = 1 - core if side else core
        for head in range(heads):
            here = pl.ds(pl.multiple_of(parity * half + head * BLOCK, BLOCK), BLOCK)
            raw = raw_all[:, head * HD : (head + 1) * HD].astype(F32)
            q_hat[here, :] = normed(raw, gain).astype(BF16)
            rows[here, :] = grad_all[:, head * HD : (head + 1) * HD]
            raw_t[:, here] = raw.T.astype(BF16)
        source = facts_p if side else facts
        both[pl.ds(pl.multiple_of(8 + 8 * parity, 8), 8), :] = source[8:]
    both[:8, :] = facts[:8]
    kept[...] = message[...]


def place(kv_local, source, other, first, core, keys, values, keys_t, docs):
    after = (kv_local - 1) * BLOCK
    for block, skip, parity in ((source, 0, core), (other, after, 1 - core)):
        at = pl.ds(pl.multiple_of((first + parity) * BLOCK, BLOCK), BLOCK)
        key = block[skip : skip + BLOCK, :HD]
        keys[at, :] = key
        values[at, :] = block[skip : skip + BLOCK, HD:]
        keys_t[:, at] = key.astype(F32).T.astype(BF16)
        docs[first + parity] = block[kv_local * BLOCK :, :].astype(F32)[0:8]


def masks(own_doc, docs):
    return [jnp.where((doc == own_doc) & (doc > 0.0), 0.0, NEG) for doc in docs]


def exponents(scores, expo, dots, at, bias, triangle, total, weighted):
    value = jnp.exp2(scores * (SCALE * math.log2(math.e)) + bias)
    if triangle is not None:
        value = jnp.where(triangle, value, 0.0)
    expo[at] = value.astype(expo.dtype)
    wide = value.shape[1]
    total = total + jnp.sum(value.reshape(BLOCK // 8, 8, wide), axis=0)
    weighted = weighted + jnp.sum((value * dots[at]).reshape(BLOCK // 8, 8, wide), axis=0)
    return total, weighted


def near_kernel(kv_local, heads, n_near, *refs):
    mine, others = refs[:n_near], refs[n_near : 2 * n_near]
    q_hat, rows, weight = refs[2 * n_near : 2 * n_near + 3]
    held, keys_t, expo, dots, sums, keys, values, docs, raw, sems = refs[2 * n_near + 3 :]
    core = lax.rem(lax.axis_index("ctx"), 2)

    copies = fetch(weight, held, sems, heads)
    blocks = 2 * n_near
    for index in range(n_near):
        first = blocks - 2 - 2 * index
        place(kv_local, mine[index], others[index], first, core, keys, values, keys_t, docs)
    wide = 2 * BLOCK
    row = lax.broadcasted_iota(jnp.int32, (BLOCK, wide), 0)
    col = lax.rem(lax.broadcasted_iota(jnp.int32, (BLOCK, wide), 1), BLOCK)
    triangle = row <= col
    doc_rows = [docs[slot][0:1] for slot in range(blocks)]
    pairs = heads // 2
    for side in range(2):
        count = blocks - 1 + side
        reach = count * BLOCK
        bias = masks(doc_rows[blocks - 2 + side], doc_rows[:count])
        for pair in range(pairs):
            step = side * pairs + pair
            here = slice(step * wide, (step + 1) * wide)
            raw[step % 2, :reach, :] = lax.dot_general(
                keys[:reach, :], q_hat[here, :], NT, preferred_element_type=F32
            )
            dots[step, :reach, :] = lax.dot_general(
                values[:reach, :], rows[here, :], NT, preferred_element_type=F32
            )
            total = jnp.zeros((8, wide), F32)
            weighted = jnp.zeros((8, wide), F32)
            for block in range(count):
                r = slice(block * BLOCK, (block + 1) * BLOCK)
                total, weighted = exponents(
                    raw[step % 2, r, :],
                    expo,
                    dots,
                    (step, r, slice(None)),
                    bias[block],
                    triangle if block == count - 1 else None,
                    total,
                    weighted,
                )
            sums[step, :8, :] = total
            sums[step, 8:, :] = weighted
    for copy in copies:
        copy.wait()


def sum_products(step, side_rows, dk, dv, pw, ds, q_two, g_two):
    span = slice(0, side_rows)
    dv_part = jnp.dot(pw, g_two, preferred_element_type=F32)
    dk_part = jnp.dot(ds, q_two, preferred_element_type=F32)
    if step == 0:
        dv[span, :] = dv_part
        dk[span, :] = dk_part
        if side_rows < dk.shape[0]:
            dv[side_rows:, :] = jnp.zeros((dk.shape[0] - side_rows, HD), F32)
            dk[side_rows:, :] = jnp.zeros((dk.shape[0] - side_rows, HD), F32)
    else:
        dv[span, :] += dv_part
        dk[span, :] += dk_part


def hand_out(core, firsts, outs, dk, dv):
    for first, out in zip(firsts, outs):
        for block, parity in ((0, core), (1, 1 - core)):
            at = pl.ds(pl.multiple_of((first + parity) * BLOCK, BLOCK), BLOCK)
            r = slice(block * BLOCK, (block + 1) * BLOCK)
            out[r, :HD] = (dk[at, :] * SCALE).astype(out.dtype)
            out[r, HD:] = dv[at, :].astype(out.dtype)


def far_kernel(kv_local, heads, n_near, n_far, *refs):
    mine, others = refs[: 1 + n_far], refs[1 + n_far : 2 + 2 * n_far]
    q_hat, rows, facts, near_expo, near_dots, sums = refs[2 + 2 * n_far : 8 + 2 * n_far]
    keys_t, pw_near, ds, *parts = refs[8 + 2 * n_far : 13 + 2 * n_far]
    keys, values, docs, expo, dots, pw_far, dk, dv = refs[13 + 2 * n_far :]
    core = lax.rem(lax.axis_index("ctx"), 2)
    blocks = 2 * n_far
    for index in range(n_far):
        source, other = mine[1 + index], others[1 + index]
        place(kv_local, source, other, 2 * index, core, keys, values, keys_t, docs)
    for source, parity in ((mine[0], core), (others[0], 1 - core)):
        docs[blocks + parity] = source[kv_local * BLOCK :, :].astype(F32)[0:8]
    wide = 2 * BLOCK
    far_rows = blocks * BLOCK
    doc_rows = [docs[slot][0:1] for slot in range(blocks + 2)]
    pairs = heads // 2
    steps = 2 * pairs
    biases, weights = [], []
    for side in range(2):
        biases.append(masks(doc_rows[blocks + side], doc_rows[:blocks]))
        weights.append(jnp.concatenate([facts[8 * (side + 1) : 8 * (side + 1) + 1]] * 2, axis=1))

    def scores(step):
        here, buf = slice(step * wide, (step + 1) * wide), step % 2
        expo[buf] = lax.dot_general(keys[...], q_hat[here, :], NT, preferred_element_type=F32)
        dots[buf] = lax.dot_general(values[...], rows[here, :], NT, preferred_element_type=F32)

    def middle(step):
        side, buf = step // pairs, step % 2
        total, weighted = sums[step, :8, :], sums[step, 8:, :]
        for block in range(blocks):
            at = (buf, slice(block * BLOCK, (block + 1) * BLOCK), slice(None))
            total, weighted = exponents(
                expo[at], expo, dots, at, biases[side][block], None, total, weighted
            )
        inverse = 1.0 / jnp.sum(total, axis=0, keepdims=True)
        shift = jnp.sum(weighted, axis=0, keepdims=True) * inverse
        level = inverse * weights[side]
        for block in range(blocks):
            r = slice(block * BLOCK, (block + 1) * BLOCK)
            scaled = expo[buf, r, :] * level
            pw_far[buf, r, :] = scaled.astype(BF16)
            ds[step, r, :] = (scaled * (dots[buf, r, :] - shift)).astype(BF16)
        for block in range(2 * n_near - 1 + side):
            r = slice(block * BLOCK, (block + 1) * BLOCK)
            scaled = near_expo[step, r, :].astype(F32) * level
            pw_near[step, r, :] = scaled.astype(BF16)
            to = slice(far_rows + block * BLOCK, far_rows + (block + 1) * BLOCK)
            ds[step, to, :] = (scaled * (near_dots[step, r, :] - shift)).astype(BF16)

    scores(0)
    for step in range(steps):
        if step + 1 < steps:
            scores(step + 1)
        middle(step)
        here = slice(step * wide, (step + 1) * wide)
        sum_products(
            step,
            far_rows,
            dk,
            dv,
            pw_far[step % 2],
            ds[step, :far_rows, :],
            q_hat[here, :],
            rows[here, :],
        )
    part_a, part_ce = parts
    span = 2 * BLOCK
    outs = [part_a, part_ce.at[:span, :], part_ce.at[span:, :]]
    hand_out(core, [2 * index for index in range(n_far)], outs, dk, dv)


def last_kernel(heads, n_near, n_far, *refs):
    q_hat, rows, raw_t, facts, near_t, far_t, pw_near, ds = refs[:8]
    dq, *parts = refs[8 : 9 + n_near]
    dk, dv = refs[9 + n_near :]
    core = lax.rem(lax.axis_index("ctx"), 2)
    wide = 2 * BLOCK
    far_rows = 2 * n_far * BLOCK
    gain_t = jnp.broadcast_to(facts[0:1] * SCALE, (HD, HD)).T
    gain_t = jnp.concatenate([gain_t] * 2, axis=1)
    pairs = heads // 2
    for step in range(2 * pairs):
        side, here = step // pairs, slice(step * wide, (step + 1) * wide)
        reach = (2 * n_near - 1 + side) * BLOCK
        to = slice(far_rows, far_rows + reach)
        sum_products(
            step,
            reach,
            dk,
            dv,
            pw_near[step, :reach, :],
            ds[step, to, :],
            q_hat[here, :],
            rows[here, :],
        )
        dq_t = jnp.dot(far_t[...], ds[step, :far_rows, :], preferred_element_type=F32)
        dq_t = dq_t + jnp.dot(near_t[:, :reach], ds[step, to, :], preferred_element_type=F32)
        x = raw_t[:, here].astype(F32)
        inverse = lax.rsqrt(jnp.mean(x * x, axis=0, keepdims=True) + norm_eps)
        dy = dq_t * gain_t
        inner = jnp.mean(x * dy, axis=0, keepdims=True)
        dx = inverse * dy - x * (inverse * inverse * inverse * inner)
        for part in range(2):
            at = (step % pairs) * wide + part * HD
            dq[at : at + HD, side * BLOCK : (side + 1) * BLOCK] = dx[
                :, part * BLOCK : (part + 1) * BLOCK
            ].astype(BF16)
    firsts = [2 * n_near - 2 - 2 * index for index in range(n_near)]
    hand_out(core, firsts, parts, dk, dv)


def project_kernel(first, dq, weight, keep, *sends):
    core = lax.rem(lax.axis_index("ctx"), 2)
    width = keep.shape[1]
    piece = width // len(sends)
    rows = min(256, piece)
    for i in range(width // rows):
        lanes = slice(i * rows, (i + 1) * rows)
        at = slice(first + i * rows, first + (i + 1) * rows)
        term = jnp.dot(weight[at, :], dq[...], preferred_element_type=F32).T
        even, odd = term[:BLOCK], term[BLOCK:]
        keep[:, lanes] = jnp.where(core == 0, even, odd).astype(keep.dtype)
        send = sends[i * rows // piece]
        inside = slice(i * rows % piece, i * rows % piece + rows)
        send[:, inside] = jnp.where(core == 0, odd, even).astype(send.dtype)


def project(dq, weight, first, width, pieces):
    tokens = dq.shape[1] // 2
    keep = jax.ShapeDtypeStruct((tokens, width), BF16)
    send = jax.ShapeDtypeStruct((tokens, width // pieces), BF16)
    return pl.pallas_call(
        functools.partial(project_kernel, first),
        in_specs=[vmem()] * 2,
        out_specs=[vmem()] * (1 + pieces),
        out_shape=[keep] + [send] * pieces,
        compiler_params=params(16),
        cost_estimate=SMALL,
    )(dq, weight)


def add_kernel(*refs):
    *terms, out = refs
    result = terms[0][...].astype(F32)
    for term in terms[1:]:
        result = result + term[...].astype(F32)
    out[...] = result.astype(out.dtype)


def add_pieces_kernel(whole, *refs):
    *pieces, out = refs
    width = pieces[0].shape[1]
    for i, piece in enumerate(pieces):
        lanes = slice(i * width, (i + 1) * width)
        out[:, lanes] = (whole[:, lanes].astype(F32) + piece[...].astype(F32)).astype(out.dtype)


def add_pieces(whole, pieces):
    return pl.pallas_call(
        add_pieces_kernel,
        in_specs=[vmem()] * (1 + len(pieces)),
        out_specs=vmem(),
        out_shape=jax.ShapeDtypeStruct(whole.shape, whole.dtype),
        compiler_params=params(16),
        cost_estimate=SMALL,
    )(whole, *pieces)


def add(first, second, dtype, *more):
    return pl.pallas_call(
        add_kernel,
        in_specs=[vmem()] * (2 + len(more)),
        out_specs=vmem(),
        out_shape=jax.ShapeDtypeStruct(first.shape, dtype),
        compiler_params=params(16),
        cost_estimate=SMALL,
    )(first, second, *more)


def two_sums_kernel(b, d, turn, sum_b, sum_d):
    half = turn.shape[0] // 2
    sum_b[...] = (b[...].astype(F32) + turn[:half].astype(F32)).astype(sum_b.dtype)
    sum_d[...] = (d[...].astype(F32) + turn[half:].astype(F32)).astype(sum_d.dtype)


def collect_kernel(part_own, a, b, d, keep, send):
    result = part_own[...]
    for back in (a, b, d):
        result = result + back[...].astype(F32)
    keep[...] = result[:BLOCK]
    send[...] = result[BLOCK:].astype(BF16)


def finish_kernel(
    kv_local, keep, recv, key, gain, grad_key, grad_value, key_v, gain_v, sems
):
    copies = [
        pltpu.make_async_copy(key, key_v, sems.at[0]),
        pltpu.make_async_copy(gain, gain_v, sems.at[1]),
    ]
    for copy in copies:
        copy.start()
    for copy in copies:
        copy.wait()
    core = lax.rem(lax.axis_index("ctx"), 2)
    if kv_local > 1:
        parts = [(core, keep[...]), (1 - core, recv[...].astype(F32))]
    else:
        parts = [(0, keep[...] + recv[...].astype(F32))]
    for head, part in parts:
        lanes = pl.ds(pl.multiple_of(head * HD, HD), HD)
        raw = key_v[:, lanes].astype(F32)
        inverse = lax.rsqrt(jnp.mean(raw * raw, axis=-1, keepdims=True) + norm_eps)
        dy = part[:, :HD] * gain_v[...]
        inner = jnp.mean(raw * dy, axis=-1, keepdims=True)
        dx = inverse * dy - raw * (inverse * inverse * inverse * inner)
        grad_key[:, lanes] = dx.astype(BF16)
        grad_value[:, lanes] = part[:, HD:].astype(BF16)


def local(
    query_raw,
    key_raw,
    value_in,
    grad_out,
    query_gain,
    key_gain,
    loss_table,
    loss_bucket,
    block_docs,
    query_weight,
):
    tokens = query_raw.shape[0]
    kv_local = key_raw.shape[1] // HD
    half = query_raw.shape[1] // 2
    heads = half // HD
    key_row = key_gain.reshape(1, HD)
    query_row = query_gain.reshape(1, HD)
    shape = jax.ShapeDtypeStruct
    n_head = lax.axis_size("head")
    width = query_weight.shape[0] // n_head

    partner = lambda i: i ^ 1
    message, facts = pl.pallas_call(
        functools.partial(message_kernel, kv_local),
        in_specs=[smem(), smem()] + [vmem()] * 5,
        out_specs=[vmem()] * 2,
        out_shape=[
            shape((kv_local * BLOCK + EXTRA, 2 * HD), BF16),
            shape((16, HD), F32),
        ],
    )(
        block_docs,
        loss_table,
        key_raw,
        value_in,
        key_row,
        query_row,
        loss_bucket.reshape(1, tokens),
    )

    far_d = moved(message, "ctx", lambda i: i + 8)
    far_b = moved(message, "ctx", lambda i: i + 4)
    far_a = moved(message, "ctx", lambda i: i + 2 if (i // 2) % 2 == 0 else i + 10)
    query_in, grad_in, _ = lax.optimization_barrier((query_raw, grad_out, message))
    query_p = moved(query_in, "ctx", partner)
    grad_p = moved(grad_in, "ctx", partner)
    facts_p = moved(facts, "ctx", partner)
    total = 2 * heads * BLOCK
    queries = pl.pallas_call(
        functools.partial(queries_kernel, heads),
        in_specs=[vmem()] * 7,
        out_specs=[vmem()] * 5,
        out_shape=[
            shape((total, HD), BF16),
            shape((total, HD), BF16),
            shape((HD, total), BF16),
            shape((24, HD), F32),
            shape(message.shape, BF16),
        ],
        compiler_params=params(16),
    )(query_in, grad_in, facts, message, query_p, grad_p, facts_p)
    far_c = moved(far_b, "ctx", lambda i: i ^ 2 if i >= 4 else None)
    far_d, *queries = lax.optimization_barrier((far_d, *queries))
    far_e = moved(far_d, "ctx", lambda i: i ^ 2 if i >= 8 else None)
    *queries, kept = queries
    q_hat, rows, raw_t, both = queries
    near = (kept, far_b, far_d)
    near_shared = [moved(source, "ctx", partner) for source in (message, far_b, far_d)]
    n_near, n_far = 3, 3
    steps = heads
    span = 2 * BLOCK
    near_rows, far_rows = n_near * span, n_far * span
    weight, near_t, near_expo, near_dots, sums = pl.pallas_call(
        functools.partial(near_kernel, kv_local, heads, n_near),
        in_specs=[vmem()] * (2 * n_near + 2) + [hbm()],
        out_specs=[vmem()] * 5,
        out_shape=[
            shape((query_weight.shape[0], half), BF16),
            shape((HD, near_rows), BF16),
            shape((steps, near_rows, span), BF16),
            shape((steps, near_rows, span), F32),
            shape((steps, 16, span), F32),
        ],
        scratch_shapes=[
            pltpu.VMEM((near_rows, HD), BF16),
            pltpu.VMEM((near_rows, HD), BF16),
            pltpu.VMEM((2 * n_near, 8, 2 * HD), F32),
            pltpu.VMEM((2, near_rows, span), F32),
            pltpu.SemaphoreType.DMA((2 * n_head,)),
        ],
        compiler_params=params(20),
    )(*near, *near_shared, q_hat, rows, query_weight)

    far_e, sums = lax.optimization_barrier((far_e, sums))
    far = (far_a, far_c, far_e)
    far_shared = [moved(source, "ctx", partner) for source in far]
    part_shape = shape((span, 2 * HD), BF16)
    far_t, pw_near, ds, part_a, part_ce = pl.pallas_call(
        functools.partial(far_kernel, kv_local, heads, n_near, n_far),
        in_specs=[vmem()] * (2 * n_far + 8),
        out_specs=[vmem()] * 5,
        out_shape=[
            shape((HD, far_rows), BF16),
            shape((steps, near_rows, span), BF16),
            shape((steps, far_rows + near_rows, span), BF16),
            part_shape,
            shape((2 * span, 2 * HD), BF16),
        ],
        input_output_aliases={2 * n_far + 5: 1},
        scratch_shapes=[
            pltpu.VMEM((far_rows, HD), BF16),
            pltpu.VMEM((far_rows, HD), BF16),
            pltpu.VMEM((2 * n_far + 2, 8, 2 * HD), F32),
            pltpu.VMEM((2, far_rows, span), F32),
            pltpu.VMEM((2, far_rows, span), F32),
            pltpu.VMEM((2, far_rows, span), BF16),
            pltpu.VMEM((far_rows, HD), F32),
            pltpu.VMEM((far_rows, HD), F32),
        ],
        compiler_params=params(20),
        cost_estimate=SMALL,
    )(
        kept,
        *far,
        near_shared[0],
        *far_shared,
        q_hat,
        rows,
        both,
        near_expo,
        near_dots,
        sums,
    )

    back_a = moved(part_a, "ctx", lambda i: i - 2 if (i // 2) % 2 == 1 else i - 10)
    turn = moved(part_ce, "ctx", lambda i: i ^ 2 if i >= 4 else None)

    dq, part_own, part_b, part_d = pl.pallas_call(
        functools.partial(last_kernel, heads, n_near, n_far),
        in_specs=[vmem()] * 8,
        out_specs=[vmem()] * 4,
        out_shape=[shape((half, 2 * tokens), BF16), shape((span, 2 * HD), F32)] + [part_shape] * 2,
        scratch_shapes=[pltpu.VMEM((near_rows, HD), F32)] * 2,
        compiler_params=params(20),
        cost_estimate=SMALL,
    )(q_hat, rows, raw_t, both, near_t, far_t, pw_near, ds)

    arrived = []
    for shift in range(1, n_head):
        keep, *sends = project(dq, weight, shift * width, width, 4)
        term = add_pieces(keep, [moved(send, "ctx", partner) for send in sends])
        term, turn = lax.optimization_barrier((term, turn))
        arrived.append(moved(term, "head", lambda i, s=shift: (i + s) % n_head))
    sum_b, sum_d = pl.pallas_call(
        two_sums_kernel,
        in_specs=[vmem()] * 3,
        out_specs=[vmem()] * 2,
        out_shape=[part_shape] * 2,
        compiler_params=params(16),
        cost_estimate=SMALL,
    )(part_b, part_d, turn)
    back_d = moved(sum_d, "ctx", lambda i: i - 8)
    back_b = moved(sum_b, "ctx", lambda i: i - 4)
    mine, mine_send = project(dq, weight, 0, width, 1)
    mine_recv = moved(mine_send, "ctx", partner)

    grad_input = mine
    for index, piece in enumerate(arrived):
        last = index == len(arrived) - 1
        grad_input = add(grad_input, piece, BF16 if last else F32, *([mine_recv] if last else []))
    back_b, grad_input = lax.optimization_barrier((back_b, grad_input))
    sum_keep, sum_send = pl.pallas_call(
        collect_kernel,
        in_specs=[vmem()] * 4,
        out_specs=[vmem()] * 2,
        out_shape=[shape((BLOCK, 2 * HD), F32), shape((BLOCK, 2 * HD), BF16)],
        compiler_params=params(16),
    )(part_own, back_a, back_b, back_d)
    sum_recv = moved(sum_send, "ctx", partner)
    grad_key, grad_value = pl.pallas_call(
        functools.partial(finish_kernel, kv_local),
        in_specs=[vmem(), vmem(), hbm(), hbm()],
        out_specs=[vmem()] * 2,
        out_shape=[shape(key_raw.shape, BF16), shape(value_in.shape, BF16)],
        scratch_shapes=[
            pltpu.VMEM(key_raw.shape, BF16),
            pltpu.VMEM((1, HD), F32),
            pltpu.SemaphoreType.DMA((2,)),
        ],
        compiler_params=params(16),
    )(sum_keep, sum_recv, key_raw, key_row)

    return grad_input, grad_key, grad_value


def solution(mesh):
    placed = (
        P("ctx", "head"),
        P("ctx", "head"),
        P("ctx", "head"),
        P("ctx", "head"),
        P(),
        P(),
        P(),
        P("ctx"),
        P("ctx"),
        P(None, "head"),
    )
    return jax.shard_map(
        local,
        mesh=mesh,
        in_specs=placed,
        out_specs=(P("ctx", "head"), P("ctx", "head"), P("ctx", "head")),
        check_vma=False,
    )
```

time: 73.3 us -> 68.2 us (0.930)
  waiting for transfers between devices: 22.6 us -> 18 us
    ppermute x23 -> x25, waiting for transfers between devices: 22.6 us -> 18 us  [moved(): lax.ppermute(array, axis, [(i, t) for i, t in pairs if t is not None and...]
    ppermute x23 -> x25, starting transfers between devices: 25.1 us -> 24.4 us  [moved(): lax.ppermute(array, axis, [(i, t) for i, t in pairs if t is not None and...]
    pallas_call x6 -> x9, Pallas kernels: 16.4 us -> 16.8 us  [the longest x1 5.12 us: local(): pl.pallas_call(functools.partial(far_kernel, kv_local, heads, n_near, n_f...]
  transfers between devices with their start and end apart: 23 -> 25, of which waited for: 10 -> 4; matrix products, arithmetic and copies ran while one was open for 0% -> 0% of each run, Pallas kernels for 2% -> 18%
where the time goes in v4:
time: 68.2 us; the launch traced here: 67.7 us
  starting transfers between devices  24.4 us (36%)
  Pallas kernels  19.9 us (29%)
  waiting for transfers between devices  18 us (26%)
  local copies, waits for them, and re-layouts  3.69 us (5%)
  between operations  1.69 us (2%)
    ppermute x25, starting transfers between devices, moved(): lax.ppermute(array, axis, [(i, t) for i, t in pairs if t is not None and...  24.4 us
    ppermute x25, waiting for transfers between devices, moved(): lax.ppermute(array, axis, [(i, t) for i, t in pairs if t is not None and...  18 us
    pallas_call x1, Pallas kernels, local(): pl.pallas_call(functools.partial(far_kernel, kv_local, heads, n_near, n_f...  5.12 us
    pallas_call x1, Pallas kernels, local(): pl.pallas_call(functools.partial(near_kernel, kv_local, heads, n_near), i...  4.93 us
    unnamed x12, local copies, waits for them, and re-layouts  3.69 us
    pallas_call x1, Pallas kernels, local(): pl.pallas_call(functools.partial(last_kernel, heads, n_near, n_far), in_s...  2.76 us
    pallas_call x2, Pallas kernels, project(): pl.pallas_call(functools.partial(project_kernel, first), in_specs=[vmem()...  2.72 us
    pallas_call x1, Pallas kernels, local(): pl.pallas_call(functools.partial(message_kernel, kv_local), in_specs=[sme...  1.7 us
  transfers between devices with their start and end apart: 25, of which 4 were waited for; matrix products, arithmetic and copies ran while one was open for 0% of the time, Pallas kernels for 18%

profile of v4, /device:TPU:0, one launch (start us, length us, event | category | flops | bytes accessed | tf_op | source)
XLA Modules:
  0.0 67.7 jit_solution(5211614197856308441)
XLA Ops:
  1.3 1.7 %shard_map.121 = (bf16[272,256]{1,0:T(8,128)(2,1)}, f32[16,128]{1,0:T(8,128)}) custom-call(s32[1]{0:T(128)S(6)} %copy.15.docs, f32[16]{0:T(128)} %table.1, bf16[128,256]{1,0:T(8,128)(2,1)} %key.3, bf16[128,256]{1,0:T(8,128)(2,1)} %value.1, f32[1,128]{1,0:T(1,128)} %bitcast.3, f32[1,128]{1,0:T(1,128)} %bitcast.5, s32[1,128]{1,0:T(1,128)} %bitcast.6), custom_call_target="tpu_custom_call" | custom-call | tf_op jit(solution)/shard_map/pallas_call | solution.py:471
  3.0 0.5 collective-permute-start.1
  3.4 0.1 collective-permute-start.2
  3.5 0.5 collective-permute-start.3
  3.9 4.5 %collective-permute-start.4 = (bf16[272,256]{1,0:T(8,128)(2,1)}, bf16[272,256]{1,0:T(8,128)(2,1)S(1)}, u32[]{:S(2)}, u32[]{:S(2)}) collective-permute-start(bf16[272,256]{1,0:T(8,128)(2,1)} %get-tuple-element.51.message), channel_id=1, source_target_pairs={{0,8},{2,10},{4,12},{6,14},{8,16},{10,18},{12,20},{14,22},{16,24},... | collective-permute-start | bytes 417800 | tf_op jit(solution)/shard_map/ppermute | solution.py:26
  8.4 4.5 %collective-permute-start = (bf16[272,256]{1,0:T(8,128)(2,1)}, bf16[272,256]{1,0:T(8,128)(2,1)S(1)}, u32[]{:S(2)}, u32[]{:S(2)}) collective-permute-start(bf16[272,256]{1,0:T(8,128)(2,1)} %get-tuple-element.51.message), channel_id=1, source_target_pairs={{0,16},{2,18},{4,20},{6,22},{8,24},{10,26},{12,28},{14,30},{1,17},... | collective-permute-start | bytes 417800 | tf_op jit(solution)/shard_map/ppermute | solution.py:26
  12.9 3.4 %collective-permute-start.8 = (bf16[272,256]{1,0:T(8,128)(2,1)}, bf16[272,256]{1,0:T(8,128)(2,1)S(1)}, u32[]{:S(2)}, u32[]{:S(2)}) collective-permute-start(bf16[272,256]{1,0:T(8,128)(2,1)} %get-tuple-element.51.message), channel_id=1, source_target_pairs={{0,4},{2,6},{4,24},{6,26},{8,12},{10,14},{16,20},{18,22},{24,28},{... | collective-permute-start | bytes 417800 | tf_op jit(solution)/shard_map/ppermute | solution.py:26
  16.4 0.0 collective-permute-done.4.refs_1_
  16.4 0.1 collective-permute-start.5
  16.5 0.7 collective-permute-start.9
  17.2 0.5 collective-permute-start.6
  17.7 1.0 %copy-done = bf16[128,2048]{1,0:T(8,128)(2,1)S(1)} copy-done((bf16[128,2048]{1,0:T(8,128)(2,1)S(1)}, bf16[128,2048]{1,0:T(8,128)(2,1)}, u32[]{:S(2)}) %copy-start) | copy-done | bytes 524312
  18.8 1.0 %copy-done.1 = bf16[128,2048]{1,0:T(8,128)(2,1)S(1)} copy-done((bf16[128,2048]{1,0:T(8,128)(2,1)S(1)}, bf16[128,2048]{1,0:T(8,128)(2,1)}, u32[]{:S(2)}) %copy-start.1) | copy-done | bytes 524312
  19.8 0.9 %copy-done.3 = bf16[272,256]{1,0:T(8,128)(2,1)S(1)} copy-done((bf16[272,256]{1,0:T(8,128)(2,1)S(1)}, bf16[272,256]{1,0:T(8,128)(2,1)}, u32[]{:S(2)}) %copy-start.3) | copy-done | bytes 139288
  20.7 0.7 %copy-done.4 = f32[16,128]{1,0:T(8,128)S(1)} copy-done((f32[16,128]{1,0:T(8,128)S(1)}, f32[16,128]{1,0:T(8,128)}, u32[]{:S(2)}) %copy-start.4) | copy-done | bytes 8216
  21.4 0.5 shard_map.122
  21.9 0.0 collective-permute-done.refs_2_
  21.9 0.1 collective-permute-start.7
  22.0 0.7 collective-permute-start.10
  22.7 0.5 collective-permute-start.11
  23.3 0.1 collective-permute-start.12
  23.4 0.0 collective-permute-done.7.refs_5_
  23.4 4.9 %shard_map.123 = (bf16[4096,1024]{1,0:T(8,128)(2,1)S(1)}, bf16[128,768]{1,0:T(8,128)(2,1)S(1)}, bf16[8,768,256]{2,1,0:T(8,128)(2,1)S(1)}, f32[8,768,256]{2,1,0:T(8,128)S(1)}, f32[8,16,256]{2,1,0:T(8,128)S(1)}) custom-call(bf16[272,256]{1,0:T(8,128)(2,1)S(1)} %get-tuple-element.64.refs_0_, bf16[272,256]{1,0:T(8,128)(2,1)S(1)} %collective-permute-done.4.refs_1_, ...), custom_call_target="tpu_custom_call" | custom-call | tf_op jit(solution)/shard_map/pallas_call | solution.py:521
  28.3 0.5 collective-permute-start.13
  28.8 1.0 %collective-permute-done.13.refs_7_ = bf16[272,256]{1,0:T(8,128)(2,1)S(1)} collective-permute-done((bf16[272,256]{1,0:T(8,128)(2,1)S(1)}, bf16[272,256]{1,0:T(8,128)(2,1)S(1)}, u32[]{:S(2)}, u32[]{:S(2)}) %collective-permute-start.13) | collective-permute-done | bytes 139296 | tf_op jit(solution)/shard_map/ppermute | solution.py:26
  29.8 5.1 %shard_map.124 = (bf16[128,768]{1,0:T(8,128)(2,1)S(1)}, bf16[8,768,256]{2,1,0:T(8,128)(2,1)S(1)}, bf16[8,1536,256]{2,1,0:T(8,128)(2,1)S(1)}, bf16[256,256]{1,0:T(8,128)(2,1)S(1)}, bf16[512,256]{1,0:T(8,128)(2,1)S(1)}) custom-call(bf16[272,256]{1,0:T(8,128)(2,1)S(1)} %get-tuple-element.64.refs_0_, ...), custom_call_target="tpu_custom_call", output_to_operand_aliasing={{1}: (11, {})} | custom-call | flops 1 | bytes 1 | tf_op jit(solution)/shard_map/pallas_call | solution.py:546
  34.9 0.9 %collective-permute-start.18 = (bf16[512,256]{1,0:T(8,128)(2,1)S(1)}, bf16[512,256]{1,0:T(8,128)(2,1)S(1)}, u32[]{:S(2)}, u32[]{:S(2)}) collective-permute-start(bf16[512,256]{1,0:T(8,128)(2,1)S(1)} %get-tuple-element.84), channel_id=1, source_target_pairs={{8,12},{10,14},{12,8},{14,10},{16,20},{18,22},{20,16},{22,18},{24,... | collective-permute-start | bytes 786440 | tf_op jit(solution)/shard_map/ppermute | solution.py:26
  35.8 2.8 %shard_map.125 = (bf16[1024,256]{1,0:T(8,128)(2,1)S(1)}, f32[256,256]{1,0:T(8,128)S(1)}, bf16[256,256]{1,0:T(8,128)(2,1)S(1)}, bf16[256,256]{1,0:T(8,128)(2,1)S(1)}) custom-call(bf16[2048,128]{1,0:T(8,128)(2,1)S(1)} %get-tuple-element.60.refs_6_.refs_8_.refs_0_, bf16[2048,128]{1,0:T(8,128)(2,1)S(1)} %get-tuple-element.61.refs_7_.refs_9_.refs_1_, ...), custom_call_target="tpu_custom_call" | custom-call | flops 1 | bytes 1 | tf_op jit(solution)/shard_map/pallas_call | solution.py:586
  38.6 1.4 %shard_map.126 = (bf16[128,2048]{1,0:T(8,128)(2,1)S(1)}, bf16[128,512]{1,0:T(8,128)(2,1)S(1)}, bf16[128,512]{1,0:T(8,128)(2,1)S(1)}, bf16[128,512]{1,0:T(8,128)(2,1)S(1)}, bf16[128,512]{1,0:T(8,128)(2,1)S(1)}) custom-call(bf16[1024,256]{1,0:T(8,128)(2,1)S(1)} %get-tuple-element.77.dq, bf16[4096,1024]{1,0:T(8,128)(2,1)S(1)} %get-tuple-element.78.weight), custom_call_target="tpu_custom_call" | custom-call | flops 1 | bytes 1 | tf_op jit(solution)/shard_map/pallas_call | solution.py:359
  39.9 0.4 collective-permute-start.14
  40.4 0.1 collective-permute-start.15
  40.5 0.4 collective-permute-start.16
  40.9 0.1 collective-permute-start.17
  41.0 1.4 %shard_map.129 = (bf16[128,2048]{1,0:T(8,128)(2,1)S(1)}, bf16[128,2048]{1,0:T(8,128)(2,1)S(1)}) custom-call(bf16[1024,256]{1,0:T(8,128)(2,1)S(1)} %get-tuple-element.77.dq, bf16[4096,1024]{1,0:T(8,128)(2,1)S(1)} %get-tuple-element.78.weight), custom_call_target="tpu_custom_call" | custom-call | flops 1 | bytes 1 | tf_op jit(solution)/shard_map/pallas_call | solution.py:359
  42.4 0.4 collective-permute-start.21
  42.9 0.1 shard_map.127
  43.0 1.6 %collective-permute-start.20 = (bf16[128,2048]{1,0:T(8,128)(2,1)S(1)}, bf16[128,2048]{1,0:T(8,128)(2,1)S(1)}, u32[]{:S(2)}, u32[]{:S(2)}) collective-permute-start(bf16[128,2048]{1,0:T(8,128)(2,1)S(1)} %shard_map.127), channel_id=1, source_target_pairs={{0,1},{1,0},{2,3},{3,2},{4,5},{5,4},{6,7},{7,6},{8,9},{9,8},{10,11... | collective-permute-start | bytes 1572872 | tf_op jit(solution)/shard_map/ppermute | solution.py:26
  44.5 0.1 shard_map.128
  44.6 1.3 %collective-permute-start.19 = (bf16[256,256]{1,0:T(8,128)(2,1)S(1)}, bf16[256,256]{1,0:T(8,128)(2,1)S(1)}, u32[]{:S(2)}, u32[]{:S(2)}) collective-permute-start(bf16[256,256]{1,0:T(8,128)(2,1)S(1)} %get-tuple-element.86), channel_id=1, source_target_pairs={{8,0},{10,2},{12,4},{14,6},{16,8},{18,10},{20,12},{22,14},{24,16},... | collective-permute-start | bytes 393224 | tf_op jit(solution)/shard_map/ppermute | solution.py:26
  45.9 1.3 %collective-permute-start.22 = (bf16[256,256]{1,0:T(8,128)(2,1)S(1)}, bf16[256,256]{1,0:T(8,128)(2,1)S(1)}, u32[]{:S(2)}, u32[]{:S(2)}) collective-permute-start(bf16[256,256]{1,0:T(8,128)(2,1)S(1)} %get-tuple-element.92), channel_id=1, source_target_pairs={{4,0},{6,2},{12,8},{14,10},{20,16},{22,18},{24,4},{26,6},{28,24},{... | collective-permute-start | bytes 393224 | tf_op jit(solution)/shard_map/ppermute | solution.py:26
  47.2 1.3 %collective-permute-start.23 = (bf16[256,256]{1,0:T(8,128)(2,1)S(1)}, bf16[256,256]{1,0:T(8,128)(2,1)S(1)}, u32[]{:S(2)}, u32[]{:S(2)}) collective-permute-start(bf16[256,256]{1,0:T(8,128)(2,1)S(1)} %get-tuple-element.94), channel_id=1, source_target_pairs={{16,0},{18,2},{20,4},{22,6},{24,8},{26,10},{28,12},{30,14},{17,1},... | collective-permute-start | bytes 393224 | tf_op jit(solution)/shard_map/ppermute | solution.py:26
  48.5 8.5 %collective-permute-done.20.refs_1_ = bf16[128,2048]{1,0:T(8,128)(2,1)S(1)} collective-permute-done((bf16[128,2048]{1,0:T(8,128)(2,1)S(1)}, bf16[128,2048]{1,0:T(8,128)(2,1)S(1)}, u32[]{:S(2)}, u32[]{:S(2)}) %collective-permute-start.20) | collective-permute-done | bytes 524320 | tf_op jit(solution)/shard_map/ppermute | solution.py:26
  57.0 1.0 %shard_map.130 = bf16[128,2048]{1,0:T(8,128)(2,1)} custom-call(bf16[128,2048]{1,0:T(8,128)(2,1)S(1)} %get-tuple-element.87.refs_0_, bf16[128,2048]{1,0:T(8,128)(2,1)S(1)} %collective-permute-done.20.refs_1_, bf16[128,2048]{1,0:T(8,128)(2,1)S(1)} %collective-permute-done.21.refs_2_), custom_call_target="tpu_custom_call" | custom-call | flops 1 | bytes 1 | tf_op jit(solution)/shard_map/pallas_call | solution.py:397
  58.0 7.2 %collective-permute-done.23.d = bf16[256,256]{1,0:T(8,128)(2,1)S(1)} collective-permute-done((bf16[256,256]{1,0:T(8,128)(2,1)S(1)}, bf16[256,256]{1,0:T(8,128)(2,1)S(1)}, u32[]{:S(2)}, u32[]{:S(2)}) %collective-permute-start.23) | collective-permute-done | bytes 131104 | tf_op jit(solution)/shard_map/ppermute | solution.py:26
  65.2 0.1 shard_map.131
  65.3 0.1 collective-permute-start.24
  65.4 1.2 %collective-permute-done.24.recv = bf16[128,256]{1,0:T(8,128)(2,1)S(1)} collective-permute-done((bf16[128,256]{1,0:T(8,128)(2,1)S(1)}, bf16[128,256]{1,0:T(8,128)(2,1)S(1)}, u32[]{:S(2)}, u32[]{:S(2)}) %collective-permute-start.24) | collective-permute-done | bytes 65568 | tf_op jit(solution)/shard_map/ppermute | solution.py:26
  66.6 0.9 %shard_map.132 = (bf16[128,256]{1,0:T(8,128)(2,1)}, bf16[128,256]{1,0:T(8,128)(2,1)}) custom-call(f32[128,256]{1,0:T(8,128)S(1)} %get-tuple-element.95.keep, bf16[128,256]{1,0:T(8,128)(2,1)S(1)} %collective-permute-done.24.recv, bf16[128,256]{1,0:T(8,128)(2,1)S(1)} %copy-done.2, f32[1,128]{1,0:T(1,128)S(1)} %bitcast.4), custom_call_target="tpu_custom_call" | custom-call | tf_op jit(solution)/shard_map/pallas_call | solution.py:628
  (26 shorter events, 0.1 us)
Async XLA Ops:
  3.0 13.5 %collective-permute-start.1 = (bf16[128,2048]{1,0:T(8,128)(2,1)}, bf16[128,2048]{1,0:T(8,128)(2,1)S(1)}, u32[]{:S(2)}, u32[]{:S(2)}) collective-permute-start(bf16[128,2048]{1,0:T(8,128)(2,1)} %query), channel_id=1, source_target_pairs={{0,2},{2,0},{4,6},{6,4},{8,10},{10,8},{12,14},{14,12},{16,18},{18,... | collective-permute-start | bytes 1572872 | tf_op jit(solution)/shard_map/ppermute | solution.py:26
  3.4 13.7 %collective-permute-start.2 = (bf16[128,2048]{1,0:T(8,128)(2,1)}, bf16[128,2048]{1,0:T(8,128)(2,1)S(1)}, u32[]{:S(2)}, u32[]{:S(2)}) collective-permute-start(bf16[128,2048]{1,0:T(8,128)(2,1)} %grad), channel_id=1, source_target_pairs={{0,2},{2,0},{4,6},{6,4},{8,10},{10,8},{12,14},{14,12},{16,18},{18,... | collective-permute-start | bytes 1572872 | tf_op jit(solution)/shard_map/ppermute | solution.py:26
  3.5 9.4 %collective-permute-start.3 = (f32[16,128]{1,0:T(8,128)}, f32[16,128]{1,0:T(8,128)S(1)}, u32[]{:S(2)}, u32[]{:S(2)}) collective-permute-start(f32[16,128]{1,0:T(8,128)} %get-tuple-element.54.facts), channel_id=1, source_target_pairs={{0,2},{2,0},{4,6},{6,4},{8,10},{10,8},{12,14},{14,12},{16,18},{18,... | collective-permute-start | bytes 24584 | tf_op jit(solution)/shard_map/ppermute | solution.py:26
  3.9 12.4 %collective-permute-start.4 = (bf16[272,256]{1,0:T(8,128)(2,1)}, bf16[272,256]{1,0:T(8,128)(2,1)S(1)}, u32[]{:S(2)}, u32[]{:S(2)}) collective-permute-start(bf16[272,256]{1,0:T(8,128)(2,1)} %get-tuple-element.51.message), channel_id=1, source_target_pairs={{0,8},{2,10},{4,12},{6,14},{8,16},{10,18},{12,20},{14,22},{16,24},... | collective-permute-start | bytes 417800 | tf_op jit(solution)/shard_map/ppermute | solution.py:26
  8.4 13.5 %collective-permute-start = (bf16[272,256]{1,0:T(8,128)(2,1)}, bf16[272,256]{1,0:T(8,128)(2,1)S(1)}, u32[]{:S(2)}, u32[]{:S(2)}) collective-permute-start(bf16[272,256]{1,0:T(8,128)(2,1)} %get-tuple-element.51.message), channel_id=1, source_target_pairs={{0,16},{2,18},{4,20},{6,22},{8,24},{10,26},{12,28},{14,30},{1,17},... | collective-permute-start | bytes 417800 | tf_op jit(solution)/shard_map/ppermute | solution.py:26
  12.9 9.1 %collective-permute-start.8 = (bf16[272,256]{1,0:T(8,128)(2,1)}, bf16[272,256]{1,0:T(8,128)(2,1)S(1)}, u32[]{:S(2)}, u32[]{:S(2)}) collective-permute-start(bf16[272,256]{1,0:T(8,128)(2,1)} %get-tuple-element.51.message), channel_id=1, source_target_pairs={{0,4},{2,6},{4,24},{6,26},{8,12},{10,14},{16,20},{18,22},{24,28},{... | collective-permute-start | bytes 417800 | tf_op jit(solution)/shard_map/ppermute | solution.py:26
  16.4 6.3 %collective-permute-start.5 = (bf16[272,256]{1,0:T(8,128)(2,1)}, bf16[272,256]{1,0:T(8,128)(2,1)S(1)}, u32[]{:S(2)}, u32[]{:S(2)}) collective-permute-start(bf16[272,256]{1,0:T(8,128)(2,1)} %get-tuple-element.51.message), channel_id=1, source_target_pairs={{0,2},{2,0},{4,6},{6,4},{8,10},{10,8},{12,14},{14,12},{16,18},{18,... | collective-permute-start | bytes 417800 | tf_op jit(solution)/shard_map/ppermute | solution.py:26
  16.5 6.8 %collective-permute-start.9 = (bf16[272,256]{1,0:T(8,128)(2,1)S(1)}, bf16[272,256]{1,0:T(8,128)(2,1)S(1)}, u32[]{:S(2)}, u32[]{:S(2)}) collective-permute-start(bf16[272,256]{1,0:T(8,128)(2,1)S(1)} %collective-permute-done.4.refs_1_), channel_id=1, source_target_pairs={{8,12},{10,14},{12,8},{14,10},{16,20},{18,22},{20,16},{22,18},{24,... | collective-permute-start | bytes 417800 | tf_op jit(solution)/shard_map/ppermute | solution.py:26
  17.2 6.2 %collective-permute-start.6 = (bf16[272,256]{1,0:T(8,128)(2,1)S(1)}, bf16[272,256]{1,0:T(8,128)(2,1)S(1)}, u32[]{:S(2)}, u32[]{:S(2)}) collective-permute-start(bf16[272,256]{1,0:T(8,128)(2,1)S(1)} %collective-permute-done.4.refs_1_), channel_id=1, source_target_pairs={{0,2},{2,0},{4,6},{6,4},{8,10},{10,8},{12,14},{14,12},{16,18},{18,... | collective-permute-start | bytes 417800 | tf_op jit(solution)/shard_map/ppermute | solution.py:26
  17.7 1.0 %copy-start = (bf16[128,2048]{1,0:T(8,128)(2,1)S(1)}, bf16[128,2048]{1,0:T(8,128)(2,1)}, u32[]{:S(2)}) copy-start(bf16[128,2048]{1,0:T(8,128)(2,1)} %query) | copy-start | bytes 1572868
  18.8 1.0 %copy-start.1 = (bf16[128,2048]{1,0:T(8,128)(2,1)S(1)}, bf16[128,2048]{1,0:T(8,128)(2,1)}, u32[]{:S(2)}) copy-start(bf16[128,2048]{1,0:T(8,128)(2,1)} %grad) | copy-start | bytes 1572868
  19.8 0.9 %copy-start.3 = (bf16[272,256]{1,0:T(8,128)(2,1)S(1)}, bf16[272,256]{1,0:T(8,128)(2,1)}, u32[]{:S(2)}) copy-start(bf16[272,256]{1,0:T(8,128)(2,1)} %get-tuple-element.51.message) | copy-start | bytes 417796
  20.7 0.7 %copy-start.4 = (f32[16,128]{1,0:T(8,128)S(1)}, f32[16,128]{1,0:T(8,128)}, u32[]{:S(2)}) copy-start(f32[16,128]{1,0:T(8,128)} %get-tuple-element.54.facts) | copy-start | bytes 24580
  21.9 1.4 %collective-permute-start.7 = (bf16[272,256]{1,0:T(8,128)(2,1)S(1)}, bf16[272,256]{1,0:T(8,128)(2,1)S(1)}, u32[]{:S(2)}, u32[]{:S(2)}) collective-permute-start(bf16[272,256]{1,0:T(8,128)(2,1)S(1)} %collective-permute-done.refs_2_), channel_id=1, source_target_pairs={{0,2},{2,0},{4,6},{6,4},{8,10},{10,8},{12,14},{14,12},{16,18},{18,... | collective-permute-start | bytes 417800 | tf_op jit(solution)/shard_map/ppermute | solution.py:26
  22.0 6.3 %collective-permute-start.10 = (bf16[272,256]{1,0:T(8,128)(2,1)S(1)}, bf16[272,256]{1,0:T(8,128)(2,1)S(1)}, u32[]{:S(2)}, u32[]{:S(2)}) collective-permute-start(bf16[272,256]{1,0:T(8,128)(2,1)S(1)} %collective-permute-done.refs_2_), channel_id=1, source_target_pairs={{16,20},{18,22},{20,16},{22,18},{24,28},{26,30},{28,24},{30,26},{1... | collective-permute-start | bytes 417800 | tf_op jit(solution)/shard_map/ppermute | solution.py:26
  22.7 6.1 %collective-permute-start.11 = (bf16[272,256]{1,0:T(8,128)(2,1)S(1)}, bf16[272,256]{1,0:T(8,128)(2,1)S(1)}, u32[]{:S(2)}, u32[]{:S(2)}) collective-permute-start(bf16[272,256]{1,0:T(8,128)(2,1)S(1)} %collective-permute-done.8.refs_1_), channel_id=1, source_target_pairs={{0,2},{2,0},{4,6},{6,4},{8,10},{10,8},{12,14},{14,12},{16,18},{18,... | collective-permute-start | bytes 417800 | tf_op jit(solution)/shard_map/ppermute | solution.py:26
  23.3 5.5 %collective-permute-start.12 = (bf16[272,256]{1,0:T(8,128)(2,1)S(1)}, bf16[272,256]{1,0:T(8,128)(2,1)S(1)}, u32[]{:S(2)}, u32[]{:S(2)}) collective-permute-start(bf16[272,256]{1,0:T(8,128)(2,1)S(1)} %collective-permute-done.9.refs_2_), channel_id=1, source_target_pairs={{0,2},{2,0},{4,6},{6,4},{8,10},{10,8},{12,14},{14,12},{16,18},{18,... | collective-permute-start | bytes 417800 | tf_op jit(solution)/shard_map/ppermute | solution.py:26
  28.3 1.5 %collective-permute-start.13 = (bf16[272,256]{1,0:T(8,128)(2,1)S(1)}, bf16[272,256]{1,0:T(8,128)(2,1)S(1)}, u32[]{:S(2)}, u32[]{:S(2)}) collective-permute-start(bf16[272,256]{1,0:T(8,128)(2,1)S(1)} %collective-permute-done.10.refs_3_), channel_id=1, source_target_pairs={{0,2},{2,0},{4,6},{6,4},{8,10},{10,8},{12,14},{14,12},{16,18},{18,... | collective-permute-start | bytes 417800 | tf_op jit(solution)/shard_map/ppermute | solution.py:26
  34.9 8.1 %collective-permute-start.18 = (bf16[512,256]{1,0:T(8,128)(2,1)S(1)}, bf16[512,256]{1,0:T(8,128)(2,1)S(1)}, u32[]{:S(2)}, u32[]{:S(2)}) collective-permute-start(bf16[512,256]{1,0:T(8,128)(2,1)S(1)} %get-tuple-element.84), channel_id=1, source_target_pairs={{8,12},{10,14},{12,8},{14,10},{16,20},{18,22},{20,16},{22,18},{24,... | collective-permute-start | bytes 786440 | tf_op jit(solution)/shard_map/ppermute | solution.py:26
  39.9 2.5 %collective-permute-start.14 = (bf16[128,512]{1,0:T(8,128)(2,1)S(1)}, bf16[128,512]{1,0:T(8,128)(2,1)S(1)}, u32[]{:S(2)}, u32[]{:S(2)}) collective-permute-start(bf16[128,512]{1,0:T(8,128)(2,1)S(1)} %get-tuple-element.80), channel_id=1, source_target_pairs={{0,2},{2,0},{4,6},{6,4},{8,10},{10,8},{12,14},{14,12},{16,18},{18,... | collective-permute-start | bytes 393224 | tf_op jit(solution)/shard_map/ppermute | solution.py:26
  40.4 2.5 %collective-permute-start.15 = (bf16[128,512]{1,0:T(8,128)(2,1)S(1)}, bf16[128,512]{1,0:T(8,128)(2,1)S(1)}, u32[]{:S(2)}, u32[]{:S(2)}) collective-permute-start(bf16[128,512]{1,0:T(8,128)(2,1)S(1)} %get-tuple-element.81), channel_id=1, source_target_pairs={{0,2},{2,0},{4,6},{6,4},{8,10},{10,8},{12,14},{14,12},{16,18},{18,... | collective-permute-start | bytes 393224 | tf_op jit(solution)/shard_map/ppermute | solution.py:26
  40.5 2.4 %collective-permute-start.16 = (bf16[128,512]{1,0:T(8,128)(2,1)S(1)}, bf16[128,512]{1,0:T(8,128)(2,1)S(1)}, u32[]{:S(2)}, u32[]{:S(2)}) collective-permute-start(bf16[128,512]{1,0:T(8,128)(2,1)S(1)} %get-tuple-element.82), channel_id=1, source_target_pairs={{0,2},{2,0},{4,6},{6,4},{8,10},{10,8},{12,14},{14,12},{16,18},{18,... | collective-permute-start | bytes 393224 | tf_op jit(solution)/shard_map/ppermute | solution.py:26
  40.9 25.7 %copy-start.2 = (bf16[128,256]{1,0:T(8,128)(2,1)S(1)}, bf16[128,256]{1,0:T(8,128)(2,1)}, u32[]{:S(2)}) copy-start(bf16[128,256]{1,0:T(8,128)(2,1)} %key.3) | copy-start | bytes 196612
  40.9 25.7 %copy-start.5 = (f32[128]{0:T(128)S(1)}, f32[128]{0:T(128)}, u32[]{:S(2)}) copy-start(f32[128]{0:T(128)} %param.15) | copy-start | bytes 1540
  40.9 2.0 %collective-permute-start.17 = (bf16[128,512]{1,0:T(8,128)(2,1)S(1)}, bf16[128,512]{1,0:T(8,128)(2,1)S(1)}, u32[]{:S(2)}, u32[]{:S(2)}) collective-permute-start(bf16[128,512]{1,0:T(8,128)(2,1)S(1)} %get-tuple-element.83), channel_id=1, source_target_pairs={{0,2},{2,0},{4,6},{6,4},{8,10},{10,8},{12,14},{14,12},{16,18},{18,... | collective-permute-start | bytes 393224 | tf_op jit(solution)/shard_map/ppermute | solution.py:26
  42.4 6.1 %collective-permute-start.21 = (bf16[128,2048]{1,0:T(8,128)(2,1)S(1)}, bf16[128,2048]{1,0:T(8,128)(2,1)S(1)}, u32[]{:S(2)}, u32[]{:S(2)}) collective-permute-start(bf16[128,2048]{1,0:T(8,128)(2,1)S(1)} %get-tuple-element.89), channel_id=1, source_target_pairs={{0,2},{2,0},{4,6},{6,4},{8,10},{10,8},{12,14},{14,12},{16,18},{18,... | collective-permute-start | bytes 1572872 | tf_op jit(solution)/shard_map/ppermute | solution.py:26
  43.0 14.0 %collective-permute-start.20 = (bf16[128,2048]{1,0:T(8,128)(2,1)S(1)}, bf16[128,2048]{1,0:T(8,128)(2,1)S(1)}, u32[]{:S(2)}, u32[]{:S(2)}) collective-permute-start(bf16[128,2048]{1,0:T(8,128)(2,1)S(1)} %shard_map.127), channel_id=1, source_target_pairs={{0,1},{1,0},{2,3},{3,2},{4,5},{5,4},{6,7},{7,6},{8,9},{9,8},{10,11... | collective-permute-start | bytes 1572872 | tf_op jit(solution)/shard_map/ppermute | solution.py:26
  44.6 13.4 %collective-permute-start.19 = (bf16[256,256]{1,0:T(8,128)(2,1)S(1)}, bf16[256,256]{1,0:T(8,128)(2,1)S(1)}, u32[]{:S(2)}, u32[]{:S(2)}) collective-permute-start(bf16[256,256]{1,0:T(8,128)(2,1)S(1)} %get-tuple-element.86), channel_id=1, source_target_pairs={{8,0},{10,2},{12,4},{14,6},{16,8},{18,10},{20,12},{22,14},{24,16},... | collective-permute-start | bytes 393224 | tf_op jit(solution)/shard_map/ppermute | solution.py:26
  45.9 12.1 %collective-permute-start.22 = (bf16[256,256]{1,0:T(8,128)(2,1)S(1)}, bf16[256,256]{1,0:T(8,128)(2,1)S(1)}, u32[]{:S(2)}, u32[]{:S(2)}) collective-permute-start(bf16[256,256]{1,0:T(8,128)(2,1)S(1)} %get-tuple-element.92), channel_id=1, source_target_pairs={{4,0},{6,2},{12,8},{14,10},{20,16},{22,18},{24,4},{26,6},{28,24},{... | collective-permute-start | bytes 393224 | tf_op jit(solution)/shard_map/ppermute | solution.py:26
  47.2 18.0 %collective-permute-start.23 = (bf16[256,256]{1,0:T(8,128)(2,1)S(1)}, bf16[256,256]{1,0:T(8,128)(2,1)S(1)}, u32[]{:S(2)}, u32[]{:S(2)}) collective-permute-start(bf16[256,256]{1,0:T(8,128)(2,1)S(1)} %get-tuple-element.94), channel_id=1, source_target_pairs={{16,0},{18,2},{20,4},{22,6},{24,8},{26,10},{28,12},{30,14},{17,1},... | collective-permute-start | bytes 393224 | tf_op jit(solution)/shard_map/ppermute | solution.py:26
  65.3 1.3 %collective-permute-start.24 = (bf16[128,256]{1,0:T(8,128)(2,1)S(1)}, bf16[128,256]{1,0:T(8,128)(2,1)S(1)}, u32[]{:S(2)}, u32[]{:S(2)}) collective-permute-start(bf16[128,256]{1,0:T(8,128)(2,1)S(1)} %get-tuple-element.96), channel_id=1, source_target_pairs={{0,2},{2,0},{4,6},{6,4},{8,10},{10,8},{12,14},{14,12},{16,18},{18,... | collective-permute-start | bytes 196616 | tf_op jit(solution)/shard_map/ppermute | solution.py:26

commit v5 on v4

--- a/solution.py
+++ b/solution.py
@@ -20,10 +20,12 @@
 SMALL = pl.CostEstimate(flops=1, bytes_accessed=1, transcendentals=0)
 
 
-def moved(array, axis, target):
+def moved(array, axis, target, around=False):
     size = lax.axis_size(axis)
     pairs = [(i, target(i)) for i in range(size)]
-    return lax.ppermute(array, axis, [(i, t) for i, t in pairs if t is not None and 0 <= t < size])
+    if around:
+        return lax.ppermute(array, axis, [(i, t % size) for i, t in pairs])
+    return lax.ppermute(array, axis, [(i, t) for i, t in pairs if 0 <= t < size])
 
 
 def vmem():
@@ -109,8 +111,8 @@
     own = pl.ds(pl.multiple_of(core * half, HD), half)
     gain = facts[0:1]
     for side in range(2):
-        raw_all = query_p[:, own] if side else query[:, own]
-        grad_all = grad_p[:, own] if side else grad[:, own]
+        raw_all = query_p[:, own] if side else query[...]
+        grad_all = grad_p[:, own] if side else grad[...]
         parity = 1 - core if side else core
         for head in range(heads):
             here = pl.ds(pl.multiple_of(parity * half + head * BLOCK, BLOCK), BLOCK)
@@ -124,7 +126,8 @@
     kept[...] = message[...]
 
 
-def place(kv_local, source, other, first, core, keys, values, keys_t, docs):
+def place(kv_local, source, other, first, steps_back, core, keys, values, keys_t, docs):
+    there = lax.div(lax.axis_index("ctx"), 4) >= steps_back
     after = (kv_local - 1) * BLOCK
     for block, skip, parity in ((source, 0, core), (other, after, 1 - core)):
         at = pl.ds(pl.multiple_of((first + parity) * BLOCK, BLOCK), BLOCK)
@@ -132,7 +135,8 @@
         keys[at, :] = key
         values[at, :] = block[skip : skip + BLOCK, HD:]
         keys_t[:, at] = key.astype(F32).T.astype(BF16)
-        docs[first + parity] = block[kv_local * BLOCK :, :].astype(F32)[0:8]
+        ids = block[kv_local * BLOCK :, :].astype(F32)[0:8]
+        docs[first + parity] = jnp.where(there, ids, 0.0)
 
 
 def masks(own_doc, docs):
@@ -160,7 +164,7 @@
     blocks = 2 * n_near
     for index in range(n_near):
         first = blocks - 2 - 2 * index
-        place(kv_local, mine[index], others[index], first, core, keys, values, keys_t, docs)
+        place(kv_local, mine[index], others[index], first, index, core, keys, values, keys_t, docs)
     wide = 2 * BLOCK
     row = lax.broadcasted_iota(jnp.int32, (BLOCK, wide), 0)
     col = lax.rem(lax.broadcasted_iota(jnp.int32, (BLOCK, wide), 1), BLOCK)
@@ -233,7 +237,7 @@
     blocks = 2 * n_far
     for index in range(n_far):
         source, other = mine[1 + index], others[1 + index]
-        place(kv_local, source, other, 2 * index, core, keys, values, keys_t, docs)
+        place(kv_local, source, other, 2 * index, index, core, keys, values, keys_t, docs)
     for source, parity in ((mine[0], core), (others[0], 1 - core)):
         docs[blocks + parity] = source[kv_local * BLOCK :, :].astype(F32)[0:8]
     wide = 2 * BLOCK
@@ -410,10 +414,8 @@
     sum_d[...] = (d[...].astype(F32) + turn[half:].astype(F32)).astype(sum_d.dtype)
 
 
-def collect_kernel(part_own, a, b, d, keep, send):
-    result = part_own[...]
-    for back in (a, b, d):
-        result = result + back[...].astype(F32)
+def collect_kernel(part, back, keep, send):
+    result = part[...] + back[...].astype(F32)
     keep[...] = result[:BLOCK]
     send[...] = result[BLOCK:].astype(BF16)
 
@@ -486,13 +488,16 @@
         loss_bucket.reshape(1, tokens),
     )
 
-    far_d = moved(message, "ctx", lambda i: i + 8)
-    far_b = moved(message, "ctx", lambda i: i + 4)
+    far_d = moved(message, "ctx", lambda i: i + 8, around=True)
+    far_b = moved(message, "ctx", lambda i: i + 4, around=True)
     far_a = moved(message, "ctx", lambda i: i + 2 if (i // 2) % 2 == 0 else i + 10)
     query_in, grad_in, _ = lax.optimization_barrier((query_raw, grad_out, message))
     query_p = moved(query_in, "ctx", partner)
     grad_p = moved(grad_in, "ctx", partner)
     facts_p = moved(facts, "ctx", partner)
+    core = lax.axis_index("ctx") % 2
+    query_o = lax.dynamic_slice_in_dim(query_in, core * half, half, 1)
+    grad_o = lax.dynamic_slice_in_dim(grad_in, core * half, half, 1)
     total = 2 * heads * BLOCK
     queries = pl.pallas_call(
         functools.partial(queries_kernel, heads),
@@ -506,10 +511,10 @@
             shape(message.shape, BF16),
         ],
         compiler_params=params(16),
-    )(query_in, grad_in, facts, message, query_p, grad_p, facts_p)
-    far_c = moved(far_b, "ctx", lambda i: i ^ 2 if i >= 4 else None)
+    )(query_o, grad_o, facts, message, query_p, grad_p, facts_p)
+    far_c = moved(far_b, "ctx", lambda i: i ^ 2)
     far_d, *queries = lax.optimization_barrier((far_d, *queries))
-    far_e = moved(far_d, "ctx", lambda i: i ^ 2 if i >= 8 else None)
+    far_e = moved(far_d, "ctx", lambda i: i ^ 2)
     *queries, kept = queries
     q_hat, rows, raw_t, both = queries
     near = (kept, far_b, far_d)
@@ -581,7 +586,7 @@
     )
 
     back_a = moved(part_a, "ctx", lambda i: i - 2 if (i // 2) % 2 == 1 else i - 10)
-    turn = moved(part_ce, "ctx", lambda i: i ^ 2 if i >= 4 else None)
+    turn = moved(part_ce, "ctx", lambda i: i ^ 2)
 
     dq, part_own, part_b, part_d = pl.pallas_call(
         functools.partial(last_kernel, heads, n_near, n_far),
@@ -607,8 +612,8 @@
         compiler_params=params(16),
         cost_estimate=SMALL,
     )(part_b, part_d, turn)
-    back_d = moved(sum_d, "ctx", lambda i: i - 8)
-    back_b = moved(sum_b, "ctx", lambda i: i - 4)
+    back_d = moved(sum_d, "ctx", lambda i: i - 8, around=True)
+    back_b = moved(sum_b, "ctx", lambda i: i - 4, around=True)
     mine, mine_send = project(dq, weight, 0, width, 1)
     mine_recv = moved(mine_send, "ctx", partner)
 
@@ -619,11 +624,11 @@
     back_b, grad_input = lax.optimization_barrier((back_b, grad_input))
     sum_keep, sum_send = pl.pallas_call(
         collect_kernel,
-        in_specs=[vmem()] * 4,
+        in_specs=[vmem()] * 2,
         out_specs=[vmem()] * 2,
         out_shape=[shape((BLOCK, 2 * HD), F32), shape((BLOCK, 2 * HD), BF16)],
         compiler_params=params(16),
-    )(part_own, back_a, back_b, back_d)
+    )(add(add(part_own, back_d, F32), back_b, F32), back_a)
     sum_recv = moved(sum_send, "ctx", partner)
     grad_key, grad_value = pl.pallas_call(
         functools.partial(finish_kernel, kv_local),

time: 68.2 us -> 61.5 us (0.902)
  waiting for transfers between devices: 18 us -> 12.4 us
  local copies, waits for them, and re-layouts: 3.69 us -> 2.68 us
    ppermute x25, waiting for transfers between devices: 18 us -> 12.4 us  [the longest x4 9.18 us: moved(): return lax.ppermute(array, axis, [(i, t % size) for i, t in pairs])]
    unnamed x12 -> x8, local copies, waits for them, and re-layouts: 3.69 us -> 1.61 us
    dynamic_slice x0 -> x1, local copies, waits for them, and re-layouts: none -> 1.07 us  [local(): grad_o = lax.dynamic_slice_in_dim(grad_in, core * half, half, 1)]
  transfers between devices with their start and end apart: 25 -> 25, of which waited for: 4 -> 6; matrix products, arithmetic and copies ran while one was open for 0% -> 2% of each run, Pallas kernels for 18% -> 20%
where the time goes in v5:
time: 61.5 us; the launch traced here: 61.2 us
  starting transfers between devices  24.8 us (40%)
  Pallas kernels  19.9 us (32%)
  waiting for transfers between devices  12.4 us (20%)
  local copies, waits for them, and re-layouts  2.68 us (4%)
  between operations  1.49 us (2%)
    ppermute x21, starting transfers between devices, moved(): lax.ppermute(array, axis, [(i, t) for i, t in pairs if 0 <= t < size])  13.7 us
    ppermute x4, starting transfers between devices, moved(): return lax.ppermute(array, axis, [(i, t % size) for i, t in pairs])  11.1 us
    ppermute x4, waiting for transfers between devices, moved(): return lax.ppermute(array, axis, [(i, t % size) for i, t in pairs])  9.18 us
    pallas_call x1, Pallas kernels, local(): pl.pallas_call(functools.partial(far_kernel, kv_local, heads, n_near, n_f...  5.13 us
    pallas_call x1, Pallas kernels, local(): pl.pallas_call(functools.partial(near_kernel, kv_local, heads, n_near), i...  4.93 us
    ppermute x21, waiting for transfers between devices, moved(): lax.ppermute(array, axis, [(i, t) for i, t in pairs if 0 <= t < size])  3.19 us
    pallas_call x1, Pallas kernels, local(): pl.pallas_call(functools.partial(last_kernel, heads, n_near, n_far), in_s...  2.75 us
    pallas_call x2, Pallas kernels, project(): pl.pallas_call(functools.partial(project_kernel, first), in_specs=[vmem()...  2.71 us
  transfers between devices with their start and end apart: 25, of which 6 were waited for; matrix products, arithmetic and copies ran while one was open for 2% of the time, Pallas kernels for 20%

profile of v5, /device:TPU:0, one launch (start us, length us, event | category | flops | bytes accessed | tf_op | source)
XLA Modules:
  0.0 61.2 jit_solution(9028509227103446014)
XLA Ops:
  1.3 1.7 %shard_map.121 = (bf16[272,256]{1,0:T(8,128)(2,1)}, f32[16,128]{1,0:T(8,128)}) custom-call(s32[1]{0:T(128)S(6)} %copy.15.docs, f32[16]{0:T(128)} %table.1, bf16[128,256]{1,0:T(8,128)(2,1)} %key.3, bf16[128,256]{1,0:T(8,128)(2,1)} %value.1, f32[1,128]{1,0:T(1,128)} %bitcast.3, f32[1,128]{1,0:T(1,128)} %bitcast.5, s32[1,128]{1,0:T(1,128)} %bitcast.6), custom_call_target="tpu_custom_call" | custom-call | tf_op jit(solution)/shard_map/pallas_call | solution.py:473
  3.0 0.5 collective-permute-start.1
  3.4 0.1 collective-permute-start.2
  3.5 0.5 collective-permute-start.3
  3.9 2.6 %collective-permute-start.4 = (bf16[272,256]{1,0:T(8,128)(2,1)}, bf16[272,256]{1,0:T(8,128)(2,1)S(1)}, u32[]{:S(2)}, u32[]{:S(2)}) collective-permute-start(bf16[272,256]{1,0:T(8,128)(2,1)} %get-tuple-element.51.message), channel_id=1, source_target_pairs={{0,8},{2,10},{4,12},{6,14},{8,16},{10,18},{12,20},{14,22},{16,24},... | collective-permute-start | bytes 417800 | tf_op jit(solution)/shard_map/ppermute | solution.py:27
  6.5 2.6 %collective-permute-start = (bf16[272,256]{1,0:T(8,128)(2,1)}, bf16[272,256]{1,0:T(8,128)(2,1)S(1)}, u32[]{:S(2)}, u32[]{:S(2)}) collective-permute-start(bf16[272,256]{1,0:T(8,128)(2,1)} %get-tuple-element.51.message), channel_id=1, source_target_pairs={{0,16},{2,18},{4,20},{6,22},{8,24},{10,26},{12,28},{14,30},{16,0},... | collective-permute-start | bytes 417800 | tf_op jit(solution)/shard_map/ppermute | solution.py:27
  9.1 0.0 collective-permute-done.3.facts_p
  9.1 3.4 %collective-permute-start.8 = (bf16[272,256]{1,0:T(8,128)(2,1)}, bf16[272,256]{1,0:T(8,128)(2,1)S(1)}, u32[]{:S(2)}, u32[]{:S(2)}) collective-permute-start(bf16[272,256]{1,0:T(8,128)(2,1)} %get-tuple-element.51.message), channel_id=1, source_target_pairs={{0,4},{2,6},{4,24},{6,26},{8,12},{10,14},{16,20},{18,22},{24,28},{... | collective-permute-start | bytes 417800 | tf_op jit(solution)/shard_map/ppermute | solution.py:28
  12.6 1.1 %constant_dynamic-slice_fusion = (bf16[128,1024]{1,0:T(8,128)(2,1)S(1)}, bf16[128,1024]{1,0:T(8,128)(2,1)S(1)}) fusion(bf16[128,2048]{1,0:T(8,128)(2,1)} %param.13, s32[]{:T(128)S(6)} %select_n.12, bf16[128,2048]{1,0:T(8,128)(2,1)} %param.10), kind=kLoop, calls=%fused_computation | loop fusion | bytes 1048580 | tf_op jit(solution)/shard_map/dynamic_slice | solution.py:500
  13.6 0.1 collective-permute-start.5
  13.7 0.0 collective-permute-done.1.query_p
  13.7 1.8 %collective-permute-start.9 = (bf16[272,256]{1,0:T(8,128)(2,1)S(1)}, bf16[272,256]{1,0:T(8,128)(2,1)S(1)}, u32[]{:S(2)}, u32[]{:S(2)}) collective-permute-start(bf16[272,256]{1,0:T(8,128)(2,1)S(1)} %collective-permute-done.4.refs_1_), channel_id=1, source_target_pairs={{0,4},{2,6},{4,0},{6,2},{8,12},{10,14},{12,8},{14,10},{16,20},{18,... | collective-permute-start | bytes 417800 | tf_op jit(solution)/shard_map/ppermute | solution.py:28
  15.5 0.2 collective-permute-start.6
  15.7 0.9 %copy-done.1 = bf16[272,256]{1,0:T(8,128)(2,1)S(1)} copy-done((bf16[272,256]{1,0:T(8,128)(2,1)S(1)}, bf16[272,256]{1,0:T(8,128)(2,1)}, u32[]{:S(2)}) %copy-start.1) | copy-done | bytes 139288
  16.6 0.7 %copy-done.2 = f32[16,128]{1,0:T(8,128)S(1)} copy-done((f32[16,128]{1,0:T(8,128)S(1)}, f32[16,128]{1,0:T(8,128)}, u32[]{:S(2)}) %copy-start.2) | copy-done | bytes 8216
  17.3 0.5 shard_map.122
  17.8 1.2 %collective-permute-done.refs_2_ = bf16[272,256]{1,0:T(8,128)(2,1)S(1)} collective-permute-done((bf16[272,256]{1,0:T(8,128)(2,1)}, bf16[272,256]{1,0:T(8,128)(2,1)S(1)}, u32[]{:S(2)}, u32[]{:S(2)}) %collective-permute-start) | collective-permute-done | bytes 139296 | tf_op jit(solution)/shard_map/ppermute | solution.py:27
  19.1 0.0 collective-permute-start.7
  19.1 0.0 collective-permute-done.8.refs_1_
  19.1 1.5 %collective-permute-start.10 = (bf16[272,256]{1,0:T(8,128)(2,1)S(1)}, bf16[272,256]{1,0:T(8,128)(2,1)S(1)}, u32[]{:S(2)}, u32[]{:S(2)}) collective-permute-start(bf16[272,256]{1,0:T(8,128)(2,1)S(1)} %collective-permute-done.refs_2_), channel_id=1, source_target_pairs={{0,4},{2,6},{4,0},{6,2},{8,12},{10,14},{12,8},{14,10},{16,20},{18,... | collective-permute-start | bytes 417800 | tf_op jit(solution)/shard_map/ppermute | solution.py:28
  20.6 0.2 collective-permute-start.11
  20.8 0.3 collective-permute-start.12
  21.2 4.9 %shard_map.123 = (bf16[4096,1024]{1,0:T(8,128)(2,1)S(1)}, bf16[128,768]{1,0:T(8,128)(2,1)S(1)}, bf16[8,768,256]{2,1,0:T(8,128)(2,1)S(1)}, f32[8,768,256]{2,1,0:T(8,128)S(1)}, f32[8,16,256]{2,1,0:T(8,128)S(1)}) custom-call(bf16[272,256]{1,0:T(8,128)(2,1)S(1)} %get-tuple-element.64.refs_0_, bf16[272,256]{1,0:T(8,128)(2,1)S(1)} %collective-permute-done.4.refs_1_, ...), custom_call_target="tpu_custom_call" | custom-call | tf_op jit(solution)/shard_map/pallas_call | solution.py:526
  26.1 0.3 collective-permute-start.13
  26.4 1.2 %collective-permute-done.13.refs_7_ = bf16[272,256]{1,0:T(8,128)(2,1)S(1)} collective-permute-done((bf16[272,256]{1,0:T(8,128)(2,1)S(1)}, bf16[272,256]{1,0:T(8,128)(2,1)S(1)}, u32[]{:S(2)}, u32[]{:S(2)}) %collective-permute-start.13) | collective-permute-done | bytes 139296 | tf_op jit(solution)/shard_map/ppermute | solution.py:28
  27.5 5.1 %shard_map.124 = (bf16[128,768]{1,0:T(8,128)(2,1)S(1)}, bf16[8,768,256]{2,1,0:T(8,128)(2,1)S(1)}, bf16[8,1536,256]{2,1,0:T(8,128)(2,1)S(1)}, bf16[256,256]{1,0:T(8,128)(2,1)S(1)}, bf16[512,256]{1,0:T(8,128)(2,1)S(1)}) custom-call(bf16[272,256]{1,0:T(8,128)(2,1)S(1)} %get-tuple-element.64.refs_0_, ...), custom_call_target="tpu_custom_call", output_to_operand_aliasing={{1}: (11, {})} | custom-call | flops 1 | bytes 1 | tf_op jit(solution)/shard_map/pallas_call | solution.py:551
  32.7 0.9 %collective-permute-start.18 = (bf16[512,256]{1,0:T(8,128)(2,1)S(1)}, bf16[512,256]{1,0:T(8,128)(2,1)S(1)}, u32[]{:S(2)}, u32[]{:S(2)}) collective-permute-start(bf16[512,256]{1,0:T(8,128)(2,1)S(1)} %get-tuple-element.84), channel_id=1, source_target_pairs={{0,4},{2,6},{4,0},{6,2},{8,12},{10,14},{12,8},{14,10},{16,20},{18,... | collective-permute-start | bytes 786440 | tf_op jit(solution)/shard_map/ppermute | solution.py:28
  33.5 2.8 %shard_map.125 = (bf16[1024,256]{1,0:T(8,128)(2,1)S(1)}, f32[256,256]{1,0:T(8,128)S(1)}, bf16[256,256]{1,0:T(8,128)(2,1)S(1)}, bf16[256,256]{1,0:T(8,128)(2,1)S(1)}) custom-call(bf16[2048,128]{1,0:T(8,128)(2,1)S(1)} %get-tuple-element.60.refs_6_.refs_8_.refs_0_, bf16[2048,128]{1,0:T(8,128)(2,1)S(1)} %get-tuple-element.61.refs_7_.refs_9_.refs_1_, ...), custom_call_target="tpu_custom_call" | custom-call | flops 1 | bytes 1 | tf_op jit(solution)/shard_map/pallas_call | solution.py:591
  36.3 1.4 %shard_map.126 = (bf16[128,2048]{1,0:T(8,128)(2,1)S(1)}, bf16[128,512]{1,0:T(8,128)(2,1)S(1)}, bf16[128,512]{1,0:T(8,128)(2,1)S(1)}, bf16[128,512]{1,0:T(8,128)(2,1)S(1)}, bf16[128,512]{1,0:T(8,128)(2,1)S(1)}) custom-call(bf16[1024,256]{1,0:T(8,128)(2,1)S(1)} %get-tuple-element.77.dq, bf16[4096,1024]{1,0:T(8,128)(2,1)S(1)} %get-tuple-element.78.weight), custom_call_target="tpu_custom_call" | custom-call | flops 1 | bytes 1 | tf_op jit(solution)/shard_map/pallas_call | solution.py:363
  37.6 0.1 collective-permute-start.14
  37.7 0.5 collective-permute-start.15
  38.2 0.1 collective-permute-start.16
  38.3 0.4 collective-permute-start.17
  38.7 1.4 %shard_map.129 = (bf16[128,2048]{1,0:T(8,128)(2,1)S(1)}, bf16[128,2048]{1,0:T(8,128)(2,1)S(1)}) custom-call(bf16[1024,256]{1,0:T(8,128)(2,1)S(1)} %get-tuple-element.77.dq, bf16[4096,1024]{1,0:T(8,128)(2,1)S(1)} %get-tuple-element.78.weight), custom_call_target="tpu_custom_call" | custom-call | flops 1 | bytes 1 | tf_op jit(solution)/shard_map/pallas_call | solution.py:363
  40.1 0.1 collective-permute-start.21
  40.3 0.1 shard_map.127
  40.4 0.7 %collective-permute-done.18.turn = bf16[512,256]{1,0:T(8,128)(2,1)S(1)} collective-permute-done((bf16[512,256]{1,0:T(8,128)(2,1)S(1)}, bf16[512,256]{1,0:T(8,128)(2,1)S(1)}, u32[]{:S(2)}, u32[]{:S(2)}) %collective-permute-start.18) | collective-permute-done | bytes 262176 | tf_op jit(solution)/shard_map/ppermute | solution.py:28
  41.1 1.5 %collective-permute-start.20 = (bf16[128,2048]{1,0:T(8,128)(2,1)S(1)}, bf16[128,2048]{1,0:T(8,128)(2,1)S(1)}, u32[]{:S(2)}, u32[]{:S(2)}) collective-permute-start(bf16[128,2048]{1,0:T(8,128)(2,1)S(1)} %shard_map.127), channel_id=1, source_target_pairs={{0,1},{1,0},{2,3},{3,2},{4,5},{5,4},{6,7},{7,6},{8,9},{9,8},{10,11... | collective-permute-start | bytes 1572872 | tf_op jit(solution)/shard_map/ppermute | solution.py:28
  42.6 0.1 shard_map.128
  42.7 5.5 %collective-permute-start.22 = (bf16[256,256]{1,0:T(8,128)(2,1)S(1)}, bf16[256,256]{1,0:T(8,128)(2,1)S(1)}, u32[]{:S(2)}, u32[]{:S(2)}) collective-permute-start(bf16[256,256]{1,0:T(8,128)(2,1)S(1)} %get-tuple-element.92), channel_id=1, source_target_pairs={{0,16},{2,18},{4,20},{6,22},{8,24},{10,26},{12,28},{14,30},{16,0},... | collective-permute-start | bytes 393224 | tf_op jit(solution)/shard_map/ppermute | solution.py:27
  48.2 0.4 collective-permute-start.19
  48.6 1.3 %collective-permute-start.23 = (bf16[256,256]{1,0:T(8,128)(2,1)S(1)}, bf16[256,256]{1,0:T(8,128)(2,1)S(1)}, u32[]{:S(2)}, u32[]{:S(2)}) collective-permute-start(bf16[256,256]{1,0:T(8,128)(2,1)S(1)} %get-tuple-element.94), channel_id=1, source_target_pairs={{4,0},{6,2},{12,8},{14,10},{20,16},{22,18},{24,4},{26,6},{28,24},{... | collective-permute-start | bytes 393224 | tf_op jit(solution)/shard_map/ppermute | solution.py:28
  49.9 5.5 %collective-permute-done.22.refs_1_ = bf16[256,256]{1,0:T(8,128)(2,1)S(1)} collective-permute-done((bf16[256,256]{1,0:T(8,128)(2,1)S(1)}, bf16[256,256]{1,0:T(8,128)(2,1)S(1)}, u32[]{:S(2)}, u32[]{:S(2)}) %collective-permute-start.22) | collective-permute-done | bytes 131104 | tf_op jit(solution)/shard_map/ppermute | solution.py:27
  55.4 1.0 %shard_map.130 = bf16[128,2048]{1,0:T(8,128)(2,1)} custom-call(bf16[128,2048]{1,0:T(8,128)(2,1)S(1)} %get-tuple-element.87.refs_0_, bf16[128,2048]{1,0:T(8,128)(2,1)S(1)} %collective-permute-done.20.refs_1_, bf16[128,2048]{1,0:T(8,128)(2,1)S(1)} %collective-permute-done.21.refs_2_), custom_call_target="tpu_custom_call" | custom-call | flops 1 | bytes 1 | tf_op jit(solution)/shard_map/pallas_call | solution.py:401
  56.4 2.5 %collective-permute-done.19.refs_1_ = bf16[256,256]{1,0:T(8,128)(2,1)S(1)} collective-permute-done((bf16[256,256]{1,0:T(8,128)(2,1)S(1)}, bf16[256,256]{1,0:T(8,128)(2,1)S(1)}, u32[]{:S(2)}, u32[]{:S(2)}) %collective-permute-start.19) | collective-permute-done | bytes 131104 | tf_op jit(solution)/shard_map/ppermute | solution.py:27
  59.0 0.1 collective-permute-start.24
  59.0 1.2 %collective-permute-done.24.recv = bf16[128,256]{1,0:T(8,128)(2,1)S(1)} collective-permute-done((bf16[128,256]{1,0:T(8,128)(2,1)S(1)}, bf16[128,256]{1,0:T(8,128)(2,1)S(1)}, u32[]{:S(2)}, u32[]{:S(2)}) %collective-permute-start.24) | collective-permute-done | bytes 65568 | tf_op jit(solution)/shard_map/ppermute | solution.py:28
  60.3 0.9 %shard_map.134 = (bf16[128,256]{1,0:T(8,128)(2,1)}, bf16[128,256]{1,0:T(8,128)(2,1)}) custom-call(f32[128,256]{1,0:T(8,128)S(1)} %get-tuple-element.95.keep, bf16[128,256]{1,0:T(8,128)(2,1)S(1)} %collective-permute-done.24.recv, bf16[128,256]{1,0:T(8,128)(2,1)S(1)} %copy-done, f32[1,128]{1,0:T(1,128)S(1)} %bitcast.4), custom_call_target="tpu_custom_call" | custom-call | tf_op jit(solution)/shard_map/pallas_call | solution.py:633
  (25 shorter events, 0.1 us)
Async XLA Ops:
  3.0 10.7 %collective-permute-start.1 = (bf16[128,2048]{1,0:T(8,128)(2,1)}, bf16[128,2048]{1,0:T(8,128)(2,1)S(1)}, u32[]{:S(2)}, u32[]{:S(2)}) collective-permute-start(bf16[128,2048]{1,0:T(8,128)(2,1)} %param.10), channel_id=1, source_target_pairs={{0,2},{2,0},{4,6},{6,4},{8,10},{10,8},{12,14},{14,12},{16,18},{18,... | collective-permute-start | bytes 1572872 | tf_op jit(solution)/shard_map/ppermute | solution.py:28
  3.4 12.1 %collective-permute-start.2 = (bf16[128,2048]{1,0:T(8,128)(2,1)}, bf16[128,2048]{1,0:T(8,128)(2,1)S(1)}, u32[]{:S(2)}, u32[]{:S(2)}) collective-permute-start(bf16[128,2048]{1,0:T(8,128)(2,1)} %param.13), channel_id=1, source_target_pairs={{0,2},{2,0},{4,6},{6,4},{8,10},{10,8},{12,14},{14,12},{16,18},{18,... | collective-permute-start | bytes 1572872 | tf_op jit(solution)/shard_map/ppermute | solution.py:28
  3.5 5.6 %collective-permute-start.3 = (f32[16,128]{1,0:T(8,128)}, f32[16,128]{1,0:T(8,128)S(1)}, u32[]{:S(2)}, u32[]{:S(2)}) collective-permute-start(f32[16,128]{1,0:T(8,128)} %get-tuple-element.54.facts), channel_id=1, source_target_pairs={{0,2},{2,0},{4,6},{6,4},{8,10},{10,8},{12,14},{14,12},{16,18},{18,... | collective-permute-start | bytes 24584 | tf_op jit(solution)/shard_map/ppermute | solution.py:28
  3.9 9.7 %collective-permute-start.4 = (bf16[272,256]{1,0:T(8,128)(2,1)}, bf16[272,256]{1,0:T(8,128)(2,1)S(1)}, u32[]{:S(2)}, u32[]{:S(2)}) collective-permute-start(bf16[272,256]{1,0:T(8,128)(2,1)} %get-tuple-element.51.message), channel_id=1, source_target_pairs={{0,8},{2,10},{4,12},{6,14},{8,16},{10,18},{12,20},{14,22},{16,24},... | collective-permute-start | bytes 417800 | tf_op jit(solution)/shard_map/ppermute | solution.py:27
  6.5 12.5 %collective-permute-start = (bf16[272,256]{1,0:T(8,128)(2,1)}, bf16[272,256]{1,0:T(8,128)(2,1)S(1)}, u32[]{:S(2)}, u32[]{:S(2)}) collective-permute-start(bf16[272,256]{1,0:T(8,128)(2,1)} %get-tuple-element.51.message), channel_id=1, source_target_pairs={{0,16},{2,18},{4,20},{6,22},{8,24},{10,26},{12,28},{14,30},{16,0},... | collective-permute-start | bytes 417800 | tf_op jit(solution)/shard_map/ppermute | solution.py:27
  9.1 10.0 %collective-permute-start.8 = (bf16[272,256]{1,0:T(8,128)(2,1)}, bf16[272,256]{1,0:T(8,128)(2,1)S(1)}, u32[]{:S(2)}, u32[]{:S(2)}) collective-permute-start(bf16[272,256]{1,0:T(8,128)(2,1)} %get-tuple-element.51.message), channel_id=1, source_target_pairs={{0,4},{2,6},{4,24},{6,26},{8,12},{10,14},{16,20},{18,22},{24,28},{... | collective-permute-start | bytes 417800 | tf_op jit(solution)/shard_map/ppermute | solution.py:28
  13.6 7.0 %collective-permute-start.5 = (bf16[272,256]{1,0:T(8,128)(2,1)}, bf16[272,256]{1,0:T(8,128)(2,1)S(1)}, u32[]{:S(2)}, u32[]{:S(2)}) collective-permute-start(bf16[272,256]{1,0:T(8,128)(2,1)} %get-tuple-element.51.message), channel_id=1, source_target_pairs={{0,2},{2,0},{4,6},{6,4},{8,10},{10,8},{12,14},{14,12},{16,18},{18,... | collective-permute-start | bytes 417800 | tf_op jit(solution)/shard_map/ppermute | solution.py:28
  13.7 7.1 %collective-permute-start.9 = (bf16[272,256]{1,0:T(8,128)(2,1)S(1)}, bf16[272,256]{1,0:T(8,128)(2,1)S(1)}, u32[]{:S(2)}, u32[]{:S(2)}) collective-permute-start(bf16[272,256]{1,0:T(8,128)(2,1)S(1)} %collective-permute-done.4.refs_1_), channel_id=1, source_target_pairs={{0,4},{2,6},{4,0},{6,2},{8,12},{10,14},{12,8},{14,10},{16,20},{18,... | collective-permute-start | bytes 417800 | tf_op jit(solution)/shard_map/ppermute | solution.py:28
  15.5 5.6 %collective-permute-start.6 = (bf16[272,256]{1,0:T(8,128)(2,1)S(1)}, bf16[272,256]{1,0:T(8,128)(2,1)S(1)}, u32[]{:S(2)}, u32[]{:S(2)}) collective-permute-start(bf16[272,256]{1,0:T(8,128)(2,1)S(1)} %collective-permute-done.4.refs_1_), channel_id=1, source_target_pairs={{0,2},{2,0},{4,6},{6,4},{8,10},{10,8},{12,14},{14,12},{16,18},{18,... | collective-permute-start | bytes 417800 | tf_op jit(solution)/shard_map/ppermute | solution.py:28
  15.7 0.9 %copy-start.1 = (bf16[272,256]{1,0:T(8,128)(2,1)S(1)}, bf16[272,256]{1,0:T(8,128)(2,1)}, u32[]{:S(2)}) copy-start(bf16[272,256]{1,0:T(8,128)(2,1)} %get-tuple-element.51.message) | copy-start | bytes 417796
  16.6 0.7 %copy-start.2 = (f32[16,128]{1,0:T(8,128)S(1)}, f32[16,128]{1,0:T(8,128)}, u32[]{:S(2)}) copy-start(f32[16,128]{1,0:T(8,128)} %get-tuple-element.54.facts) | copy-start | bytes 24580
  19.1 2.1 %collective-permute-start.7 = (bf16[272,256]{1,0:T(8,128)(2,1)S(1)}, bf16[272,256]{1,0:T(8,128)(2,1)S(1)}, u32[]{:S(2)}, u32[]{:S(2)}) collective-permute-start(bf16[272,256]{1,0:T(8,128)(2,1)S(1)} %collective-permute-done.refs_2_), channel_id=1, source_target_pairs={{0,2},{2,0},{4,6},{6,4},{8,10},{10,8},{12,14},{14,12},{16,18},{18,... | collective-permute-start | bytes 417800 | tf_op jit(solution)/shard_map/ppermute | solution.py:28
  19.1 7.0 %collective-permute-start.10 = (bf16[272,256]{1,0:T(8,128)(2,1)S(1)}, bf16[272,256]{1,0:T(8,128)(2,1)S(1)}, u32[]{:S(2)}, u32[]{:S(2)}) collective-permute-start(bf16[272,256]{1,0:T(8,128)(2,1)S(1)} %collective-permute-done.refs_2_), channel_id=1, source_target_pairs={{0,4},{2,6},{4,0},{6,2},{8,12},{10,14},{12,8},{14,10},{16,20},{18,... | collective-permute-start | bytes 417800 | tf_op jit(solution)/shard_map/ppermute | solution.py:28
  20.6 5.7 %collective-permute-start.11 = (bf16[272,256]{1,0:T(8,128)(2,1)S(1)}, bf16[272,256]{1,0:T(8,128)(2,1)S(1)}, u32[]{:S(2)}, u32[]{:S(2)}) collective-permute-start(bf16[272,256]{1,0:T(8,128)(2,1)S(1)} %collective-permute-done.8.refs_1_), channel_id=1, source_target_pairs={{0,2},{2,0},{4,6},{6,4},{8,10},{10,8},{12,14},{14,12},{16,18},{18,... | collective-permute-start | bytes 417800 | tf_op jit(solution)/shard_map/ppermute | solution.py:28
  20.8 5.5 %collective-permute-start.12 = (bf16[272,256]{1,0:T(8,128)(2,1)S(1)}, bf16[272,256]{1,0:T(8,128)(2,1)S(1)}, u32[]{:S(2)}, u32[]{:S(2)}) collective-permute-start(bf16[272,256]{1,0:T(8,128)(2,1)S(1)} %collective-permute-done.9.refs_2_), channel_id=1, source_target_pairs={{0,2},{2,0},{4,6},{6,4},{8,10},{10,8},{12,14},{14,12},{16,18},{18,... | collective-permute-start | bytes 417800 | tf_op jit(solution)/shard_map/ppermute | solution.py:28
  26.1 1.4 %collective-permute-start.13 = (bf16[272,256]{1,0:T(8,128)(2,1)S(1)}, bf16[272,256]{1,0:T(8,128)(2,1)S(1)}, u32[]{:S(2)}, u32[]{:S(2)}) collective-permute-start(bf16[272,256]{1,0:T(8,128)(2,1)S(1)} %collective-permute-done.10.refs_3_), channel_id=1, source_target_pairs={{0,2},{2,0},{4,6},{6,4},{8,10},{10,8},{12,14},{14,12},{16,18},{18,... | collective-permute-start | bytes 417800 | tf_op jit(solution)/shard_map/ppermute | solution.py:28
  32.7 8.5 %collective-permute-start.18 = (bf16[512,256]{1,0:T(8,128)(2,1)S(1)}, bf16[512,256]{1,0:T(8,128)(2,1)S(1)}, u32[]{:S(2)}, u32[]{:S(2)}) collective-permute-start(bf16[512,256]{1,0:T(8,128)(2,1)S(1)} %get-tuple-element.84), channel_id=1, source_target_pairs={{0,4},{2,6},{4,0},{6,2},{8,12},{10,14},{12,8},{14,10},{16,20},{18,... | collective-permute-start | bytes 786440 | tf_op jit(solution)/shard_map/ppermute | solution.py:28
  37.6 2.5 %collective-permute-start.14 = (bf16[128,512]{1,0:T(8,128)(2,1)S(1)}, bf16[128,512]{1,0:T(8,128)(2,1)S(1)}, u32[]{:S(2)}, u32[]{:S(2)}) collective-permute-start(bf16[128,512]{1,0:T(8,128)(2,1)S(1)} %get-tuple-element.80), channel_id=1, source_target_pairs={{0,2},{2,0},{4,6},{6,4},{8,10},{10,8},{12,14},{14,12},{16,18},{18,... | collective-permute-start | bytes 393224 | tf_op jit(solution)/shard_map/ppermute | solution.py:28
  37.7 2.5 %collective-permute-start.15 = (bf16[128,512]{1,0:T(8,128)(2,1)S(1)}, bf16[128,512]{1,0:T(8,128)(2,1)S(1)}, u32[]{:S(2)}, u32[]{:S(2)}) collective-permute-start(bf16[128,512]{1,0:T(8,128)(2,1)S(1)} %get-tuple-element.81), channel_id=1, source_target_pairs={{0,2},{2,0},{4,6},{6,4},{8,10},{10,8},{12,14},{14,12},{16,18},{18,... | collective-permute-start | bytes 393224 | tf_op jit(solution)/shard_map/ppermute | solution.py:28
  38.2 2.0 %collective-permute-start.16 = (bf16[128,512]{1,0:T(8,128)(2,1)S(1)}, bf16[128,512]{1,0:T(8,128)(2,1)S(1)}, u32[]{:S(2)}, u32[]{:S(2)}) collective-permute-start(bf16[128,512]{1,0:T(8,128)(2,1)S(1)} %get-tuple-element.82), channel_id=1, source_target_pairs={{0,2},{2,0},{4,6},{6,4},{8,10},{10,8},{12,14},{14,12},{16,18},{18,... | collective-permute-start | bytes 393224 | tf_op jit(solution)/shard_map/ppermute | solution.py:28
  38.3 22.0 %copy-start = (bf16[128,256]{1,0:T(8,128)(2,1)S(1)}, bf16[128,256]{1,0:T(8,128)(2,1)}, u32[]{:S(2)}) copy-start(bf16[128,256]{1,0:T(8,128)(2,1)} %key.3) | copy-start | bytes 196612
  38.3 22.0 %copy-start.3 = (f32[128]{0:T(128)S(1)}, f32[128]{0:T(128)}, u32[]{:S(2)}) copy-start(f32[128]{0:T(128)} %param.15) | copy-start | bytes 1540
  38.3 2.0 %collective-permute-start.17 = (bf16[128,512]{1,0:T(8,128)(2,1)S(1)}, bf16[128,512]{1,0:T(8,128)(2,1)S(1)}, u32[]{:S(2)}, u32[]{:S(2)}) collective-permute-start(bf16[128,512]{1,0:T(8,128)(2,1)S(1)} %get-tuple-element.83), channel_id=1, source_target_pairs={{0,2},{2,0},{4,6},{6,4},{8,10},{10,8},{12,14},{14,12},{16,18},{18,... | collective-permute-start | bytes 393224 | tf_op jit(solution)/shard_map/ppermute | solution.py:28
  40.1 15.3 %collective-permute-start.21 = (bf16[128,2048]{1,0:T(8,128)(2,1)S(1)}, bf16[128,2048]{1,0:T(8,128)(2,1)S(1)}, u32[]{:S(2)}, u32[]{:S(2)}) collective-permute-start(bf16[128,2048]{1,0:T(8,128)(2,1)S(1)} %get-tuple-element.89), channel_id=1, source_target_pairs={{0,2},{2,0},{4,6},{6,4},{8,10},{10,8},{12,14},{14,12},{16,18},{18,... | collective-permute-start | bytes 1572872 | tf_op jit(solution)/shard_map/ppermute | solution.py:28
  41.1 14.3 %collective-permute-start.20 = (bf16[128,2048]{1,0:T(8,128)(2,1)S(1)}, bf16[128,2048]{1,0:T(8,128)(2,1)S(1)}, u32[]{:S(2)}, u32[]{:S(2)}) collective-permute-start(bf16[128,2048]{1,0:T(8,128)(2,1)S(1)} %shard_map.127), channel_id=1, source_target_pairs={{0,1},{1,0},{2,3},{3,2},{4,5},{5,4},{6,7},{7,6},{8,9},{9,8},{10,11... | collective-permute-start | bytes 1572872 | tf_op jit(solution)/shard_map/ppermute | solution.py:28
  42.7 12.7 %collective-permute-start.22 = (bf16[256,256]{1,0:T(8,128)(2,1)S(1)}, bf16[256,256]{1,0:T(8,128)(2,1)S(1)}, u32[]{:S(2)}, u32[]{:S(2)}) collective-permute-start(bf16[256,256]{1,0:T(8,128)(2,1)S(1)} %get-tuple-element.92), channel_id=1, source_target_pairs={{0,16},{2,18},{4,20},{6,22},{8,24},{10,26},{12,28},{14,30},{16,0},... | collective-permute-start | bytes 393224 | tf_op jit(solution)/shard_map/ppermute | solution.py:27
  48.2 10.7 %collective-permute-start.19 = (bf16[256,256]{1,0:T(8,128)(2,1)S(1)}, bf16[256,256]{1,0:T(8,128)(2,1)S(1)}, u32[]{:S(2)}, u32[]{:S(2)}) collective-permute-start(bf16[256,256]{1,0:T(8,128)(2,1)S(1)} %get-tuple-element.86), channel_id=1, source_target_pairs={{0,24},{2,26},{4,28},{6,30},{8,0},{10,2},{12,4},{14,6},{16,8},{18,... | collective-permute-start | bytes 393224 | tf_op jit(solution)/shard_map/ppermute | solution.py:27
  48.6 10.3 %collective-permute-start.23 = (bf16[256,256]{1,0:T(8,128)(2,1)S(1)}, bf16[256,256]{1,0:T(8,128)(2,1)S(1)}, u32[]{:S(2)}, u32[]{:S(2)}) collective-permute-start(bf16[256,256]{1,0:T(8,128)(2,1)S(1)} %get-tuple-element.94), channel_id=1, source_target_pairs={{4,0},{6,2},{12,8},{14,10},{20,16},{22,18},{24,4},{26,6},{28,24},{... | collective-permute-start | bytes 393224 | tf_op jit(solution)/shard_map/ppermute | solution.py:28
  59.0 1.3 %collective-permute-start.24 = (bf16[128,256]{1,0:T(8,128)(2,1)S(1)}, bf16[128,256]{1,0:T(8,128)(2,1)S(1)}, u32[]{:S(2)}, u32[]{:S(2)}) collective-permute-start(bf16[128,256]{1,0:T(8,128)(2,1)S(1)} %get-tuple-element.96), channel_id=1, source_target_pairs={{0,2},{2,0},{4,6},{6,4},{8,10},{10,8},{12,14},{14,12},{16,18},{18,... | collective-permute-start | bytes 196616 | tf_op jit(solution)/shard_map/ppermute | solution.py:28

commit v6 on v5

--- a/solution.py
+++ b/solution.py
@@ -59,13 +59,13 @@
         rows = slice(part * BLOCK, (part + 1) * BLOCK)
         out[rows, :HD] = normed(key[:, lanes].astype(F32), key_gain[...]).astype(BF16)
         out[rows, HD:] = value[:, lanes]
-    doc = jnp.full((EXTRA, 2 * HD), docs[0] + 1, jnp.int32).astype(F32)
+    doc = jnp.broadcast_to((docs[...] + 1).astype(F32), (EXTRA, 2 * HD))
     out[kv_local * BLOCK :, :] = doc.astype(BF16)
     facts[:8, :] = jnp.broadcast_to(query_gain[...], (8, HD))
     picks = bucket[...]
     found = jnp.zeros((1, HD), F32)
-    for b in range(table.shape[0]):
-        found = found + jnp.where(picks == b, table[b], 0.0)
+    for b in range(table.shape[1]):
+        found = found + jnp.where(picks == b, table[:, b : b + 1], 0.0)
     facts[8:, :] = jnp.broadcast_to(found, (8, HD))
 
 
@@ -472,15 +472,15 @@
     partner = lambda i: i ^ 1
     message, facts = pl.pallas_call(
         functools.partial(message_kernel, kv_local),
-        in_specs=[smem(), smem()] + [vmem()] * 5,
+        in_specs=[vmem()] * 7,
         out_specs=[vmem()] * 2,
         out_shape=[
             shape((kv_local * BLOCK + EXTRA, 2 * HD), BF16),
             shape((16, HD), F32),
         ],
     )(
-        block_docs,
-        loss_table,
+        block_docs.reshape(1, 1),
+        loss_table.reshape(1, -1),
         key_raw,
         value_in,
         key_row,
@@ -488,7 +488,7 @@
         loss_bucket.reshape(1, tokens),
     )
 
-    far_d = moved(message, "ctx", lambda i: i + 8, around=True)
+    far_d = moved(message, "ctx", lambda i: i + 8)
     far_b = moved(message, "ctx", lambda i: i + 4, around=True)
     far_a = moved(message, "ctx", lambda i: i + 2 if (i // 2) % 2 == 0 else i + 10)
     query_in, grad_in, _ = lax.optimization_barrier((query_raw, grad_out, message))
@@ -512,8 +512,8 @@
         ],
         compiler_params=params(16),
     )(query_o, grad_o, facts, message, query_p, grad_p, facts_p)
+    far_d, far_b, *queries = lax.optimization_barrier((far_d, far_b, *queries))
     far_c = moved(far_b, "ctx", lambda i: i ^ 2)
-    far_d, *queries = lax.optimization_barrier((far_d, *queries))
     far_e = moved(far_d, "ctx", lambda i: i ^ 2)
     *queries, kept = queries
     q_hat, rows, raw_t, both = queries
@@ -585,7 +585,9 @@
         sums,
     )
 
-    back_a = moved(part_a, "ctx", lambda i: i - 2 if (i // 2) % 2 == 1 else i - 10)
+    back_a = moved(
+        part_a, "ctx", lambda i: i - 2 if (i // 2) % 2 == 1 else i - 10, around=True
+    )
     turn = moved(part_ce, "ctx", lambda i: i ^ 2)
 
     dq, part_own, part_b, part_d = pl.pallas_call(
@@ -598,11 +600,12 @@
         cost_estimate=SMALL,
     )(q_hat, rows, raw_t, both, near_t, far_t, pw_near, ds)
 
+    mine, mine_send = project(dq, weight, 0, width, 1)
     arrived = []
     for shift in range(1, n_head):
         keep, *sends = project(dq, weight, shift * width, width, 4)
         term = add_pieces(keep, [moved(send, "ctx", partner) for send in sends])
-        term, turn = lax.optimization_barrier((term, turn))
+        term, turn, mine_send = lax.optimization_barrier((term, turn, mine_send))
         arrived.append(moved(term, "head", lambda i, s=shift: (i + s) % n_head))
     sum_b, sum_d = pl.pallas_call(
         two_sums_kernel,
@@ -614,14 +617,8 @@
     )(part_b, part_d, turn)
     back_d = moved(sum_d, "ctx", lambda i: i - 8, around=True)
     back_b = moved(sum_b, "ctx", lambda i: i - 4, around=True)
-    mine, mine_send = project(dq, weight, 0, width, 1)
     mine_recv = moved(mine_send, "ctx", partner)
 
-    grad_input = mine
-    for index, piece in enumerate(arrived):
-        last = index == len(arrived) - 1
-        grad_input = add(grad_input, piece, BF16 if last else F32, *([mine_recv] if last else []))
-    back_b, grad_input = lax.optimization_barrier((back_b, grad_input))
     sum_keep, sum_send = pl.pallas_call(
         collect_kernel,
         in_specs=[vmem()] * 2,
@@ -630,6 +627,12 @@
         compiler_params=params(16),
     )(add(add(part_own, back_d, F32), back_b, F32), back_a)
     sum_recv = moved(sum_send, "ctx", partner)
+    arrived[-1], sum_send = lax.optimization_barrier((arrived[-1], sum_send))
+    grad_input = mine
+    for index, piece in enumerate(arrived):
+        last = index == len(arrived) - 1
+        grad_input = add(grad_input, piece, BF16 if last else F32, *([mine_recv] if last else []))
+    sum_recv, grad_input = lax.optimization_barrier((sum_recv, grad_input))
     grad_key, grad_value = pl.pallas_call(
         functools.partial(finish_kernel, kv_local),
         in_specs=[vmem(), vmem(), hbm(), hbm()],

time: 61.5 us -> 61 us (level)
  the two profiles are of different devices: /device:TPU:0 before, /device:TPU:5 now
where the time goes in v6:
time: 61 us; the launch traced here: 60.7 us
  starting transfers between devices  24.4 us (40%)
  Pallas kernels  20 us (33%)
  waiting for transfers between devices  12.1 us (20%)
  local copies, waits for them, and re-layouts  2.68 us (4%)
  between operations  1.48 us (2%)
    ppermute x21, starting transfers between devices, moved(): lax.ppermute(array, axis, [(i, t) for i, t in pairs if 0 <= t < size])  16.7 us
    ppermute x4, waiting for transfers between devices, moved(): return lax.ppermute(array, axis, [(i, t % size) for i, t in pairs])  9.17 us
    ppermute x4, starting transfers between devices, moved(): return lax.ppermute(array, axis, [(i, t % size) for i, t in pairs])  7.73 us
    pallas_call x1, Pallas kernels, local(): pl.pallas_call(functools.partial(far_kernel, kv_local, heads, n_near, n_f...  5.13 us
    pallas_call x1, Pallas kernels, local(): pl.pallas_call(functools.partial(near_kernel, kv_local, heads, n_near), i...  4.93 us
    ppermute x21, waiting for transfers between devices, moved(): lax.ppermute(array, axis, [(i, t) for i, t in pairs if 0 <= t < size])  2.95 us
    pallas_call x1, Pallas kernels, local(): pl.pallas_call(functools.partial(last_kernel, heads, n_near, n_far), in_s...  2.77 us
    pallas_call x2, Pallas kernels, project(): pl.pallas_call(functools.partial(project_kernel, first), in_specs=[vmem()...  2.71 us
  transfers between devices with their start and end apart: 25, of which 5 were waited for; matrix products, arithmetic and copies ran while one was open for 2% of the time, Pallas kernels for 20%

profile of v6, /device:TPU:5, one launch (start us, length us, event | category | flops | bytes accessed | tf_op | source)
XLA Modules:
  0.0 60.7 jit_solution(1680774058826649385)
XLA Ops:
  1.3 1.8 %shard_map.121 = (bf16[272,256]{1,0:T(8,128)(2,1)}, f32[16,128]{1,0:T(8,128)}) custom-call(s32[1,1]{1,0:T(1,128)} %bitcast.5.docs, f32[1,16]{1,0:T(1,128)} %bitcast.8, bf16[128,256]{1,0:T(8,128)(2,1)} %key.3, bf16[128,256]{1,0:T(8,128)(2,1)} %value.1, f32[1,128]{1,0:T(1,128)} %bitcast.6, f32[1,128]{1,0:T(1,128)} %bitcast.9, s32[1,128]{1,0:T(1,128)} %bitcast.10), custom_call_target="tpu_custom_call" | custom-call | tf_op jit(solution)/shard_map/pallas_call | solution.py:473
  3.0 0.7 %collective-permute-start.2 = (bf16[128,2048]{1,0:T(8,128)(2,1)}, bf16[128,2048]{1,0:T(8,128)(2,1)S(1)}, u32[]{:S(2)}, u32[]{:S(2)}) collective-permute-start(bf16[128,2048]{1,0:T(8,128)(2,1)} %param.10), channel_id=1, source_target_pairs={{0,2},{2,0},{4,6},{6,4},{8,10},{10,8},{12,14},{14,12},{16,18},{18,... | collective-permute-start | bytes 1572872 | tf_op jit(solution)/shard_map/ppermute | solution.py:28
  3.7 0.0 collective-permute-start.3
  3.7 0.5 collective-permute-start.4
  4.2 1.3 %collective-permute-start.1 = (bf16[272,256]{1,0:T(8,128)(2,1)}, bf16[272,256]{1,0:T(8,128)(2,1)S(1)}, u32[]{:S(2)}, u32[]{:S(2)}) collective-permute-start(bf16[272,256]{1,0:T(8,128)(2,1)} %get-tuple-element.54.message), channel_id=1, source_target_pairs={{0,8},{2,10},{4,12},{6,14},{8,16},{10,18},{12,20},{14,22},{16,24},... | collective-permute-start | bytes 417800 | tf_op jit(solution)/shard_map/ppermute | solution.py:27
  5.5 4.2 %collective-permute-start = (bf16[272,256]{1,0:T(8,128)(2,1)}, bf16[272,256]{1,0:T(8,128)(2,1)S(1)}, u32[]{:S(2)}, u32[]{:S(2)}) collective-permute-start(bf16[272,256]{1,0:T(8,128)(2,1)} %get-tuple-element.54.message), channel_id=1, source_target_pairs={{0,16},{2,18},{4,20},{6,22},{8,24},{10,26},{12,28},{14,30},{1,17},... | collective-permute-start | bytes 417800 | tf_op jit(solution)/shard_map/ppermute | solution.py:28
  9.7 0.0 collective-permute-done.4.facts_p
  9.8 1.9 %collective-permute-start.8 = (bf16[272,256]{1,0:T(8,128)(2,1)}, bf16[272,256]{1,0:T(8,128)(2,1)S(1)}, u32[]{:S(2)}, u32[]{:S(2)}) collective-permute-start(bf16[272,256]{1,0:T(8,128)(2,1)} %get-tuple-element.54.message), channel_id=1, source_target_pairs={{0,4},{2,6},{4,24},{6,26},{8,12},{10,14},{16,20},{18,22},{24,28},{... | collective-permute-start | bytes 417800 | tf_op jit(solution)/shard_map/ppermute | solution.py:28
  11.7 1.1 %constant_dynamic-slice_fusion = (bf16[128,1024]{1,0:T(8,128)(2,1)S(1)}, bf16[128,1024]{1,0:T(8,128)(2,1)S(1)}) fusion(bf16[128,2048]{1,0:T(8,128)(2,1)} %param.13, s32[]{:T(128)S(6)} %select_n.12, bf16[128,2048]{1,0:T(8,128)(2,1)} %param.10), kind=kLoop, calls=%fused_computation | loop fusion | bytes 1048580 | tf_op jit(solution)/shard_map/dynamic_slice | solution.py:500
  12.8 0.6 %collective-permute-start.5 = (bf16[272,256]{1,0:T(8,128)(2,1)}, bf16[272,256]{1,0:T(8,128)(2,1)S(1)}, u32[]{:S(2)}, u32[]{:S(2)}) collective-permute-start(bf16[272,256]{1,0:T(8,128)(2,1)} %get-tuple-element.54.message), channel_id=1, source_target_pairs={{0,2},{2,0},{4,6},{6,4},{8,10},{10,8},{12,14},{14,12},{16,18},{18,... | collective-permute-start | bytes 417800 | tf_op jit(solution)/shard_map/ppermute | solution.py:28
  13.4 0.0 collective-permute-done.3.grad_p
  13.4 0.9 %copy-done.1 = bf16[272,256]{1,0:T(8,128)(2,1)S(1)} copy-done((bf16[272,256]{1,0:T(8,128)(2,1)S(1)}, bf16[272,256]{1,0:T(8,128)(2,1)}, u32[]{:S(2)}) %copy-start.1) | copy-done | bytes 139288
  14.3 0.7 %copy-done.2 = f32[16,128]{1,0:T(8,128)S(1)} copy-done((f32[16,128]{1,0:T(8,128)S(1)}, f32[16,128]{1,0:T(8,128)}, u32[]{:S(2)}) %copy-start.2) | copy-done | bytes 8216
  15.0 0.5 shard_map.122
  15.6 0.0 collective-permute-done.refs_2_
  15.6 0.1 collective-permute-start.6
  15.7 0.5 collective-permute-start.7
  16.2 1.8 %collective-permute-start.10 = (bf16[272,256]{1,0:T(8,128)(2,1)S(1)}, bf16[272,256]{1,0:T(8,128)(2,1)S(1)}, u32[]{:S(2)}, u32[]{:S(2)}) collective-permute-start(bf16[272,256]{1,0:T(8,128)(2,1)S(1)} %collective-permute-done.refs_2_), channel_id=1, source_target_pairs={{0,4},{2,6},{4,0},{6,2},{8,12},{10,14},{12,8},{14,10},{16,20},{18,... | collective-permute-start | bytes 417800 | tf_op jit(solution)/shard_map/ppermute | solution.py:28
  17.9 0.0 collective-permute-start.9
  17.9 0.0 collective-permute-done.5.refs_3_.refs_4_
  17.9 0.4 collective-permute-start.11
  18.3 4.9 %shard_map.123 = (bf16[4096,1024]{1,0:T(8,128)(2,1)S(1)}, bf16[128,768]{1,0:T(8,128)(2,1)S(1)}, bf16[8,768,256]{2,1,0:T(8,128)(2,1)S(1)}, f32[8,768,256]{2,1,0:T(8,128)S(1)}, f32[8,16,256]{2,1,0:T(8,128)S(1)}) custom-call(bf16[272,256]{1,0:T(8,128)(2,1)S(1)} %get-tuple-element.67.refs_0_, bf16[272,256]{1,0:T(8,128)(2,1)S(1)} %collective-permute-done.1.refs_1_, ...), custom_call_target="tpu_custom_call" | custom-call | tf_op jit(solution)/shard_map/pallas_call | solution.py:526
  23.3 1.6 %collective-permute-done.9.refs_2_ = bf16[272,256]{1,0:T(8,128)(2,1)S(1)} collective-permute-done((bf16[272,256]{1,0:T(8,128)(2,1)S(1)}, bf16[272,256]{1,0:T(8,128)(2,1)S(1)}, u32[]{:S(2)}, u32[]{:S(2)}) %collective-permute-start.9) | collective-permute-done | bytes 139296 | tf_op jit(solution)/shard_map/ppermute | solution.py:28
  24.8 0.7 %collective-permute-start.12 = (bf16[272,256]{1,0:T(8,128)(2,1)S(1)}, bf16[272,256]{1,0:T(8,128)(2,1)S(1)}, u32[]{:S(2)}, u32[]{:S(2)}) collective-permute-start(bf16[272,256]{1,0:T(8,128)(2,1)S(1)} %collective-permute-done.9.refs_2_), channel_id=1, source_target_pairs={{0,2},{2,0},{4,6},{6,4},{8,10},{10,8},{12,14},{14,12},{16,18},{18,... | collective-permute-start | bytes 417800 | tf_op jit(solution)/shard_map/ppermute | solution.py:28
  25.5 0.0 collective-permute-start.13
  25.5 1.0 %collective-permute-done.12.refs_6_ = bf16[272,256]{1,0:T(8,128)(2,1)S(1)} collective-permute-done((bf16[272,256]{1,0:T(8,128)(2,1)S(1)}, bf16[272,256]{1,0:T(8,128)(2,1)S(1)}, u32[]{:S(2)}, u32[]{:S(2)}) %collective-permute-start.12) | collective-permute-done | bytes 139296 | tf_op jit(solution)/shard_map/ppermute | solution.py:28
  26.5 0.4 collective-permute-done.13.refs_7_
  26.9 5.1 %shard_map.124 = (bf16[128,768]{1,0:T(8,128)(2,1)S(1)}, bf16[8,768,256]{2,1,0:T(8,128)(2,1)S(1)}, bf16[8,1536,256]{2,1,0:T(8,128)(2,1)S(1)}, bf16[256,256]{1,0:T(8,128)(2,1)S(1)}, bf16[512,256]{1,0:T(8,128)(2,1)S(1)}) custom-call(bf16[272,256]{1,0:T(8,128)(2,1)S(1)} %get-tuple-element.67.refs_0_, ...), custom_call_target="tpu_custom_call", output_to_operand_aliasing={{1}: (11, {})} | custom-call | flops 1 | bytes 1 | tf_op jit(solution)/shard_map/pallas_call | solution.py:551
  32.0 1.5 %collective-permute-start.18 = (bf16[512,256]{1,0:T(8,128)(2,1)S(1)}, bf16[512,256]{1,0:T(8,128)(2,1)S(1)}, u32[]{:S(2)}, u32[]{:S(2)}) collective-permute-start(bf16[512,256]{1,0:T(8,128)(2,1)S(1)} %get-tuple-element.89), channel_id=1, source_target_pairs={{0,4},{2,6},{4,0},{6,2},{8,12},{10,14},{12,8},{14,10},{16,20},{18,... | collective-permute-start | bytes 786440 | tf_op jit(solution)/shard_map/ppermute | solution.py:28
  33.5 2.8 %shard_map.125 = (bf16[1024,256]{1,0:T(8,128)(2,1)S(1)}, f32[256,256]{1,0:T(8,128)S(1)}, bf16[256,256]{1,0:T(8,128)(2,1)S(1)}, bf16[256,256]{1,0:T(8,128)(2,1)S(1)}) custom-call(bf16[2048,128]{1,0:T(8,128)(2,1)S(1)} %get-tuple-element.63.refs_6_.refs_8_.refs_0_, bf16[2048,128]{1,0:T(8,128)(2,1)S(1)} %get-tuple-element.64.refs_7_.refs_9_.refs_1_, ...), custom_call_target="tpu_custom_call" | custom-call | flops 1 | bytes 1 | tf_op jit(solution)/shard_map/pallas_call | solution.py:593
  36.3 1.4 %shard_map.126 = (bf16[128,2048]{1,0:T(8,128)(2,1)S(1)}, bf16[128,512]{1,0:T(8,128)(2,1)S(1)}, bf16[128,512]{1,0:T(8,128)(2,1)S(1)}, bf16[128,512]{1,0:T(8,128)(2,1)S(1)}, bf16[128,512]{1,0:T(8,128)(2,1)S(1)}) custom-call(bf16[1024,256]{1,0:T(8,128)(2,1)S(1)} %get-tuple-element.82.dq, bf16[4096,1024]{1,0:T(8,128)(2,1)S(1)} %get-tuple-element.83.weight), custom_call_target="tpu_custom_call" | custom-call | flops 1 | bytes 1 | tf_op jit(solution)/shard_map/pallas_call | solution.py:363
  37.7 0.5 collective-permute-start.14
  38.2 0.1 collective-permute-start.15
  38.3 0.4 collective-permute-start.16
  38.7 0.1 collective-permute-start.17
  38.8 1.4 %shard_map.128 = (bf16[128,2048]{1,0:T(8,128)(2,1)S(1)}, bf16[128,2048]{1,0:T(8,128)(2,1)S(1)}) custom-call(bf16[1024,256]{1,0:T(8,128)(2,1)S(1)} %get-tuple-element.82.dq, bf16[4096,1024]{1,0:T(8,128)(2,1)S(1)} %get-tuple-element.83.weight), custom_call_target="tpu_custom_call" | custom-call | flops 1 | bytes 1 | tf_op jit(solution)/shard_map/pallas_call | solution.py:363
  40.2 0.1 shard_map.127
  40.3 1.3 %collective-permute-start.23 = (bf16[128,2048]{1,0:T(8,128)(2,1)S(1)}, bf16[128,2048]{1,0:T(8,128)(2,1)S(1)}, u32[]{:S(2)}, u32[]{:S(2)}) collective-permute-start(bf16[128,2048]{1,0:T(8,128)(2,1)S(1)} %shard_map.127), channel_id=1, source_target_pairs={{0,1},{1,0},{2,3},{3,2},{4,5},{5,4},{6,7},{7,6},{8,9},{9,8},{10,11... | collective-permute-start | bytes 1572872 | tf_op jit(solution)/shard_map/ppermute | solution.py:28
  41.6 0.7 %collective-permute-start.24 = (bf16[128,2048]{1,0:T(8,128)(2,1)S(1)}, bf16[128,2048]{1,0:T(8,128)(2,1)S(1)}, u32[]{:S(2)}, u32[]{:S(2)}) collective-permute-start(bf16[128,2048]{1,0:T(8,128)(2,1)S(1)} %get-tuple-element.99), channel_id=1, source_target_pairs={{0,2},{2,0},{4,6},{6,4},{8,10},{10,8},{12,14},{14,12},{16,18},{18,... | collective-permute-start | bytes 1572872 | tf_op jit(solution)/shard_map/ppermute | solution.py:28
  42.3 0.1 shard_map.129
  42.4 1.3 %collective-permute-start.19 = (bf16[256,256]{1,0:T(8,128)(2,1)S(1)}, bf16[256,256]{1,0:T(8,128)(2,1)S(1)}, u32[]{:S(2)}, u32[]{:S(2)}) collective-permute-start(bf16[256,256]{1,0:T(8,128)(2,1)S(1)} %get-tuple-element.92), channel_id=1, source_target_pairs={{0,16},{2,18},{4,20},{6,22},{8,24},{10,26},{12,28},{14,30},{16,0},... | collective-permute-start | bytes 393224 | tf_op jit(solution)/shard_map/ppermute | solution.py:27
  43.7 5.1 %collective-permute-start.20 = (bf16[256,256]{1,0:T(8,128)(2,1)S(1)}, bf16[256,256]{1,0:T(8,128)(2,1)S(1)}, u32[]{:S(2)}, u32[]{:S(2)}) collective-permute-start(bf16[256,256]{1,0:T(8,128)(2,1)S(1)} %get-tuple-element.93), channel_id=1, source_target_pairs={{0,24},{2,26},{4,28},{6,30},{8,0},{10,2},{12,4},{14,6},{16,8},{18,... | collective-permute-start | bytes 393224 | tf_op jit(solution)/shard_map/ppermute | solution.py:27
  48.8 0.1 collective-permute-start.21
  48.9 3.8 %collective-permute-done.20.refs_1_ = bf16[256,256]{1,0:T(8,128)(2,1)S(1)} collective-permute-done((bf16[256,256]{1,0:T(8,128)(2,1)S(1)}, bf16[256,256]{1,0:T(8,128)(2,1)S(1)}, u32[]{:S(2)}, u32[]{:S(2)}) %collective-permute-start.20) | collective-permute-done | bytes 131104 | tf_op jit(solution)/shard_map/ppermute | solution.py:27
  52.7 5.4 %collective-permute-done.21.back = bf16[256,256]{1,0:T(8,128)(2,1)S(1)} collective-permute-done((bf16[256,256]{1,0:T(8,128)(2,1)S(1)}, bf16[256,256]{1,0:T(8,128)(2,1)S(1)}, u32[]{:S(2)}, u32[]{:S(2)}) %collective-permute-start.21) | collective-permute-done | bytes 131104 | tf_op jit(solution)/shard_map/ppermute | solution.py:27
  58.1 0.7 %collective-permute-start.22 = (bf16[128,256]{1,0:T(8,128)(2,1)S(1)}, bf16[128,256]{1,0:T(8,128)(2,1)S(1)}, u32[]{:S(2)}, u32[]{:S(2)}) collective-permute-start(bf16[128,256]{1,0:T(8,128)(2,1)S(1)} %get-tuple-element.95), channel_id=1, source_target_pairs={{0,2},{2,0},{4,6},{6,4},{8,10},{10,8},{12,14},{14,12},{16,18},{18,... | collective-permute-start | bytes 196616 | tf_op jit(solution)/shard_map/ppermute | solution.py:28
  58.8 1.0 %shard_map.133 = bf16[128,2048]{1,0:T(8,128)(2,1)} custom-call(bf16[128,2048]{1,0:T(8,128)(2,1)S(1)} %get-tuple-element.96.refs_0_, bf16[128,2048]{1,0:T(8,128)(2,1)S(1)} %collective-permute-done.23.refs_1_, bf16[128,2048]{1,0:T(8,128)(2,1)S(1)} %collective-permute-done.24.refs_2_), custom_call_target="tpu_custom_call" | custom-call | flops 1 | bytes 1 | tf_op jit(solution)/shard_map/pallas_call | solution.py:401
  59.8 0.9 %shard_map.134 = (bf16[128,256]{1,0:T(8,128)(2,1)}, bf16[128,256]{1,0:T(8,128)(2,1)}) custom-call(f32[128,256]{1,0:T(8,128)S(1)} %get-tuple-element.101.keep, bf16[128,256]{1,0:T(8,128)(2,1)S(1)} %collective-permute-done.22.recv, bf16[128,256]{1,0:T(8,128)(2,1)S(1)} %copy-done, f32[1,128]{1,0:T(1,128)S(1)} %bitcast.7), custom_call_target="tpu_custom_call" | custom-call | tf_op jit(solution)/shard_map/pallas_call | solution.py:636
  (25 shorter events, 0.1 us)
Async XLA Ops:
  3.0 9.7 %collective-permute-start.2 = (bf16[128,2048]{1,0:T(8,128)(2,1)}, bf16[128,2048]{1,0:T(8,128)(2,1)S(1)}, u32[]{:S(2)}, u32[]{:S(2)}) collective-permute-start(bf16[128,2048]{1,0:T(8,128)(2,1)} %param.10), channel_id=1, source_target_pairs={{0,2},{2,0},{4,6},{6,4},{8,10},{10,8},{12,14},{14,12},{16,18},{18,... | collective-permute-start | bytes 1572872 | tf_op jit(solution)/shard_map/ppermute | solution.py:28
  3.7 9.7 %collective-permute-start.3 = (bf16[128,2048]{1,0:T(8,128)(2,1)}, bf16[128,2048]{1,0:T(8,128)(2,1)S(1)}, u32[]{:S(2)}, u32[]{:S(2)}) collective-permute-start(bf16[128,2048]{1,0:T(8,128)(2,1)} %param.13), channel_id=1, source_target_pairs={{0,2},{2,0},{4,6},{6,4},{8,10},{10,8},{12,14},{14,12},{16,18},{18,... | collective-permute-start | bytes 1572872 | tf_op jit(solution)/shard_map/ppermute | solution.py:28
  3.7 6.0 %collective-permute-start.4 = (f32[16,128]{1,0:T(8,128)}, f32[16,128]{1,0:T(8,128)S(1)}, u32[]{:S(2)}, u32[]{:S(2)}) collective-permute-start(f32[16,128]{1,0:T(8,128)} %get-tuple-element.57.facts), channel_id=1, source_target_pairs={{0,2},{2,0},{4,6},{6,4},{8,10},{10,8},{12,14},{14,12},{16,18},{18,... | collective-permute-start | bytes 24584 | tf_op jit(solution)/shard_map/ppermute | solution.py:28
  4.2 11.3 %collective-permute-start.1 = (bf16[272,256]{1,0:T(8,128)(2,1)}, bf16[272,256]{1,0:T(8,128)(2,1)S(1)}, u32[]{:S(2)}, u32[]{:S(2)}) collective-permute-start(bf16[272,256]{1,0:T(8,128)(2,1)} %get-tuple-element.54.message), channel_id=1, source_target_pairs={{0,8},{2,10},{4,12},{6,14},{8,16},{10,18},{12,20},{14,22},{16,24},... | collective-permute-start | bytes 417800 | tf_op jit(solution)/shard_map/ppermute | solution.py:27
  5.5 10.0 %collective-permute-start = (bf16[272,256]{1,0:T(8,128)(2,1)}, bf16[272,256]{1,0:T(8,128)(2,1)S(1)}, u32[]{:S(2)}, u32[]{:S(2)}) collective-permute-start(bf16[272,256]{1,0:T(8,128)(2,1)} %get-tuple-element.54.message), channel_id=1, source_target_pairs={{0,16},{2,18},{4,20},{6,22},{8,24},{10,26},{12,28},{14,30},{1,17},... | collective-permute-start | bytes 417800 | tf_op jit(solution)/shard_map/ppermute | solution.py:28
  9.8 8.2 %collective-permute-start.8 = (bf16[272,256]{1,0:T(8,128)(2,1)}, bf16[272,256]{1,0:T(8,128)(2,1)S(1)}, u32[]{:S(2)}, u32[]{:S(2)}) collective-permute-start(bf16[272,256]{1,0:T(8,128)(2,1)} %get-tuple-element.54.message), channel_id=1, source_target_pairs={{0,4},{2,6},{4,24},{6,26},{8,12},{10,14},{16,20},{18,22},{24,28},{... | collective-permute-start | bytes 417800 | tf_op jit(solution)/shard_map/ppermute | solution.py:28
  12.8 5.1 %collective-permute-start.5 = (bf16[272,256]{1,0:T(8,128)(2,1)}, bf16[272,256]{1,0:T(8,128)(2,1)S(1)}, u32[]{:S(2)}, u32[]{:S(2)}) collective-permute-start(bf16[272,256]{1,0:T(8,128)(2,1)} %get-tuple-element.54.message), channel_id=1, source_target_pairs={{0,2},{2,0},{4,6},{6,4},{8,10},{10,8},{12,14},{14,12},{16,18},{18,... | collective-permute-start | bytes 417800 | tf_op jit(solution)/shard_map/ppermute | solution.py:28
  13.4 0.9 %copy-start.1 = (bf16[272,256]{1,0:T(8,128)(2,1)S(1)}, bf16[272,256]{1,0:T(8,128)(2,1)}, u32[]{:S(2)}) copy-start(bf16[272,256]{1,0:T(8,128)(2,1)} %get-tuple-element.54.message) | copy-start | bytes 417796
  14.3 0.7 %copy-start.2 = (f32[16,128]{1,0:T(8,128)S(1)}, f32[16,128]{1,0:T(8,128)}, u32[]{:S(2)}) copy-start(f32[16,128]{1,0:T(8,128)} %get-tuple-element.57.facts) | copy-start | bytes 24580
  15.6 2.8 %collective-permute-start.6 = (bf16[272,256]{1,0:T(8,128)(2,1)S(1)}, bf16[272,256]{1,0:T(8,128)(2,1)S(1)}, u32[]{:S(2)}, u32[]{:S(2)}) collective-permute-start(bf16[272,256]{1,0:T(8,128)(2,1)S(1)} %collective-permute-done.1.refs_1_), channel_id=1, source_target_pairs={{0,2},{2,0},{4,6},{6,4},{8,10},{10,8},{12,14},{14,12},{16,18},{18,... | collective-permute-start | bytes 417800 | tf_op jit(solution)/shard_map/ppermute | solution.py:28
  15.7 2.7 %collective-permute-start.7 = (bf16[272,256]{1,0:T(8,128)(2,1)S(1)}, bf16[272,256]{1,0:T(8,128)(2,1)S(1)}, u32[]{:S(2)}, u32[]{:S(2)}) collective-permute-start(bf16[272,256]{1,0:T(8,128)(2,1)S(1)} %collective-permute-done.refs_2_), channel_id=1, source_target_pairs={{0,2},{2,0},{4,6},{6,4},{8,10},{10,8},{12,14},{14,12},{16,18},{18,... | collective-permute-start | bytes 417800 | tf_op jit(solution)/shard_map/ppermute | solution.py:28
  16.2 7.1 %collective-permute-start.10 = (bf16[272,256]{1,0:T(8,128)(2,1)S(1)}, bf16[272,256]{1,0:T(8,128)(2,1)S(1)}, u32[]{:S(2)}, u32[]{:S(2)}) collective-permute-start(bf16[272,256]{1,0:T(8,128)(2,1)S(1)} %collective-permute-done.refs_2_), channel_id=1, source_target_pairs={{0,4},{2,6},{4,0},{6,2},{8,12},{10,14},{12,8},{14,10},{16,20},{18,... | collective-permute-start | bytes 417800 | tf_op jit(solution)/shard_map/ppermute | solution.py:28
  17.9 6.9 %collective-permute-start.9 = (bf16[272,256]{1,0:T(8,128)(2,1)S(1)}, bf16[272,256]{1,0:T(8,128)(2,1)S(1)}, u32[]{:S(2)}, u32[]{:S(2)}) collective-permute-start(bf16[272,256]{1,0:T(8,128)(2,1)S(1)} %collective-permute-done.1.refs_1_), channel_id=1, source_target_pairs={{0,4},{2,6},{4,0},{6,2},{8,12},{10,14},{12,8},{14,10},{16,20},{18,... | collective-permute-start | bytes 417800 | tf_op jit(solution)/shard_map/ppermute | solution.py:28
  17.9 7.6 %collective-permute-start.11 = (bf16[272,256]{1,0:T(8,128)(2,1)S(1)}, bf16[272,256]{1,0:T(8,128)(2,1)S(1)}, u32[]{:S(2)}, u32[]{:S(2)}) collective-permute-start(bf16[272,256]{1,0:T(8,128)(2,1)S(1)} %collective-permute-done.8.refs_1_), channel_id=1, source_target_pairs={{0,2},{2,0},{4,6},{6,4},{8,10},{10,8},{12,14},{14,12},{16,18},{18,... | collective-permute-start | bytes 417800 | tf_op jit(solution)/shard_map/ppermute | solution.py:28
  24.8 1.7 %collective-permute-start.12 = (bf16[272,256]{1,0:T(8,128)(2,1)S(1)}, bf16[272,256]{1,0:T(8,128)(2,1)S(1)}, u32[]{:S(2)}, u32[]{:S(2)}) collective-permute-start(bf16[272,256]{1,0:T(8,128)(2,1)S(1)} %collective-permute-done.9.refs_2_), channel_id=1, source_target_pairs={{0,2},{2,0},{4,6},{6,4},{8,10},{10,8},{12,14},{14,12},{16,18},{18,... | collective-permute-start | bytes 417800 | tf_op jit(solution)/shard_map/ppermute | solution.py:28
  25.5 1.4 %collective-permute-start.13 = (bf16[272,256]{1,0:T(8,128)(2,1)S(1)}, bf16[272,256]{1,0:T(8,128)(2,1)S(1)}, u32[]{:S(2)}, u32[]{:S(2)}) collective-permute-start(bf16[272,256]{1,0:T(8,128)(2,1)S(1)} %collective-permute-done.10.refs_3_), channel_id=1, source_target_pairs={{0,2},{2,0},{4,6},{6,4},{8,10},{10,8},{12,14},{14,12},{16,18},{18,... | collective-permute-start | bytes 417800 | tf_op jit(solution)/shard_map/ppermute | solution.py:28
  32.0 8.3 %collective-permute-start.18 = (bf16[512,256]{1,0:T(8,128)(2,1)S(1)}, bf16[512,256]{1,0:T(8,128)(2,1)S(1)}, u32[]{:S(2)}, u32[]{:S(2)}) collective-permute-start(bf16[512,256]{1,0:T(8,128)(2,1)S(1)} %get-tuple-element.89), channel_id=1, source_target_pairs={{0,4},{2,6},{4,0},{6,2},{8,12},{10,14},{12,8},{14,10},{16,20},{18,... | collective-permute-start | bytes 786440 | tf_op jit(solution)/shard_map/ppermute | solution.py:28
  37.7 2.5 %collective-permute-start.14 = (bf16[128,512]{1,0:T(8,128)(2,1)S(1)}, bf16[128,512]{1,0:T(8,128)(2,1)S(1)}, u32[]{:S(2)}, u32[]{:S(2)}) collective-permute-start(bf16[128,512]{1,0:T(8,128)(2,1)S(1)} %get-tuple-element.85), channel_id=1, source_target_pairs={{0,2},{2,0},{4,6},{6,4},{8,10},{10,8},{12,14},{14,12},{16,18},{18,... | collective-permute-start | bytes 393224 | tf_op jit(solution)/shard_map/ppermute | solution.py:28
  38.2 2.0 %collective-permute-start.15 = (bf16[128,512]{1,0:T(8,128)(2,1)S(1)}, bf16[128,512]{1,0:T(8,128)(2,1)S(1)}, u32[]{:S(2)}, u32[]{:S(2)}) collective-permute-start(bf16[128,512]{1,0:T(8,128)(2,1)S(1)} %get-tuple-element.86), channel_id=1, source_target_pairs={{0,2},{2,0},{4,6},{6,4},{8,10},{10,8},{12,14},{14,12},{16,18},{18,... | collective-permute-start | bytes 393224 | tf_op jit(solution)/shard_map/ppermute | solution.py:28
  38.3 1.9 %collective-permute-start.16 = (bf16[128,512]{1,0:T(8,128)(2,1)S(1)}, bf16[128,512]{1,0:T(8,128)(2,1)S(1)}, u32[]{:S(2)}, u32[]{:S(2)}) collective-permute-start(bf16[128,512]{1,0:T(8,128)(2,1)S(1)} %get-tuple-element.87), channel_id=1, source_target_pairs={{0,2},{2,0},{4,6},{6,4},{8,10},{10,8},{12,14},{14,12},{16,18},{18,... | collective-permute-start | bytes 393224 | tf_op jit(solution)/shard_map/ppermute | solution.py:28
  38.7 21.1 %copy-start = (bf16[128,256]{1,0:T(8,128)(2,1)S(1)}, bf16[128,256]{1,0:T(8,128)(2,1)}, u32[]{:S(2)}) copy-start(bf16[128,256]{1,0:T(8,128)(2,1)} %key.3) | copy-start | bytes 196612
  38.7 21.1 %copy-start.3 = (f32[128]{0:T(128)S(1)}, f32[128]{0:T(128)}, u32[]{:S(2)}) copy-start(f32[128]{0:T(128)} %param.15) | copy-start | bytes 1540
  38.7 1.5 %collective-permute-start.17 = (bf16[128,512]{1,0:T(8,128)(2,1)S(1)}, bf16[128,512]{1,0:T(8,128)(2,1)S(1)}, u32[]{:S(2)}, u32[]{:S(2)}) collective-permute-start(bf16[128,512]{1,0:T(8,128)(2,1)S(1)} %get-tuple-element.88), channel_id=1, source_target_pairs={{0,2},{2,0},{4,6},{6,4},{8,10},{10,8},{12,14},{14,12},{16,18},{18,... | collective-permute-start | bytes 393224 | tf_op jit(solution)/shard_map/ppermute | solution.py:28
  40.3 18.5 %collective-permute-start.23 = (bf16[128,2048]{1,0:T(8,128)(2,1)S(1)}, bf16[128,2048]{1,0:T(8,128)(2,1)S(1)}, u32[]{:S(2)}, u32[]{:S(2)}) collective-permute-start(bf16[128,2048]{1,0:T(8,128)(2,1)S(1)} %shard_map.127), channel_id=1, source_target_pairs={{0,1},{1,0},{2,3},{3,2},{4,5},{5,4},{6,7},{7,6},{8,9},{9,8},{10,11... | collective-permute-start | bytes 1572872 | tf_op jit(solution)/shard_map/ppermute | solution.py:28
  41.6 17.2 %collective-permute-start.24 = (bf16[128,2048]{1,0:T(8,128)(2,1)S(1)}, bf16[128,2048]{1,0:T(8,128)(2,1)S(1)}, u32[]{:S(2)}, u32[]{:S(2)}) collective-permute-start(bf16[128,2048]{1,0:T(8,128)(2,1)S(1)} %get-tuple-element.99), channel_id=1, source_target_pairs={{0,2},{2,0},{4,6},{6,4},{8,10},{10,8},{12,14},{14,12},{16,18},{18,... | collective-permute-start | bytes 1572872 | tf_op jit(solution)/shard_map/ppermute | solution.py:28
  42.4 6.4 %collective-permute-start.19 = (bf16[256,256]{1,0:T(8,128)(2,1)S(1)}, bf16[256,256]{1,0:T(8,128)(2,1)S(1)}, u32[]{:S(2)}, u32[]{:S(2)}) collective-permute-start(bf16[256,256]{1,0:T(8,128)(2,1)S(1)} %get-tuple-element.92), channel_id=1, source_target_pairs={{0,16},{2,18},{4,20},{6,22},{8,24},{10,26},{12,28},{14,30},{16,0},... | collective-permute-start | bytes 393224 | tf_op jit(solution)/shard_map/ppermute | solution.py:27
  43.7 9.0 %collective-permute-start.20 = (bf16[256,256]{1,0:T(8,128)(2,1)S(1)}, bf16[256,256]{1,0:T(8,128)(2,1)S(1)}, u32[]{:S(2)}, u32[]{:S(2)}) collective-permute-start(bf16[256,256]{1,0:T(8,128)(2,1)S(1)} %get-tuple-element.93), channel_id=1, source_target_pairs={{0,24},{2,26},{4,28},{6,30},{8,0},{10,2},{12,4},{14,6},{16,8},{18,... | collective-permute-start | bytes 393224 | tf_op jit(solution)/shard_map/ppermute | solution.py:27
  48.8 9.3 %collective-permute-start.21 = (bf16[256,256]{1,0:T(8,128)(2,1)S(1)}, bf16[256,256]{1,0:T(8,128)(2,1)S(1)}, u32[]{:S(2)}, u32[]{:S(2)}) collective-permute-start(bf16[256,256]{1,0:T(8,128)(2,1)S(1)} %get-tuple-element.94), channel_id=1, source_target_pairs={{0,12},{2,14},{4,0},{6,2},{8,20},{10,22},{12,8},{14,10},{16,28},{1... | collective-permute-start | bytes 393224 | tf_op jit(solution)/shard_map/ppermute | solution.py:27
  58.1 1.7 %collective-permute-start.22 = (bf16[128,256]{1,0:T(8,128)(2,1)S(1)}, bf16[128,256]{1,0:T(8,128)(2,1)S(1)}, u32[]{:S(2)}, u32[]{:S(2)}) collective-permute-start(bf16[128,256]{1,0:T(8,128)(2,1)S(1)} %get-tuple-element.95), channel_id=1, source_target_pairs={{0,2},{2,0},{4,6},{6,4},{8,10},{10,8},{12,14},{14,12},{16,18},{18,... | collective-permute-start | bytes 196616 | tf_op jit(solution)/shard_map/ppermute | solution.py:28

commit v7 on v6

--- a/solution.py
+++ b/solution.py
@@ -512,8 +512,8 @@
         ],
         compiler_params=params(16),
     )(query_o, grad_o, facts, message, query_p, grad_p, facts_p)
-    far_d, far_b, *queries = lax.optimization_barrier((far_d, far_b, *queries))
     far_c = moved(far_b, "ctx", lambda i: i ^ 2)
+    far_d, *queries = lax.optimization_barrier((far_d, *queries))
     far_e = moved(far_d, "ctx", lambda i: i ^ 2)
     *queries, kept = queries
     q_hat, rows, raw_t, both = queries

time: 61 us -> 59.7 us (0.979)
  the two profiles are of different devices: /device:TPU:5 before, /device:TPU:9 now
where the time goes in v7:
time: 59.7 us; the launch traced here: 59.4 us
  starting transfers between devices  24.5 us (41%)
  Pallas kernels  20 us (34%)
  waiting for transfers between devices  10.8 us (18%)
  local copies, waits for them, and re-layouts  2.68 us (4%)
  between operations  1.48 us (2%)
    ppermute x21, starting transfers between devices, moved(): lax.ppermute(array, axis, [(i, t) for i, t in pairs if 0 <= t < size])  18.4 us
    ppermute x4, waiting for transfers between devices, moved(): return lax.ppermute(array, axis, [(i, t % size) for i, t in pairs])  9.44 us
    ppermute x4, starting transfers between devices, moved(): return lax.ppermute(array, axis, [(i, t % size) for i, t in pairs])  6.05 us
    pallas_call x1, Pallas kernels, local(): pl.pallas_call(functools.partial(far_kernel, kv_local, heads, n_near, n_f...  5.13 us
    pallas_call x1, Pallas kernels, local(): pl.pallas_call(functools.partial(near_kernel, kv_local, heads, n_near), i...  4.93 us
    pallas_call x1, Pallas kernels, local(): pl.pallas_call(functools.partial(last_kernel, heads, n_near, n_far), in_s...  2.77 us
    pallas_call x2, Pallas kernels, project(): pl.pallas_call(functools.partial(project_kernel, first), in_specs=[vmem()...  2.71 us
    pallas_call x1, Pallas kernels, local(): pl.pallas_call(functools.partial(message_kernel, kv_local), in_specs=[vme...  1.77 us
  transfers between devices with their start and end apart: 25, of which 4 were waited for; matrix products, arithmetic and copies ran while one was open for 2% of the time, Pallas kernels for 21%

profile of v7, /device:TPU:9, one launch (start us, length us, event | category | flops | bytes accessed | tf_op | source)
XLA Modules:
  0.0 59.4 jit_solution(8221272147132702014)
XLA Ops:
  1.3 1.8 %shard_map.121 = (bf16[272,256]{1,0:T(8,128)(2,1)}, f32[16,128]{1,0:T(8,128)}) custom-call(s32[1,1]{1,0:T(1,128)} %bitcast.5.docs, f32[1,16]{1,0:T(1,128)} %bitcast.8, bf16[128,256]{1,0:T(8,128)(2,1)} %key.3, bf16[128,256]{1,0:T(8,128)(2,1)} %value.1, f32[1,128]{1,0:T(1,128)} %bitcast.6, f32[1,128]{1,0:T(1,128)} %bitcast.9, s32[1,128]{1,0:T(1,128)} %bitcast.10), custom_call_target="tpu_custom_call" | custom-call | tf_op jit(solution)/shard_map/pallas_call | solution.py:473
  3.0 0.7 %collective-permute-start.1 = (bf16[128,2048]{1,0:T(8,128)(2,1)}, bf16[128,2048]{1,0:T(8,128)(2,1)S(1)}, u32[]{:S(2)}, u32[]{:S(2)}) collective-permute-start(bf16[128,2048]{1,0:T(8,128)(2,1)} %param.10), channel_id=1, source_target_pairs={{0,2},{2,0},{4,6},{6,4},{8,10},{10,8},{12,14},{14,12},{16,18},{18,... | collective-permute-start | bytes 1572872 | tf_op jit(solution)/shard_map/ppermute | solution.py:28
  3.7 0.0 collective-permute-start.2
  3.7 0.5 collective-permute-start.3
  4.2 1.3 %collective-permute-start.4 = (bf16[272,256]{1,0:T(8,128)(2,1)}, bf16[272,256]{1,0:T(8,128)(2,1)S(1)}, u32[]{:S(2)}, u32[]{:S(2)}) collective-permute-start(bf16[272,256]{1,0:T(8,128)(2,1)} %get-tuple-element.53.message), channel_id=1, source_target_pairs={{0,8},{2,10},{4,12},{6,14},{8,16},{10,18},{12,20},{14,22},{16,24},... | collective-permute-start | bytes 417800 | tf_op jit(solution)/shard_map/ppermute | solution.py:27
  5.5 2.9 %collective-permute-start = (bf16[272,256]{1,0:T(8,128)(2,1)}, bf16[272,256]{1,0:T(8,128)(2,1)S(1)}, u32[]{:S(2)}, u32[]{:S(2)}) collective-permute-start(bf16[272,256]{1,0:T(8,128)(2,1)} %get-tuple-element.53.message), channel_id=1, source_target_pairs={{0,16},{2,18},{4,20},{6,22},{8,24},{10,26},{12,28},{14,30},{1,17},... | collective-permute-start | bytes 417800 | tf_op jit(solution)/shard_map/ppermute | solution.py:28
  8.5 0.0 collective-permute-done.3.facts_p
  8.5 3.2 %collective-permute-start.8 = (bf16[272,256]{1,0:T(8,128)(2,1)}, bf16[272,256]{1,0:T(8,128)(2,1)S(1)}, u32[]{:S(2)}, u32[]{:S(2)}) collective-permute-start(bf16[272,256]{1,0:T(8,128)(2,1)} %get-tuple-element.53.message), channel_id=1, source_target_pairs={{0,4},{2,6},{4,24},{6,26},{8,12},{10,14},{16,20},{18,22},{24,28},{... | collective-permute-start | bytes 417800 | tf_op jit(solution)/shard_map/ppermute | solution.py:28
  11.6 1.1 %constant_dynamic-slice_fusion = (bf16[128,1024]{1,0:T(8,128)(2,1)S(1)}, bf16[128,1024]{1,0:T(8,128)(2,1)S(1)}) fusion(bf16[128,2048]{1,0:T(8,128)(2,1)} %param.13, s32[]{:T(128)S(6)} %select_n.12, bf16[128,2048]{1,0:T(8,128)(2,1)} %param.10), kind=kLoop, calls=%fused_computation | loop fusion | bytes 1048580 | tf_op jit(solution)/shard_map/dynamic_slice | solution.py:500
  12.7 0.8 %collective-permute-start.5 = (bf16[272,256]{1,0:T(8,128)(2,1)}, bf16[272,256]{1,0:T(8,128)(2,1)S(1)}, u32[]{:S(2)}, u32[]{:S(2)}) collective-permute-start(bf16[272,256]{1,0:T(8,128)(2,1)} %get-tuple-element.53.message), channel_id=1, source_target_pairs={{0,2},{2,0},{4,6},{6,4},{8,10},{10,8},{12,14},{14,12},{16,18},{18,... | collective-permute-start | bytes 417800 | tf_op jit(solution)/shard_map/ppermute | solution.py:28
  13.6 0.0 collective-permute-done.2.grad_p
  13.6 0.2 collective-permute-start.6
  13.7 0.9 %copy-done.1 = bf16[272,256]{1,0:T(8,128)(2,1)S(1)} copy-done((bf16[272,256]{1,0:T(8,128)(2,1)S(1)}, bf16[272,256]{1,0:T(8,128)(2,1)}, u32[]{:S(2)}) %copy-start.1) | copy-done | bytes 139288
  14.7 0.7 %copy-done.2 = f32[16,128]{1,0:T(8,128)S(1)} copy-done((f32[16,128]{1,0:T(8,128)S(1)}, f32[16,128]{1,0:T(8,128)}, u32[]{:S(2)}) %copy-start.2) | copy-done | bytes 8216
  15.3 0.5 shard_map.122
  15.9 0.0 collective-permute-done.refs_2_
  15.9 0.5 collective-permute-start.7
  16.4 0.0 collective-permute-done.8.refs_1_
  16.4 3.6 %collective-permute-start.10 = (bf16[272,256]{1,0:T(8,128)(2,1)S(1)}, bf16[272,256]{1,0:T(8,128)(2,1)S(1)}, u32[]{:S(2)}, u32[]{:S(2)}) collective-permute-start(bf16[272,256]{1,0:T(8,128)(2,1)S(1)} %collective-permute-done.refs_2_), channel_id=1, source_target_pairs={{0,4},{2,6},{4,0},{6,2},{8,12},{10,14},{12,8},{14,10},{16,20},{18,... | collective-permute-start | bytes 417800 | tf_op jit(solution)/shard_map/ppermute | solution.py:28
  20.0 0.0 collective-permute-done.5.refs_3_.refs_4_
  20.0 0.3 collective-permute-start.11
  20.3 0.2 collective-permute-start.12
  20.5 0.0 collective-permute-done.6.refs_4_
  20.5 0.0 collective-permute-done.7.refs_5_
  20.5 4.9 %shard_map.123 = (bf16[4096,1024]{1,0:T(8,128)(2,1)S(1)}, bf16[128,768]{1,0:T(8,128)(2,1)S(1)}, bf16[8,768,256]{2,1,0:T(8,128)(2,1)S(1)}, f32[8,768,256]{2,1,0:T(8,128)S(1)}, f32[8,16,256]{2,1,0:T(8,128)S(1)}) custom-call(bf16[272,256]{1,0:T(8,128)(2,1)S(1)} %get-tuple-element.66.refs_0_, bf16[272,256]{1,0:T(8,128)(2,1)S(1)} %collective-permute-done.4.refs_1_, ...), custom_call_target="tpu_custom_call" | custom-call | tf_op jit(solution)/shard_map/pallas_call | solution.py:526
  25.4 0.3 collective-permute-start.13
  25.8 1.1 %collective-permute-done.13.refs_7_ = bf16[272,256]{1,0:T(8,128)(2,1)S(1)} collective-permute-done((bf16[272,256]{1,0:T(8,128)(2,1)S(1)}, bf16[272,256]{1,0:T(8,128)(2,1)S(1)}, u32[]{:S(2)}, u32[]{:S(2)}) %collective-permute-start.13) | collective-permute-done | bytes 139296 | tf_op jit(solution)/shard_map/ppermute | solution.py:28
  26.9 5.1 %shard_map.124 = (bf16[128,768]{1,0:T(8,128)(2,1)S(1)}, bf16[8,768,256]{2,1,0:T(8,128)(2,1)S(1)}, bf16[8,1536,256]{2,1,0:T(8,128)(2,1)S(1)}, bf16[256,256]{1,0:T(8,128)(2,1)S(1)}, bf16[512,256]{1,0:T(8,128)(2,1)S(1)}) custom-call(bf16[272,256]{1,0:T(8,128)(2,1)S(1)} %get-tuple-element.66.refs_0_, ...), custom_call_target="tpu_custom_call", output_to_operand_aliasing={{1}: (11, {})} | custom-call | flops 1 | bytes 1 | tf_op jit(solution)/shard_map/pallas_call | solution.py:551
  32.0 0.5 collective-permute-start.18
  32.5 2.8 %shard_map.125 = (bf16[1024,256]{1,0:T(8,128)(2,1)S(1)}, f32[256,256]{1,0:T(8,128)S(1)}, bf16[256,256]{1,0:T(8,128)(2,1)S(1)}, bf16[256,256]{1,0:T(8,128)(2,1)S(1)}) custom-call(bf16[2048,128]{1,0:T(8,128)(2,1)S(1)} %get-tuple-element.62.refs_6_.refs_8_.refs_0_, bf16[2048,128]{1,0:T(8,128)(2,1)S(1)} %get-tuple-element.63.refs_7_.refs_9_.refs_1_, ...), custom_call_target="tpu_custom_call" | custom-call | flops 1 | bytes 1 | tf_op jit(solution)/shard_map/pallas_call | solution.py:593
  35.3 1.4 %shard_map.126 = (bf16[128,2048]{1,0:T(8,128)(2,1)S(1)}, bf16[128,512]{1,0:T(8,128)(2,1)S(1)}, bf16[128,512]{1,0:T(8,128)(2,1)S(1)}, bf16[128,512]{1,0:T(8,128)(2,1)S(1)}, bf16[128,512]{1,0:T(8,128)(2,1)S(1)}) custom-call(bf16[1024,256]{1,0:T(8,128)(2,1)S(1)} %get-tuple-element.80.dq, bf16[4096,1024]{1,0:T(8,128)(2,1)S(1)} %get-tuple-element.81.weight), custom_call_target="tpu_custom_call" | custom-call | flops 1 | bytes 1 | tf_op jit(solution)/shard_map/pallas_call | solution.py:363
  36.7 0.7 %collective-permute-start.14 = (bf16[128,512]{1,0:T(8,128)(2,1)S(1)}, bf16[128,512]{1,0:T(8,128)(2,1)S(1)}, u32[]{:S(2)}, u32[]{:S(2)}) collective-permute-start(bf16[128,512]{1,0:T(8,128)(2,1)S(1)} %get-tuple-element.83), channel_id=1, source_target_pairs={{0,2},{2,0},{4,6},{6,4},{8,10},{10,8},{12,14},{14,12},{16,18},{18,... | collective-permute-start | bytes 393224 | tf_op jit(solution)/shard_map/ppermute | solution.py:28
  37.4 0.1 collective-permute-start.15
  37.4 0.4 collective-permute-start.16
  37.9 0.1 collective-permute-start.17
  38.0 1.4 %shard_map.128 = (bf16[128,2048]{1,0:T(8,128)(2,1)S(1)}, bf16[128,2048]{1,0:T(8,128)(2,1)S(1)}) custom-call(bf16[1024,256]{1,0:T(8,128)(2,1)S(1)} %get-tuple-element.80.dq, bf16[4096,1024]{1,0:T(8,128)(2,1)S(1)} %get-tuple-element.81.weight), custom_call_target="tpu_custom_call" | custom-call | flops 1 | bytes 1 | tf_op jit(solution)/shard_map/pallas_call | solution.py:363
  39.4 0.1 shard_map.127
  39.5 0.2 collective-permute-done.18.turn
  39.7 1.2 %collective-permute-start.23 = (bf16[128,2048]{1,0:T(8,128)(2,1)S(1)}, bf16[128,2048]{1,0:T(8,128)(2,1)S(1)}, u32[]{:S(2)}, u32[]{:S(2)}) collective-permute-start(bf16[128,2048]{1,0:T(8,128)(2,1)S(1)} %shard_map.127), channel_id=1, source_target_pairs={{0,1},{1,0},{2,3},{3,2},{4,5},{5,4},{6,7},{7,6},{8,9},{9,8},{10,11... | collective-permute-start | bytes 1572872 | tf_op jit(solution)/shard_map/ppermute | solution.py:28
  40.9 1.4 %collective-permute-start.24 = (bf16[128,2048]{1,0:T(8,128)(2,1)S(1)}, bf16[128,2048]{1,0:T(8,128)(2,1)S(1)}, u32[]{:S(2)}, u32[]{:S(2)}) collective-permute-start(bf16[128,2048]{1,0:T(8,128)(2,1)S(1)} %get-tuple-element.97), channel_id=1, source_target_pairs={{0,2},{2,0},{4,6},{6,4},{8,10},{10,8},{12,14},{14,12},{16,18},{18,... | collective-permute-start | bytes 1572872 | tf_op jit(solution)/shard_map/ppermute | solution.py:28
  42.3 0.1 shard_map.129
  42.4 3.1 %collective-permute-start.19 = (bf16[256,256]{1,0:T(8,128)(2,1)S(1)}, bf16[256,256]{1,0:T(8,128)(2,1)S(1)}, u32[]{:S(2)}, u32[]{:S(2)}) collective-permute-start(bf16[256,256]{1,0:T(8,128)(2,1)S(1)} %get-tuple-element.90), channel_id=1, source_target_pairs={{0,16},{2,18},{4,20},{6,22},{8,24},{10,26},{12,28},{14,30},{16,0},... | collective-permute-start | bytes 393224 | tf_op jit(solution)/shard_map/ppermute | solution.py:27
  45.5 1.6 %collective-permute-start.21 = (bf16[256,256]{1,0:T(8,128)(2,1)S(1)}, bf16[256,256]{1,0:T(8,128)(2,1)S(1)}, u32[]{:S(2)}, u32[]{:S(2)}) collective-permute-start(bf16[256,256]{1,0:T(8,128)(2,1)S(1)} %get-tuple-element.92), channel_id=1, source_target_pairs={{0,12},{2,14},{4,0},{6,2},{8,20},{10,22},{12,8},{14,10},{16,28},{1... | collective-permute-start | bytes 393224 | tf_op jit(solution)/shard_map/ppermute | solution.py:27
  47.1 4.7 %collective-permute-done.19.refs_1_ = bf16[256,256]{1,0:T(8,128)(2,1)S(1)} collective-permute-done((bf16[256,256]{1,0:T(8,128)(2,1)S(1)}, bf16[256,256]{1,0:T(8,128)(2,1)S(1)}, u32[]{:S(2)}, u32[]{:S(2)}) %collective-permute-start.19) | collective-permute-done | bytes 131104 | tf_op jit(solution)/shard_map/ppermute | solution.py:27
  51.8 4.7 %collective-permute-done.20.refs_1_ = bf16[256,256]{1,0:T(8,128)(2,1)S(1)} collective-permute-done((bf16[256,256]{1,0:T(8,128)(2,1)S(1)}, bf16[256,256]{1,0:T(8,128)(2,1)S(1)}, u32[]{:S(2)}, u32[]{:S(2)}) %collective-permute-start.20) | collective-permute-done | bytes 131104 | tf_op jit(solution)/shard_map/ppermute | solution.py:27
  56.6 0.8 %collective-permute-start.22 = (bf16[128,256]{1,0:T(8,128)(2,1)S(1)}, bf16[128,256]{1,0:T(8,128)(2,1)S(1)}, u32[]{:S(2)}, u32[]{:S(2)}) collective-permute-start(bf16[128,256]{1,0:T(8,128)(2,1)S(1)} %get-tuple-element.93), channel_id=1, source_target_pairs={{0,2},{2,0},{4,6},{6,4},{8,10},{10,8},{12,14},{14,12},{16,18},{18,... | collective-permute-start | bytes 196616 | tf_op jit(solution)/shard_map/ppermute | solution.py:28
  57.5 1.0 %shard_map.133 = bf16[128,2048]{1,0:T(8,128)(2,1)} custom-call(bf16[128,2048]{1,0:T(8,128)(2,1)S(1)} %get-tuple-element.94.refs_0_, bf16[128,2048]{1,0:T(8,128)(2,1)S(1)} %collective-permute-done.23.refs_1_, bf16[128,2048]{1,0:T(8,128)(2,1)S(1)} %collective-permute-done.24.refs_2_), custom_call_target="tpu_custom_call" | custom-call | flops 1 | bytes 1 | tf_op jit(solution)/shard_map/pallas_call | solution.py:401
  58.5 0.9 %shard_map.134 = (bf16[128,256]{1,0:T(8,128)(2,1)}, bf16[128,256]{1,0:T(8,128)(2,1)}) custom-call(f32[128,256]{1,0:T(8,128)S(1)} %get-tuple-element.99.keep, bf16[128,256]{1,0:T(8,128)(2,1)S(1)} %collective-permute-done.22.recv, bf16[128,256]{1,0:T(8,128)(2,1)S(1)} %copy-done, f32[1,128]{1,0:T(1,128)S(1)} %bitcast.7), custom_call_target="tpu_custom_call" | custom-call | tf_op jit(solution)/shard_map/pallas_call | solution.py:636
  (25 shorter events, 0.1 us)
Async XLA Ops:
  3.0 10.5 %collective-permute-start.1 = (bf16[128,2048]{1,0:T(8,128)(2,1)}, bf16[128,2048]{1,0:T(8,128)(2,1)S(1)}, u32[]{:S(2)}, u32[]{:S(2)}) collective-permute-start(bf16[128,2048]{1,0:T(8,128)(2,1)} %param.10), channel_id=1, source_target_pairs={{0,2},{2,0},{4,6},{6,4},{8,10},{10,8},{12,14},{14,12},{16,18},{18,... | collective-permute-start | bytes 1572872 | tf_op jit(solution)/shard_map/ppermute | solution.py:28
  3.7 9.9 %collective-permute-start.2 = (bf16[128,2048]{1,0:T(8,128)(2,1)}, bf16[128,2048]{1,0:T(8,128)(2,1)S(1)}, u32[]{:S(2)}, u32[]{:S(2)}) collective-permute-start(bf16[128,2048]{1,0:T(8,128)(2,1)} %param.13), channel_id=1, source_target_pairs={{0,2},{2,0},{4,6},{6,4},{8,10},{10,8},{12,14},{14,12},{16,18},{18,... | collective-permute-start | bytes 1572872 | tf_op jit(solution)/shard_map/ppermute | solution.py:28
  3.7 4.7 %collective-permute-start.3 = (f32[16,128]{1,0:T(8,128)}, f32[16,128]{1,0:T(8,128)S(1)}, u32[]{:S(2)}, u32[]{:S(2)}) collective-permute-start(f32[16,128]{1,0:T(8,128)} %get-tuple-element.56.facts), channel_id=1, source_target_pairs={{0,2},{2,0},{4,6},{6,4},{8,10},{10,8},{12,14},{14,12},{16,18},{18,... | collective-permute-start | bytes 24584 | tf_op jit(solution)/shard_map/ppermute | solution.py:28
  4.2 8.5 %collective-permute-start.4 = (bf16[272,256]{1,0:T(8,128)(2,1)}, bf16[272,256]{1,0:T(8,128)(2,1)S(1)}, u32[]{:S(2)}, u32[]{:S(2)}) collective-permute-start(bf16[272,256]{1,0:T(8,128)(2,1)} %get-tuple-element.53.message), channel_id=1, source_target_pairs={{0,8},{2,10},{4,12},{6,14},{8,16},{10,18},{12,20},{14,22},{16,24},... | collective-permute-start | bytes 417800 | tf_op jit(solution)/shard_map/ppermute | solution.py:27
  5.5 10.4 %collective-permute-start = (bf16[272,256]{1,0:T(8,128)(2,1)}, bf16[272,256]{1,0:T(8,128)(2,1)S(1)}, u32[]{:S(2)}, u32[]{:S(2)}) collective-permute-start(bf16[272,256]{1,0:T(8,128)(2,1)} %get-tuple-element.53.message), channel_id=1, source_target_pairs={{0,16},{2,18},{4,20},{6,22},{8,24},{10,26},{12,28},{14,30},{1,17},... | collective-permute-start | bytes 417800 | tf_op jit(solution)/shard_map/ppermute | solution.py:28
  8.5 7.9 %collective-permute-start.8 = (bf16[272,256]{1,0:T(8,128)(2,1)}, bf16[272,256]{1,0:T(8,128)(2,1)S(1)}, u32[]{:S(2)}, u32[]{:S(2)}) collective-permute-start(bf16[272,256]{1,0:T(8,128)(2,1)} %get-tuple-element.53.message), channel_id=1, source_target_pairs={{0,4},{2,6},{4,24},{6,26},{8,12},{10,14},{16,20},{18,22},{24,28},{... | collective-permute-start | bytes 417800 | tf_op jit(solution)/shard_map/ppermute | solution.py:28
  12.7 7.3 %collective-permute-start.5 = (bf16[272,256]{1,0:T(8,128)(2,1)}, bf16[272,256]{1,0:T(8,128)(2,1)S(1)}, u32[]{:S(2)}, u32[]{:S(2)}) collective-permute-start(bf16[272,256]{1,0:T(8,128)(2,1)} %get-tuple-element.53.message), channel_id=1, source_target_pairs={{0,2},{2,0},{4,6},{6,4},{8,10},{10,8},{12,14},{14,12},{16,18},{18,... | collective-permute-start | bytes 417800 | tf_op jit(solution)/shard_map/ppermute | solution.py:28
  13.6 6.7 %collective-permute-start.9 = (bf16[272,256]{1,0:T(8,128)(2,1)S(1)}, bf16[272,256]{1,0:T(8,128)(2,1)S(1)}, u32[]{:S(2)}, u32[]{:S(2)}) collective-permute-start(bf16[272,256]{1,0:T(8,128)(2,1)S(1)} %collective-permute-done.4.refs_1_), channel_id=1, source_target_pairs={{0,4},{2,6},{4,0},{6,2},{8,12},{10,14},{12,8},{14,10},{16,20},{18,... | collective-permute-start | bytes 417800 | tf_op jit(solution)/shard_map/ppermute | solution.py:28
  13.6 6.9 %collective-permute-start.6 = (bf16[272,256]{1,0:T(8,128)(2,1)S(1)}, bf16[272,256]{1,0:T(8,128)(2,1)S(1)}, u32[]{:S(2)}, u32[]{:S(2)}) collective-permute-start(bf16[272,256]{1,0:T(8,128)(2,1)S(1)} %collective-permute-done.4.refs_1_), channel_id=1, source_target_pairs={{0,2},{2,0},{4,6},{6,4},{8,10},{10,8},{12,14},{14,12},{16,18},{18,... | collective-permute-start | bytes 417800 | tf_op jit(solution)/shard_map/ppermute | solution.py:28
  13.7 0.9 %copy-start.1 = (bf16[272,256]{1,0:T(8,128)(2,1)S(1)}, bf16[272,256]{1,0:T(8,128)(2,1)}, u32[]{:S(2)}) copy-start(bf16[272,256]{1,0:T(8,128)(2,1)} %get-tuple-element.53.message) | copy-start | bytes 417796
  14.7 0.7 %copy-start.2 = (f32[16,128]{1,0:T(8,128)S(1)}, f32[16,128]{1,0:T(8,128)}, u32[]{:S(2)}) copy-start(f32[16,128]{1,0:T(8,128)} %get-tuple-element.56.facts) | copy-start | bytes 24580
  15.9 4.6 %collective-permute-start.7 = (bf16[272,256]{1,0:T(8,128)(2,1)S(1)}, bf16[272,256]{1,0:T(8,128)(2,1)S(1)}, u32[]{:S(2)}, u32[]{:S(2)}) collective-permute-start(bf16[272,256]{1,0:T(8,128)(2,1)S(1)} %collective-permute-done.refs_2_), channel_id=1, source_target_pairs={{0,2},{2,0},{4,6},{6,4},{8,10},{10,8},{12,14},{14,12},{16,18},{18,... | collective-permute-start | bytes 417800 | tf_op jit(solution)/shard_map/ppermute | solution.py:28
  16.4 9.1 %collective-permute-start.10 = (bf16[272,256]{1,0:T(8,128)(2,1)S(1)}, bf16[272,256]{1,0:T(8,128)(2,1)S(1)}, u32[]{:S(2)}, u32[]{:S(2)}) collective-permute-start(bf16[272,256]{1,0:T(8,128)(2,1)S(1)} %collective-permute-done.refs_2_), channel_id=1, source_target_pairs={{0,4},{2,6},{4,0},{6,2},{8,12},{10,14},{12,8},{14,10},{16,20},{18,... | collective-permute-start | bytes 417800 | tf_op jit(solution)/shard_map/ppermute | solution.py:28
  20.0 5.8 %collective-permute-start.11 = (bf16[272,256]{1,0:T(8,128)(2,1)S(1)}, bf16[272,256]{1,0:T(8,128)(2,1)S(1)}, u32[]{:S(2)}, u32[]{:S(2)}) collective-permute-start(bf16[272,256]{1,0:T(8,128)(2,1)S(1)} %collective-permute-done.8.refs_1_), channel_id=1, source_target_pairs={{0,2},{2,0},{4,6},{6,4},{8,10},{10,8},{12,14},{14,12},{16,18},{18,... | collective-permute-start | bytes 417800 | tf_op jit(solution)/shard_map/ppermute | solution.py:28
  20.3 5.5 %collective-permute-start.12 = (bf16[272,256]{1,0:T(8,128)(2,1)S(1)}, bf16[272,256]{1,0:T(8,128)(2,1)S(1)}, u32[]{:S(2)}, u32[]{:S(2)}) collective-permute-start(bf16[272,256]{1,0:T(8,128)(2,1)S(1)} %collective-permute-done.9.refs_2_), channel_id=1, source_target_pairs={{0,2},{2,0},{4,6},{6,4},{8,10},{10,8},{12,14},{14,12},{16,18},{18,... | collective-permute-start | bytes 417800 | tf_op jit(solution)/shard_map/ppermute | solution.py:28
  25.4 1.4 %collective-permute-start.13 = (bf16[272,256]{1,0:T(8,128)(2,1)S(1)}, bf16[272,256]{1,0:T(8,128)(2,1)S(1)}, u32[]{:S(2)}, u32[]{:S(2)}) collective-permute-start(bf16[272,256]{1,0:T(8,128)(2,1)S(1)} %collective-permute-done.10.refs_3_), channel_id=1, source_target_pairs={{0,2},{2,0},{4,6},{6,4},{8,10},{10,8},{12,14},{14,12},{16,18},{18,... | collective-permute-start | bytes 417800 | tf_op jit(solution)/shard_map/ppermute | solution.py:28
  32.0 7.7 %collective-permute-start.18 = (bf16[512,256]{1,0:T(8,128)(2,1)S(1)}, bf16[512,256]{1,0:T(8,128)(2,1)S(1)}, u32[]{:S(2)}, u32[]{:S(2)}) collective-permute-start(bf16[512,256]{1,0:T(8,128)(2,1)S(1)} %get-tuple-element.87), channel_id=1, source_target_pairs={{0,4},{2,6},{4,0},{6,2},{8,12},{10,14},{12,8},{14,10},{16,20},{18,... | collective-permute-start | bytes 786440 | tf_op jit(solution)/shard_map/ppermute | solution.py:28
  36.7 2.6 %collective-permute-start.14 = (bf16[128,512]{1,0:T(8,128)(2,1)S(1)}, bf16[128,512]{1,0:T(8,128)(2,1)S(1)}, u32[]{:S(2)}, u32[]{:S(2)}) collective-permute-start(bf16[128,512]{1,0:T(8,128)(2,1)S(1)} %get-tuple-element.83), channel_id=1, source_target_pairs={{0,2},{2,0},{4,6},{6,4},{8,10},{10,8},{12,14},{14,12},{16,18},{18,... | collective-permute-start | bytes 393224 | tf_op jit(solution)/shard_map/ppermute | solution.py:28
  37.4 2.0 %collective-permute-start.15 = (bf16[128,512]{1,0:T(8,128)(2,1)S(1)}, bf16[128,512]{1,0:T(8,128)(2,1)S(1)}, u32[]{:S(2)}, u32[]{:S(2)}) collective-permute-start(bf16[128,512]{1,0:T(8,128)(2,1)S(1)} %get-tuple-element.84), channel_id=1, source_target_pairs={{0,2},{2,0},{4,6},{6,4},{8,10},{10,8},{12,14},{14,12},{16,18},{18,... | collective-permute-start | bytes 393224 | tf_op jit(solution)/shard_map/ppermute | solution.py:28
  37.4 1.9 %collective-permute-start.16 = (bf16[128,512]{1,0:T(8,128)(2,1)S(1)}, bf16[128,512]{1,0:T(8,128)(2,1)S(1)}, u32[]{:S(2)}, u32[]{:S(2)}) collective-permute-start(bf16[128,512]{1,0:T(8,128)(2,1)S(1)} %get-tuple-element.85), channel_id=1, source_target_pairs={{0,2},{2,0},{4,6},{6,4},{8,10},{10,8},{12,14},{14,12},{16,18},{18,... | collective-permute-start | bytes 393224 | tf_op jit(solution)/shard_map/ppermute | solution.py:28
  37.9 20.6 %copy-start = (bf16[128,256]{1,0:T(8,128)(2,1)S(1)}, bf16[128,256]{1,0:T(8,128)(2,1)}, u32[]{:S(2)}) copy-start(bf16[128,256]{1,0:T(8,128)(2,1)} %key.3) | copy-start | bytes 196612
  37.9 20.6 %copy-start.3 = (f32[128]{0:T(128)S(1)}, f32[128]{0:T(128)}, u32[]{:S(2)}) copy-start(f32[128]{0:T(128)} %param.15) | copy-start | bytes 1540
  37.9 1.5 %collective-permute-start.17 = (bf16[128,512]{1,0:T(8,128)(2,1)S(1)}, bf16[128,512]{1,0:T(8,128)(2,1)S(1)}, u32[]{:S(2)}, u32[]{:S(2)}) collective-permute-start(bf16[128,512]{1,0:T(8,128)(2,1)S(1)} %get-tuple-element.86), channel_id=1, source_target_pairs={{0,2},{2,0},{4,6},{6,4},{8,10},{10,8},{12,14},{14,12},{16,18},{18,... | collective-permute-start | bytes 393224 | tf_op jit(solution)/shard_map/ppermute | solution.py:28
  39.7 17.8 %collective-permute-start.23 = (bf16[128,2048]{1,0:T(8,128)(2,1)S(1)}, bf16[128,2048]{1,0:T(8,128)(2,1)S(1)}, u32[]{:S(2)}, u32[]{:S(2)}) collective-permute-start(bf16[128,2048]{1,0:T(8,128)(2,1)S(1)} %shard_map.127), channel_id=1, source_target_pairs={{0,1},{1,0},{2,3},{3,2},{4,5},{5,4},{6,7},{7,6},{8,9},{9,8},{10,11... | collective-permute-start | bytes 1572872 | tf_op jit(solution)/shard_map/ppermute | solution.py:28
  40.9 16.6 %collective-permute-start.24 = (bf16[128,2048]{1,0:T(8,128)(2,1)S(1)}, bf16[128,2048]{1,0:T(8,128)(2,1)S(1)}, u32[]{:S(2)}, u32[]{:S(2)}) collective-permute-start(bf16[128,2048]{1,0:T(8,128)(2,1)S(1)} %get-tuple-element.97), channel_id=1, source_target_pairs={{0,2},{2,0},{4,6},{6,4},{8,10},{10,8},{12,14},{14,12},{16,18},{18,... | collective-permute-start | bytes 1572872 | tf_op jit(solution)/shard_map/ppermute | solution.py:28
  42.4 9.5 %collective-permute-start.19 = (bf16[256,256]{1,0:T(8,128)(2,1)S(1)}, bf16[256,256]{1,0:T(8,128)(2,1)S(1)}, u32[]{:S(2)}, u32[]{:S(2)}) collective-permute-start(bf16[256,256]{1,0:T(8,128)(2,1)S(1)} %get-tuple-element.90), channel_id=1, source_target_pairs={{0,16},{2,18},{4,20},{6,22},{8,24},{10,26},{12,28},{14,30},{16,0},... | collective-permute-start | bytes 393224 | tf_op jit(solution)/shard_map/ppermute | solution.py:27
  45.5 11.1 %collective-permute-start.20 = (bf16[256,256]{1,0:T(8,128)(2,1)S(1)}, bf16[256,256]{1,0:T(8,128)(2,1)S(1)}, u32[]{:S(2)}, u32[]{:S(2)}) collective-permute-start(bf16[256,256]{1,0:T(8,128)(2,1)S(1)} %get-tuple-element.91), channel_id=1, source_target_pairs={{0,24},{2,26},{4,28},{6,30},{8,0},{10,2},{12,4},{14,6},{16,8},{18,... | collective-permute-start | bytes 393224 | tf_op jit(solution)/shard_map/ppermute | solution.py:27
  45.5 11.1 %collective-permute-start.21 = (bf16[256,256]{1,0:T(8,128)(2,1)S(1)}, bf16[256,256]{1,0:T(8,128)(2,1)S(1)}, u32[]{:S(2)}, u32[]{:S(2)}) collective-permute-start(bf16[256,256]{1,0:T(8,128)(2,1)S(1)} %get-tuple-element.92), channel_id=1, source_target_pairs={{0,12},{2,14},{4,0},{6,2},{8,20},{10,22},{12,8},{14,10},{16,28},{1... | collective-permute-start | bytes 393224 | tf_op jit(solution)/shard_map/ppermute | solution.py:27
  56.6 1.8 %collective-permute-start.22 = (bf16[128,256]{1,0:T(8,128)(2,1)S(1)}, bf16[128,256]{1,0:T(8,128)(2,1)S(1)}, u32[]{:S(2)}, u32[]{:S(2)}) collective-permute-start(bf16[128,256]{1,0:T(8,128)(2,1)S(1)} %get-tuple-element.93), channel_id=1, source_target_pairs={{0,2},{2,0},{4,6},{6,4},{8,10},{10,8},{12,14},{14,12},{16,18},{18,... | collective-permute-start | bytes 196616 | tf_op jit(solution)/shard_map/ppermute | solution.py:28

commit v8 on v7

--- a/solution.py
+++ b/solution.py
@@ -69,16 +69,16 @@
     facts[8:, :] = jnp.broadcast_to(found, (8, HD))
 
 
-def fetch(weight, held, sems, heads):
+def fetch(weight, held, sems, heads, first):
     n_head = lax.axis_size("head")
     width = weight.shape[0] // n_head
     core = lax.rem(lax.axis_index("ctx"), 2)
     features = pl.ds(pl.multiple_of(core * heads * HD, HD), heads * HD)
-    pieces = sems.shape[0] // n_head
+    pieces = sems.shape[0] * width // held.shape[0]
     part = width // pieces
     copies = []
     for i in range(sems.shape[0]):
-        owner = lax.rem(lax.axis_index("head") + i // pieces, n_head)
+        owner = lax.rem(lax.axis_index("head") + first + i // pieces, n_head)
         at = pl.multiple_of(owner * width + (i % pieces) * part, part)
         copies.append(
             pltpu.make_async_copy(
@@ -160,7 +160,7 @@
     held, keys_t, expo, dots, sums, keys, values, docs, raw, sems = refs[2 * n_near + 3 :]
     core = lax.rem(lax.axis_index("ctx"), 2)
 
-    copies = fetch(weight, held, sems, heads)
+    copies = fetch(weight, held, sems, heads, 1)
     blocks = 2 * n_near
     for index in range(n_near):
         first = blocks - 2 - 2 * index
@@ -301,9 +301,10 @@
 
 
 def last_kernel(heads, n_near, n_far, *refs):
-    q_hat, rows, raw_t, facts, near_t, far_t, pw_near, ds = refs[:8]
-    dq, *parts = refs[8 : 9 + n_near]
-    dk, dv = refs[9 + n_near :]
+    q_hat, rows, raw_t, facts, near_t, far_t, pw_near, ds, weight = refs[:9]
+    dq, held, *parts = refs[9 : 11 + n_near]
+    dk, dv, sems = refs[11 + n_near :]
+    copies = fetch(weight, held, sems, heads, 0)
     core = lax.rem(lax.axis_index("ctx"), 2)
     wide = 2 * BLOCK
     far_rows = 2 * n_far * BLOCK
@@ -338,6 +339,8 @@
             ].astype(BF16)
     firsts = [2 * n_near - 2 - 2 * index for index in range(n_near)]
     hand_out(core, firsts, parts, dk, dv)
+    for copy in copies:
+        copy.wait()
 
 
 def project_kernel(first, dq, weight, keep, *sends):
@@ -528,7 +531,7 @@
         in_specs=[vmem()] * (2 * n_near + 2) + [hbm()],
         out_specs=[vmem()] * 5,
         out_shape=[
-            shape((query_weight.shape[0], half), BF16),
+            shape((query_weight.shape[0] - width, half), BF16),
             shape((HD, near_rows), BF16),
             shape((steps, near_rows, span), BF16),
             shape((steps, near_rows, span), F32),
@@ -539,9 +542,9 @@
             pltpu.VMEM((near_rows, HD), BF16),
             pltpu.VMEM((2 * n_near, 8, 2 * HD), F32),
             pltpu.VMEM((2, near_rows, span), F32),
-            pltpu.SemaphoreType.DMA((2 * n_head,)),
+            pltpu.SemaphoreType.DMA((2 * (n_head - 1),)),
         ],
-        compiler_params=params(20),
+        compiler_params=params(34),
     )(*near, *near_shared, q_hat, rows, query_weight)
 
     far_e, sums = lax.optimization_barrier((far_e, sums))
@@ -590,20 +593,25 @@
     )
     turn = moved(part_ce, "ctx", lambda i: i ^ 2)
 
-    dq, part_own, part_b, part_d = pl.pallas_call(
+    dq, mine_weight, part_own, part_b, part_d = pl.pallas_call(
         functools.partial(last_kernel, heads, n_near, n_far),
-        in_specs=[vmem()] * 8,
-        out_specs=[vmem()] * 4,
-        out_shape=[shape((half, 2 * tokens), BF16), shape((span, 2 * HD), F32)] + [part_shape] * 2,
-        scratch_shapes=[pltpu.VMEM((near_rows, HD), F32)] * 2,
-        compiler_params=params(20),
+        in_specs=[vmem()] * 8 + [hbm()],
+        out_specs=[vmem()] * 5,
+        out_shape=[
+            shape((half, 2 * tokens), BF16),
+            shape((width, half), BF16),
+            shape((span, 2 * HD), F32),
+        ]
+        + [part_shape] * 2,
+        scratch_shapes=[pltpu.VMEM((near_rows, HD), F32)] * 2 + [pltpu.SemaphoreType.DMA((2,))],
+        compiler_params=params(32),
         cost_estimate=SMALL,
-    )(q_hat, rows, raw_t, both, near_t, far_t, pw_near, ds)
-
-    mine, mine_send = project(dq, weight, 0, width, 1)
+    )(q_hat, rows, raw_t, both, near_t, far_t, pw_near, ds, query_weight)
+
+    mine, mine_send = project(dq, mine_weight, 0, width, 1)
     arrived = []
     for shift in range(1, n_head):
-        keep, *sends = project(dq, weight, shift * width, width, 4)
+        keep, *sends = project(dq, weight, (shift - 1) * width, width, 4)
         term = add_pieces(keep, [moved(send, "ctx", partner) for send in sends])
         term, turn, mine_send = lax.optimization_barrier((term, turn, mine_send))
         arrived.append(moved(term, "head", lambda i, s=shift: (i + s) % n_head))

time: 59.7 us -> 60.3 us (1.010)
  Pallas kernels: 20 us -> 21 us
    pallas_call x1, Pallas kernels: 2.77 us -> 4.83 us  [local(): pl.pallas_call(functools.partial(last_kernel, heads, n_near, n_far), in_s...]
    pallas_call x1, Pallas kernels: 4.93 us -> 3.93 us  [local(): pl.pallas_call(functools.partial(near_kernel, kv_local, heads, n_near), i...]
  transfers between devices with their start and end apart: 25 -> 25, of which waited for: 4 -> 3; matrix products, arithmetic and copies ran while one was open for 2% -> 2% of each run, Pallas kernels for 21% -> 22%
where the time goes in v8:
time: 60.3 us; the launch traced here: 60 us
  starting transfers between devices  24.4 us (40%)
  Pallas kernels  21 us (35%)
  waiting for transfers between devices  10.4 us (17%)
  local copies, waits for them, and re-layouts  2.68 us (4%)
  between operations  1.49 us (2%)
    ppermute x21, starting transfers between devices, moved(): lax.ppermute(array, axis, [(i, t) for i, t in pairs if 0 <= t < size])  18.6 us
    ppermute x4, waiting for transfers between devices, moved(): return lax.ppermute(array, axis, [(i, t % size) for i, t in pairs])  9.26 us
    ppermute x4, starting transfers between devices, moved(): return lax.ppermute(array, axis, [(i, t % size) for i, t in pairs])  5.81 us
    pallas_call x1, Pallas kernels, local(): pl.pallas_call(functools.partial(far_kernel, kv_local, heads, n_near, n_f...  5.1 us
    pallas_call x1, Pallas kernels, local(): pl.pallas_call(functools.partial(last_kernel, heads, n_near, n_far), in_s...  4.83 us
    pallas_call x1, Pallas kernels, local(): pl.pallas_call(functools.partial(near_kernel, kv_local, heads, n_near), i...  3.93 us
    pallas_call x2, Pallas kernels, project(): pl.pallas_call(functools.partial(project_kernel, first), in_specs=[vmem()...  2.73 us
    pallas_call x1, Pallas kernels, local(): pl.pallas_call(functools.partial(message_kernel, kv_local), in_specs=[vme...  1.77 us
  transfers between devices with their start and end apart: 25, of which 3 were waited for; matrix products, arithmetic and copies ran while one was open for 2% of the time, Pallas kernels for 22%

profile of v8, /device:TPU:9, one launch (start us, length us, event | category | flops | bytes accessed | tf_op | source)
XLA Modules:
  0.0 60.0 jit_solution(16062731158481571641)
XLA Ops:
  1.3 1.8 %shard_map.121 = (bf16[272,256]{1,0:T(8,128)(2,1)}, f32[16,128]{1,0:T(8,128)}) custom-call(s32[1,1]{1,0:T(1,128)} %bitcast.5.docs, f32[1,16]{1,0:T(1,128)} %bitcast.8, bf16[128,256]{1,0:T(8,128)(2,1)} %key.3, bf16[128,256]{1,0:T(8,128)(2,1)} %value.1, f32[1,128]{1,0:T(1,128)} %bitcast.6, f32[1,128]{1,0:T(1,128)} %bitcast.9, s32[1,128]{1,0:T(1,128)} %bitcast.10), custom_call_target="tpu_custom_call" | custom-call | tf_op jit(solution)/shard_map/pallas_call | solution.py:476
  3.0 0.7 %collective-permute-start.1 = (bf16[128,2048]{1,0:T(8,128)(2,1)}, bf16[128,2048]{1,0:T(8,128)(2,1)S(1)}, u32[]{:S(2)}, u32[]{:S(2)}) collective-permute-start(bf16[128,2048]{1,0:T(8,128)(2,1)} %param.10), channel_id=1, source_target_pairs={{0,2},{2,0},{4,6},{6,4},{8,10},{10,8},{12,14},{14,12},{16,18},{18,... | collective-permute-start | bytes 1572872 | tf_op jit(solution)/shard_map/ppermute | solution.py:28
  3.7 0.0 collective-permute-start.2
  3.7 0.5 collective-permute-start.3
  4.2 1.3 %collective-permute-start.4 = (bf16[272,256]{1,0:T(8,128)(2,1)}, bf16[272,256]{1,0:T(8,128)(2,1)S(1)}, u32[]{:S(2)}, u32[]{:S(2)}) collective-permute-start(bf16[272,256]{1,0:T(8,128)(2,1)} %get-tuple-element.54.message), channel_id=1, source_target_pairs={{0,8},{2,10},{4,12},{6,14},{8,16},{10,18},{12,20},{14,22},{16,24},... | collective-permute-start | bytes 417800 | tf_op jit(solution)/shard_map/ppermute | solution.py:27
  5.5 2.9 %collective-permute-start = (bf16[272,256]{1,0:T(8,128)(2,1)}, bf16[272,256]{1,0:T(8,128)(2,1)S(1)}, u32[]{:S(2)}, u32[]{:S(2)}) collective-permute-start(bf16[272,256]{1,0:T(8,128)(2,1)} %get-tuple-element.54.message), channel_id=1, source_target_pairs={{0,16},{2,18},{4,20},{6,22},{8,24},{10,26},{12,28},{14,30},{1,17},... | collective-permute-start | bytes 417800 | tf_op jit(solution)/shard_map/ppermute | solution.py:28
  8.5 0.0 collective-permute-done.3.facts_p
  8.5 3.2 %collective-permute-start.8 = (bf16[272,256]{1,0:T(8,128)(2,1)}, bf16[272,256]{1,0:T(8,128)(2,1)S(1)}, u32[]{:S(2)}, u32[]{:S(2)}) collective-permute-start(bf16[272,256]{1,0:T(8,128)(2,1)} %get-tuple-element.54.message), channel_id=1, source_target_pairs={{0,4},{2,6},{4,24},{6,26},{8,12},{10,14},{16,20},{18,22},{24,28},{... | collective-permute-start | bytes 417800 | tf_op jit(solution)/shard_map/ppermute | solution.py:28
  11.6 1.1 %constant_dynamic-slice_fusion = (bf16[128,1024]{1,0:T(8,128)(2,1)S(1)}, bf16[128,1024]{1,0:T(8,128)(2,1)S(1)}) fusion(bf16[128,2048]{1,0:T(8,128)(2,1)} %param.13, s32[]{:T(128)S(6)} %select_n.12, bf16[128,2048]{1,0:T(8,128)(2,1)} %param.10), kind=kLoop, calls=%fused_computation | loop fusion | bytes 1048580 | tf_op jit(solution)/shard_map/dynamic_slice | solution.py:503
  12.7 0.8 %collective-permute-start.5 = (bf16[272,256]{1,0:T(8,128)(2,1)}, bf16[272,256]{1,0:T(8,128)(2,1)S(1)}, u32[]{:S(2)}, u32[]{:S(2)}) collective-permute-start(bf16[272,256]{1,0:T(8,128)(2,1)} %get-tuple-element.54.message), channel_id=1, source_target_pairs={{0,2},{2,0},{4,6},{6,4},{8,10},{10,8},{12,14},{14,12},{16,18},{18,... | collective-permute-start | bytes 417800 | tf_op jit(solution)/shard_map/ppermute | solution.py:28
  13.6 0.0 collective-permute-done.2.grad_p
  13.6 0.2 collective-permute-start.6
  13.7 0.9 %copy-done.1 = bf16[272,256]{1,0:T(8,128)(2,1)S(1)} copy-done((bf16[272,256]{1,0:T(8,128)(2,1)S(1)}, bf16[272,256]{1,0:T(8,128)(2,1)}, u32[]{:S(2)}) %copy-start.1) | copy-done | bytes 139288
  14.7 0.7 %copy-done.2 = f32[16,128]{1,0:T(8,128)S(1)} copy-done((f32[16,128]{1,0:T(8,128)S(1)}, f32[16,128]{1,0:T(8,128)}, u32[]{:S(2)}) %copy-start.2) | copy-done | bytes 8216
  15.3 0.5 shard_map.122
  15.9 0.0 collective-permute-done.refs_2_
  15.9 0.5 collective-permute-start.7
  16.4 0.0 collective-permute-done.8.refs_1_
  16.4 3.6 %collective-permute-start.10 = (bf16[272,256]{1,0:T(8,128)(2,1)S(1)}, bf16[272,256]{1,0:T(8,128)(2,1)S(1)}, u32[]{:S(2)}, u32[]{:S(2)}) collective-permute-start(bf16[272,256]{1,0:T(8,128)(2,1)S(1)} %collective-permute-done.refs_2_), channel_id=1, source_target_pairs={{0,4},{2,6},{4,0},{6,2},{8,12},{10,14},{12,8},{14,10},{16,20},{18,... | collective-permute-start | bytes 417800 | tf_op jit(solution)/shard_map/ppermute | solution.py:28
  20.0 0.0 collective-permute-done.5.refs_3_.refs_4_
  20.0 0.3 collective-permute-start.11
  20.3 0.2 collective-permute-start.12
  20.5 0.0 collective-permute-done.6.refs_4_
  20.5 0.0 collective-permute-done.7.refs_5_
  20.5 3.9 %shard_map.123 = (bf16[2048,1024]{1,0:T(8,128)(2,1)S(1)}, bf16[128,768]{1,0:T(8,128)(2,1)S(1)}, bf16[8,768,256]{2,1,0:T(8,128)(2,1)S(1)}, f32[8,768,256]{2,1,0:T(8,128)S(1)}, f32[8,16,256]{2,1,0:T(8,128)S(1)}) custom-call(bf16[272,256]{1,0:T(8,128)(2,1)S(1)} %get-tuple-element.67.refs_0_, bf16[272,256]{1,0:T(8,128)(2,1)S(1)} %collective-permute-done.4.refs_1_, ...), custom_call_target="tpu_custom_call" | custom-call | tf_op jit(solution)/shard_map/pallas_call | solution.py:529
  24.5 0.3 collective-permute-start.13
  24.8 1.1 %collective-permute-done.13.refs_7_ = bf16[272,256]{1,0:T(8,128)(2,1)S(1)} collective-permute-done((bf16[272,256]{1,0:T(8,128)(2,1)S(1)}, bf16[272,256]{1,0:T(8,128)(2,1)S(1)}, u32[]{:S(2)}, u32[]{:S(2)}) %collective-permute-start.13) | collective-permute-done | bytes 139296 | tf_op jit(solution)/shard_map/ppermute | solution.py:28
  25.9 5.1 %shard_map.124 = (bf16[128,768]{1,0:T(8,128)(2,1)S(1)}, bf16[8,768,256]{2,1,0:T(8,128)(2,1)S(1)}, bf16[8,1536,256]{2,1,0:T(8,128)(2,1)S(1)}, bf16[256,256]{1,0:T(8,128)(2,1)S(1)}, bf16[512,256]{1,0:T(8,128)(2,1)S(1)}) custom-call(bf16[272,256]{1,0:T(8,128)(2,1)S(1)} %get-tuple-element.67.refs_0_, ...), custom_call_target="tpu_custom_call", output_to_operand_aliasing={{1}: (11, {})} | custom-call | flops 1 | bytes 1 | tf_op jit(solution)/shard_map/pallas_call | solution.py:554
  31.0 1.2 %collective-permute-start.18 = (bf16[512,256]{1,0:T(8,128)(2,1)S(1)}, bf16[512,256]{1,0:T(8,128)(2,1)S(1)}, u32[]{:S(2)}, u32[]{:S(2)}) collective-permute-start(bf16[512,256]{1,0:T(8,128)(2,1)S(1)} %get-tuple-element.88), channel_id=1, source_target_pairs={{0,4},{2,6},{4,0},{6,2},{8,12},{10,14},{12,8},{14,10},{16,20},{18,... | collective-permute-start | bytes 786440 | tf_op jit(solution)/shard_map/ppermute | solution.py:28
  32.2 4.8 %shard_map.125 = (bf16[1024,256]{1,0:T(8,128)(2,1)S(1)}, bf16[2048,1024]{1,0:T(8,128)(2,1)S(1)}, f32[256,256]{1,0:T(8,128)S(1)}, bf16[256,256]{1,0:T(8,128)(2,1)S(1)}, bf16[256,256]{1,0:T(8,128)(2,1)S(1)}) custom-call(bf16[2048,128]{1,0:T(8,128)(2,1)S(1)} %get-tuple-element.63.refs_6_.refs_8_.refs_0_, ...), custom_call_target="tpu_custom_call" | custom-call | flops 1 | bytes 1 | tf_op jit(solution)/shard_map/pallas_call | solution.py:596
  37.1 1.4 %shard_map.126 = (bf16[128,2048]{1,0:T(8,128)(2,1)S(1)}, bf16[128,512]{1,0:T(8,128)(2,1)S(1)}, bf16[128,512]{1,0:T(8,128)(2,1)S(1)}, bf16[128,512]{1,0:T(8,128)(2,1)S(1)}, bf16[128,512]{1,0:T(8,128)(2,1)S(1)}) custom-call(bf16[1024,256]{1,0:T(8,128)(2,1)S(1)} %get-tuple-element.81.dq, bf16[2048,1024]{1,0:T(8,128)(2,1)S(1)} %get-tuple-element.82.weight), custom_call_target="tpu_custom_call" | custom-call | flops 1 | bytes 1 | tf_op jit(solution)/shard_map/pallas_call | solution.py:366
  38.4 0.7 %collective-permute-start.14 = (bf16[128,512]{1,0:T(8,128)(2,1)S(1)}, bf16[128,512]{1,0:T(8,128)(2,1)S(1)}, u32[]{:S(2)}, u32[]{:S(2)}) collective-permute-start(bf16[128,512]{1,0:T(8,128)(2,1)S(1)} %get-tuple-element.84), channel_id=1, source_target_pairs={{0,2},{2,0},{4,6},{6,4},{8,10},{10,8},{12,14},{14,12},{16,18},{18,... | collective-permute-start | bytes 393224 | tf_op jit(solution)/shard_map/ppermute | solution.py:28
  39.1 0.1 collective-permute-start.15
  39.2 0.4 collective-permute-start.16
  39.6 0.1 collective-permute-start.17
  39.7 1.4 %shard_map.128 = (bf16[128,2048]{1,0:T(8,128)(2,1)S(1)}, bf16[128,2048]{1,0:T(8,128)(2,1)S(1)}) custom-call(bf16[1024,256]{1,0:T(8,128)(2,1)S(1)} %get-tuple-element.81.dq, bf16[2048,1024]{1,0:T(8,128)(2,1)S(1)} %get-tuple-element.89.weight), custom_call_target="tpu_custom_call" | custom-call | flops 1 | bytes 1 | tf_op jit(solution)/shard_map/pallas_call | solution.py:366
  41.1 0.0 collective-permute-done.15.refs_1_
  41.1 0.1 shard_map.127
  41.3 1.3 %collective-permute-start.23 = (bf16[128,2048]{1,0:T(8,128)(2,1)S(1)}, bf16[128,2048]{1,0:T(8,128)(2,1)S(1)}, u32[]{:S(2)}, u32[]{:S(2)}) collective-permute-start(bf16[128,2048]{1,0:T(8,128)(2,1)S(1)} %shard_map.127), channel_id=1, source_target_pairs={{0,1},{1,0},{2,3},{3,2},{4,5},{5,4},{6,7},{7,6},{8,9},{9,8},{10,11... | collective-permute-start | bytes 1572872 | tf_op jit(solution)/shard_map/ppermute | solution.py:28
  42.6 0.7 %collective-permute-start.24 = (bf16[128,2048]{1,0:T(8,128)(2,1)S(1)}, bf16[128,2048]{1,0:T(8,128)(2,1)S(1)}, u32[]{:S(2)}, u32[]{:S(2)}) collective-permute-start(bf16[128,2048]{1,0:T(8,128)(2,1)S(1)} %get-tuple-element.99), channel_id=1, source_target_pairs={{0,2},{2,0},{4,6},{6,4},{8,10},{10,8},{12,14},{14,12},{16,18},{18,... | collective-permute-start | bytes 1572872 | tf_op jit(solution)/shard_map/ppermute | solution.py:28
  43.3 0.1 shard_map.129
  43.3 3.1 %collective-permute-start.19 = (bf16[256,256]{1,0:T(8,128)(2,1)S(1)}, bf16[256,256]{1,0:T(8,128)(2,1)S(1)}, u32[]{:S(2)}, u32[]{:S(2)}) collective-permute-start(bf16[256,256]{1,0:T(8,128)(2,1)S(1)} %get-tuple-element.92), channel_id=1, source_target_pairs={{0,16},{2,18},{4,20},{6,22},{8,24},{10,26},{12,28},{14,30},{16,0},... | collective-permute-start | bytes 393224 | tf_op jit(solution)/shard_map/ppermute | solution.py:27
  46.5 1.4 %collective-permute-start.21 = (bf16[256,256]{1,0:T(8,128)(2,1)S(1)}, bf16[256,256]{1,0:T(8,128)(2,1)S(1)}, u32[]{:S(2)}, u32[]{:S(2)}) collective-permute-start(bf16[256,256]{1,0:T(8,128)(2,1)S(1)} %get-tuple-element.94), channel_id=1, source_target_pairs={{0,12},{2,14},{4,0},{6,2},{8,20},{10,22},{12,8},{14,10},{16,28},{1... | collective-permute-start | bytes 393224 | tf_op jit(solution)/shard_map/ppermute | solution.py:27
  47.9 4.4 %collective-permute-done.19.refs_1_ = bf16[256,256]{1,0:T(8,128)(2,1)S(1)} collective-permute-done((bf16[256,256]{1,0:T(8,128)(2,1)S(1)}, bf16[256,256]{1,0:T(8,128)(2,1)S(1)}, u32[]{:S(2)}, u32[]{:S(2)}) %collective-permute-start.19) | collective-permute-done | bytes 131104 | tf_op jit(solution)/shard_map/ppermute | solution.py:27
  52.3 4.9 %collective-permute-done.20.refs_1_ = bf16[256,256]{1,0:T(8,128)(2,1)S(1)} collective-permute-done((bf16[256,256]{1,0:T(8,128)(2,1)S(1)}, bf16[256,256]{1,0:T(8,128)(2,1)S(1)}, u32[]{:S(2)}, u32[]{:S(2)}) %collective-permute-start.20) | collective-permute-done | bytes 131104 | tf_op jit(solution)/shard_map/ppermute | solution.py:27
  57.2 0.8 %collective-permute-start.22 = (bf16[128,256]{1,0:T(8,128)(2,1)S(1)}, bf16[128,256]{1,0:T(8,128)(2,1)S(1)}, u32[]{:S(2)}, u32[]{:S(2)}) collective-permute-start(bf16[128,256]{1,0:T(8,128)(2,1)S(1)} %get-tuple-element.95), channel_id=1, source_target_pairs={{0,2},{2,0},{4,6},{6,4},{8,10},{10,8},{12,14},{14,12},{16,18},{18,... | collective-permute-start | bytes 196616 | tf_op jit(solution)/shard_map/ppermute | solution.py:28
  58.1 1.0 %shard_map.133 = bf16[128,2048]{1,0:T(8,128)(2,1)} custom-call(bf16[128,2048]{1,0:T(8,128)(2,1)S(1)} %get-tuple-element.96.refs_0_, bf16[128,2048]{1,0:T(8,128)(2,1)S(1)} %collective-permute-done.23.refs_1_, bf16[128,2048]{1,0:T(8,128)(2,1)S(1)} %collective-permute-done.24.refs_2_), custom_call_target="tpu_custom_call" | custom-call | flops 1 | bytes 1 | tf_op jit(solution)/shard_map/pallas_call | solution.py:404
  59.1 0.9 %shard_map.134 = (bf16[128,256]{1,0:T(8,128)(2,1)}, bf16[128,256]{1,0:T(8,128)(2,1)}) custom-call(f32[128,256]{1,0:T(8,128)S(1)} %get-tuple-element.101.keep, bf16[128,256]{1,0:T(8,128)(2,1)S(1)} %collective-permute-done.22.recv, bf16[128,256]{1,0:T(8,128)(2,1)S(1)} %copy-done, f32[1,128]{1,0:T(1,128)S(1)} %bitcast.7), custom_call_target="tpu_custom_call" | custom-call | tf_op jit(solution)/shard_map/pallas_call | solution.py:644
  (25 shorter events, 0.1 us)
Async XLA Ops:
  3.0 10.5 %collective-permute-start.1 = (bf16[128,2048]{1,0:T(8,128)(2,1)}, bf16[128,2048]{1,0:T(8,128)(2,1)S(1)}, u32[]{:S(2)}, u32[]{:S(2)}) collective-permute-start(bf16[128,2048]{1,0:T(8,128)(2,1)} %param.10), channel_id=1, source_target_pairs={{0,2},{2,0},{4,6},{6,4},{8,10},{10,8},{12,14},{14,12},{16,18},{18,... | collective-permute-start | bytes 1572872 | tf_op jit(solution)/shard_map/ppermute | solution.py:28
  3.7 9.9 %collective-permute-start.2 = (bf16[128,2048]{1,0:T(8,128)(2,1)}, bf16[128,2048]{1,0:T(8,128)(2,1)S(1)}, u32[]{:S(2)}, u32[]{:S(2)}) collective-permute-start(bf16[128,2048]{1,0:T(8,128)(2,1)} %param.13), channel_id=1, source_target_pairs={{0,2},{2,0},{4,6},{6,4},{8,10},{10,8},{12,14},{14,12},{16,18},{18,... | collective-permute-start | bytes 1572872 | tf_op jit(solution)/shard_map/ppermute | solution.py:28
  3.7 4.7 %collective-permute-start.3 = (f32[16,128]{1,0:T(8,128)}, f32[16,128]{1,0:T(8,128)S(1)}, u32[]{:S(2)}, u32[]{:S(2)}) collective-permute-start(f32[16,128]{1,0:T(8,128)} %get-tuple-element.57.facts), channel_id=1, source_target_pairs={{0,2},{2,0},{4,6},{6,4},{8,10},{10,8},{12,14},{14,12},{16,18},{18,... | collective-permute-start | bytes 24584 | tf_op jit(solution)/shard_map/ppermute | solution.py:28
  4.2 8.5 %collective-permute-start.4 = (bf16[272,256]{1,0:T(8,128)(2,1)}, bf16[272,256]{1,0:T(8,128)(2,1)S(1)}, u32[]{:S(2)}, u32[]{:S(2)}) collective-permute-start(bf16[272,256]{1,0:T(8,128)(2,1)} %get-tuple-element.54.message), channel_id=1, source_target_pairs={{0,8},{2,10},{4,12},{6,14},{8,16},{10,18},{12,20},{14,22},{16,24},... | collective-permute-start | bytes 417800 | tf_op jit(solution)/shard_map/ppermute | solution.py:27
  5.5 10.4 %collective-permute-start = (bf16[272,256]{1,0:T(8,128)(2,1)}, bf16[272,256]{1,0:T(8,128)(2,1)S(1)}, u32[]{:S(2)}, u32[]{:S(2)}) collective-permute-start(bf16[272,256]{1,0:T(8,128)(2,1)} %get-tuple-element.54.message), channel_id=1, source_target_pairs={{0,16},{2,18},{4,20},{6,22},{8,24},{10,26},{12,28},{14,30},{1,17},... | collective-permute-start | bytes 417800 | tf_op jit(solution)/shard_map/ppermute | solution.py:28
  8.5 7.9 %collective-permute-start.8 = (bf16[272,256]{1,0:T(8,128)(2,1)}, bf16[272,256]{1,0:T(8,128)(2,1)S(1)}, u32[]{:S(2)}, u32[]{:S(2)}) collective-permute-start(bf16[272,256]{1,0:T(8,128)(2,1)} %get-tuple-element.54.message), channel_id=1, source_target_pairs={{0,4},{2,6},{4,24},{6,26},{8,12},{10,14},{16,20},{18,22},{24,28},{... | collective-permute-start | bytes 417800 | tf_op jit(solution)/shard_map/ppermute | solution.py:28
  12.7 7.3 %collective-permute-start.5 = (bf16[272,256]{1,0:T(8,128)(2,1)}, bf16[272,256]{1,0:T(8,128)(2,1)S(1)}, u32[]{:S(2)}, u32[]{:S(2)}) collective-permute-start(bf16[272,256]{1,0:T(8,128)(2,1)} %get-tuple-element.54.message), channel_id=1, source_target_pairs={{0,2},{2,0},{4,6},{6,4},{8,10},{10,8},{12,14},{14,12},{16,18},{18,... | collective-permute-start | bytes 417800 | tf_op jit(solution)/shard_map/ppermute | solution.py:28
  13.6 6.7 %collective-permute-start.9 = (bf16[272,256]{1,0:T(8,128)(2,1)S(1)}, bf16[272,256]{1,0:T(8,128)(2,1)S(1)}, u32[]{:S(2)}, u32[]{:S(2)}) collective-permute-start(bf16[272,256]{1,0:T(8,128)(2,1)S(1)} %collective-permute-done.4.refs_1_), channel_id=1, source_target_pairs={{0,4},{2,6},{4,0},{6,2},{8,12},{10,14},{12,8},{14,10},{16,20},{18,... | collective-permute-start | bytes 417800 | tf_op jit(solution)/shard_map/ppermute | solution.py:28
  13.6 6.9 %collective-permute-start.6 = (bf16[272,256]{1,0:T(8,128)(2,1)S(1)}, bf16[272,256]{1,0:T(8,128)(2,1)S(1)}, u32[]{:S(2)}, u32[]{:S(2)}) collective-permute-start(bf16[272,256]{1,0:T(8,128)(2,1)S(1)} %collective-permute-done.4.refs_1_), channel_id=1, source_target_pairs={{0,2},{2,0},{4,6},{6,4},{8,10},{10,8},{12,14},{14,12},{16,18},{18,... | collective-permute-start | bytes 417800 | tf_op jit(solution)/shard_map/ppermute | solution.py:28
  13.7 0.9 %copy-start.1 = (bf16[272,256]{1,0:T(8,128)(2,1)S(1)}, bf16[272,256]{1,0:T(8,128)(2,1)}, u32[]{:S(2)}) copy-start(bf16[272,256]{1,0:T(8,128)(2,1)} %get-tuple-element.54.message) | copy-start | bytes 417796
  14.7 0.7 %copy-start.2 = (f32[16,128]{1,0:T(8,128)S(1)}, f32[16,128]{1,0:T(8,128)}, u32[]{:S(2)}) copy-start(f32[16,128]{1,0:T(8,128)} %get-tuple-element.57.facts) | copy-start | bytes 24580
  15.9 4.6 %collective-permute-start.7 = (bf16[272,256]{1,0:T(8,128)(2,1)S(1)}, bf16[272,256]{1,0:T(8,128)(2,1)S(1)}, u32[]{:S(2)}, u32[]{:S(2)}) collective-permute-start(bf16[272,256]{1,0:T(8,128)(2,1)S(1)} %collective-permute-done.refs_2_), channel_id=1, source_target_pairs={{0,2},{2,0},{4,6},{6,4},{8,10},{10,8},{12,14},{14,12},{16,18},{18,... | collective-permute-start | bytes 417800 | tf_op jit(solution)/shard_map/ppermute | solution.py:28
  16.4 8.1 %collective-permute-start.10 = (bf16[272,256]{1,0:T(8,128)(2,1)S(1)}, bf16[272,256]{1,0:T(8,128)(2,1)S(1)}, u32[]{:S(2)}, u32[]{:S(2)}) collective-permute-start(bf16[272,256]{1,0:T(8,128)(2,1)S(1)} %collective-permute-done.refs_2_), channel_id=1, source_target_pairs={{0,4},{2,6},{4,0},{6,2},{8,12},{10,14},{12,8},{14,10},{16,20},{18,... | collective-permute-start | bytes 417800 | tf_op jit(solution)/shard_map/ppermute | solution.py:28
  20.0 4.8 %collective-permute-start.11 = (bf16[272,256]{1,0:T(8,128)(2,1)S(1)}, bf16[272,256]{1,0:T(8,128)(2,1)S(1)}, u32[]{:S(2)}, u32[]{:S(2)}) collective-permute-start(bf16[272,256]{1,0:T(8,128)(2,1)S(1)} %collective-permute-done.8.refs_1_), channel_id=1, source_target_pairs={{0,2},{2,0},{4,6},{6,4},{8,10},{10,8},{12,14},{14,12},{16,18},{18,... | collective-permute-start | bytes 417800 | tf_op jit(solution)/shard_map/ppermute | solution.py:28
  20.3 4.5 %collective-permute-start.12 = (bf16[272,256]{1,0:T(8,128)(2,1)S(1)}, bf16[272,256]{1,0:T(8,128)(2,1)S(1)}, u32[]{:S(2)}, u32[]{:S(2)}) collective-permute-start(bf16[272,256]{1,0:T(8,128)(2,1)S(1)} %collective-permute-done.9.refs_2_), channel_id=1, source_target_pairs={{0,2},{2,0},{4,6},{6,4},{8,10},{10,8},{12,14},{14,12},{16,18},{18,... | collective-permute-start | bytes 417800 | tf_op jit(solution)/shard_map/ppermute | solution.py:28
  24.5 1.4 %collective-permute-start.13 = (bf16[272,256]{1,0:T(8,128)(2,1)S(1)}, bf16[272,256]{1,0:T(8,128)(2,1)S(1)}, u32[]{:S(2)}, u32[]{:S(2)}) collective-permute-start(bf16[272,256]{1,0:T(8,128)(2,1)S(1)} %collective-permute-done.10.refs_3_), channel_id=1, source_target_pairs={{0,2},{2,0},{4,6},{6,4},{8,10},{10,8},{12,14},{14,12},{16,18},{18,... | collective-permute-start | bytes 417800 | tf_op jit(solution)/shard_map/ppermute | solution.py:28
  31.0 10.3 %collective-permute-start.18 = (bf16[512,256]{1,0:T(8,128)(2,1)S(1)}, bf16[512,256]{1,0:T(8,128)(2,1)S(1)}, u32[]{:S(2)}, u32[]{:S(2)}) collective-permute-start(bf16[512,256]{1,0:T(8,128)(2,1)S(1)} %get-tuple-element.88), channel_id=1, source_target_pairs={{0,4},{2,6},{4,0},{6,2},{8,12},{10,14},{12,8},{14,10},{16,20},{18,... | collective-permute-start | bytes 786440 | tf_op jit(solution)/shard_map/ppermute | solution.py:28
  38.4 2.7 %collective-permute-start.14 = (bf16[128,512]{1,0:T(8,128)(2,1)S(1)}, bf16[128,512]{1,0:T(8,128)(2,1)S(1)}, u32[]{:S(2)}, u32[]{:S(2)}) collective-permute-start(bf16[128,512]{1,0:T(8,128)(2,1)S(1)} %get-tuple-element.84), channel_id=1, source_target_pairs={{0,2},{2,0},{4,6},{6,4},{8,10},{10,8},{12,14},{14,12},{16,18},{18,... | collective-permute-start | bytes 393224 | tf_op jit(solution)/shard_map/ppermute | solution.py:28
  39.1 2.0 %collective-permute-start.15 = (bf16[128,512]{1,0:T(8,128)(2,1)S(1)}, bf16[128,512]{1,0:T(8,128)(2,1)S(1)}, u32[]{:S(2)}, u32[]{:S(2)}) collective-permute-start(bf16[128,512]{1,0:T(8,128)(2,1)S(1)} %get-tuple-element.85), channel_id=1, source_target_pairs={{0,2},{2,0},{4,6},{6,4},{8,10},{10,8},{12,14},{14,12},{16,18},{18,... | collective-permute-start | bytes 393224 | tf_op jit(solution)/shard_map/ppermute | solution.py:28
  39.2 1.9 %collective-permute-start.16 = (bf16[128,512]{1,0:T(8,128)(2,1)S(1)}, bf16[128,512]{1,0:T(8,128)(2,1)S(1)}, u32[]{:S(2)}, u32[]{:S(2)}) collective-permute-start(bf16[128,512]{1,0:T(8,128)(2,1)S(1)} %get-tuple-element.86), channel_id=1, source_target_pairs={{0,2},{2,0},{4,6},{6,4},{8,10},{10,8},{12,14},{14,12},{16,18},{18,... | collective-permute-start | bytes 393224 | tf_op jit(solution)/shard_map/ppermute | solution.py:28
  39.6 1.5 %collective-permute-start.17 = (bf16[128,512]{1,0:T(8,128)(2,1)S(1)}, bf16[128,512]{1,0:T(8,128)(2,1)S(1)}, u32[]{:S(2)}, u32[]{:S(2)}) collective-permute-start(bf16[128,512]{1,0:T(8,128)(2,1)S(1)} %get-tuple-element.87), channel_id=1, source_target_pairs={{0,2},{2,0},{4,6},{6,4},{8,10},{10,8},{12,14},{14,12},{16,18},{18,... | collective-permute-start | bytes 393224 | tf_op jit(solution)/shard_map/ppermute | solution.py:28
  39.7 19.3 %copy-start = (bf16[128,256]{1,0:T(8,128)(2,1)S(1)}, bf16[128,256]{1,0:T(8,128)(2,1)}, u32[]{:S(2)}) copy-start(bf16[128,256]{1,0:T(8,128)(2,1)} %key.3) | copy-start | bytes 196612
  39.7 19.3 %copy-start.3 = (f32[128]{0:T(128)S(1)}, f32[128]{0:T(128)}, u32[]{:S(2)}) copy-start(f32[128]{0:T(128)} %param.15) | copy-start | bytes 1540
  41.3 16.8 %collective-permute-start.23 = (bf16[128,2048]{1,0:T(8,128)(2,1)S(1)}, bf16[128,2048]{1,0:T(8,128)(2,1)S(1)}, u32[]{:S(2)}, u32[]{:S(2)}) collective-permute-start(bf16[128,2048]{1,0:T(8,128)(2,1)S(1)} %shard_map.127), channel_id=1, source_target_pairs={{0,1},{1,0},{2,3},{3,2},{4,5},{5,4},{6,7},{7,6},{8,9},{9,8},{10,11... | collective-permute-start | bytes 1572872 | tf_op jit(solution)/shard_map/ppermute | solution.py:28
  42.6 15.5 %collective-permute-start.24 = (bf16[128,2048]{1,0:T(8,128)(2,1)S(1)}, bf16[128,2048]{1,0:T(8,128)(2,1)S(1)}, u32[]{:S(2)}, u32[]{:S(2)}) collective-permute-start(bf16[128,2048]{1,0:T(8,128)(2,1)S(1)} %get-tuple-element.99), channel_id=1, source_target_pairs={{0,2},{2,0},{4,6},{6,4},{8,10},{10,8},{12,14},{14,12},{16,18},{18,... | collective-permute-start | bytes 1572872 | tf_op jit(solution)/shard_map/ppermute | solution.py:28
  43.3 8.9 %collective-permute-start.19 = (bf16[256,256]{1,0:T(8,128)(2,1)S(1)}, bf16[256,256]{1,0:T(8,128)(2,1)S(1)}, u32[]{:S(2)}, u32[]{:S(2)}) collective-permute-start(bf16[256,256]{1,0:T(8,128)(2,1)S(1)} %get-tuple-element.92), channel_id=1, source_target_pairs={{0,16},{2,18},{4,20},{6,22},{8,24},{10,26},{12,28},{14,30},{16,0},... | collective-permute-start | bytes 393224 | tf_op jit(solution)/shard_map/ppermute | solution.py:27
  46.5 10.7 %collective-permute-start.20 = (bf16[256,256]{1,0:T(8,128)(2,1)S(1)}, bf16[256,256]{1,0:T(8,128)(2,1)S(1)}, u32[]{:S(2)}, u32[]{:S(2)}) collective-permute-start(bf16[256,256]{1,0:T(8,128)(2,1)S(1)} %get-tuple-element.93), channel_id=1, source_target_pairs={{0,24},{2,26},{4,28},{6,30},{8,0},{10,2},{12,4},{14,6},{16,8},{18,... | collective-permute-start | bytes 393224 | tf_op jit(solution)/shard_map/ppermute | solution.py:27
  46.5 10.7 %collective-permute-start.21 = (bf16[256,256]{1,0:T(8,128)(2,1)S(1)}, bf16[256,256]{1,0:T(8,128)(2,1)S(1)}, u32[]{:S(2)}, u32[]{:S(2)}) collective-permute-start(bf16[256,256]{1,0:T(8,128)(2,1)S(1)} %get-tuple-element.94), channel_id=1, source_target_pairs={{0,12},{2,14},{4,0},{6,2},{8,20},{10,22},{12,8},{14,10},{16,28},{1... | collective-permute-start | bytes 393224 | tf_op jit(solution)/shard_map/ppermute | solution.py:27
  57.2 1.8 %collective-permute-start.22 = (bf16[128,256]{1,0:T(8,128)(2,1)S(1)}, bf16[128,256]{1,0:T(8,128)(2,1)S(1)}, u32[]{:S(2)}, u32[]{:S(2)}) collective-permute-start(bf16[128,256]{1,0:T(8,128)(2,1)S(1)} %get-tuple-element.95), channel_id=1, source_target_pairs={{0,2},{2,0},{4,6},{6,4},{8,10},{10,8},{12,14},{14,12},{16,18},{18,... | collective-permute-start | bytes 196616 | tf_op jit(solution)/shard_map/ppermute | solution.py:28
